TPU v7x, 32 devices: a whole 2x2x4 slice. The times are simulated.
32 devices in a mesh: rows: 4 (over y, x), batch: 8 (over z, core).
Axes of the slice: x: 2, y: 2, z: 4, core: 2. Of those that a mesh axis runs over, the one named last changes fastest.
Arguments:
- images: float32 [64, 16, 16, 1024], P('batch', 'rows'), may hold values from -6 to 6
- w_reduce: float32 [1024, 256], replicated, may hold values from -0.1875 to 0.1875
- gain_one: float32 [256], replicated, may hold values from 0.25 to 1.75
- shift_one: float32 [256], replicated, may hold values from -3 to 3
- w_group: float32 [3, 3, 128, 512], replicated, may hold values from -0.1875 to 0.1875
- gain_two: float32 [512], replicated, may hold values from 0.25 to 1.75
- shift_two: float32 [512], replicated, may hold values from -3 to 3
- w_squeeze: float32 [256, 128], replicated, may hold values from -0.375 to 0.375
- gain_fc: float32 [128], replicated, may hold values from 0.25 to 1.75
- shift_fc: float32 [128], replicated, may hold values from -3 to 3
- w_excite: float32 [128, 512], replicated, may hold values from -0.75 to 0.75
- excite_bias: float32 [512], replicated, may hold values from -4 to 4
- w_expand: float32 [256, 1024], replicated, may hold values from -0.375 to 0.375
- gain_three: float32 [1024], replicated, may hold values from 0.25 to 1.75
- shift_three: float32 [1024], replicated, may hold values from -3 to 3
- valid_rows: int32 [64, 16], P('batch'), may hold values from 0 to 1, as said below
- valid_cols: int32 [64, 16], P('batch'), may hold values from 0 to 1, as said below
- cotangent: float32 [64, 16, 16, 1024], P('batch', 'rows'), may hold values from -6 to 6
Outputs:
- block_out: float32 [64, 16, 16, 1024], P('batch', 'rows')
- grad_images: float32 [64, 16, 16, 1024], P('batch', 'rows')
- grad_w_reduce: float32 [1024, 256], replicated
- grad_gain_one: float32 [256], replicated
- grad_shift_one: float32 [256], replicated
- grad_w_group: float32 [3, 3, 128, 512], replicated
- grad_gain_two: float32 [512], replicated
- grad_shift_two: float32 [512], replicated
- grad_w_squeeze: float32 [256, 128], replicated
- grad_gain_fc: float32 [128], replicated
- grad_shift_fc: float32 [128], replicated
- grad_w_excite: float32 [128, 512], replicated
- grad_excite_bias: float32 [512], replicated
- grad_w_expand: float32 [256, 1024], replicated
- grad_gain_three: float32 [1024], replicated
- grad_shift_three: float32 [1024], replicated
Inputs may be any that keep to these rules, and one draw needn't show every extreme that they name: `valid_rows`: each image's valid rows form one run of 12, 14 or 16 consecutive rows, and its valid columns a run of the same length; at least one image is valid on the whole map. `valid_cols`: each image's valid columns form one run as long as its run of valid rows.
All inputs are finite; a program needn't handle non-finite values.
Results may differ from a plain program's by a relative error of at most 0.0003.
Values sent between devices are 32-bit elements; how exact they have to be, the bound alone decides.
No kernel may reach another device: no remote copies, remote signals or barrier semaphores. Data moves between devices by JAX's collectives and lax.ppermute only.
A program may use at most 128 MiB of HBM per device.

v0:
```python
import jax
import jax.numpy as jnp
from jax import lax
from jax.sharding import PartitionSpec as P

epsilon = 1e-05
highest = lax.Precision.HIGHEST


def extended(cells, sides, width):
    for axis, dim in sides:
        count = lax.axis_size(axis)
        ends = count - 1
        head = lax.slice_in_dim(cells, 0, width, axis=dim)
        tail = lax.slice_in_dim(cells, cells.shape[dim] - width, cells.shape[dim], axis=dim)
        cells = jnp.concatenate(
            [
                lax.ppermute(tail, axis, [(i, (i + 1) % count) for i in range(ends)]),
                cells,
                lax.ppermute(head, axis, [((i + 1) % count, i) for i in range(ends)]),
            ],
            axis=dim,
        )
    return cells


def smooth(values):
    return values * jax.nn.sigmoid(values)


def smooth_slope(values):
    sigma = jax.nn.sigmoid(values)
    return sigma * (1.0 + values * (1.0 - sigma))


def pad_width(values):
    return jnp.pad(values, ((0, 0), (0, 0), (1, 1), (0, 0)))


def normalize(values, validity, own_count):
    sum_values, total_count = lax.psum(
        (jnp.sum(values * validity, axis=(0, 1, 2)), own_count), ("rows", "batch")
    )
    mean_value = sum_values / total_count
    centered = values - mean_value
    variance = (
        lax.psum(jnp.sum(centered * centered * validity, axis=(0, 1, 2)), ("rows", "batch"))
        / total_count
    )
    inv_std = lax.rsqrt(variance + epsilon)
    return ((values - mean_value) * inv_std, inv_std, total_count)


def norm_back(grad_out, normed, inv_std, gain, total_count, validity):
    sum_grad, sum_cross = lax.psum(
        (jnp.sum(grad_out, axis=(0, 1, 2)), jnp.sum(grad_out * normed, axis=(0, 1, 2))),
        ("rows", "batch"),
    )
    grad_in = (
        gain * inv_std * (grad_out - sum_grad / total_count - normed * sum_cross / total_count)
    )
    return (grad_in * validity, sum_cross, sum_grad)


def group_conv(padded, kernel):
    batch_count = padded.shape[0]
    row_count = padded.shape[1] - 2
    col_count = padded.shape[2] - 2
    group_in = kernel.shape[2]
    group_out = kernel.shape[3] // 2
    grouped = padded.reshape(batch_count, row_count + 2, col_count + 2, 2, group_in)
    kernel_split = kernel.reshape(3, 3, group_in, 2, group_out)
    total = jnp.zeros((batch_count, row_count, col_count, 2, group_out), jnp.float32)
    for tap_row in range(3):
        for tap_col in range(3):
            window = grouped[:, tap_row : tap_row + row_count, tap_col : tap_col + col_count]
            total = total + jnp.einsum(
                "bhwgi,igo->bhwgo", window, kernel_split[tap_row, tap_col], precision=highest
            )
    return total.reshape(batch_count, row_count, col_count, 2 * group_out)


def group_kernel_grad(padded, grad_out):
    batch_count, row_count, col_count, out_width = grad_out.shape
    group_in = padded.shape[3] // 2
    grouped = padded.reshape(batch_count, row_count + 2, col_count + 2, 2, group_in)
    grad_split = grad_out.reshape(batch_count, row_count, col_count, 2, out_width // 2)
    tap_grads = []
    for tap_row in range(3):
        for tap_col in range(3):
            window = grouped[:, tap_row : tap_row + row_count, tap_col : tap_col + col_count]
            tap_grads.append(jnp.einsum("bhwgi,bhwgo->igo", window, grad_split, precision=highest))
    return jnp.stack(tap_grads).reshape(3, 3, group_in, out_width)


def group_input_grad(padded_grad, kernel):
    batch_count = padded_grad.shape[0]
    row_count = padded_grad.shape[1] - 2
    col_count = padded_grad.shape[2] - 2
    group_in = kernel.shape[2]
    group_out = kernel.shape[3] // 2
    grouped = padded_grad.reshape(batch_count, row_count + 2, col_count + 2, 2, group_out)
    kernel_split = kernel.reshape(3, 3, group_in, 2, group_out)
    total = jnp.zeros((batch_count, row_count, col_count, 2, group_in), jnp.float32)
    for tap_row in range(3):
        for tap_col in range(3):
            window = grouped[
                :, 2 - tap_row : 2 - tap_row + row_count, 2 - tap_col : 2 - tap_col + col_count
            ]
            total = total + jnp.einsum(
                "bhwgo,igo->bhwgi", window, kernel_split[tap_row, tap_col], precision=highest
            )
    return total.reshape(batch_count, row_count, col_count, 2 * group_in)


def on_device(
    images,
    w_reduce,
    gain_one,
    shift_one,
    w_group,
    gain_two,
    shift_two,
    w_squeeze,
    gain_fc,
    shift_fc,
    w_excite,
    excite_bias,
    w_expand,
    gain_three,
    shift_three,
    valid_rows,
    valid_cols,
    cotangent,
):
    batch_count, row_count, col_count, chan_width = images.shape
    mid_width = w_reduce.shape[1]
    row_start = lax.axis_index("rows") * row_count
    row_valid = valid_rows.astype(jnp.float32)
    col_valid = valid_cols.astype(jnp.float32)
    local_rows = lax.dynamic_slice_in_dim(row_valid, row_start, row_count, 1)
    validity = local_rows[:, :, None, None] * col_valid[:, None, :, None]
    pixels = (jnp.sum(row_valid, axis=1) * jnp.sum(col_valid, axis=1))[:, None]
    own_count = jnp.sum(validity)
    first_row = (lax.axis_index("rows") == 0).astype(jnp.float32)
    z_one = jnp.einsum("bhwc,cm->bhwm", images, w_reduce, precision=highest)
    normed_one, inv_one, total_count = normalize(z_one, validity, own_count)
    y_one = normed_one * gain_one + shift_one
    a_one = smooth(y_one) * validity
    padded_one = pad_width(extended(a_one, (("rows", 1),), 1))
    z_two = group_conv(padded_one, w_group)
    normed_two, inv_two, total_count = normalize(z_two, validity, own_count)
    y_two = normed_two * gain_two + shift_two
    a_two = smooth(y_two) * validity
    half_first = a_two[..., :mid_width]
    half_second = a_two[..., mid_width:]
    pooled = lax.psum(jnp.sum(half_first + half_second, axis=(1, 2)), "rows") / pixels
    f_one = jnp.dot(pooled, w_squeeze, precision=highest)
    fc_sum, fc_squares = lax.psum((jnp.sum(f_one, axis=0), jnp.sum(f_one * f_one, axis=0)), "batch")
    images_all = batch_count * lax.axis_size("batch")
    fc_mean = fc_sum / images_all
    fc_inv = lax.rsqrt(fc_squares / images_all - fc_mean * fc_mean + epsilon)
    fc_normed = (f_one - fc_mean) * fc_inv
    fc_pre = fc_normed * gain_fc + shift_fc
    fc_act = smooth(fc_pre)
    logits = jnp.dot(fc_act, w_excite, precision=highest) + excite_bias
    weights = jax.nn.softmax(jnp.stack([logits[:, :mid_width], logits[:, mid_width:]]), axis=0)
    att_first = weights[0][:, None, None, :]
    att_second = weights[1][:, None, None, :]
    mixed = att_first * half_first + att_second * half_second
    z_three = jnp.einsum("bhwm,mc->bhwc", mixed, w_expand, precision=highest)
    normed_three, inv_three, total_count = normalize(z_three, validity, own_count)
    pre_act = normed_three * gain_three + shift_three + images
    block_out = smooth(pre_act) * validity
    grad_pre = cotangent * validity * smooth_slope(pre_act)
    dz_three, grad_gain_three, grad_shift_three = norm_back(
        grad_pre, normed_three, inv_three, gain_three, total_count, validity
    )
    grad_w_expand = jnp.einsum("bhwm,bhwc->mc", mixed, dz_three, precision=highest)
    grad_mixed = jnp.einsum("bhwc,mc->bhwm", dz_three, w_expand, precision=highest)
    gate_first, gate_second = lax.psum(
        (
            jnp.sum(grad_mixed * half_first, axis=(1, 2)),
            jnp.sum(grad_mixed * half_second, axis=(1, 2)),
        ),
        "rows",
    )
    mean_gate = weights[0] * gate_first + weights[1] * gate_second
    grad_logits = jnp.concatenate(
        [weights[0] * (gate_first - mean_gate), weights[1] * (gate_second - mean_gate)], axis=1
    )
    grad_bias_term = jnp.sum(grad_logits, axis=0)
    grad_excite_term = jnp.dot(fc_act.T, grad_logits, precision=highest)
    grad_fc = jnp.dot(grad_logits, w_excite.T, precision=highest) * smooth_slope(fc_pre)
    grad_shift_fc, grad_gain_fc = lax.psum(
        (jnp.sum(grad_fc, axis=0), jnp.sum(grad_fc * fc_normed, axis=0)), "batch"
    )
    grad_f_one = (
        gain_fc
        * fc_inv
        * (grad_fc - grad_shift_fc / images_all - fc_normed * grad_gain_fc / images_all)
    )
    grad_squeeze_term = jnp.dot(pooled.T, grad_f_one, precision=highest)
    grad_pooled = jnp.dot(grad_f_one, w_squeeze.T, precision=highest) / pixels
    spread = grad_pooled[:, None, None, :]
    grad_a_two = jnp.concatenate(
        [att_first * grad_mixed + spread, att_second * grad_mixed + spread], axis=3
    )
    grad_y_two = grad_a_two * validity * smooth_slope(y_two)
    dz_two, grad_gain_two, grad_shift_two = norm_back(
        grad_y_two, normed_two, inv_two, gain_two, total_count, validity
    )
    grad_group_term = group_kernel_grad(padded_one, dz_two)
    padded_grad = pad_width(extended(dz_two, (("rows", 1),), 1))
    grad_a_one = group_input_grad(padded_grad, w_group)
    grad_y_one = grad_a_one * validity * smooth_slope(y_one)
    dz_one, grad_gain_one, grad_shift_one = norm_back(
        grad_y_one, normed_one, inv_one, gain_one, total_count, validity
    )
    grad_reduce_term = jnp.einsum("bhwc,bhwm->cm", images, dz_one, precision=highest)
    grad_images = jnp.einsum("bhwm,cm->bhwc", dz_one, w_reduce, precision=highest) + grad_pre
    grad_w_reduce, grad_w_group, grad_w_expand, grad_w_squeeze, grad_w_excite, grad_excite_bias = (
        lax.psum(
            (
                grad_reduce_term,
                grad_group_term,
                grad_w_expand,
                grad_squeeze_term * first_row,
                grad_excite_term * first_row,
                grad_bias_term * first_row,
            ),
            ("rows", "batch"),
        )
    )
    return (
        block_out,
        grad_images,
        grad_w_reduce,
        grad_gain_one,
        grad_shift_one,
        grad_w_group,
        grad_gain_two,
        grad_shift_two,
        grad_w_squeeze,
        grad_gain_fc,
        grad_shift_fc,
        grad_w_excite,
        grad_excite_bias,
        grad_w_expand,
        grad_gain_three,
        grad_shift_three,
    )


def solution(mesh):
    return jax.shard_map(
        on_device,
        mesh=mesh,
        in_specs=(
            P("batch", "rows", None, None),
            P(),
            P(),
            P(),
            P(),
            P(),
            P(),
            P(),
            P(),
            P(),
            P(),
            P(),
            P(),
            P(),
            P(),
            P("batch", None),
            P("batch", None),
            P("batch", "rows", None, None),
        ),
        out_specs=(
            P("batch", "rows", None, None),
            P("batch", "rows", None, None),
            P(),
            P(),
            P(),
            P(),
            P(),
            P(),
            P(),
            P(),
            P(),
            P(),
            P(),
            P(),
            P(),
            P(),
        ),
        check_vma=False,
    )
```

profile of v0, /device:TPU:0, one launch (start us, length us, event | category | flops | bytes accessed | tf_op | source)
XLA Modules:
  0.0 730.6 jit_solution(17673367158907274159)
XLA Ops:
  9.6 3.7 multiply_reduce_fusion.9
  13.4 42.3 %all-reduce.5 = (f32[256]{0:T(256)S(1)}, f32[]{:T(128)}) all-reduce(f32[256]{0:T(256)S(1)} %get-tuple-element.140, f32[]{:T(128)} %multiply_reduce_fusion.10), channel_id=1, replica_groups=mesh['rows'=4,'batch'=8] {'rows','batch'}, use_global_device_ids=true, to_apply=%region_1.0 | all-reduce | flops 257 | bytes 2056 | tf_op jit(solution)/shard_map/psum | solution.py:41
  56.4 40.3 %psum.190 = f32[256]{0:T(256)S(1)} all-reduce(f32[256]{0:T(256)S(1)} %multiply_reduce_fusion.8), channel_id=1, replica_groups=mesh['rows'=4,'batch'=8] {'rows','batch'}, use_global_device_ids=true, to_apply=%region_5.0 | all-reduce | flops 256 | bytes 2048 | tf_op jit(solution)/shard_map/psum | solution.py:47
  98.8 4.2 collective-permute-start
  123.6 40.9 %psum.191 = f32[512]{0:T(512)S(1)} all-reduce(f32[512]{0:T(512)S(1)} %bitcast.304), channel_id=1, replica_groups=mesh['rows'=4,'batch'=8] {'rows','batch'}, use_global_device_ids=true, to_apply=%region_7.0 | all-reduce | flops 512 | bytes 4096 | tf_op jit(solution)/shard_map/psum | solution.py:41
  165.6 40.3 %psum.192 = f32[512]{0:T(512)S(1)} all-reduce(f32[512]{0:T(512)S(1)} %bitcast.305), channel_id=1, replica_groups=mesh['rows'=4,'batch'=8] {'rows','batch'}, use_global_device_ids=true, to_apply=%region_9.10 | all-reduce | flops 512 | bytes 4096 | tf_op jit(solution)/shard_map/psum | solution.py:47
  211.0 11.2 %psum.193 = f32[8,256]{1,0:T(8,128)} all-reduce(f32[8,256]{1,0:T(8,128)} %add_reduce_fusion), channel_id=1, replica_groups=mesh['rows'=4,'batch'=8] {'rows'}, use_global_device_ids=true, to_apply=%region_11.12 | all-reduce | flops 2048 | bytes 16384 | tf_op jit(solution)/shard_map/psum | solution.py:157
  224.2 14.7 %all-reduce.8 = (f32[128]{0:T(128)}, f32[128]{0:T(128)}) all-reduce(f32[128]{0:T(128)} %get-tuple-element.75, f32[128]{0:T(128)} %get-tuple-element.74), channel_id=1, replica_groups=mesh['rows'=4,'batch'=8] {'batch'}, use_global_device_ids=true, to_apply=%region_17.18 | all-reduce | flops 256 | bytes 2048 | tf_op jit(solution)/shard_map/psum | solution.py:159
  243.0 5.0 multiply_reduce_fusion.2
  248.0 37.1 %psum.196 = f32[1024]{0:T(1024)} all-reduce(f32[1024]{0:T(1024)} %get-tuple-element.145), channel_id=1, replica_groups=mesh['rows'=4,'batch'=8] {'rows','batch'}, use_global_device_ids=true, to_apply=%region_20.21 | all-reduce | flops 1024 | bytes 8192 | tf_op jit(solution)/shard_map/psum | solution.py:41
  289.4 42.2 %psum.197 = f32[1024]{0:T(1024)} all-reduce(f32[1024]{0:T(1024)} %multiply_reduce_fusion.1), channel_id=1, replica_groups=mesh['rows'=4,'batch'=8] {'rows','batch'}, use_global_device_ids=true, to_apply=%region_22.23 | all-reduce | flops 1024 | bytes 8192 | tf_op jit(solution)/shard_map/psum | solution.py:47
  333.5 7.0 fusion.76
  340.5 39.6 %all-reduce.4 = (f32[1024]{0:T(1024)}, f32[1024]{0:T(1024)}) all-reduce(f32[1024]{0:T(1024)} %get-tuple-element.65, f32[1024]{0:T(1024)} %get-tuple-element.64), channel_id=1, replica_groups=mesh['rows'=4,'batch'=8] {'rows','batch'}, use_global_device_ids=true, to_apply=%region_26.27 | all-reduce | flops 2048 | bytes 16384 | tf_op jit(solution)/shard_map/psum | solution.py:55
  381.4 7.3 multiply_reduce_fusion.7
  388.8 4.1 convolution_bitcast_fusion
  392.9 16.5 %all-reduce.9 = (f32[8,256]{1,0:T(8,128)S(1)}, f32[8,256]{1,0:T(8,128)S(1)}) all-reduce(f32[8,256]{1,0:T(8,128)S(1)} %copy-done.91, f32[8,256]{1,0:T(8,128)S(1)} %copy-done.90), channel_id=1, replica_groups=mesh['rows'=4,'batch'=8] {'rows'}, use_global_device_ids=true, to_apply=%region_30.31 | all-reduce | flops 4096 | bytes 32768 | tf_op jit(solution)/shard_map/psum | solution.py:181
  410.5 13.6 %all-reduce.7 = (f32[128]{0:T(128)S(1)}, f32[128]{0:T(128)S(1)}) all-reduce(f32[128]{0:T(128)S(1)} %get-tuple-element.73, f32[128]{0:T(128)S(1)} %get-tuple-element.72), channel_id=1, replica_groups=mesh['rows'=4,'batch'=8] {'batch'}, use_global_device_ids=true, to_apply=%region_34.35 | all-reduce | flops 256 | bytes 2048 | tf_op jit(solution)/shard_map/psum | solution.py:195
  428.3 36.9 %all-reduce.3 = (f32[512]{0:T(512)S(1)}, f32[512]{0:T(512)S(1)}) all-reduce(f32[512]{0:T(512)S(1)} %bitcast.303, f32[512]{0:T(512)S(1)} %bitcast.302), channel_id=1, replica_groups=mesh['rows'=4,'batch'=8] {'rows','batch'}, use_global_device_ids=true, to_apply=%region_38.39 | all-reduce | flops 1024 | bytes 8192 | tf_op jit(solution)/shard_map/psum | solution.py:55
  470.5 4.9 collective-permute-start.2
  505.6 5.1 fusion.86
  520.5 42.3 %all-reduce.2 = (f32[256]{0:T(256)S(1)}, f32[256]{0:T(256)S(1)}, f32[512]{0:T(512)}) all-reduce(f32[256]{0:T(256)S(1)} %get-tuple-element.71, f32[256]{0:T(256)S(1)} %get-tuple-element.70, f32[512]{0:T(512)S(1)} %broadcast_multiply_fusion.1), channel_id=1, replica_groups=mesh['rows'=4,'batch'=8] {'rows','batch'}, use_global_device_ids=true, to_apply=%region_42.43 | all-reduce | flops 1024 | bytes 8192 | tf_op jit(solution)/shard_map/psum | solution.py:55
  563.4 3.6 convolution_bitcast_fusion.1
  568.6 5.0 convolution_add_fusion
  573.6 141.4 %all-reduce.12.cloned.1.call-done = (f32[1024,256]{0,1:T(8,128)}, f32[3,3,128,512]{3,2,1,0:T(8,128)}, f32[256,128]{1,0:T(8,128)}, f32[128,512]{1,0:T(8,128)}, f32[256,1024]{1,0:T(8,128)}) async-done(((f32[1024,256]{0,1:T(8,128)}, f32[3,3,128,512]{3,2,1,0:T(8,128)}, f32[256,128]{1,0:T(8,128)}, f32[128,512]{1,0:T(8,128)}, f32[256,1024]{1,0:T(8,128)}), (f32[1024,256]{0,1:T(8,128)}, ...) | async-done | bytes 4849680 | tf_op jit(solution)/shard_map/psum | solution.py:223
  (322 shorter events, 105.4 us)
Async XLA Ops:
  7.2 235.8 %copy-start = (f32[256,1024]{1,0:T(8,128)S(1)}, f32[256,1024]{1,0:T(8,128)}, u32[]{:S(2)}) copy-start(f32[256,1024]{1,0:T(8,128)} %param.30) | copy-start | bytes 3145732
  7.2 707.8 %all-reduce.12.cloned.1.call-start = ((), (), s32[]{:S(2)}) async-start(), calls=%async_computation | async-start | bytes 9699328 | tf_op jit(solution)/shard_map/psum | solution.py:223
  9.6 87.1 %copy-start.84 = (f32[256]{0:T(256)S(1)}, f32[256]{0:T(256)}, u32[]{:S(2)}) copy-start(f32[256]{0:T(256)} %param.20) | copy-start | bytes 3076
  9.6 88.2 %copy-start.100 = (f32[256]{0:T(256)S(1)}, f32[256]{0:T(256)}, u32[]{:S(2)}) copy-start(f32[256]{0:T(256)} %param.21) | copy-start | bytes 3076
  9.6 94.9 %copy-start.81 = (s32[8,16]{1,0:T(8,128)S(1)}, s32[8,16]{1,0:T(8,128)}, u32[]{:S(2)}) copy-start(s32[8,16]{1,0:T(8,128)} %param.33) | copy-start | bytes 1540
  9.6 95.5 %copy-start.77 = (f32[512]{0:T(512)S(1)}, f32[512]{0:T(512)}, u32[]{:S(2)}) copy-start(f32[512]{0:T(512)} %param.24) | copy-start | bytes 6148
  9.6 96.1 %copy-start.57 = (f32[512]{0:T(512)S(1)}, f32[512]{0:T(512)}, u32[]{:S(2)}) copy-start(f32[512]{0:T(512)} %param.23) | copy-start | bytes 6148
  13.4 92.4 %copy-start.5 = (f32[8,4,16,256]{3,2,1,0:T(8,128)}, f32[8,4,16,256]{3,2,1,0:T(8,128)S(1)}, u32[]{:S(2)}) copy-start(f32[8,4,16,256]{3,2,1,0:T(8,128)S(1)} %get-tuple-element.141) | copy-start | bytes 1572868
  56.2 49.5 %copy-start.66 = (f32[256]{0:T(256)}, f32[256]{0:T(256)S(1)}, u32[]{:S(2)}) copy-start(f32[256]{0:T(256)S(1)} %broadcast_divide_fusion.8) | copy-start | bytes 3076
  98.8 11.6 %collective-permute-start = (f32[8,1,16,256]{3,2,1,0:T(8,128)}, f32[8,1,16,256]{3,2,1,0:T(8,128)S(1)}, u32[]{:S(2)}, u32[]{:S(2)}) collective-permute-start(f32[8,1,16,256]{3,2,1,0:T(8,128)} %get-tuple-element.128), channel_id=1, source_target_pairs={{0,8},{8,16},{16,24},{1,9},{9,17},{17,25},{2,10},{10,18},{18,26},{... | collective-permute-start | bytes 393224 | tf_op jit(solution)/shard_map/ppermute | solution.py:18
  103.0 7.5 %collective-permute-start.1 = (f32[8,1,16,256]{3,2,1,0:T(8,128)}, f32[8,1,16,256]{3,2,1,0:T(8,128)}, u32[]{:S(2)}, u32[]{:S(2)}) collective-permute-start(f32[8,1,16,256]{3,2,1,0:T(8,128)} %get-tuple-element.129), channel_id=1, source_target_pairs={{8,0},{16,8},{24,16},{9,1},{17,9},{25,17},{10,2},{18,10},{26,18},{... | collective-permute-start | bytes 393224 | tf_op jit(solution)/shard_map/ppermute | solution.py:20
  121.5 84.4 %copy-start.58 = (f32[512]{0:T(512)S(1)}, f32[512]{0:T(512)}, u32[]{:S(2)}) copy-start(f32[512]{0:T(512)} %param.23) | copy-start | bytes 6148
  165.0 42.6 %copy-start.55 = (f32[2,256]{1,0:T(2,128)}, f32[2,256]{1,0:T(2,128)S(1)}, u32[]{:S(2)}) copy-start(f32[2,256]{1,0:T(2,128)S(1)} %sub.146) | copy-start | bytes 6148
  424.1 44.3 %copy-start.102 = (f32[128]{0:T(128)}, f32[128]{0:T(128)S(1)}, u32[]{:S(2)}) copy-start(f32[128]{0:T(128)S(1)} %get-tuple-element.158) | copy-start | bytes 1540
  424.6 41.3 %copy-start.59 = (f32[512]{0:T(512)S(1)}, f32[512]{0:T(512)}, u32[]{:S(2)}) copy-start(f32[512]{0:T(512)} %param.23) | copy-start | bytes 6148
  424.6 41.3 %copy-start.62 = (f32[512]{0:T(512)S(1)}, f32[512]{0:T(512)}, u32[]{:S(2)}) copy-start(f32[512]{0:T(512)} %copy-done.60) | copy-start | bytes 6148
  424.6 41.3 %copy-start.65 = (f32[512]{0:T(512)S(1)}, f32[512]{0:T(512)}, u32[]{:S(2)}) copy-start(f32[512]{0:T(512)} %copy-done.63) | copy-start | bytes 6148
  424.6 41.3 %copy-start.76 = (f32[512]{0:T(512)S(1)}, f32[512]{0:T(512)}, u32[]{:S(2)}) copy-start(f32[512]{0:T(512)} %get-tuple-element.99) | copy-start | bytes 6148
  424.6 41.3 %copy-start.78 = (f32[512]{0:T(512)S(1)}, f32[512]{0:T(512)}, u32[]{:S(2)}) copy-start(f32[512]{0:T(512)} %param.24) | copy-start | bytes 6148
  428.3 40.2 %copy-start.70 = (f32[128]{0:T(128)S(1)}, f32[128]{0:T(128)}, u32[]{:S(2)}) copy-start(f32[128]{0:T(128)} %copy-done.68) | copy-start | bytes 1540
  470.5 29.7 %collective-permute-start.2 = (f32[8,1,16,512]{3,2,1,0:T(8,128)}, f32[8,1,16,512]{3,2,1,0:T(8,128)}, u32[]{:S(2)}, u32[]{:S(2)}) collective-permute-start(f32[8,1,16,512]{3,2,1,0:T(8,128)} %get-tuple-element.115), channel_id=1, source_target_pairs={{0,8},{8,16},{16,24},{1,9},{9,17},{17,25},{2,10},{10,18},{18,26},{... | collective-permute-start | bytes 786440 | tf_op jit(solution)/shard_map/ppermute | solution.py:18
  475.3 24.8 %collective-permute-start.3 = (f32[8,1,16,512]{3,2,1,0:T(8,128)}, f32[8,1,16,512]{3,2,1,0:T(8,128)}, u32[]{:S(2)}, u32[]{:S(2)}) collective-permute-start(f32[8,1,16,512]{3,2,1,0:T(8,128)} %get-tuple-element.116), channel_id=1, source_target_pairs={{8,0},{16,8},{24,16},{9,1},{17,9},{25,17},{10,2},{18,10},{26,18},{... | collective-permute-start | bytes 786440 | tf_op jit(solution)/shard_map/ppermute | solution.py:20
  519.1 44.3 %copy-start.9 = (f32[8,4,16,1024]{3,2,1,0:T(8,128)S(1)}, f32[8,4,16,1024]{3,2,1,0:T(8,128)}, u32[]{:S(2)}) copy-start(f32[8,4,16,1024]{3,2,1,0:T(8,128)} %param.18) | copy-start | bytes 6291460
  519.1 44.3 %copy-start.98 = (f32[256]{0:T(256)S(1)}, f32[256]{0:T(256)}, u32[]{:S(2)}) copy-start(f32[256]{0:T(256)} %get-tuple-element.96) | copy-start | bytes 3076
  (89 other events, 907.7 us)
Sparse Core Ops, SparseCore 0:
  567.1 147.8 all-reduce.11
where the time goes:
time: 737 us; the launch traced here: 731 us
  blocking collectives  418 us (57%)
  waiting for transfers between devices  141 us (19%)
  matrix products  72.1 us (10%)
  other arithmetic  39.9 us (5%)
  local copies, waits for them, and re-layouts  31.1 us (4%)
  between operations  16.1 us (2%)
  starting transfers between devices  12.1 us (2%)
    psum x1, waiting for transfers between devices, on_device(): lax.psum((grad_reduce_term, grad_group_term, grad_w_expand, grad_squeeze_...  141 us
    psum x3, blocking collectives, normalize(): lax.psum(jnp.sum(centered * centered * validity, axis=(0, 1, 2)), ('rows'...  123 us
    psum x3, blocking collectives, normalize(): lax.psum((jnp.sum(values * validity, axis=(0, 1, 2)), own_count), ('rows'...  120 us
    psum x3, blocking collectives, norm_back(): lax.psum((jnp.sum(grad_out, axis=(0, 1, 2)), jnp.sum(grad_out * normed, a...  119 us
    dot_general x9, matrix products, group_kernel_grad(): jnp.einsum('bhwgi,bhwgo->igo', window, grad_split, precision=highest)  17.7 us
    unnamed x227, local copies, waits for them, and re-layouts  17.2 us
    psum x1, blocking collectives, on_device(): lax.psum((jnp.sum(grad_mixed * half_first, axis=(1, 2)), jnp.sum(grad_mix...  16.5 us
  transfers between devices with their start and end apart: 5, of which 2 were waited for; matrix products, arithmetic and copies ran while one was open for 5% of the time, Pallas kernels for 0%

commit v1 on v0

v1 whole, which is shorter than its diff:
```python
import functools

import jax
import jax.numpy as jnp
from jax import lax
from jax.experimental import pallas as pl
from jax.experimental.pallas import tpu as pltpu
from jax.sharding import PartitionSpec as P

epsilon = 1e-05
f32 = jnp.float32
bf16 = jnp.bfloat16
highest = lax.Precision.HIGHEST
both = ("rows", "batch")
NN = ((1,), (0,))
NT = ((1,), (1,))
TN = ((0,), (0,))


def split(values):
    high = values.astype(bf16)
    return high, (values - high.astype(f32)).astype(bf16)


def dot(left, right, dims):
    return lax.dot_general(left, right, (dims, ((), ())), preferred_element_type=f32)


def product(left, right, dims):
    return dot(left[0], right[0], dims) + (
        dot(left[0], right[1], dims) + dot(left[1], right[0], dims)
    )


def exact(left, right, dims):
    return lax.dot_general(
        left, right, (dims, ((), ())), preferred_element_type=f32, precision=highest
    )


def put(tile, row, vector):
    for j in range(vector.shape[1] // 128):
        tile[row + j : row + j + 1, :] = vector[:, j * 128 : (j + 1) * 128]


def get(tile, row, count):
    return jnp.concatenate([tile[row + j : row + j + 1, :] for j in range(count)], axis=1)


def wide(mask, width):
    return jnp.concatenate([mask] * (width // 128), axis=1)


def column_sum(values):
    return jnp.sum(values, axis=0, keepdims=True)


def image_sum(values, images):
    return jnp.sum(values.reshape(images, values.shape[0] // images, values.shape[1]), axis=1)


def per_image(vector, values):
    count, width = vector.shape
    each = values.shape[0] // count
    return jnp.broadcast_to(vector[:, None, :], (count, each, width)).reshape(values.shape[0], width)


def merge_stats(gathered, counts, width):
    groups = width // 128
    own = jnp.maximum(counts, 1.0)
    total = jnp.sum(counts, axis=0)
    means, inverses = [], []
    for j in range(groups):
        sums = gathered[:, j, :]
        squares = gathered[:, groups + j, :]
        mean = jnp.sum(sums, axis=0, keepdims=True) / total
        shift = sums / own - mean
        spread = jnp.sum(squares + counts * shift * shift, axis=0, keepdims=True) / total
        means.append(mean)
        inverses.append(lax.rsqrt(spread + epsilon))
    return jnp.concatenate(means, axis=1), jnp.concatenate(inverses, axis=1), total


def local_stats(values, mask, count):
    sums = column_sum(values * mask)
    centered = values - sums / jnp.maximum(count, 1.0)
    return sums, column_sum(centered * centered * mask)


def own_rows(extended, images):
    rows, width = extended.shape
    tall = rows // images // 16
    return extended.reshape(images, tall, 16, width)[:, 1 : tall - 1].reshape(-1, width)


def call(body, outs, ins, scratch=(), limit=40, **extra):
    specs = [jax.ShapeDtypeStruct(shape, kind) for shape, kind in outs]
    return pl.pallas_call(
        body,
        out_shape=specs,
        scratch_shapes=list(scratch),
        compiler_params=pltpu.CompilerParams(vmem_limit_bytes=limit * 2**20),
        **extra,
    )(*ins)


def share(tile):
    return lax.all_to_all(tile, both, 0, 0)


def halos(first, last):
    count = lax.axis_size("rows")
    above = lax.ppermute(last, "rows", [(i, i + 1) for i in range(count - 1)])
    below = lax.ppermute(first, "rows", [(i + 1, i) for i in range(count - 1)])
    return above, below


def reduce_kernel(rows_ref, cols_ref, x_ref, w_ref, z_ref, ext_ref, own_ref, first_ref, last_ref, pay_ref, tile):
    images = rows_ref.shape[0]
    tall = x_ref.shape[0] // images // 16
    shape = (images, tall + 2, 16, 16)
    start = lax.axis_index("rows") * tall - 1
    lane = lax.broadcasted_iota(jnp.int32, shape, 3).reshape(-1, 16)
    at_row = lax.broadcasted_iota(jnp.int32, shape, 1).reshape(-1, 16) + start
    at_col = lax.broadcasted_iota(jnp.int32, shape, 2).reshape(-1, 16)
    row_valid = per_image(rows_ref[...].astype(f32), lane)
    col_valid = per_image(cols_ref[...].astype(f32), lane)
    in_row = jnp.sum(jnp.where(lane == at_row, row_valid, 0.0), axis=1, keepdims=True)
    in_col = jnp.sum(jnp.where(lane == at_col, col_valid, 0.0), axis=1, keepdims=True)
    mask = jnp.broadcast_to(in_row * in_col, ext_ref.shape)
    ext_ref[...] = mask
    own = own_rows(mask, images)
    own_ref[...] = own
    z = product(split(x_ref[...]), split(w_ref[...]), NN)
    z_ref[...] = z
    edges = z.reshape(images, tall, 16, -1)
    first_ref[...] = edges[:, 0].reshape(first_ref.shape)
    last_ref[...] = edges[:, tall - 1].reshape(last_ref.shape)
    count = column_sum(own)
    both_counts = wide(count, z.shape[1])
    sums, squares = local_stats(z, wide(own, z.shape[1]), both_counts)
    tile[...] = jnp.zeros_like(tile)
    put(tile, 0, sums)
    put(tile, 2, squares)
    put(tile, 4, count)
    pay_ref[...] = jnp.broadcast_to(tile[...][None], pay_ref.shape)


def parts_kernel(*refs):
    half = len(refs) // 3
    for i in range(half):
        high, low = split(refs[i][...])
        refs[half + 2 * i][...] = high
        refs[half + 2 * i + 1][...] = low


def turned_kernel(x_ref, high_ref, low_ref):
    high_ref[...], low_ref[...] = split(x_ref[...].T)


def moved(values, step):
    count = values.shape[0]
    at = lax.broadcasted_iota(jnp.int32, values.shape, 0) & 15
    if step == 0:
        return values
    if step > 0:
        return jnp.where(at < 15, pltpu.roll(values, count - 1, 0), 0.0)
    return jnp.where(at > 0, pltpu.roll(values, 1, 0), 0.0)


def window(extended, images, row, width):
    tall = extended.shape[0] // images // 16
    cells = extended.reshape(images, tall, 16, extended.shape[1])
    return cells[:, row : row + tall - 2, :, width].reshape(images * (tall - 2) * 16, -1)


def conv_kernel(z_ref, above_ref, below_ref, ext_ref, own_ref, g1_ref, gain_ref, shift_ref, wh_ref, wl_ref,
                a_ref, z2_ref, first_ref, last_ref, stat_ref, pay_ref, tile, zext):
    images = zext.shape[0]
    tall = zext.shape[1] - 2
    width = z_ref.shape[1]
    group = width // 2
    gathered = g1_ref[...]
    mean, inv, total = merge_stats(gathered, gathered[:, 4, :], width)
    tile[...] = jnp.zeros_like(tile)
    put(tile, 0, mean)
    put(tile, 2, inv)
    put(tile, 4, total[None] if total.ndim == 1 else total)
    stat_ref[...] = tile[...]
    zext[:, 1 : tall + 1] = z_ref[...].reshape(images, tall, 16, width)
    zext[:, 0] = above_ref[...].reshape(images, 16, width)
    zext[:, tall + 1] = below_ref[...].reshape(images, 16, width)
    y = (zext[...].reshape(-1, width) - mean) * inv * gain_ref[...] + shift_ref[...]
    a = y * jax.nn.sigmoid(y) * wide(ext_ref[...], width)
    a_ref[...] = a
    shifted = [split(moved(a, step)) for step in (-1, 0, 1)]
    half = z2_ref.shape[1] // 2
    for g in range(2):
        cols = slice(g * group, (g + 1) * group)
        left = [
            jnp.concatenate(
                [window(shifted[tap % 3][part], images, tap // 3, cols) for tap in range(9)], axis=1
            )
            for part in range(2)
        ]
        outs = slice(g * half, (g + 1) * half)
        z2_ref[:, outs] = product(left, (wh_ref[:, outs], wl_ref[:, outs]), NN)
    z2 = z2_ref[...]
    edges = z2.reshape(images, tall, 16, -1)
    first_ref[...] = edges[:, 0].reshape(first_ref.shape)
    last_ref[...] = edges[:, tall - 1].reshape(last_ref.shape)
    own = wide(own_ref[...], z2.shape[1])
    sums, squares = local_stats(z2, own, wide(column_sum(own_ref[...]), z2.shape[1]))
    put(tile, 0, sums)
    put(tile, 4, squares)
    pay_ref[...] = jnp.broadcast_to(tile[...][None], pay_ref.shape)


def taps_kernel(images, a_ref, high_ref, low_ref):
    group = a_ref.shape[1] // 2
    a = a_ref[...]
    shifted = [moved(a, step) for step in (-1, 0, 1)]
    for g in range(2):
        cols = slice(g * group, (g + 1) * group)
        for tap in range(9):
            high, low = split(window(shifted[tap % 3], images, tap // 3, cols).T)
            high_ref[g, tap * group : (tap + 1) * group, :] = high
            low_ref[g, tap * group : (tap + 1) * group, :] = low


def pixel_count(rows_ref, cols_ref):
    rows = jnp.sum(rows_ref[...].astype(f32), axis=1, keepdims=True)
    return rows * jnp.sum(cols_ref[...].astype(f32), axis=1, keepdims=True)


def pool_kernel(z_ref, own_ref, g1_ref, g2_ref, gain_ref, shift_ref, rows_ref, cols_ref, w_ref,
                a_ref, stat_ref, pooled_ref, pay_ref):
    images = rows_ref.shape[0]
    width = z_ref.shape[1]
    mid = width // 2
    mean, inv, total = merge_stats(g2_ref[...], g1_ref[:, 4, :], width)
    put(stat_ref, 0, mean)
    put(stat_ref, 4, inv)
    y = (z_ref[...] - mean) * inv * gain_ref[...] + shift_ref[...]
    a = y * jax.nn.sigmoid(y) * wide(own_ref[...], width)
    a_ref[...] = a
    sums = image_sum(a, images)
    pooled = (sums[:, :mid] + sums[:, mid:]) / pixel_count(rows_ref, cols_ref)
    pooled_ref[...] = pooled
    pay_ref[...] = jnp.broadcast_to(exact(pooled, w_ref[...], NN)[None], pay_ref.shape)


def slope_kernel(z_ref, above_ref, below_ref, ext_ref, stat_ref, gain_ref, shift_ref, rows_ref, cols_ref,
                 slope_ref, normed_ref, sums_ref, zext):
    images = zext.shape[0]
    tall = zext.shape[1] - 2
    width = z_ref.shape[1]
    zext[:, 1 : tall + 1] = z_ref[...].reshape(images, tall, 16, width)
    zext[:, 0] = above_ref[...].reshape(images, 16, width)
    zext[:, tall + 1] = below_ref[...].reshape(images, 16, width)
    mean, inv = get(stat_ref, 0, 4), get(stat_ref, 4, 4)
    normed = (zext[...].reshape(-1, width) - mean) * inv
    y = normed * gain_ref[...] + shift_ref[...]
    sigma = jax.nn.sigmoid(y)
    slope = sigma * (1.0 + y * (1.0 - sigma)) * wide(ext_ref[...], width)
    slope_ref[...] = slope
    normed_ref[...] = normed
    pixels = pixel_count(rows_ref, cols_ref)
    inner = own_rows(slope, images)
    sums_ref[:, :width] = image_sum(inner, images) / pixels
    sums_ref[:, width:] = image_sum(inner * own_rows(normed, images), images) / pixels


def expand_kernel(g3_ref, a_ref, own_ref, gain_ref, shift_ref, w_ref, bias_ref, wh_ref, wl_ref,
                  mixed_ref, z_ref, weights_ref, normed_ref, pre_ref, act_ref, inv_ref, pay_ref, tile, acts):
    own_images = weights_ref.shape[0]
    mid = mixed_ref.shape[1]
    devices = g3_ref.shape[0]
    rows = lax.axis_size("rows")
    f_one = jnp.sum(g3_ref[...].reshape(rows, devices // rows * own_images, -1), axis=0)
    mean = jnp.mean(f_one, axis=0, keepdims=True)
    centered = f_one - mean
    inv = lax.rsqrt(jnp.mean(centered * centered, axis=0, keepdims=True) + epsilon)
    normed = centered * inv
    pre = normed * gain_ref[...] + shift_ref[...]
    normed_ref[...] = normed
    pre_ref[...] = pre
    inv_ref[...] = inv
    acts[...] = pre * jax.nn.sigmoid(pre)
    at = pl.multiple_of(lax.axis_index("batch") * own_images, own_images)
    act = acts[pl.ds(at, own_images), :]
    act_ref[...] = act
    logits = exact(act, w_ref[...], NN) + bias_ref[...]
    lead = logits[:, :mid] - logits[:, mid:]
    first, second = jax.nn.sigmoid(lead), jax.nn.sigmoid(-lead)
    weights_ref[:, :mid] = first
    weights_ref[:, mid:] = second
    a = a_ref[...]
    mixed = per_image(first, a) * a[:, :mid] + per_image(second, a) * a[:, mid:]
    mixed_ref[...] = mixed
    z_ref[...] = product(split(mixed), (wh_ref[...], wl_ref[...]), NN)
    z = z_ref[...]
    width = z.shape[1]
    own = wide(own_ref[...], width)
    sums, squares = local_stats(z, own, wide(column_sum(own_ref[...]), width))
    put(tile, 0, sums)
    put(tile, width // 128, squares)
    pay_ref[...] = jnp.broadcast_to(tile[...][None], pay_ref.shape)


def output_kernel(g1_ref, g4_ref, gain_ref, shift_ref, z_ref, x_ref, cot_ref, own_ref,
                  out_ref, grad_ref, stat_ref, pay_ref, tile, sums):
    width = z_ref.shape[1]
    step = pl.program_id(0)

    @pl.when(step == 0)
    def _():
        mean, inv, total = merge_stats(g4_ref[...], g1_ref[:, 4, :], width)
        put(stat_ref, 0, mean)
        put(stat_ref, width // 128, inv)
        sums[...] = jnp.zeros_like(sums)

    mean, inv = get(stat_ref, 0, width // 128), get(stat_ref, width // 128, width // 128)
    own = wide(own_ref[...], width)
    normed = (z_ref[...] - mean) * inv
    pre = normed * gain_ref[...] + shift_ref[...] + x_ref[...]
    sigma = jax.nn.sigmoid(pre)
    out_ref[...] = pre * sigma * own
    grad = cot_ref[...] * own * (sigma * (1.0 + pre * (1.0 - sigma)))
    grad_ref[...] = grad
    sums[0:1, :] += column_sum(grad)
    sums[1:2, :] += column_sum(grad * normed)

    @pl.when(step == pl.num_programs(0) - 1)
    def _():
        put(tile, 0, sums[0:1, :])
        put(tile, width // 128, sums[1:2, :])
        pay_ref[...] = jnp.broadcast_to(tile[...][None], pay_ref.shape)


def mixed_kernel(g5_ref, stat1_ref, stat3_ref, gain_ref, z_ref, grad_ref, own_ref, wh_ref, wl_ref, a_ref, slope_ref,
                 normed_ref, weights_ref, w_ref, dzh_ref, dzl_ref, gm_ref, first_ref, last_ref, dsum_ref, grads_ref,
                 pay_ref, tile):
    width = z_ref.shape[1]
    mid = gm_ref.shape[1]
    images = weights_ref.shape[0]
    tall = z_ref.shape[0] // images // 16
    groups = width // 128
    grads_ref[...] = jnp.sum(g5_ref[...], axis=0)
    count = wide(stat1_ref[4:5, :], width)
    mean, inv = get(stat3_ref, 0, groups), get(stat3_ref, groups, groups)
    normed = (z_ref[...] - mean) * inv
    flat = get(grads_ref, 0, groups) / count
    cross = get(grads_ref, groups, groups) / count
    dz = gain_ref[...] * inv * (grad_ref[...] - flat - normed * cross) * wide(own_ref[...], width)
    dz_high, dz_low = split(dz)
    dzh_ref[...] = dz_high
    dzl_ref[...] = dz_low
    gm = product((dz_high, dz_low), (wh_ref[...], wl_ref[...]), NT)
    gm_ref[...] = gm
    edges = gm.reshape(images, tall, 16, mid)
    first_ref[...] = edges[:, 0].reshape(first_ref.shape)
    last_ref[...] = edges[:, tall - 1].reshape(last_ref.shape)
    a = a_ref[...]
    weights = weights_ref[...]
    gate = image_sum(gm * (a[:, :mid] - a[:, mid:]), images)
    dsum = weights[:, :mid] * weights[:, mid:] * gate
    dsum_ref[...] = dsum
    tile[...] = jnp.zeros_like(tile)
    tile[:images, :] = exact(dsum, w_ref[:, :mid] - w_ref[:, mid:], NT)
    slope = own_rows(slope_ref[...], images) * jnp.concatenate([gm, gm], axis=1)
    put(tile, 8, column_sum(weights * image_sum(slope, images)))
    put(tile, 12, column_sum(weights * image_sum(slope * own_rows(normed_ref[...], images), images)))
    pay_ref[...] = jnp.broadcast_to(tile[...][None], pay_ref.shape)


def expand_grad_kernel(mixed_ref, dzh_ref, dzl_ref, act_ref, dsum_ref, out_ref, excite_ref, bias_ref):
    out_ref[...] = product(split(mixed_ref[...].T), (dzh_ref[...], dzl_ref[...]), NN)
    dsum = dsum_ref[...]
    excite_ref[...] = exact(act_ref[...], dsum, TN)
    bias_ref[...] = column_sum(dsum)


def group_kernel(g6_ref, gs_ref, pre_ref, fcn_ref, inv_ref, gfc_ref, wsq_ref, pooled_ref, gm_ref, above_ref, below_ref,
                 slope_ref, normed_ref, ext_ref, weights_ref, stat1_ref, stat2_ref, gain_ref, rows_ref, cols_ref,
                 th_ref, tl_ref,
                 dzh_ref, dzl_ref, out_ref, gains_ref, fc_ref, squeeze_ref, dext, gf, owned):
    step = pl.program_id(0)
    images = rows_ref.shape[0]
    width = normed_ref.shape[1]
    mid = width // 2

    @pl.when(step == 0)
    def _():
        rows = lax.axis_size("rows")
        devices = g6_ref.shape[0]
        shared = g6_ref[...]
        pre = pre_ref[...]
        fcn = fcn_ref[...]
        sigma = jax.nn.sigmoid(pre)
        total = pre.shape[0]
        grad = jnp.sum(shared[:, :images].reshape(rows, total, -1), axis=0) * (sigma * (1.0 + pre * (1.0 - sigma)))
        flat, cross = column_sum(grad), column_sum(grad * fcn)
        fc_ref[0:1, :] = cross
        fc_ref[1:2, :] = flat
        gf[...] = gfc_ref[...] * inv_ref[...] * (grad - flat / total - fcn * cross / total)
        at = pl.multiple_of(lax.axis_index("batch") * images, images)
        mine = gf[pl.ds(at, images), :]
        squeeze_ref[...] = exact(pooled_ref[...], mine, TN)
        spread = exact(gf[...], wsq_ref[...], NT)
        owned[...] = spread
        own_spread = owned[pl.ds(at, images), :] / pixel_count(rows_ref, cols_ref)
        slopes = jnp.sum(gs_ref[...].reshape(rows, total, -1), axis=0)
        spread = jnp.concatenate([spread, spread], axis=1)
        base = jnp.sum(shared[:, 8:], axis=0)
        flat_two = get(base, 0, width // 128) + column_sum(spread * slopes[:, :width])
        cross_two = get(base, width // 128, width // 128) + column_sum(spread * slopes[:, width:])
        put(gains_ref, 0, cross_two)
        put(gains_ref, width // 128, flat_two)
        count = wide(stat1_ref[4:5, :], width)
        inv = get(stat2_ref, width // 128, width // 128)
        tall = dext.shape[1] - 2
        dext[:, 1 : tall + 1] = gm_ref[...].reshape(images, tall, 16, mid)
        dext[:, 0] = above_ref[...].reshape(images, 16, mid)
        dext[:, tall + 1] = below_ref[...].reshape(images, 16, mid)
        gm = dext[...].reshape(-1, mid)
        weights = weights_ref[...]
        shared_part = per_image(own_spread, gm)
        upstream = jnp.concatenate(
            [
                per_image(weights[:, :mid], gm) * gm + shared_part,
                per_image(weights[:, mid:], gm) * gm + shared_part,
            ],
            axis=1,
        )
        dz = (
            gain_ref[...]
            * inv
            * (upstream * slope_ref[...] - flat_two / count - normed_ref[...] * (cross_two / count))
            * wide(ext_ref[...], width)
        )
        high, low = split(dz)
        dzh_ref[...] = high
        dzl_ref[...] = low

    for g in range(2):
        outs = slice(g * mid, (g + 1) * mid)
        right = [window(ref[...], images, 1, outs) for ref in (dzh_ref, dzl_ref)]
        out_ref[:, outs] = product((th_ref[g], tl_ref[g]), right, NN)


def input_grad_kernel(dzh_ref, dzl_ref, wh_ref, wl_ref, z_ref, stat_ref, own_ref, gain_ref, shift_ref,
                      dy_ref, pay_ref, tile):
    images = dzh_ref.shape[0] // 16 // (z_ref.shape[0] // 16 // 8 + 2)
    width = z_ref.shape[1]
    group = width // 2
    half = dzh_ref.shape[1] // 2
    taps = 3 * group
    grads = []
    for g in range(2):
        outs = slice(g * half, (g + 1) * half)
        total = None
        for row in range(3):
            left = [window(ref[...], images, 2 - row, outs) for ref in (dzh_ref, dzl_ref)]
            right = [ref[row * taps : (row + 1) * taps, outs] for ref in (wh_ref, wl_ref)]
            term = product(left, right, NT)
            total = term if total is None else total + term
        grads.append(
            moved(total[:, :group], 1)
            + total[:, group : 2 * group]
            + moved(total[:, 2 * group :], -1)
        )
    grad = jnp.concatenate(grads, axis=1)
    mean, inv = get(stat_ref, 0, 2), get(stat_ref, 2, 2)
    normed = (z_ref[...] - mean) * inv
    y = normed * gain_ref[...] + shift_ref[...]
    sigma = jax.nn.sigmoid(y)
    dy = grad * wide(own_ref[...], width) * (sigma * (1.0 + y * (1.0 - sigma)))
    dy_ref[...] = dy
    tile[...] = jnp.zeros_like(tile)
    put(tile, 0, column_sum(dy * normed))
    put(tile, 2, column_sum(dy))
    pay_ref[...] = jnp.broadcast_to(tile[...][None], pay_ref.shape)


def final_kernel(g7_ref, dy_ref, z_ref, stat_ref, gain_ref, own_ref, wh_ref, wl_ref, th_ref, tl_ref, grad_ref,
                 out_ref, reduce_ref, gains_ref):
    width = z_ref.shape[1]
    gains_ref[...] = jnp.sum(g7_ref[...], axis=0)
    cross, flat = get(gains_ref, 0, 2), get(gains_ref, 2, 2)
    count = wide(stat_ref[4:5, :], width)
    mean, inv = get(stat_ref, 0, 2), get(stat_ref, 2, 2)
    normed = (z_ref[...] - mean) * inv
    dz = gain_ref[...] * inv * (dy_ref[...] - flat / count - normed * (cross / count)) * wide(own_ref[...], width)
    parts = split(dz)
    reduce_ref[...] = product((th_ref[...], tl_ref[...]), parts, NN)
    out_ref[...] = product(parts, (wh_ref[...], wl_ref[...]), NT) + grad_ref[...]


def on_device(
    images,
    w_reduce,
    gain_one,
    shift_one,
    w_group,
    gain_two,
    shift_two,
    w_squeeze,
    gain_fc,
    shift_fc,
    w_excite,
    excite_bias,
    w_expand,
    gain_three,
    shift_three,
    valid_rows,
    valid_cols,
    cotangent,
):
    count, tall, broad, chan = images.shape
    mid = w_reduce.shape[1]
    inter = w_squeeze.shape[1]
    duo = 2 * mid
    cells = count * tall * broad
    longer = count * (tall + 2) * broad
    edge = count * broad
    devices = lax.axis_size("rows") * lax.axis_size("batch")
    all_images = count * lax.axis_size("batch")
    x = images.reshape(cells, chan)
    cot = cotangent.reshape(cells, chan)
    row = lambda v: v.reshape(1, -1)
    pay8 = ((devices, 8, 128), f32)
    pay16 = ((devices, 16, 128), f32)
    tile8 = pltpu.VMEM((8, 128), f32)
    tile16 = pltpu.VMEM((16, 128), f32)
    flat_w = w_group.reshape(9 * mid // 2, duo)

    z_one, ext, own, first, last, pay = call(
        reduce_kernel,
        [((cells, mid), f32), ((longer, 128), f32), ((cells, 128), f32), ((edge, mid), f32), ((edge, mid), f32), pay8],
        [valid_rows, valid_cols, x, w_reduce],
        [tile8],
    )
    g1 = share(pay)
    above, below = halos(first, last)
    wgh, wgl, weh, wel, wrh, wrl = call(
        parts_kernel,
        [(w.shape, bf16) for w in (flat_w, w_expand, w_reduce) for _ in range(2)],
        [flat_w, w_expand, w_reduce],
    )
    xth, xtl = call(turned_kernel, [((chan, cells), bf16)] * 2, [x])
    a_one, z_two, first, last, stat1, pay = call(
        conv_kernel,
        [((longer, mid), f32), ((cells, duo), f32), ((edge, duo), f32), ((edge, duo), f32), ((8, 128), f32), pay8],
        [z_one, above, below, ext, own, g1, row(gain_one), row(shift_one), wgh, wgl],
        [tile8, pltpu.VMEM((count, tall + 2, broad, mid), f32)],
    )
    g2 = share(pay)
    above, below = halos(first, last)
    tph, tpl = call(functools.partial(taps_kernel, count), [((2, 9 * mid // 2, cells), bf16)] * 2, [a_one])
    a_two, stat2, pooled, pay = call(
        pool_kernel,
        [((cells, duo), f32), ((8, 128), f32), ((count, mid), f32), ((devices, count, inter), f32)],
        [z_two, own, g1, g2, row(gain_two), row(shift_two), valid_rows, valid_cols, w_squeeze],
    )
    g3 = share(pay)
    slope_two, normed_two, slopes = call(
        slope_kernel,
        [((longer, duo), f32), ((longer, duo), f32), ((count, 2 * duo), f32)],
        [z_two, above, below, ext, stat2, row(gain_two), row(shift_two), valid_rows, valid_cols],
        [pltpu.VMEM((count, tall + 2, broad, duo), f32)],
    )
    gs = lax.all_gather(slopes, both)
    mixed, z_three, weights, fc_normed, fc_pre, fc_act, fc_inv, pay = call(
        expand_kernel,
        [((cells, mid), f32), ((cells, chan), f32), ((count, duo), f32), ((all_images, inter), f32),
         ((all_images, inter), f32), ((count, inter), f32), ((1, inter), f32), pay16],
        [g3, a_two, own, row(gain_fc), row(shift_fc), w_excite, row(excite_bias), weh, wel],
        [tile16, pltpu.VMEM((all_images, inter), f32)],
    )
    g4 = share(pay)
    steps = 4
    block = pl.BlockSpec((cells // steps, chan), lambda i: (i, 0))
    whole = lambda *shape: pl.BlockSpec(shape, lambda i: (0,) * len(shape))
    block_out, grad_pre, stat3, pay = call(
        output_kernel,
        [((cells, chan), f32), ((cells, chan), f32), ((16, 128), f32), pay16],
        [g1, g4, row(gain_three), row(shift_three), z_three, x, cot, own],
        [tile16, pltpu.VMEM((8, chan), f32)],
        grid=(steps,),
        in_specs=[whole(devices, 8, 128), whole(devices, 16, 128), whole(1, chan), whole(1, chan), block, block, block,
                  pl.BlockSpec((cells // steps, 128), lambda i: (i, 0))],
        out_specs=[block, block, whole(16, 128), whole(devices, 16, 128)],
    )
    g5 = share(pay)
    dzh, dzl, grad_mixed, first, last, dsum, grads_three, pay = call(
        mixed_kernel,
        [((cells, chan), bf16), ((cells, chan), bf16), ((cells, mid), f32), ((edge, mid), f32), ((edge, mid), f32),
         ((count, mid), f32), ((16, 128), f32), pay16],
        [g5, stat1, stat3, row(gain_three), z_three, grad_pre, own, weh, wel, a_two, slope_two, normed_two, weights,
         w_excite],
        [tile16],
    )
    g6 = share(pay)
    above, below = halos(first, last)
    expand_term, excite_term, bias_term = call(
        expand_grad_kernel,
        [((mid, chan), f32), ((inter, mid), f32), ((1, mid), f32)],
        [mixed, dzh, dzl, fc_act, dsum],
    )
    taps = 3
    piece = 9 * mid // 2 // taps
    dzh, dzl, group_term, grads_two, grads_fc, squeeze_term = call(
        group_kernel,
        [((longer, duo), bf16), ((longer, duo), bf16), ((9 * mid // 2, duo), f32), ((8, 128), f32), ((2, inter), f32),
         ((mid, inter), f32)],
        [g6, gs, fc_pre, fc_normed, fc_inv, row(gain_fc), w_squeeze, pooled, grad_mixed, above, below, slope_two,
         normed_two, ext, weights, stat1, stat2, row(gain_two), valid_rows, valid_cols, tph, tpl],
        [pltpu.VMEM((count, tall + 2, broad, mid), f32), pltpu.VMEM((all_images, inter), f32),
         pltpu.VMEM((all_images, mid), f32)],
        grid=(taps,),
        in_specs=[whole(devices, 16, 128), whole(devices, count, 2 * duo), whole(all_images, inter),
                  whole(all_images, inter), whole(1, inter), whole(1, inter), whole(mid, inter), whole(count, mid),
                  whole(cells, mid), whole(edge, mid), whole(edge, mid), whole(longer, duo), whole(longer, duo),
                  whole(longer, 128), whole(count, duo), whole(8, 128), whole(8, 128), whole(1, duo),
                  whole(count, broad), whole(count, broad),
                  pl.BlockSpec((2, piece, cells), lambda i: (0, i, 0)), pl.BlockSpec((2, piece, cells), lambda i: (0, i, 0))],
        out_specs=[whole(longer, duo), whole(longer, duo), pl.BlockSpec((piece, duo), lambda i: (i, 0)), whole(8, 128),
                   whole(2, inter), whole(mid, inter)],
        limit=56,
    )
    dy_one, pay = call(
        input_grad_kernel,
        [((cells, mid), f32), pay8],
        [dzh, dzl, wgh, wgl, z_one, stat1, own, row(gain_one), row(shift_one)],
        [tile8],
    )
    g7 = share(pay)
    grad_images, reduce_term, grads_one = call(
        final_kernel,
        [((cells, chan), f32), ((chan, mid), f32), ((8, 128), f32)],
        [g7, dy_one, z_one, stat1, row(gain_one), own, wrh, wrl, xth, xtl, grad_pre],
    )
    grad_w_reduce, grad_w_group, grad_w_expand, grad_w_squeeze, grad_excite, grad_bias = lax.psum(
        (reduce_term, group_term, expand_term, squeeze_term, excite_term, bias_term), both
    )
    grads_one = grads_one.reshape(-1)
    grads_two = grads_two.reshape(-1)
    grads_three = grads_three.reshape(-1)
    grad_bias = grad_bias.reshape(-1)
    return (
        block_out.reshape(images.shape),
        grad_images.reshape(images.shape),
        grad_w_reduce,
        grads_one[:mid],
        grads_one[mid:duo],
        grad_w_group.reshape(w_group.shape),
        grads_two[:duo],
        grads_two[duo:],
        grad_w_squeeze,
        grads_fc[0],
        grads_fc[1],
        jnp.concatenate([grad_excite, -grad_excite], axis=1),
        jnp.concatenate([grad_bias, -grad_bias]),
        grad_w_expand,
        grads_three[chan:],
        grads_three[:chan],
    )


def solution(mesh):
    maps = P("batch", "rows", None, None)
    return jax.shard_map(
        on_device,
        mesh=mesh,
        in_specs=(maps,) + (P(),) * 14 + (P("batch", None), P("batch", None), maps),
        out_specs=(maps, maps) + (P(),) * 14,
        check_vma=False,
    )
```

time: 737 us -> 357 us (0.48)
  blocking collectives: 418 us -> 94.5 us
  matrix products: 72.1 us -> 0 us
  Pallas kernels: 0 us -> 37.2 us
  other arithmetic: 39.9 us -> 3.29 us
  local copies, waits for them, and re-layouts: 31.1 us -> 67 us
  waiting for transfers between devices: 141 us -> 107 us
  starting transfers between devices: 12.1 us -> 31.8 us
    psum x13 -> x1, blocking collectives: 418 us -> 41 us  [on_device(): lax.psum((reduce_term, group_term, expand_term, squeeze_term, excite_term...]
    dot_general x39 -> x0, matrix products: 72.1 us -> none  [the longest x9 17.7 us: group_kernel_grad(): jnp.einsum('bhwgi,bhwgo->igo', window, grad_split, precision=highest)]
    all_to_all x0 -> x4, blocking collectives: none -> 53.5 us  [share(): return lax.all_to_all(tile, both, 0, 0)]
    unnamed x227 -> x196, local copies, waits for them, and re-layouts: 17.2 us -> 64.8 us
    pallas_call x0 -> x14, Pallas kernels: none -> 37.2 us  [call(): pl.pallas_call(body, out_shape=specs, scratch_shapes=list(scratch), compi...]
    psum x1, waiting for transfers between devices: 141 us -> 105 us  [on_device(): lax.psum((reduce_term, group_term, expand_term, squeeze_term, excite_term...]
    reduce_sum x12 -> x0, other arithmetic: 15.9 us -> none  [the longest x3 9.67 us: norm_back(): jnp.sum(grad_out, axis=(0, 1, 2))]
    all_to_all x0 -> x3, starting transfers between devices: none -> 15.6 us  [share(): return lax.all_to_all(tile, both, 0, 0)]
  transfers between devices with their start and end apart: 5 -> 11, of which waited for: 2 -> 2; matrix products, arithmetic and copies ran while one was open for 5% -> 1% of each run, Pallas kernels for 0% -> 4%
where the time goes in v1:
time: 357 us; the launch traced here: 355 us
  waiting for transfers between devices  107 us (30%)
  blocking collectives  94.5 us (26%)
  local copies, waits for them, and re-layouts  67 us (19%)
  Pallas kernels  37.2 us (10%)
  starting transfers between devices  31.8 us (9%)
  between operations  14.5 us (4%)
    psum x1, waiting for transfers between devices, on_device(): lax.psum((reduce_term, group_term, expand_term, squeeze_term, excite_term...  105 us
    unnamed x196, local copies, waits for them, and re-layouts  64.8 us
    all_to_all x4, blocking collectives, share(): return lax.all_to_all(tile, both, 0, 0)  53.5 us
    psum x1, blocking collectives, on_device(): lax.psum((reduce_term, group_term, expand_term, squeeze_term, excite_term...  41 us
    pallas_call x14, Pallas kernels, call(): pl.pallas_call(body, out_shape=specs, scratch_shapes=list(scratch), compi...  37.2 us
    all_to_all x3, starting transfers between devices, share(): return lax.all_to_all(tile, both, 0, 0)  15.6 us
    ppermute x3, starting transfers between devices, halos(): above = lax.ppermute(last, 'rows', [(i, i + 1) for i in range(count - 1)])  12.3 us
  transfers between devices with their start and end apart: 11, of which 2 were waited for; matrix products, arithmetic and copies ran while one was open for 1% of the time, Pallas kernels for 4%

profile of v1, /device:TPU:0, one launch (start us, length us, event | category | flops | bytes accessed | tf_op | source)
XLA Modules:
  0.0 355.2 jit_solution(17312444977993641167)
XLA Ops:
  11.4 1.8 shard_map.297
  13.2 7.4 %all-to-all-start = ((f32[32,8,128]{2,1,0:T(8,128)}), f32[32,8,128]{2,1,0:T(8,128)}, u32[]{:S(2)}, u32[]{:S(2)}) async-start(f32[32,8,128]{2,1,0:T(8,128)} %get-tuple-element.79), calls=%async_computation | async-start | bytes 262144 | tf_op jit(solution)/shard_map/all_to_all | solution.py:108
  20.6 3.6 %collective-permute-start = (f32[128,256]{1,0:T(8,128)}, f32[128,256]{1,0:T(8,128)S(1)}, u32[]{:S(2)}, u32[]{:S(2)}) collective-permute-start(f32[128,256]{1,0:T(8,128)} %get-tuple-element.81), channel_id=1, source_target_pairs={{0,8},{8,16},{16,24},{1,9},{9,17},{17,25},{2,10},{10,18},{18,26},{... | collective-permute-start | bytes 393224 | tf_op jit(solution)/shard_map/ppermute | solution.py:113
  38.1 3.9 %shard_map.299 = (f32[768,256]{1,0:T(8,128)S(1)}, f32[512,512]{1,0:T(8,128)S(1)}, f32[128,512]{1,0:T(8,128)S(1)}, f32[128,512]{1,0:T(8,128)S(1)}, f32[8,128]{1,0:T(8,128)S(1)}, /*index=5*/f32[32,8,128]{2,1,0:T(8,128)S(1)}) custom-call(f32[512,256]{1,0:T(8,128)S(1)} %get-tuple-element.80.z_ref, f32[128,256]{1,0:T(8,128)S(1)} %copy-done.55, ...), custom_call_target="tpu_custom_call" | custom-call | tf_op jit(solution)/shard_map/pallas_call | solution.py:98
  42.8 4.6 %collective-permute-start.2 = (f32[128,512]{1,0:T(8,128)S(1)}, f32[128,512]{1,0:T(8,128)S(1)}, u32[]{:S(2)}, u32[]{:S(2)}) collective-permute-start(f32[128,512]{1,0:T(8,128)S(1)} %get-tuple-element.100), channel_id=1, source_target_pairs={{0,8},{8,16},{16,24},{1,9},{9,17},{17,25},{2,10},{10,18},{18,26},{... | collective-permute-start | bytes 786440 | tf_op jit(solution)/shard_map/ppermute | solution.py:113
  48.7 15.6 %all_to_all.35.g2_ref = f32[32,8,128]{2,1,0:T(8,128)S(1)} all-to-all(f32[32,8,128]{2,1,0:T(8,128)S(1)} %get-tuple-element.88), channel_id=1, replica_groups=mesh['rows'=4,'batch'=8] {'rows','batch'}, dimensions={0} | all-to-all | bytes 262144 | tf_op jit(solution)/shard_map/all_to_all | solution.py:108
  64.3 1.7 shard_map.300
  72.7 11.1 %all_to_all.36.g3_ref = f32[32,8,128]{2,1,0:T(8,128)S(1)} all-to-all(f32[32,8,128]{2,1,0:T(8,128)} %copy-done.58), channel_id=1, replica_groups=mesh['rows'=4,'batch'=8] {'rows','batch'}, dimensions={0} | all-to-all | bytes 262144 | tf_op jit(solution)/shard_map/all_to_all | solution.py:108
  90.0 1.8 shard_map.301
  94.1 13.6 %all_to_all.37.g4_ref = f32[32,16,128]{2,1,0:T(8,128)S(1)} all-to-all(f32[32,16,128]{2,1,0:T(8,128)S(1)} %get-tuple-element.93), channel_id=1, replica_groups=mesh['rows'=4,'batch'=8] {'rows','batch'}, dimensions={0} | all-to-all | bytes 524288 | tf_op jit(solution)/shard_map/all_to_all | solution.py:108
  110.7 4.2 %shard_map.302 = (f32[512,1024]{1,0:T(8,128)}, f32[512,1024]{1,0:T(8,128)S(1)}, f32[16,128]{1,0:T(8,128)S(1)}, f32[32,16,128]{2,1,0:T(8,128)S(1)}) custom-call(f32[32,8,128]{2,1,0:T(8,128)} %all-to-all-done.g1_ref, f32[32,16,128]{2,1,0:T(8,128)S(1)} %all_to_all.37.g4_ref, f32[1,1024]{1,0:T(1,128)S(1)} %bitcast.41, f32[1,1024]{1,0:T(1,128)S(1)} %bitcast.50, ...), custom_call_target="tpu_custom_call" | custom-call | tf_op jit(solution)/shard_map/pallas_call | solution.py:98
  115.0 13.3 %all_to_all.38.g5_ref = f32[32,16,128]{2,1,0:T(8,128)S(1)} all-to-all(f32[32,16,128]{2,1,0:T(8,128)S(1)} %get-tuple-element.96), channel_id=1, replica_groups=mesh['rows'=4,'batch'=8] {'rows','batch'}, dimensions={0} | all-to-all | bytes 524288 | tf_op jit(solution)/shard_map/all_to_all | solution.py:108
  128.3 1.9 shard_map.304
  135.7 3.3 all-to-all-start.5
  139.0 4.1 %collective-permute-start.4 = (f32[128,256]{1,0:T(8,128)}, f32[128,256]{1,0:T(8,128)}, u32[]{:S(2)}, u32[]{:S(2)}) collective-permute-start(f32[128,256]{1,0:T(8,128)} %copy-done.90), channel_id=1, source_target_pairs={{0,8},{8,16},{16,24},{1,9},{9,17},{17,25},{2,10},{10,18},{18,26},{... | collective-permute-start | bytes 393224 | tf_op jit(solution)/shard_map/ppermute | solution.py:113
  149.7 2.1 collective-permute-done.5.below_ref
  151.9 9.4 %shard_map.306 = (bf16[768,512]{1,0:T(8,128)(2,1)}, bf16[768,512]{1,0:T(8,128)(2,1)}, f32[1152,512]{1,0:T(8,128)}, f32[8,128]{1,0:T(8,128)}, f32[2,128]{1,0:T(2,128)}, /*index=5*/f32[256,128]{1,0:T(8,128)}) custom-call(f32[32,16,128]{2,1,0:T(8,128)} %all-to-all-done.5.g6_ref, f32[32,8,1024]{2,1,0:T(8,128)} %bitcast.57, f32[64,128]{1,0:T(8,128)} %copy-done.68, ...), custom_call_target="tpu_custom_call" | custom-call | tf_op jit(solution)/shard_map/pallas_call | solution.py:98
  163.6 2.7 shard_map.307
  167.8 4.9 %all-to-all-start.6 = ((f32[32,8,128]{2,1,0:T(8,128)}), f32[32,8,128]{2,1,0:T(8,128)}, u32[]{:S(2)}, u32[]{:S(2)}) async-start(f32[32,8,128]{2,1,0:T(8,128)} %copy-done.59), calls=%async_computation.6 | async-start | bytes 262144 | tf_op jit(solution)/shard_map/all_to_all | solution.py:108
  178.4 1.8 shard_map.310
  186.8 4.1 %shard_map.309 = (f32[512,1024]{1,0:T(8,128)}, f32[1024,256]{1,0:T(8,128)S(1)}, f32[8,128]{1,0:T(8,128)S(1)}) custom-call(f32[32,8,128]{2,1,0:T(8,128)} %all-to-all-done.6.g7_ref, f32[512,256]{1,0:T(8,128)S(1)} %copy-done.51, f32[512,256]{1,0:T(8,128)S(1)} %copy-done.12, f32[8,128]{1,0:T(8,128)S(1)} %copy-done.61, f32[1,256]{1,0:T(1,128)S(1)} %bitcast.45, ...), custom_call_target="tpu_custom_call" | custom-call | tf_op jit(solution)/shard_map/pallas_call | solution.py:98
  191.9 41.0 %psum.46 = f32[256]{0:T(256)S(1)} all-reduce(f32[256]{0:T(256)S(1)} %bitcast.54), channel_id=1, replica_groups=mesh['rows'=4,'batch'=8] {'rows','batch'}, use_global_device_ids=true, to_apply=%region_4.0 | all-reduce | flops 256 | bytes 2048 | tf_op jit(solution)/shard_map/psum | solution.py:644
  235.7 104.5 %all-reduce.3.cloned.1.call-done = (f32[1024,256]{1,0:T(8,128)}, f32[3,3,128,512]{3,2,1,0:T(8,128)}, f32[256,128]{1,0:T(8,128)}, f32[128,256]{1,0:T(8,128)}, f32[256,1024]{1,0:T(8,128)}) async-done(((f32[1024,256]{1,0:T(8,128)}, f32[3,3,128,512]{3,2,1,0:T(8,128)}, f32[256,128]{1,0:T(8,128)}, f32[128,256]{1,0:T(8,128)}, f32[256,1024]{1,0:T(8,128)}), (f32[1024,256]{1,0:T(8,128)}, ...) | async-done | bytes 4718608 | tf_op jit(solution)/shard_map/psum | solution.py:644
  343.0 2.3 copy.39
  (223 shorter events, 76.0 us)
Async XLA Ops:
  13.1 55.1 %copy-start.18 = (f32[768,128]{1,0:T(8,128)}, f32[768,128]{1,0:T(8,128)S(1)}, u32[]{:S(2)}) copy-start(f32[768,128]{1,0:T(8,128)S(1)} %get-tuple-element.83.ext_ref) | copy-start | bytes 1179652
  13.2 21.7 %all-to-all-start = ((f32[32,8,128]{2,1,0:T(8,128)}), f32[32,8,128]{2,1,0:T(8,128)}, u32[]{:S(2)}, u32[]{:S(2)}) async-start(f32[32,8,128]{2,1,0:T(8,128)} %get-tuple-element.79), calls=%async_computation | async-start | bytes 262144 | tf_op jit(solution)/shard_map/all_to_all | solution.py:108
  20.6 131.3 %all-gather.3.cloned.1.call-start = ((), (), s32[]{:S(2)}) async-start(), calls=%async_computation.7 | async-start | bytes 1081344 | tf_op jit(solution)/shard_map/all_gather | solution.py:573
  20.6 12.9 %collective-permute-start = (f32[128,256]{1,0:T(8,128)}, f32[128,256]{1,0:T(8,128)S(1)}, u32[]{:S(2)}, u32[]{:S(2)}) collective-permute-start(f32[128,256]{1,0:T(8,128)} %get-tuple-element.81), channel_id=1, source_target_pairs={{0,8},{8,16},{16,24},{1,9},{9,17},{17,25},{2,10},{10,18},{18,26},{... | collective-permute-start | bytes 393224 | tf_op jit(solution)/shard_map/ppermute | solution.py:113
  24.2 9.9 %collective-permute-start.1 = (f32[128,256]{1,0:T(8,128)}, f32[128,256]{1,0:T(8,128)S(1)}, u32[]{:S(2)}, u32[]{:S(2)}) collective-permute-start(f32[128,256]{1,0:T(8,128)} %get-tuple-element.82), channel_id=1, source_target_pairs={{8,0},{16,8},{24,16},{9,1},{17,9},{25,17},{10,2},{18,10},{26,18},{... | collective-permute-start | bytes 393224 | tf_op jit(solution)/shard_map/ppermute | solution.py:114
  33.5 30.7 %copy-start.8 = (bf16[1152,512]{1,0:T(8,128)(2,1)}, bf16[1152,512]{1,0:T(8,128)(2,1)S(1)}, u32[]{:S(2)}) copy-start(bf16[1152,512]{1,0:T(8,128)(2,1)S(1)} %get-tuple-element.86.wl_ref) | copy-start | bytes 3538948
  38.0 26.2 %copy-start.43 = (f32[256,128]{1,0:T(8,128)S(1)}, f32[256,128]{1,0:T(8,128)}, u32[]{:S(2)}) copy-start(f32[256,128]{1,0:T(8,128)} %wsq_ref.1) | copy-start | bytes 393220
  38.0 26.2 %copy-start.64 = (s32[8,16]{1,0:T(8,128)S(1)}, s32[8,16]{1,0:T(8,128)}, u32[]{:S(2)}) copy-start(s32[8,16]{1,0:T(8,128)} %rows_ref.7) | copy-start | bytes 1540
  38.0 26.2 %copy-start.66 = (s32[8,16]{1,0:T(8,128)S(1)}, s32[8,16]{1,0:T(8,128)}, u32[]{:S(2)}) copy-start(s32[8,16]{1,0:T(8,128)} %cols_ref.7) | copy-start | bytes 1540
  38.0 26.2 %copy-start.70 = (f32[512]{0:T(512)S(1)}, f32[512]{0:T(512)}, u32[]{:S(2)}) copy-start(f32[512]{0:T(512)} %param.23) | copy-start | bytes 6148
  38.0 26.2 %copy-start.78 = (f32[512]{0:T(512)S(1)}, f32[512]{0:T(512)}, u32[]{:S(2)}) copy-start(f32[512]{0:T(512)} %param.24) | copy-start | bytes 6148
  42.8 85.5 %copy-start.60 = (f32[8,128]{1,0:T(8,128)}, f32[8,128]{1,0:T(8,128)S(1)}, u32[]{:S(2)}) copy-start(f32[8,128]{1,0:T(8,128)S(1)} %get-tuple-element.97.stat1_ref.stat_ref) | copy-start | bytes 12292
  42.8 25.4 %collective-permute-start.2 = (f32[128,512]{1,0:T(8,128)S(1)}, f32[128,512]{1,0:T(8,128)S(1)}, u32[]{:S(2)}, u32[]{:S(2)}) collective-permute-start(f32[128,512]{1,0:T(8,128)S(1)} %get-tuple-element.100), channel_id=1, source_target_pairs={{0,8},{8,16},{16,24},{1,9},{9,17},{17,25},{2,10},{10,18},{18,26},{... | collective-permute-start | bytes 786440 | tf_op jit(solution)/shard_map/ppermute | solution.py:113
  47.4 20.9 %collective-permute-start.3 = (f32[128,512]{1,0:T(8,128)S(1)}, f32[128,512]{1,0:T(8,128)S(1)}, u32[]{:S(2)}, u32[]{:S(2)}) collective-permute-start(f32[128,512]{1,0:T(8,128)S(1)} %get-tuple-element.101), channel_id=1, source_target_pairs={{8,0},{16,8},{24,16},{9,1},{17,9},{25,17},{10,2},{18,10},{26,18},{... | collective-permute-start | bytes 786440 | tf_op jit(solution)/shard_map/ppermute | solution.py:114
  72.6 35.1 %copy-start.1 = (f32[8,4,16,1024]{3,2,1,0:T(8,128)S(1)}, f32[8,4,16,1024]{3,2,1,0:T(8,128)}, u32[]{:S(2)}) copy-start(f32[8,4,16,1024]{3,2,1,0:T(8,128)} %param.18) | copy-start | bytes 6291460
  94.1 34.1 %copy-start.62 = (f32[8,512]{1,0:T(8,128)}, f32[8,512]{1,0:T(8,128)S(1)}, u32[]{:S(2)}) copy-start(f32[8,512]{1,0:T(8,128)S(1)} %get-tuple-element.105.weights_ref) | copy-start | bytes 49156
  135.7 16.2 %all-to-all-start.5 = ((f32[32,16,128]{2,1,0:T(8,128)}), f32[32,16,128]{2,1,0:T(8,128)}, u32[]{:S(2)}, u32[]{:S(2)}) async-start(f32[32,16,128]{2,1,0:T(8,128)} %copy-done.53), calls=%async_computation.5 | async-start | bytes 524288 | tf_op jit(solution)/shard_map/all_to_all | solution.py:108
  139.0 10.7 %collective-permute-start.4 = (f32[128,256]{1,0:T(8,128)}, f32[128,256]{1,0:T(8,128)}, u32[]{:S(2)}, u32[]{:S(2)}) collective-permute-start(f32[128,256]{1,0:T(8,128)} %copy-done.90), channel_id=1, source_target_pairs={{0,8},{8,16},{16,24},{1,9},{9,17},{17,25},{2,10},{10,18},{18,26},{... | collective-permute-start | bytes 393224 | tf_op jit(solution)/shard_map/ppermute | solution.py:113
  143.1 8.7 %collective-permute-start.5 = (f32[128,256]{1,0:T(8,128)}, f32[128,256]{1,0:T(8,128)}, u32[]{:S(2)}, u32[]{:S(2)}) collective-permute-start(f32[128,256]{1,0:T(8,128)} %copy-done.89), channel_id=1, source_target_pairs={{8,0},{16,8},{24,16},{9,1},{17,9},{25,17},{10,2},{18,10},{26,18},{... | collective-permute-start | bytes 393224 | tf_op jit(solution)/shard_map/ppermute | solution.py:114
  167.8 13.4 %all-to-all-start.6 = ((f32[32,8,128]{2,1,0:T(8,128)}), f32[32,8,128]{2,1,0:T(8,128)}, u32[]{:S(2)}, u32[]{:S(2)}) async-start(f32[32,8,128]{2,1,0:T(8,128)} %copy-done.59), calls=%async_computation.6 | async-start | bytes 262144 | tf_op jit(solution)/shard_map/all_to_all | solution.py:108
  172.7 167.6 %all-reduce.3.cloned.1.call-start = ((), (), s32[]{:S(2)}) async-start(), calls=%async_computation.8 | async-start | bytes 9437184 | tf_op jit(solution)/shard_map/psum | solution.py:644
  191.9 41.6 %copy-start.77 = (f32[16,128]{1,0:T(8,128)S(1)}, f32[16,128]{1,0:T(8,128)}, u32[]{:S(2)}) copy-start(f32[16,128]{1,0:T(8,128)} %copy-done.76) | copy-start | bytes 24580
  191.9 42.2 %copy-start.95 = (f32[2,128]{1,0:T(2,128)S(1)}, f32[2,128]{1,0:T(2,128)}, u32[]{:S(2)}) copy-start(f32[2,128]{1,0:T(2,128)} %get-tuple-element.132) | copy-start | bytes 3076
  191.9 42.7 %copy-start.94 = (f32[8,128]{1,0:T(8,128)S(1)}, f32[8,128]{1,0:T(8,128)}, u32[]{:S(2)}) copy-start(f32[8,128]{1,0:T(8,128)} %get-tuple-element.130) | copy-start | bytes 12292
  (83 other events, 254.4 us)
Sparse Core Ops, SparseCore 0:
  72.8 52.9 all-gather.2
  192.0 148.2 all-reduce.2

commit v2 on v1

v2 whole, which is shorter than its diff:
```python
import functools

import jax
import jax.numpy as jnp
from jax import lax
from jax.experimental import pallas as pl
from jax.experimental.pallas import tpu as pltpu
from jax.sharding import PartitionSpec as P

epsilon = 1e-05
f32 = jnp.float32
bf16 = jnp.bfloat16
highest = lax.Precision.HIGHEST
both = ("rows", "batch")
NN = ((1,), (0,))
NT = ((1,), (1,))
TN = ((0,), (0,))


def split(values):
    high = values.astype(bf16)
    return high, (values - high.astype(f32)).astype(bf16)


def dot(left, right, dims):
    return lax.dot_general(left, right, (dims, ((), ())), preferred_element_type=f32)


def product(left, right, dims):
    return dot(left[0], right[0], dims) + (
        dot(left[0], right[1], dims) + dot(left[1], right[0], dims)
    )


def exact(left, right, dims):
    return lax.dot_general(
        left, right, (dims, ((), ())), preferred_element_type=f32, precision=highest
    )


def put(tile, row, vector):
    for j in range(vector.shape[1] // 128):
        tile[row + j : row + j + 1, :] = vector[:, j * 128 : (j + 1) * 128]


def get(tile, row, count):
    return jnp.concatenate([tile[row + j : row + j + 1, :] for j in range(count)], axis=1)


def wide(mask, width):
    return jnp.concatenate([mask] * (width // 128), axis=1)


def column_sum(values):
    return jnp.sum(values, axis=0, keepdims=True)


def image_sum(values, images):
    return jnp.sum(values.reshape(images, values.shape[0] // images, values.shape[1]), axis=1)


def per_image(vector, values):
    count, width = vector.shape
    each = values.shape[0] // count
    return jnp.broadcast_to(vector[:, None, :], (count, each, width)).reshape(values.shape[0], width)


def merge_stats(gathered, counts, width):
    groups = width // 128
    own = jnp.maximum(counts, 1.0)
    total = jnp.sum(counts, axis=0)
    means, inverses = [], []
    for j in range(groups):
        sums = gathered[:, j, :]
        squares = gathered[:, groups + j, :]
        mean = jnp.sum(sums, axis=0, keepdims=True) / total
        shift = sums / own - mean
        spread = jnp.sum(squares + counts * shift * shift, axis=0, keepdims=True) / total
        means.append(mean)
        inverses.append(lax.rsqrt(spread + epsilon))
    return jnp.concatenate(means, axis=1), jnp.concatenate(inverses, axis=1), total


def local_stats(values, mask, count):
    sums = column_sum(values * mask)
    centered = values - sums / jnp.maximum(count, 1.0)
    return sums, column_sum(centered * centered * mask)


def own_rows(extended, images):
    rows, width = extended.shape
    tall = rows // images // 16
    return extended.reshape(images, tall, 16, width)[:, 1 : tall - 1].reshape(-1, width)


class In:
    def __init__(self, source, target, sems, chunks):
        self.ref, self.shape, self.dtype = target, target.shape, target.dtype
        rows = self.shape[0] // chunks
        self.parts = [pl.ds(i * rows, rows) for i in range(chunks)]
        self.copies = [
            pltpu.make_async_copy(source.at[part], target.at[part], sems.at[i])
            for i, part in enumerate(self.parts)
        ]
        self.due = list(range(chunks))

    def start(self):
        for copy in self.copies:
            copy.start()

    def ready(self):
        while self.due:
            self.copies[self.due.pop(0)].wait()
        return self.ref

    def chunk(self, i):
        if i in self.due:
            self.due.remove(i)
            self.copies[i].wait()
        return self.ref[self.parts[i]]

    def __getitem__(self, index):
        return self.ready()[index]


class Out:
    def __init__(self, source, target, sems, chunks):
        self.ref, self.shape, self.dtype = source, source.shape, source.dtype
        rows = self.shape[0] // chunks
        self.parts = [pl.ds(i * rows, rows) for i in range(chunks)]
        self.copies = [
            pltpu.make_async_copy(source.at[part], target.at[part], sems.at[i])
            for i, part in enumerate(self.parts)
        ]
        self.sent = set()

    def send(self, i=None):
        for k in range(len(self.copies)) if i is None else [i]:
            if k not in self.sent:
                self.sent.add(k)
                self.copies[k].start()

    def finish(self):
        self.send()
        for copy in self.copies:
            copy.wait()

    def put(self, i, value):
        self.ref[self.parts[i]] = value
        self.send(i)

    def __getitem__(self, index):
        return self.ref[index]

    def __setitem__(self, index, value):
        self.ref[index] = value


def call(body, outs, ins, scratch=(), limit=60, chunks=None, out_chunks=None, after=()):
    chunks, out_chunks = chunks or {}, out_chunks or {}
    n, m, k = len(ins), len(outs), len(after)
    in_parts = [chunks.get(i, 1) for i in range(n)]
    out_parts = [out_chunks.get(i, 1) for i in range(m)]

    def inner(*refs):
        sources, targets, local = refs[:n], refs[n + k : n + k + m], refs[n + k + m :]
        in_sems, out_sems = local[n + m : n + m + n], local[n + m + n : n + m + n + m]
        given = [In(sources[i], local[i], in_sems[i], in_parts[i]) for i in range(n)]
        made = [Out(local[n + i], targets[i], out_sems[i], out_parts[i]) for i in range(m)]
        for each in given:
            each.start()
        body(*given, *made, *local[n + m + n + m :])
        for each in given:
            each.ready()
        for each in made:
            each.send()
        for each in made:
            each.finish()

    return pl.pallas_call(
        inner,
        out_shape=[jax.ShapeDtypeStruct(shape, kind) for shape, kind in outs],
        in_specs=[pl.BlockSpec(memory_space=pltpu.HBM)] * (n + k),
        out_specs=[pl.BlockSpec(memory_space=pltpu.HBM)] * m,
        scratch_shapes=[
            *[pltpu.VMEM(a.shape, a.dtype) for a in ins],
            *[pltpu.VMEM(shape, kind) for shape, kind in outs],
            *[pltpu.SemaphoreType.DMA((k,)) for k in in_parts + out_parts],
            *scratch,
        ],
        compiler_params=pltpu.CompilerParams(vmem_limit_bytes=limit * 2**20),
        cost_estimate=pl.CostEstimate(flops=1, bytes_accessed=1, transcendentals=0),
    )(*ins, *after)


def local_call(body, outs, ins, scratch=(), limit=16, after=()):
    n, k = len(ins), len(after)

    def inner(*refs):
        body(*refs[:n], *refs[n + k :])

    return pl.pallas_call(
        inner,
        out_shape=[jax.ShapeDtypeStruct(shape, kind) for shape, kind in outs],
        in_specs=[pl.BlockSpec(memory_space=pltpu.VMEM)] * n + [pl.BlockSpec(memory_space=pl.ANY)] * k,
        out_specs=[pl.BlockSpec(memory_space=pltpu.VMEM)] * len(outs),
        scratch_shapes=list(scratch),
        compiler_params=pltpu.CompilerParams(vmem_limit_bytes=limit * 2**20),
        cost_estimate=pl.CostEstimate(flops=1, bytes_accessed=1, transcendentals=0),
    )(*ins, *after)


def share(tile):
    return lax.all_to_all(tile, both, 0, 0)


def halos(first, last):
    count = lax.axis_size("rows")
    above = lax.ppermute(last, "rows", [(i, i + 1) for i in range(count - 1)])
    below = lax.ppermute(first, "rows", [(i + 1, i) for i in range(count - 1)])
    return above, below


def flip(values, axis, bits):
    return lax.ppermute(values, axis, [(i, i ^ bits) for i in range(lax.axis_size(axis))])


class Digit:
    def __init__(self, axis, unit, size):
        self.axis, self.unit, self.size = axis, unit, size

    def own(self):
        return lax.axis_index(self.axis) // self.unit % self.size

    def send(self, pieces):
        return [pieces[0]] + [flip(pieces[j], self.axis, j * self.unit) for j in range(1, self.size)]

    def bits(self):
        return [Digit(self.axis, self.unit << i, 2) for i in range(self.size.bit_length() - 1)]

    def scatter(self, parts, outs):
        size = outs[0].shape[0]
        own = self.own()
        for j, out in enumerate(outs):
            at = pl.ds(pl.multiple_of((own ^ j) * size, 8), size)
            total = parts[0][at, :]
            for part in parts[1:]:
                total = total + part[at, :]
            out[...] = total

    def gather(self, pieces, out):
        size = pieces[0].shape[0]
        own = self.own()
        for j, piece in enumerate(pieces):
            out[pl.ds(pl.multiple_of((own ^ j) * size, 8), size), :] = piece[...]

    def outs(self, rows, width):
        return [((rows // self.size, width), f32)] * self.size


def digits():
    rows, batch = lax.axis_size("rows"), lax.axis_size("batch")
    depth = min(4, batch // 2)
    return Digit("batch", 1, 2), Digit("rows", 1, rows), Digit("batch", 2, depth), Digit("batch", 2 * depth, batch // (2 * depth))


def gate(value, after):
    return pl.pallas_call(
        lambda *refs: None,
        out_shape=jax.ShapeDtypeStruct(value.shape, value.dtype),
        in_specs=[pl.BlockSpec(memory_space=pl.ANY)] * (1 + len(after)),
        out_specs=pl.BlockSpec(memory_space=pl.ANY),
        input_output_aliases={0: 0},
    )(value, *after)


def scatter_kernel(digit, count, *refs):
    digit.scatter(refs[:count], refs[count:])


def sum_kernel(*refs):
    total = refs[0][...]
    for ref in refs[1:-1]:
        total = total + ref[...]
    refs[-1][...] = total


def gather_kernel(digit, *refs):
    digit.gather(refs[:-1], refs[-1])


def scatter_more(digit, pieces, after=()):
    rows, width = pieces[0].shape
    body = functools.partial(scatter_kernel, digit, len(pieces))
    return local_call(body, digit.outs(rows, width), pieces, after=after)


def add_up(pieces, after=()):
    return local_call(sum_kernel, [(pieces[0].shape, f32)], pieces, after=after)[0]


def finish_sum(pieces, extra, after=()):
    total = add_up(pieces, after)
    if extra.size > 1:
        total = add_up(extra.send([total] * extra.size))
    return total


def gather_more(digit, pieces, after=()):
    rows, width = pieces[0].shape
    return local_call(functools.partial(gather_kernel, digit), [((rows * digit.size, width), f32)], pieces, after=after)[0]


def reduce_kernel(rows_ref, cols_ref, w_ref, x_ref, z_ref, ext_ref, own_ref, first_ref, last_ref, wrh_ref, wrl_ref, pay_ref,
                  tile):
    images = rows_ref.shape[0]
    tall = x_ref.shape[0] // images // 16
    shape = (images, tall + 2, 16, 16)
    start = lax.axis_index("rows") * tall - 1
    lane = lax.broadcasted_iota(jnp.int32, shape, 3).reshape(-1, 16)
    at_row = lax.broadcasted_iota(jnp.int32, shape, 1).reshape(-1, 16) + start
    at_col = lax.broadcasted_iota(jnp.int32, shape, 2).reshape(-1, 16)
    row_valid = per_image(rows_ref[...].astype(f32), lane)
    col_valid = per_image(cols_ref[...].astype(f32), lane)
    in_row = jnp.sum(jnp.where(lane == at_row, row_valid, 0.0), axis=1, keepdims=True)
    in_col = jnp.sum(jnp.where(lane == at_col, col_valid, 0.0), axis=1, keepdims=True)
    mask = jnp.broadcast_to(in_row * in_col, (in_row.shape[0], 128)).reshape(ext_ref.shape)
    ext_ref[...] = mask
    own = mask[:, 1 : tall + 1].reshape(-1, 128)
    own_ref[...] = own
    wrh_ref[...], wrl_ref[...] = split(w_ref[...])
    weight = (wrh_ref[...], wrl_ref[...])
    for i in range(len(x_ref.parts)):
        z_ref[x_ref.parts[i]] = product(split(x_ref.chunk(i)), weight, NN)
    z = z_ref[...]
    edges = z.reshape(images, tall, 16, -1)
    first_ref[...] = edges[:, 0].reshape(first_ref.shape)
    last_ref[...] = edges[:, tall - 1].reshape(last_ref.shape)
    for each in (first_ref, last_ref, z_ref, ext_ref, own_ref, wrh_ref, wrl_ref):
        each.send()
    count = column_sum(own)
    sums, squares = local_stats(z, wide(own, z.shape[1]), wide(count, z.shape[1]))
    tile[...] = jnp.zeros_like(tile)
    put(tile, 0, sums)
    put(tile, 2, squares)
    put(tile, 4, count)
    pay_ref[...] = jnp.broadcast_to(tile[...][None], pay_ref.shape)


def parts_kernel(wg_ref, we_ref, *refs):
    vectors, (wgh_ref, wgl_ref, weh_ref, wel_ref, par_ref) = refs[:-5], refs[-5:]
    row = 0
    for vector in vectors:
        put(par_ref, row, vector[...])
        row += vector.shape[1] // 128
    for source, high_ref, low_ref in ((wg_ref, wgh_ref, wgl_ref), (we_ref, weh_ref, wel_ref)):
        for i in range(len(source.parts)):
            high, low = split(source.chunk(i))
            high_ref.put(i, high)
            low_ref.put(i, low)


def turned_kernel(x_ref, high_ref, low_ref):
    high_ref[...], low_ref[...] = split(x_ref[...].T)


def moved(values, step):
    count = values.shape[0]
    at = lax.broadcasted_iota(jnp.int32, values.shape, 0) & 15
    if step == 0:
        return values
    if step > 0:
        return jnp.where(at < 15, pltpu.roll(values, count - 1, 0), 0.0)
    return jnp.where(at > 0, pltpu.roll(values, 1, 0), 0.0)


def window(extended, images, row, width):
    tall = extended.shape[0] // images // 16
    cells = extended.reshape(images, tall, 16, extended.shape[1])
    return cells[:, row : row + tall - 2, :, width].reshape(images * (tall - 2) * 16, -1)


def extend(place, cells, above, below):
    images, tall, broad, width = place.shape
    place[:, 1 : tall - 1] = cells[...].reshape(images, tall - 2, broad, width)
    place[:, 0] = above[...].reshape(images, broad, width)
    place[:, tall - 1] = below[...].reshape(images, broad, width)
    return place[...].reshape(-1, width)


def conv_kernel(g1_ref, par_ref, z_ref, ext_ref, above_ref, below_ref, own_ref, wh_ref, wl_ref,
                z2_ref, a_ref, stat_ref, counts_ref, pay_ref, tile, zext):
    images = zext.shape[0]
    tall = zext.shape[1] - 2
    width = z_ref.shape[1]
    group = width // 2
    gathered = g1_ref[...]
    counts = gathered[:, 4, :]
    counts_ref[...] = counts
    mean, inv, total = merge_stats(gathered, counts, width)
    tile[...] = jnp.zeros_like(tile)
    put(tile, 0, mean)
    put(tile, 2, inv)
    put(tile, 4, total[None])
    stat_ref[...] = tile[...]
    y = (extend(zext, z_ref, above_ref, below_ref) - mean) * inv * get(par_ref, 0, 2) + get(par_ref, 2, 2)
    a = y * jax.nn.sigmoid(y) * wide(ext_ref[...].reshape(-1, 128), width)
    a_ref[...] = a
    a_ref.send()
    shifted = [split(moved(a, step)) for step in (-1, 0, 1)]
    half = z2_ref.shape[1] // 2
    for g in range(2):
        cols = slice(g * group, (g + 1) * group)
        left = [
            jnp.concatenate(
                [window(shifted[tap % 3][part], images, tap // 3, cols) for tap in range(9)], axis=1
            )
            for part in range(2)
        ]
        outs = slice(g * half, (g + 1) * half)
        z2_ref[:, outs] = product(left, (wh_ref[:, outs], wl_ref[:, outs]), NN)
    z2_ref.send()
    z2 = z2_ref[...]
    own = own_ref[...]
    sums, squares = local_stats(z2, wide(own, z2.shape[1]), wide(column_sum(own), z2.shape[1]))
    put(tile, 0, sums)
    put(tile, 4, squares)
    pay_ref[...] = jnp.broadcast_to(tile[...][None], pay_ref.shape)


def taps_kernel(images, a_ref, high_ref, low_ref):
    group = a_ref.shape[1] // 2
    a = a_ref[...]
    shifted = [moved(a, step) for step in (-1, 0, 1)]
    for g in range(2):
        cols = slice(g * group, (g + 1) * group)
        for tap in range(9):
            high, low = split(window(shifted[tap % 3], images, tap // 3, cols).T)
            high_ref[g, tap * group : (tap + 1) * group, :] = high
            low_ref[g, tap * group : (tap + 1) * group, :] = low
        high_ref.send(g)
        low_ref.send(g)


def pixel_count(rows_ref, cols_ref):
    rows = jnp.sum(rows_ref[...].astype(f32), axis=1, keepdims=True)
    return rows * jnp.sum(cols_ref[...].astype(f32), axis=1, keepdims=True)


def pool_kernel(g2_ref, counts_ref, par_ref, rows_ref, cols_ref, z_ref, own_ref, w_ref, a_ref, stat_ref, pooled_ref, pay_ref):
    images = rows_ref.shape[0]
    width = z_ref.shape[1]
    mid = width // 2
    mean, inv, total = merge_stats(g2_ref[...], counts_ref[...], width)
    put(stat_ref, 0, mean)
    put(stat_ref, 4, inv)
    gain, shift = get(par_ref, 4, 4), get(par_ref, 8, 4)
    pieces = len(z_ref.parts)
    sums = []
    for i in range(pieces):
        y = (z_ref.chunk(i) - mean) * inv * gain + shift
        a = y * jax.nn.sigmoid(y) * wide(own_ref.chunk(i), width)
        a_ref.put(i, a)
        sums.append(image_sum(a, images // pieces))
    sums = jnp.concatenate(sums, axis=0)
    pooled = (sums[:, :mid] + sums[:, mid:]) / pixel_count(rows_ref, cols_ref)
    pooled_ref[...] = pooled
    pay_ref[...] = jnp.broadcast_to(exact(pooled, w_ref[...], NN)[None], pay_ref.shape)


def slope_of(values, mean, inv, gain, shift):
    normed = (values - mean) * inv
    y = normed * gain + shift
    sigma = jax.nn.sigmoid(y)
    return sigma * (1.0 + y * (1.0 - sigma)), normed


def slope_kernel(stat_ref, par_ref, rows_ref, cols_ref, own_ref, z_ref, slope_ref, normed_ref, sums_ref):
    images = rows_ref.shape[0]
    width = z_ref.shape[1]
    mean, inv = get(stat_ref, 0, 4), get(stat_ref, 4, 4)
    gain, shift = get(par_ref, 4, 4), get(par_ref, 8, 4)
    pieces = len(z_ref.parts)
    sums, cross = [], []
    for i in range(pieces):
        slope, normed = slope_of(z_ref.chunk(i), mean, inv, gain, shift)
        slope = slope * wide(own_ref.chunk(i), width)
        normed_ref.put(i, normed)
        slope_ref.put(i, slope)
        sums.append(image_sum(slope, images // pieces))
        cross.append(image_sum(slope * normed, images // pieces))
    pixels = pixel_count(rows_ref, cols_ref)
    sums_ref[:, :width] = jnp.concatenate(sums, axis=0) / pixels
    sums_ref[:, width:] = jnp.concatenate(cross, axis=0) / pixels


def expand_kernel(g3_ref, par_ref, w_ref, a_ref, wh_ref, wl_ref, own_ref,
                  mixed_ref, z_ref, weights_ref, normed_ref, pre_ref, act_ref, inv_ref, pay_ref, tile, acts):
    own_images = weights_ref.shape[0]
    mid = mixed_ref.shape[1]
    devices = g3_ref.shape[0]
    rows = lax.axis_size("rows")
    f_one = jnp.sum(g3_ref[...].reshape(rows, devices // rows * own_images, -1), axis=0)
    mean = jnp.mean(f_one, axis=0, keepdims=True)
    centered = f_one - mean
    inv = lax.rsqrt(jnp.mean(centered * centered, axis=0, keepdims=True) + epsilon)
    normed = centered * inv
    pre = normed * par_ref[12:13, :] + par_ref[13:14, :]
    normed_ref[...] = normed
    pre_ref[...] = pre
    inv_ref[...] = inv
    acts[...] = pre * jax.nn.sigmoid(pre)
    at = pl.multiple_of(lax.axis_index("batch") * own_images, own_images)
    act = acts[pl.ds(at, own_images), :]
    act_ref[...] = act
    logits = exact(act, w_ref[...], NN) + get(par_ref, 14, 4)
    lead = logits[:, :mid] - logits[:, mid:]
    first, second = jax.nn.sigmoid(lead), jax.nn.sigmoid(-lead)
    weights_ref[:, :mid] = first
    weights_ref[:, mid:] = second
    a = a_ref[...]
    mixed = per_image(first, a) * a[:, :mid] + per_image(second, a) * a[:, mid:]
    mixed_ref[...] = mixed
    mixed_ref.send()
    left, right = split(mixed), (wh_ref[...], wl_ref[...])
    for i, part in enumerate(z_ref.parts):
        rows = slice(part.start, part.start + part.size)
        z_ref.put(i, product([each[rows] for each in left], right, NN))
    z = z_ref[...]
    width = z.shape[1]
    own = wide(own_ref[...], width)
    sums, squares = local_stats(z, own, wide(column_sum(own_ref[...]), width))
    put(tile, 0, sums)
    put(tile, width // 128, squares)
    pay_ref[...] = jnp.broadcast_to(tile[...][None], pay_ref.shape)


def output_kernel(g4_ref, counts_ref, par_ref, own_ref, z_ref, x_ref, cot_ref, *refs):
    slope_refs, (out_ref, grad_ref, stat_ref, slopes_ref, pay_ref, tile) = refs[:-6], refs[-6:]
    width = z_ref.shape[1]
    groups = width // 128
    mean, inv, total = merge_stats(g4_ref[...], counts_ref[...], width)
    put(stat_ref, 0, mean)
    put(stat_ref, groups, inv)
    gain, shift = get(par_ref, 18, groups), get(par_ref, 26, groups)
    flat, cross = 0.0, 0.0
    for i in range(len(z_ref.parts)):
        own = wide(own_ref.chunk(i), width)
        normed = (z_ref.chunk(i) - mean) * inv
        pre = normed * gain + shift + x_ref.chunk(i)
        sigma = jax.nn.sigmoid(pre)
        out_ref.put(i, pre * sigma * own)
        grad = cot_ref.chunk(i) * own * (sigma * (1.0 + pre * (1.0 - sigma)))
        grad_ref.put(i, grad)
        flat = flat + column_sum(grad)
        cross = cross + column_sum(grad * normed)
    put(tile, 0, flat)
    put(tile, groups, cross)
    pay_ref[...] = jnp.broadcast_to(tile[...][None], pay_ref.shape)
    sum_kernel(*slope_refs, slopes_ref)


def mixed_kernel(digit, g5_ref, stat1_ref, stat3_ref, par_ref, own_ref, grad_ref, z_ref, wh_ref, wl_ref, a_ref, weights_ref,
                 w_ref, slope_ref, normed_ref, *refs):
    shares, (dzh_ref, dzl_ref, gm_ref, dsum_ref, grads_ref, slopes_ref, pay_ref, tile) = refs[: digit.size], refs[digit.size :]
    width = z_ref.shape[1]
    mid = gm_ref.shape[1]
    images = weights_ref.shape[0]
    groups = width // 128
    grads_ref[...] = jnp.sum(g5_ref[...], axis=0)
    count = wide(stat1_ref[4:5, :], width)
    mean, inv = get(stat3_ref, 0, groups), get(stat3_ref, groups, groups)
    flat = get(grads_ref, 0, groups) / count
    cross = get(grads_ref, groups, groups) / count
    scale = get(par_ref, 18, groups) * inv
    for i in range(len(z_ref.parts)):
        normed = (z_ref.chunk(i) - mean) * inv
        dz = scale * (grad_ref.chunk(i) - flat - normed * cross) * wide(own_ref.chunk(i), width)
        high, low = split(dz)
        dzh_ref.put(i, high)
        dzl_ref.put(i, low)
        gm_ref[z_ref.parts[i]] = product((high, low), (wh_ref[...], wl_ref[...]), NT)
    gm = gm_ref[...]
    gm_ref.send()
    a = a_ref[...]
    weights = weights_ref[...]
    gate = image_sum(gm * (a[:, :mid] - a[:, mid:]), images)
    dsum = weights[:, :mid] * weights[:, mid:] * gate
    dsum_ref[...] = dsum
    tile[...] = jnp.zeros_like(tile)
    tile[:images, :] = exact(dsum, w_ref[:, :mid] - w_ref[:, mid:], NT)
    slope = slope_ref[...] * jnp.concatenate([gm, gm], axis=1)
    put(tile, 8, column_sum(weights * image_sum(slope, images)))
    put(tile, 12, column_sum(weights * image_sum(slope * normed_ref[...], images)))
    pay_ref[...] = jnp.broadcast_to(tile[...][None], pay_ref.shape)
    digit.gather(shares, slopes_ref)


def expand_grad_kernel(core, mixed_ref, act_ref, dsum_ref, dzh_ref, dzl_ref, keep_ref, send_ref, excite_ref, term):
    left = split(mixed_ref[...].T)
    rows, width = left[0].shape[0], term.shape[1]
    for j in range(term.shape[0] // rows):
        cols = slice(j * width, (j + 1) * width)
        term[j * rows : (j + 1) * rows, :] = product(left, (dzh_ref[:, cols], dzl_ref[:, cols]), NN)
    core.scatter([term], [keep_ref, send_ref])
    excite_ref[...] = exact(act_ref[...], dsum_ref[...], TN)


def turned_rows(left, wh_ref, wl_ref, outs, row, taps):
    return product(left, [ref[row * taps : (row + 1) * taps, outs] for ref in (wh_ref, wl_ref)], NT)


def fold(total, group):
    return moved(total[:, :group], 1) + total[:, group : 2 * group] + moved(total[:, 2 * group :], -1)


def back_kernel(digit, g6_ref, pre_ref, fcn_ref, inv_ref, par_ref, wsq_ref, pooled_ref, stat1_ref, stat2_ref, rows_ref,
                cols_ref, weights_ref, mine_ref, other_ref, own_ref, gm_ref, slope_ref, normed_ref, wh_ref, wl_ref,
                up_ref, down_ref, dzh_ref, dzl_ref, squeeze_ref, gains_ref, fc_ref, gf, owned, slopes):
    images = rows_ref.shape[0]
    tall = dzh_ref.shape[1] - 2
    width = normed_ref.shape[1]
    mid = width // 2
    groups = width // 128
    rows = lax.axis_size("rows")
    shared = g6_ref[...]
    pre = pre_ref[...]
    fcn = fcn_ref[...]
    sigma = jax.nn.sigmoid(pre)
    total = pre.shape[0]
    grad = jnp.sum(shared[:, :images].reshape(rows, total, -1), axis=0) * (sigma * (1.0 + pre * (1.0 - sigma)))
    flat, cross = column_sum(grad), column_sum(grad * fcn)
    fc_ref[0:1, :] = cross
    fc_ref[1:2, :] = flat
    gf[...] = par_ref[12:13, :] * inv_ref[...] * (grad - flat / total - fcn * cross / total)
    at = pl.multiple_of(lax.axis_index("batch") * images, images)
    mine = gf[pl.ds(at, images), :]
    squeeze = exact(pooled_ref[...], mine, TN)
    half_rows = squeeze.shape[0] // 2
    squeeze_ref[:, : squeeze.shape[1]] = squeeze[:half_rows]
    squeeze_ref[:, squeeze.shape[1] :] = squeeze[half_rows:]
    spread = exact(gf[...], wsq_ref[...], NT)
    owned[...] = spread
    own_spread = owned[pl.ds(at, images), :] / pixel_count(rows_ref, cols_ref)
    for flipped, half in enumerate((mine_ref, other_ref)):
        for block in range(half.shape[0] // images):
            here = pl.multiple_of((2 * block + (digit.own() ^ flipped)) * images, images)
            slopes[pl.ds(here, images), :] = half[block * images : (block + 1) * images, :]
    base = jnp.sum(shared[:, 8:], axis=0)
    count = wide(stat1_ref[4:5, :], mid)
    weights = weights_ref[...]
    gm = gm_ref[...]
    shared_part = per_image(own_spread, gm)
    mask = wide(own_ref[...], mid)
    zero = jnp.zeros((images, 16, width), bf16)
    for ref in (dzh_ref, dzl_ref):
        ref[:, 0] = zero
        ref[:, tall + 1] = zero
    for g in range(2):
        outs = slice(g * mid, (g + 1) * mid)
        crosses = slice(width + g * mid, width + (g + 1) * mid)
        half = groups // 2
        flat_two = get(base, g * half, half) + column_sum(spread * slopes[:, outs])
        cross_two = get(base, groups + g * half, half) + column_sum(spread * slopes[:, crosses])
        put(gains_ref, g * half, cross_two)
        put(gains_ref, groups + g * half, flat_two)
        scale = get(par_ref, 4 + g * half, half) * get(stat2_ref, groups + g * half, half)
        upstream = per_image(weights[:, outs], gm) * gm + shared_part
        dz = scale * (upstream * slope_ref[:, outs] - flat_two / count - normed_ref[:, outs] * (cross_two / count)) * mask
        for ref, part in zip((dzh_ref, dzl_ref), split(dz)):
            ref[:, 1 : tall + 1, :, outs] = part.reshape(images, tall, 16, mid)
    dzh_ref.send()
    dzl_ref.send()
    group = up_ref.shape[1] // 2
    for g in range(2):
        outs = slice(g * mid, (g + 1) * mid)
        cols = slice(g * group, (g + 1) * group)
        for side, row, tap in ((up_ref, 1, 0), (down_ref, tall, 2)):
            left = [ref[:, row, :, outs].reshape(-1, mid) for ref in (dzh_ref, dzl_ref)]
            side[:, cols] = fold(turned_rows(left, wh_ref, wl_ref, outs, tap, 3 * group), group)


def group_kernel(core, dzh_ref, dzl_ref, squeeze_ref, excite_ref, th_ref, tl_ref, keep_ref, send_ref, out_ref):
    tall = dzh_ref.shape[1] - 2
    mid = dzh_ref.shape[3] // 2
    taps = th_ref.shape[1]
    for g in range(2):
        outs = slice(g * mid, (g + 1) * mid)
        right = [ref[:, 1 : tall + 1, :, outs].reshape(-1, mid) for ref in (dzh_ref, dzl_ref)]
        out_ref[g * taps : (g + 1) * taps, :] = product((th_ref.chunk(g)[0], tl_ref.chunk(g)[0]), right, NN)
    inter = excite_ref.shape[0]
    out_ref[2 * taps : 2 * taps + inter, :] = excite_ref[...]
    out_ref[2 * taps + inter :, :] = squeeze_ref[...]
    core.scatter([out_ref], [keep_ref, send_ref])


def input_grad_kernel(par_ref, stat_ref, dsum_ref, z_ref, own_ref, above_ref, below_ref, dzh_ref, dzl_ref, wh_ref, wl_ref,
                      dy_ref, pay_ref, tile, place):
    images = dsum_ref.shape[0]
    width = z_ref.shape[1]
    group = width // 2
    tall = dzh_ref.shape[1] - 2
    half = dzh_ref.shape[3] // 2
    grads = []
    for g in range(2):
        outs = slice(g * half, (g + 1) * half)
        total = None
        for row in range(3):
            left = [ref[:, 2 - row : 2 - row + tall, :, outs].reshape(-1, half) for ref in (dzh_ref, dzl_ref)]
            term = turned_rows(left, wh_ref, wl_ref, outs, row, 3 * group)
            total = term if total is None else total + term
        grads.append(fold(total, group))
    place[...] = jnp.concatenate(grads, axis=1).reshape(place.shape)
    place[:, 0] += above_ref[...].reshape(images, 16, width)
    place[:, tall - 1] += below_ref[...].reshape(images, 16, width)
    grad = place[...].reshape(-1, width)
    mean, inv = get(stat_ref, 0, 2), get(stat_ref, 2, 2)
    normed = (z_ref[...] - mean) * inv
    y = normed * get(par_ref, 0, 2) + get(par_ref, 2, 2)
    sigma = jax.nn.sigmoid(y)
    dy = grad * wide(own_ref[...], width) * (sigma * (1.0 + y * (1.0 - sigma)))
    dy_ref[...] = dy
    dy_ref.send()
    tile[...] = jnp.zeros_like(tile)
    put(tile, 0, column_sum(dy * normed))
    put(tile, 2, column_sum(dy))
    put(tile, 4, column_sum(dsum_ref[...]))
    pay_ref[...] = jnp.broadcast_to(tile[...][None], pay_ref.shape)


def final_kernel(core, g7_ref, par_ref, stat_ref, dy_ref, z_ref, own_ref, th_ref, tl_ref, wh_ref, wl_ref, grad_ref,
                 keep_ref, send_ref, out_ref, gains_ref, term):
    width = z_ref.shape[1]
    gains_ref[...] = jnp.sum(g7_ref[...], axis=0)
    cross, flat = get(gains_ref, 0, 2), get(gains_ref, 2, 2)
    count = wide(stat_ref[4:5, :], width)
    mean, inv = get(stat_ref, 0, 2), get(stat_ref, 2, 2)
    normed = (z_ref[...] - mean) * inv
    scale = get(par_ref, 0, 2) * inv
    dz = scale * (dy_ref[...] - flat / count - normed * (cross / count)) * wide(own_ref[...], width)
    parts = split(dz)
    term[...] = product((th_ref[...], tl_ref[...]), parts, NN)
    core.scatter([term], [keep_ref, send_ref])
    keep_ref.send()
    send_ref.send()
    for i in range(len(grad_ref.parts)):
        rows = slice(grad_ref.parts[i].start, grad_ref.parts[i].start + grad_ref.parts[i].size)
        out_ref.put(i, product([part[rows] for part in parts], (wh_ref[...], wl_ref[...]), NT) + grad_ref.chunk(i))


def deal_kernel(plan, count, *refs):
    outs = list(refs[count:])
    for digit, stretches in plan:
        own = digit.own()
        for j in range(digit.size):
            out, at = outs.pop(0), 0
            for inputs, first, rows in stretches:
                each = rows // digit.size
                here = pl.ds(pl.multiple_of(first + (own ^ j) * each, 8), each)
                total = refs[inputs[0]][here, :]
                for k in inputs[1:]:
                    total = total + refs[k][here, :]
                out[at : at + each, :] = total
                at += each


def deal(plan, ins, after=()):
    width = ins[0].shape[1]
    outs = []
    for digit, stretches in plan:
        rows = sum(rows for _, _, rows in stretches) // digit.size
        outs += [((rows, width), f32)] * digit.size
    return local_call(functools.partial(deal_kernel, plan, len(ins)), outs, ins, after=after)


def halve_kernel(blocks, whole_ref, *outs):
    each = whole_ref.shape[0] // blocks
    half = each // 2
    for k in range(blocks):
        for i, out in enumerate(outs):
            out[k * half : (k + 1) * half, :] = whole_ref[k * each + i * half : k * each + (i + 1) * half, :]


def pair_kernel(digits, *refs):
    outs = refs[4:]
    for i, digit in enumerate(digits):
        digit.gather(refs[2 * i : 2 * i + 2], outs[i] if len(outs) == 2 else outs[0].at[pl.ds(i * 2 * refs[0].shape[0], 2 * refs[0].shape[0])])


def last_kernel(core, expand_map, group_map, mine_ref, other_ref, expand_ref, group_ref, excite_ref, squeeze_ref, whole):
    core.gather([mine_ref, other_ref], whole)
    taps, mid = group_ref.shape[0], whole.shape[1]
    inter = squeeze_ref.shape[1]
    tall = expand_ref.shape[0]
    places = [
        (taps, lambda rows, value: group_ref.__setitem__((rows, slice(0, mid)), value)),
        (taps, lambda rows, value: group_ref.__setitem__((rows, slice(mid, 2 * mid)), value)),
        (inter, lambda rows, value: excite_ref.__setitem__((rows, slice(0, mid)), value)),
        (inter, lambda rows, value: squeeze_put(squeeze_ref, rows, value)),
    ]
    for at, first, rows in expand_map:
        j, m = first // tall, first % tall
        expand_ref[m : m + rows, j * mid : (j + 1) * mid] = whole[at : at + rows, :]
    for at, first, rows in group_map:
        base = 0
        for length, store in places:
            low, high = max(first, base), min(first + rows, base + length)
            if low < high:
                store(slice(low - base, high - base), whole[at + low - first : at + high - first, :])
            base += length
    excite_ref[:, mid:] = -excite_ref[:, :mid]


def squeeze_put(squeeze_ref, rows, value):
    half = squeeze_ref.shape[0] // 2
    width = squeeze_ref.shape[1]
    squeeze_ref[rows, :] = value[:, :width]
    squeeze_ref[slice(half + rows.start, half + rows.stop), :] = value[:, width:]


def on_device(
    images,
    w_reduce,
    gain_one,
    shift_one,
    w_group,
    gain_two,
    shift_two,
    w_squeeze,
    gain_fc,
    shift_fc,
    w_excite,
    excite_bias,
    w_expand,
    gain_three,
    shift_three,
    valid_rows,
    valid_cols,
    cotangent,
):
    count, tall, broad, chan = images.shape
    mid = w_reduce.shape[1]
    inter = w_squeeze.shape[1]
    duo = 2 * mid
    taps = 9 * mid // 2
    cells = count * tall * broad
    longer = count * (tall + 2) * broad
    edge = count * broad
    devices = lax.axis_size("rows") * lax.axis_size("batch")
    all_images = count * lax.axis_size("batch")
    x = images.reshape(cells, chan)
    cot = cotangent.reshape(cells, chan)
    pay8 = ((devices, 8, 128), f32)
    pay16 = ((devices, 16, 128), f32)
    tile8 = pltpu.VMEM((8, 128), f32)
    tile16 = pltpu.VMEM((16, 128), f32)
    twice = lambda *shape: [(shape, bf16)] * 2
    flat_w = w_group.reshape(taps, duo)
    vectors = (gain_one, shift_one, gain_two, shift_two, gain_fc, shift_fc, excite_bias, gain_three, shift_three)
    core, line, depth, extra = digits()

    z_one, ext, own, first, last, wrh, wrl, pay = call(
        reduce_kernel,
        [((cells, mid), f32), ((count, tall + 2, broad, 128), f32), ((cells, 128), f32), ((edge, mid), f32),
         ((edge, mid), f32), *twice(chan, mid), pay8],
        [valid_rows, valid_cols, w_reduce, x],
        [tile8],
        chunks={3: 2},
    )
    g1 = share(pay)
    above, below = halos(first, last)
    wgh, wgl, weh, wel, par = call(
        parts_kernel,
        [*twice(taps, duo), *twice(mid, chan), ((40, 128), f32)],
        [flat_w, w_expand, *[v.reshape(1, -1) for v in vectors]],
        chunks={0: 4, 1: 2},
        out_chunks={0: 4, 1: 4, 2: 2, 3: 2},
        after=[z_one],
    )
    z_two, a_one, stat1, counts, pay = call(
        conv_kernel,
        [((cells, duo), f32), ((longer, mid), f32), ((8, 128), f32), ((devices, 128), f32), pay8],
        [g1, par, z_one, ext, above, below, own, wgh, wgl],
        [tile8, pltpu.VMEM((count, tall + 2, broad, mid), f32)],
    )
    g2 = share(pay)
    xth, xtl = call(turned_kernel, twice(chan, cells), [x], after=[stat1])
    a_two, stat2, pooled, pay = call(
        pool_kernel,
        [((cells, duo), f32), ((8, 128), f32), ((count, mid), f32), ((devices, count, inter), f32)],
        [g2, counts, par, valid_rows, valid_cols, z_two, own, w_squeeze],
        chunks={5: 2, 6: 2},
        out_chunks={0: 2},
        after=[xth],
    )
    g3 = share(pay)
    slope_two, normed_two, slopes = call(
        slope_kernel,
        [((cells, duo), f32), ((cells, duo), f32), ((count, 2 * duo), f32)],
        [stat2, par, valid_rows, valid_cols, own, z_two],
        chunks={4: 2, 5: 2},
        out_chunks={0: 2, 1: 2},
    )
    mixed, z_three, weights, fc_normed, fc_pre, fc_act, fc_inv, pay = call(
        expand_kernel,
        [((cells, mid), f32), ((cells, chan), f32), ((count, duo), f32), ((all_images, inter), f32),
         ((all_images, inter), f32), ((count, inter), f32), ((1, inter), f32), pay16],
        [g3, par, w_excite, a_two, weh, wel, own],
        [tile16, pltpu.VMEM((all_images, inter), f32)],
        out_chunks={1: 2},
        after=[slopes],
    )
    g4 = share(pay)
    slopes = line.send([slopes] * line.size)
    block_out, grad_pre, stat3, slopes, pay = call(
        output_kernel,
        [((cells, chan), f32), ((cells, chan), f32), ((16, 128), f32), ((count, 2 * duo), f32), pay16],
        [g4, counts, par, own, z_three, x, cot, *slopes],
        [tile16],
        chunks={3: 4, 4: 4, 5: 4, 6: 4},
        out_chunks={0: 4, 1: 4},
    )
    g5 = share(pay)
    slopes = depth.send([slopes] * depth.size)
    tph, tpl = call(functools.partial(taps_kernel, count), twice(2, taps, cells), [a_one], out_chunks={0: 2, 1: 2}, after=[stat3])
    dzh, dzl, grad_mixed, dsum, grads_three, slopes, pay = call(
        functools.partial(mixed_kernel, depth),
        [*twice(cells, chan), ((cells, mid), f32), ((count, mid), f32),
         ((16, 128), f32), ((depth.size * count, 2 * duo), f32), pay16],
        [g5, stat1, stat3, par, own, grad_pre, z_three, weh, wel, a_two, weights, w_excite, slope_two, normed_two, *slopes],
        [tile16],
        chunks={4: 2, 5: 2, 6: 2},
        out_chunks={0: 2, 1: 2},
        after=[tph],
    )
    g6 = share(pay)
    *expand_sum, excite_term = call(
        functools.partial(expand_grad_kernel, core),
        [*core.outs(mid * chan // mid, mid), ((inter, mid), f32)],
        [mixed, fc_act, dsum, dzh, dzl],
        [pltpu.VMEM((chan, mid), f32)],
    )
    if extra.size > 1:
        slopes = gather_more(extra, extra.send([slopes] * extra.size))
    slopes = core.send([slopes] * 2)
    packed = 2 * taps + 2 * inter
    up, down, dzh, dzl, squeeze_term, grads_two, grads_fc = call(
        functools.partial(back_kernel, core),
        [((edge, mid), f32), ((edge, mid), f32), *twice(count, tall + 2, broad, duo), ((inter, mid), f32),
         ((8, 128), f32), ((2, inter), f32)],
        [g6, fc_pre, fc_normed, fc_inv, par, w_squeeze, pooled, stat1, stat2, valid_rows, valid_cols, weights, *slopes, own,
         grad_mixed, slope_two, normed_two, wgh, wgl],
        [pltpu.VMEM((all_images, inter), f32), pltpu.VMEM((all_images, mid), f32), pltpu.VMEM((all_images, 2 * duo), f32)],
        after=[excite_term],
    )
    above, below = halos(up, down)
    group_sum = call(
        functools.partial(group_kernel, core),
        core.outs(packed, mid),
        [dzh, dzl, squeeze_term, excite_term, tph, tpl],
        [pltpu.VMEM((packed, mid), f32)],
        chunks={4: 2, 5: 2},
    )
    expand_sum = core.send(expand_sum)
    group_sum = core.send([group_sum[0], gate(group_sum[1], [above, below])])
    dy_one, pay = call(
        input_grad_kernel,
        [((cells, mid), f32), pay8],
        [par, stat1, dsum, z_one, own, above, below, dzh, dzl, wgh, wgl],
        [tile8, pltpu.VMEM((count, tall, broad, mid), f32)],
    )
    first_bit, second_bit = line.bits()
    some, more = expand_sum[0].shape[0] // 2, group_sum[0].shape[0] // 2
    both_of = lambda start, a, b: [((0, 1), start * a, a), ((2, 3), start * b, b)]
    first_half = lambda digit: (digit, both_of(0, some, more))
    second_half = lambda digit: (digit, both_of(1, some, more))
    keep_a, send_a, keep_b, send_b = deal(
        [first_half(first_bit), second_half(second_bit)], [*expand_sum, *group_sum], after=[dy_one]
    )
    g7 = share(pay)
    come_a, come_b = first_bit.send([keep_a, send_a]), second_bit.send([keep_b, send_b])
    some, more = some // 2, more // 2
    turn = lambda k: [((k, k + 1), 0, some), ((k, k + 1), some, more)]
    keep_a, send_a, keep_b, send_b = deal([(second_bit, turn(0)), (first_bit, turn(2))], [*come_a, *come_b])
    *reduce_sum, grad_images, grads_one = call(
        functools.partial(final_kernel, core),
        [*core.outs(chan, mid), ((cells, chan), f32), ((8, 128), f32)],
        [g7, par, stat1, dy_one, z_one, own, xth, xtl, wrh, wrl, grad_pre],
        [pltpu.VMEM((chan, mid), f32)],
        chunks={10: 2},
        out_chunks={2: 2},
        after=[keep_a],
    )
    come_a, come_b = second_bit.send([keep_a, send_a]), first_bit.send([keep_b, send_b])
    some, more = some // 2, more // 2
    joined = deal([(depth, turn(0) + turn(2))], [*come_a, *come_b], after=[grad_images])
    reduce_sum[1] = gate(reduce_sum[1], [joined[1]])
    bits = [core, *line.bits(), *depth.bits()]
    reduce_sum = scatter_more(bits[1], bits[0].send(reduce_sum))
    joined = finish_sum(depth.send(joined), extra, after=[reduce_sum[0]])
    reduce_sum = scatter_more(bits[2], bits[1].send(reduce_sum), after=[joined])
    joined = gather_more(depth, depth.send([joined] * depth.size), after=[reduce_sum[0]])
    rows_in = joined.shape[0]
    half_a, half_b = local_call(
        functools.partial(halve_kernel, depth.size), [((rows_in // 2, mid), f32)] * 2, [joined]
    )
    for here, there in zip(bits[2:-1], bits[3:]):
        reduce_sum = scatter_more(there, here.send(reduce_sum), after=[half_a])
    half_a, half_b = local_call(
        functools.partial(pair_kernel, [second_bit, first_bit]),
        [((rows_in, mid), f32)] * 2,
        [*second_bit.send([half_a] * 2), *first_bit.send([half_b] * 2)],
        after=[reduce_sum[0]],
    )
    reduce_sum = finish_sum(bits[-1].send(reduce_sum), extra, after=[half_a])
    reduce_sum = gather_more(bits[-1], bits[-1].send([reduce_sum] * 2))
    (joined,) = local_call(
        functools.partial(pair_kernel, [first_bit, second_bit]),
        [((4 * rows_in, mid), f32)],
        [*first_bit.send([half_a] * 2), *second_bit.send([half_b] * 2)],
        after=[reduce_sum],
    )
    for here in bits[-2:0:-1]:
        reduce_sum = gather_more(here, here.send([reduce_sum] * 2), after=[joined])
    expand_map, group_map = [], []
    at = 0
    some, more = some // depth.size, more // depth.size
    for half in range(core.size):
        for part in range(2):
            for outer in range(2):
                for inner in range(2):
                    for deep in range(depth.size):
                        block = (((half * 2 + part) * 2 + outer) * 2 + inner) * depth.size + deep
                        expand_map.append((at, block * some, some))
                        group_map.append((at + some, block * more, more))
                        at += some + more
    grad_w_expand, grad_w_group, grad_w_excite, grad_w_squeeze = local_call(
        functools.partial(last_kernel, core, expand_map, group_map),
        [((mid, chan), f32), ((taps, duo), f32), ((inter, duo), f32), ((mid, inter), f32)],
        core.send([joined] * 2),
        [pltpu.VMEM((chan + packed, mid), f32)],
    )
    grad_w_reduce = gather_more(core, core.send([reduce_sum] * 2))
    grads_one = grads_one.reshape(-1)
    grads_two = grads_two.reshape(-1)
    grads_three = grads_three.reshape(-1)
    grad_bias = grads_one[duo : duo + mid]
    return (
        block_out.reshape(images.shape),
        grad_images.reshape(images.shape),
        grad_w_reduce,
        grads_one[:mid],
        grads_one[mid:duo],
        grad_w_group.reshape(w_group.shape),
        grads_two[:duo],
        grads_two[duo:],
        grad_w_squeeze,
        grads_fc[0],
        grads_fc[1],
        grad_w_excite,
        jnp.concatenate([grad_bias, -grad_bias]),
        grad_w_expand,
        grads_three[chan:],
        grads_three[:chan],
    )


def solution(mesh):
    maps = P("batch", "rows", None, None)
    return jax.shard_map(
        on_device,
        mesh=mesh,
        in_specs=(maps,) + (P(),) * 14 + (P("batch", None), P("batch", None), maps),
        out_specs=(maps, maps) + (P(),) * 14,
        check_vma=False,
    )
```

time: 357 us -> 257 us (0.72)
  blocking collectives: 94.5 us -> 0 us
  local copies, waits for them, and re-layouts: 67 us -> 13.5 us
  Pallas kernels: 37.2 us -> 80.4 us
  starting transfers between devices: 31.8 us -> 67.3 us
  waiting for transfers between devices: 107 us -> 93 us
  between operations: 14.5 us -> 1.29 us
    psum x1 -> x0, waiting for transfers between devices: 105 us -> none  [on_device(): lax.psum((reduce_term, group_term, expand_term, squeeze_term, excite_term...]
    ppermute x0 -> x34, waiting for transfers between devices: none -> 70.9 us  [flip(): lax.ppermute(values, axis, [(i, i ^ bits) for i in range(lax.axis_size(ax...]
    all_to_all x4 -> x0, blocking collectives: 53.5 us -> none  [share(): return lax.all_to_all(tile, both, 0, 0)]
    unnamed x196 -> x68, local copies, waits for them, and re-layouts: 64.8 us -> 11.3 us
    pallas_call x14 -> x36, Pallas kernels: 37.2 us -> 80.4 us  [the longest x15 75.3 us: call(): pl.pallas_call(inner, out_shape=[jax.ShapeDtypeStruct(shape, kind) for sh...]
    psum x1 -> x0, blocking collectives: 41 us -> none  [on_device(): lax.psum((reduce_term, group_term, expand_term, squeeze_term, excite_term...]
    ppermute x0 -> x34, starting transfers between devices: none -> 32 us  [flip(): lax.ppermute(values, axis, [(i, i ^ bits) for i in range(lax.axis_size(ax...]
    all_to_all x3 -> x7, waiting for transfers between devices: 0.01 us -> 19 us  [share(): return lax.all_to_all(tile, both, 0, 0)]
  transfers between devices with their start and end apart: 11 -> 45, of which waited for: 2 -> 25; matrix products, arithmetic and copies ran while one was open for 1% -> 1% of each run, Pallas kernels for 4% -> 16%
where the time goes in v2:
time: 257 us; the launch traced here: 256 us
  waiting for transfers between devices  93 us (36%)
  Pallas kernels  80.4 us (31%)
  starting transfers between devices  67.3 us (26%)
  local copies, waits for them, and re-layouts  13.5 us (5%)
    pallas_call x15, Pallas kernels, call(): pl.pallas_call(inner, out_shape=[jax.ShapeDtypeStruct(shape, kind) for sh...  75.3 us
    ppermute x34, waiting for transfers between devices, flip(): lax.ppermute(values, axis, [(i, i ^ bits) for i in range(lax.axis_size(ax...  70.9 us
    ppermute x34, starting transfers between devices, flip(): lax.ppermute(values, axis, [(i, i ^ bits) for i in range(lax.axis_size(ax...  32 us
    all_to_all x7, starting transfers between devices, share(): return lax.all_to_all(tile, both, 0, 0)  26.4 us
    all_to_all x7, waiting for transfers between devices, share(): return lax.all_to_all(tile, both, 0, 0)  19 us
    unnamed x68, local copies, waits for them, and re-layouts  11.3 us
    ppermute x2, starting transfers between devices, halos(): above = lax.ppermute(last, 'rows', [(i, i + 1) for i in range(count - 1)])  6.09 us
    pallas_call x19, Pallas kernels, local_call(): pl.pallas_call(inner, out_shape=[jax.ShapeDtypeStruct(shape, kind) for sh...  5.16 us
  transfers between devices with their start and end apart: 45, of which 25 were waited for; matrix products, arithmetic and copies ran while one was open for 1% of the time, Pallas kernels for 16%

profile of v2, /device:TPU:0, one launch (start us, length us, event | category | flops | bytes accessed | tf_op | source)
XLA Modules:
  0.0 256.1 jit_solution(812809989861040929)
XLA Ops:
  0.6 5.0 %shard_map.297 = (f32[512,256]{1,0:T(8,128)}, f32[8,6,16,128]{3,2,1,0:T(8,128)}, f32[512,128]{1,0:T(8,128)}, f32[128,256]{1,0:T(8,128)}, f32[128,256]{1,0:T(8,12...) custom-call(s32[8,16]{1,0:T(8,128)} %refs_9_.1, s32[8,16]{1,0:T(8,128)} %refs_10_.1, ...), custom_call_target="tpu_custom_call" | custom-call | flops 1 | bytes 1 | tf_op jit(solution)/shard_map/pallas_call | solution.py:180
  5.7 7.3 %all-to-all-start = ((f32[32,8,128]{2,1,0:T(8,128)}), f32[32,8,128]{2,1,0:T(8,128)S(1)}, u32[]{:S(2)}, u32[]{:S(2)}) async-start(f32[32,8,128]{2,1,0:T(8,128)} %get-tuple-element.111), calls=%async_computation | async-start | bytes 262144 | tf_op jit(solution)/shard_map/all_to_all | solution.py:214
  25.8 5.5 %shard_map.299 = (f32[512,512]{1,0:T(8,128)}, f32[768,256]{1,0:T(8,128)}, f32[8,128]{1,0:T(8,128)}, f32[32,128]{1,0:T(8,128)}, f32[32,8,128]{2,1,0:T(8,128)}) custom-call(f32[32,8,128]{2,1,0:T(8,128)} %copy-done.17, f32[40,128]{1,0:T(8,128)} %get-tuple-element.113.refs_1_.refs_2_.refs_3_.refs_4_.refs_0_, ...), custom_call_target="tpu_custom_call" | custom-call | flops 1 | bytes 1 | tf_op jit(solution)/shard_map/pallas_call | solution.py:180
  31.3 4.5 %all-to-all-start.1 = ((f32[32,8,128]{2,1,0:T(8,128)}), f32[32,8,128]{2,1,0:T(8,128)S(1)}, u32[]{:S(2)}, u32[]{:S(2)}) async-start(f32[32,8,128]{2,1,0:T(8,128)} %get-tuple-element.120), calls=%async_computation.1 | async-start | bytes 262144 | tf_op jit(solution)/shard_map/all_to_all | solution.py:214
  39.3 4.6 %all-to-all-done.1.refs_0_ = f32[32,8,128]{2,1,0:T(8,128)S(1)} async-done(((f32[32,8,128]{2,1,0:T(8,128)}), f32[32,8,128]{2,1,0:T(8,128)S(1)}, u32[]{:S(2)}, u32[]{:S(2)}) %all-to-all-start.1) | async-done | bytes 131104 | tf_op jit(solution)/shard_map/all_to_all | solution.py:214
  52.9 5.2 %all-to-all-done.2.refs_0_ = f32[32,8,128]{2,1,0:T(8,128)S(1)} async-done(((f32[32,8,128]{2,1,0:T(8,128)}), f32[32,8,128]{2,1,0:T(8,128)S(1)}, u32[]{:S(2)}, u32[]{:S(2)}) %all-to-all-start.2) | async-done | bytes 131104 | tf_op jit(solution)/shard_map/all_to_all | solution.py:214
  58.8 4.3 %shard_map.303 = (f32[512,256]{1,0:T(8,128)}, f32[512,1024]{1,0:T(8,128)}, f32[8,512]{1,0:T(8,128)}, f32[64,128]{1,0:T(8,128)}, f32[64,128]{1,0:T(8,128)}, /*ind...) custom-call(f32[32,8,128]{2,1,0:T(8,128)} %copy-done.18, ...), custom_call_target="tpu_custom_call" | custom-call | flops 1 | bytes 1 | tf_op jit(solution)/shard_map/pallas_call | solution.py:180
  76.8 5.6 %shard_map.304 = (f32[512,1024]{1,0:T(8,128)}, f32[512,1024]{1,0:T(8,128)}, f32[16,128]{1,0:T(8,128)}, f32[8,1024]{1,0:T(8,128)}, f32[32,16,128]{2,1,0:T(8,128)}) custom-call(f32[32,16,128]{2,1,0:T(8,128)} %copy-done.13, f32[32,128]{1,0:T(8,128)} %get-tuple-element.121.refs_1_, f32[40,128]{1,0:T(8,128)} %get-tuple-element.113.refs_1_.refs_2_.refs_3_.refs_4_.refs_0_, ...), custom_call_target="tpu_custom_call" | custom-call | flops 1 | bytes 1 | tf_op jit(solution)/shard_map/pallas_call | solution.py:180
  89.5 4.0 %shard_map.305 = (bf16[2,1152,512]{2,1,0:T(8,128)(2,1)}, bf16[2,1152,512]{2,1,0:T(8,128)(2,1)}) custom-call(f32[768,256]{1,0:T(8,128)} %get-tuple-element.141.refs_0_, f32[16,128]{1,0:T(8,128)} %get-tuple-element.135.refs_1_.refs_2_), custom_call_target="tpu_custom_call" | custom-call | flops 1 | bytes 1 | tf_op jit(solution)/shard_map/pallas_call | solution.py:180
  97.9 6.9 %shard_map.306 = (bf16[512,1024]{1,0:T(8,128)(2,1)}, bf16[512,1024]{1,0:T(8,128)(2,1)}, f32[512,256]{1,0:T(8,128)}, f32[8,256]{1,0:T(8,128)}, f32[16,128]{1,0:T(...) custom-call(f32[32,16,128]{2,1,0:T(8,128)} %copy-done.11, f32[8,128]{1,0:T(8,128)} %get-tuple-element.123.refs_1_.refs_7_.refs_2_, ...), custom_call_target="tpu_custom_call" | custom-call | flops 1 | bytes 1 | tf_op jit(solution)/shard_map/pallas_call | solution.py:180
  112.7 6.0 %all-to-all-done.5.refs_0_ = f32[32,16,128]{2,1,0:T(8,128)S(1)} async-done(((f32[32,16,128]{2,1,0:T(8,128)}), f32[32,16,128]{2,1,0:T(8,128)S(1)}, u32[]{:S(2)}, u32[]{:S(2)}) %all-to-all-start.5) | async-done | bytes 262176 | tf_op jit(solution)/shard_map/all_to_all | solution.py:214
  119.5 4.6 %shard_map.308 = (f32[128,256]{1,0:T(8,128)}, f32[128,256]{1,0:T(8,128)}, bf16[8,6,16,512]{3,2,1,0:T(8,128)(2,1)}, bf16[8,6,16,512]{3,2,1,0:T(8,128)(2,1)}, f32[...) custom-call(f32[32,16,128]{2,1,0:T(8,128)} %copy-done.12, f32[64,128]{1,0:T(8,128)} %get-tuple-element.145.refs_1_, ...), custom_call_target="tpu_custom_call" | custom-call | flops 1 | bytes 1 | tf_op jit(solution)/shard_map/pallas_call | solution.py:180
  128.0 7.9 %shard_map.310 = (f32[1280,256]{1,0:T(8,128)}, f32[1280,256]{1,0:T(8,128)}) custom-call(bf16[8,6,16,512]{3,2,1,0:T(8,128)(2,1)} %get-tuple-element.158.refs_7_.refs_0_, bf16[8,6,16,512]{3,2,1,0:T(8,128)(2,1)} %get-tuple-element.159.refs_8_.refs_1_, f32[128,256]{1,0:T(8,128)} %get-tuple-element.167.refs_2_, f32[128,256]{1,0:T(8,128)} %get-tuple-element.155.refs_20_.refs_3_, ...), custom_call_target="tpu_custom_call" | custom-call | flops 1 | bytes 1 | tf_op jit(solution)/shard_map/pallas_call | solution.py:180
  137.1 6.5 %shard_map.309 = (f32[512,256]{1,0:T(8,128)}, f32[32,8,128]{2,1,0:T(8,128)}) custom-call(f32[40,128]{1,0:T(8,128)} %get-tuple-element.113.refs_1_.refs_2_.refs_3_.refs_4_.refs_0_, f32[8,128]{1,0:T(8,128)} %get-tuple-element.123.refs_1_.refs_7_.refs_2_, f32[8,256]{1,0:T(8,128)} %get-tuple-element.143.refs_2_, ...), custom_call_target="tpu_custom_call" | custom-call | flops 1 | bytes 1 | tf_op jit(solution)/shard_map/pallas_call | solution.py:180
  153.3 8.3 %collective-permute-done.13.refs_1_ = f32[448,256]{1,0:T(8,128)S(1)} collective-permute-done((f32[448,256]{1,0:T(8,128)}, f32[448,256]{1,0:T(8,128)S(1)}, u32[]{:S(2)}, u32[]{:S(2)}) %collective-permute-start.13) | collective-permute-done | bytes 458784 | tf_op jit(solution)/shard_map/ppermute | solution.py:225
  168.5 7.7 %shard_map.314 = (f32[512,256]{1,0:T(8,128)}, f32[512,256]{1,0:T(8,128)}, f32[512,1024]{1,0:T(8,128)}, f32[8,128]{1,0:T(8,128)}) custom-call(f32[32,8,128]{2,1,0:T(8,128)} %copy-done.16, f32[40,128]{1,0:T(8,128)} %get-tuple-element.113.refs_1_.refs_2_.refs_3_.refs_4_.refs_0_, f32[8,128]{1,0:T(8,128)} %get-tuple-element.123.refs_1_.refs_7_.refs_2_, ...), custom_call_target="tpu_custom_call" | custom-call | flops 1 | bytes 1 | tf_op jit(solution)/shard_map/pallas_call | solution.py:180
  184.5 7.3 %collective-permute-done.20.refs_2_ = f32[112,256]{1,0:T(8,128)S(1)} collective-permute-done((f32[112,256]{1,0:T(8,128)S(1)}, f32[112,256]{1,0:T(8,128)S(1)}, u32[]{:S(2)}, u32[]{:S(2)}) %collective-permute-start.20) | collective-permute-done | bytes 114720 | tf_op jit(solution)/shard_map/ppermute | solution.py:225
  201.0 5.5 %collective-permute-done.24.refs_2_ = f32[112,256]{1,0:T(8,128)S(1)} collective-permute-done((f32[112,256]{1,0:T(8,128)S(1)}, f32[112,256]{1,0:T(8,128)S(1)}, u32[]{:S(2)}, u32[]{:S(2)}) %collective-permute-start.24) | collective-permute-done | bytes 114720 | tf_op jit(solution)/shard_map/ppermute | solution.py:225
  210.3 8.0 %collective-permute-done.22.refs_1_ = f32[128,256]{1,0:T(8,128)S(1)} collective-permute-done((f32[128,256]{1,0:T(8,128)S(1)}, f32[128,256]{1,0:T(8,128)S(1)}, u32[]{:S(2)}, u32[]{:S(2)}) %collective-permute-start.22) | collective-permute-done | bytes 131104 | tf_op jit(solution)/shard_map/ppermute | solution.py:225
  218.4 4.3 %collective-permute-done.26.refs_1_ = f32[64,256]{1,0:T(8,128)S(1)} collective-permute-done((f32[64,256]{1,0:T(8,128)S(1)}, f32[64,256]{1,0:T(8,128)S(1)}, u32[]{:S(2)}, u32[]{:S(2)}) %collective-permute-start.26) | collective-permute-done | bytes 65568 | tf_op jit(solution)/shard_map/ppermute | solution.py:225
  223.5 5.3 %collective-permute-done.27.refs_1_ = f32[32,256]{1,0:T(8,128)S(1)} collective-permute-done((f32[32,256]{1,0:T(8,128)S(1)}, f32[32,256]{1,0:T(8,128)S(1)}, u32[]{:S(2)}, u32[]{:S(2)}) %collective-permute-start.27) | collective-permute-done | bytes 32800 | tf_op jit(solution)/shard_map/ppermute | solution.py:225
  228.8 4.8 %collective-permute-done.30.refs_1_ = f32[32,256]{1,0:T(8,128)S(1)} collective-permute-done((f32[32,256]{1,0:T(8,128)S(1)}, f32[32,256]{1,0:T(8,128)S(1)}, u32[]{:S(2)}, u32[]{:S(2)}) %collective-permute-start.30) | collective-permute-done | bytes 32800 | tf_op jit(solution)/shard_map/ppermute | solution.py:225
  234.0 4.4 %collective-permute-done.31.refs_1_ = f32[64,256]{1,0:T(8,128)S(1)} collective-permute-done((f32[64,256]{1,0:T(8,128)S(1)}, f32[64,256]{1,0:T(8,128)S(1)}, u32[]{:S(2)}, u32[]{:S(2)}) %collective-permute-start.31) | collective-permute-done | bytes 65568 | tf_op jit(solution)/shard_map/ppermute | solution.py:225
  246.5 4.2 %collective-permute-done.35.refs_1_ = f32[256,256]{1,0:T(8,128)S(1)} collective-permute-done((f32[256,256]{1,0:T(8,128)S(1)}, f32[256,256]{1,0:T(8,128)S(1)}, u32[]{:S(2)}, u32[]{:S(2)}) %collective-permute-start.35) | collective-permute-done | bytes 262176 | tf_op jit(solution)/shard_map/ppermute | solution.py:225
  (176 shorter events, 117.1 us)
Async XLA Ops:
  5.7 19.4 %all-to-all-start = ((f32[32,8,128]{2,1,0:T(8,128)}), f32[32,8,128]{2,1,0:T(8,128)S(1)}, u32[]{:S(2)}, u32[]{:S(2)}) async-start(f32[32,8,128]{2,1,0:T(8,128)} %get-tuple-element.111), calls=%async_computation | async-start | bytes 262144 | tf_op jit(solution)/shard_map/all_to_all | solution.py:214
  31.3 12.7 %all-to-all-start.1 = ((f32[32,8,128]{2,1,0:T(8,128)}), f32[32,8,128]{2,1,0:T(8,128)S(1)}, u32[]{:S(2)}, u32[]{:S(2)}) async-start(f32[32,8,128]{2,1,0:T(8,128)} %get-tuple-element.120), calls=%async_computation.1 | async-start | bytes 262144 | tf_op jit(solution)/shard_map/all_to_all | solution.py:214
  47.4 10.8 %all-to-all-start.2 = ((f32[32,8,128]{2,1,0:T(8,128)}), f32[32,8,128]{2,1,0:T(8,128)S(1)}, u32[]{:S(2)}, u32[]{:S(2)}) async-start(f32[32,8,128]{2,1,0:T(8,128)} %get-tuple-element.125), calls=%async_computation.2 | async-start | bytes 262144 | tf_op jit(solution)/shard_map/all_to_all | solution.py:214
  63.1 13.0 %all-to-all-start.3 = ((f32[32,16,128]{2,1,0:T(8,128)}), f32[32,16,128]{2,1,0:T(8,128)S(1)}, u32[]{:S(2)}, u32[]{:S(2)}) async-start(f32[32,16,128]{2,1,0:T(8,128)} %get-tuple-element.131), calls=%async_computation.3 | async-start | bytes 524288 | tf_op jit(solution)/shard_map/all_to_all | solution.py:214
  82.4 14.8 %all-to-all-start.4 = ((f32[32,16,128]{2,1,0:T(8,128)}), f32[32,16,128]{2,1,0:T(8,128)S(1)}, u32[]{:S(2)}, u32[]{:S(2)}) async-start(f32[32,16,128]{2,1,0:T(8,128)} %get-tuple-element.134), calls=%async_computation.4 | async-start | bytes 524288 | tf_op jit(solution)/shard_map/all_to_all | solution.py:214
  85.0 10.1 %collective-permute-start.7 = (f32[8,1024]{1,0:T(8,128)}, f32[8,1024]{1,0:T(8,128)S(1)}, u32[]{:S(2)}, u32[]{:S(2)}) collective-permute-start(f32[8,1024]{1,0:T(8,128)} %get-tuple-element.140.refs_14_), channel_id=1, source_target_pairs={{0,6},{1,7},{2,4},{3,5},{4,2},{5,3},{6,0},{7,1},{8,14},{9,15},{10,... | collective-permute-start | bytes 98312 | tf_op jit(solution)/shard_map/ppermute | solution.py:225
  104.8 13.9 %all-to-all-start.5 = ((f32[32,16,128]{2,1,0:T(8,128)}), f32[32,16,128]{2,1,0:T(8,128)S(1)}, u32[]{:S(2)}, u32[]{:S(2)}) async-start(f32[32,16,128]{2,1,0:T(8,128)} %get-tuple-element.144), calls=%async_computation.5 | async-start | bytes 524288 | tf_op jit(solution)/shard_map/all_to_all | solution.py:214
  124.0 11.9 %collective-permute-start.9 = (f32[128,256]{1,0:T(8,128)}, f32[128,256]{1,0:T(8,128)S(1)}, u32[]{:S(2)}, u32[]{:S(2)}) collective-permute-start(f32[128,256]{1,0:T(8,128)} %get-tuple-element.156), channel_id=1, source_target_pairs={{0,8},{8,16},{16,24},{1,9},{9,17},{17,25},{2,10},{10,18},{18,26},{... | collective-permute-start | bytes 393224 | tf_op jit(solution)/shard_map/ppermute | solution.py:219
  146.6 14.9 %collective-permute-start.13 = (f32[448,256]{1,0:T(8,128)}, f32[448,256]{1,0:T(8,128)S(1)}, u32[]{:S(2)}, u32[]{:S(2)}) collective-permute-start(f32[448,256]{1,0:T(8,128)} %get-tuple-element.172), channel_id=1, source_target_pairs={{0,8},{8,0},{16,24},{24,16},{1,9},{9,1},{17,25},{25,17},{2,10},{10... | collective-permute-start | bytes 1376264 | tf_op jit(solution)/shard_map/ppermute | solution.py:225
  149.3 13.7 %collective-permute-start.14 = (f32[448,256]{1,0:T(8,128)}, f32[448,256]{1,0:T(8,128)S(1)}, u32[]{:S(2)}, u32[]{:S(2)}) collective-permute-start(f32[448,256]{1,0:T(8,128)} %get-tuple-element.174), channel_id=1, source_target_pairs={{0,16},{8,24},{16,0},{24,8},{1,17},{9,25},{17,1},{25,9},{2,18},{10... | collective-permute-start | bytes 1376264 | tf_op jit(solution)/shard_map/ppermute | solution.py:225
  150.2 17.6 %all-to-all-start.6 = ((f32[32,8,128]{2,1,0:T(8,128)}), f32[32,8,128]{2,1,0:T(8,128)S(1)}, u32[]{:S(2)}, u32[]{:S(2)}) async-start(f32[32,8,128]{2,1,0:T(8,128)} %get-tuple-element.160), calls=%async_computation.6 | async-start | bytes 262144 | tf_op jit(solution)/shard_map/all_to_all | solution.py:214
  164.8 11.4 %collective-permute-start.15 = (f32[224,256]{1,0:T(8,128)S(1)}, f32[224,256]{1,0:T(8,128)S(1)}, u32[]{:S(2)}, u32[]{:S(2)}) collective-permute-start(f32[224,256]{1,0:T(8,128)S(1)} %get-tuple-element.179), channel_id=1, source_target_pairs={{0,16},{8,24},{16,0},{24,8},{1,17},{9,25},{17,1},{25,9},{2,18},{10... | collective-permute-start | bytes 688136 | tf_op jit(solution)/shard_map/ppermute | solution.py:225
  166.1 10.1 %collective-permute-start.16 = (f32[224,256]{1,0:T(8,128)S(1)}, f32[224,256]{1,0:T(8,128)S(1)}, u32[]{:S(2)}, u32[]{:S(2)}) collective-permute-start(f32[224,256]{1,0:T(8,128)S(1)} %get-tuple-element.181), channel_id=1, source_target_pairs={{0,8},{8,0},{16,24},{24,16},{1,9},{9,1},{17,25},{25,17},{2,10},{10... | collective-permute-start | bytes 688136 | tf_op jit(solution)/shard_map/ppermute | solution.py:225
  180.7 16.9 %collective-permute-start.18 = (f32[256,256]{1,0:T(8,128)S(1)}, f32[256,256]{1,0:T(8,128)S(1)}, u32[]{:S(2)}, u32[]{:S(2)}) collective-permute-start(f32[256,256]{1,0:T(8,128)S(1)} %get-tuple-element.184), channel_id=1, source_target_pairs={{0,8},{8,0},{16,24},{24,16},{1,9},{9,1},{17,25},{25,17},{2,10},{10... | collective-permute-start | bytes 786440 | tf_op jit(solution)/shard_map/ppermute | solution.py:225
  181.1 10.8 %collective-permute-start.20 = (f32[112,256]{1,0:T(8,128)S(1)}, f32[112,256]{1,0:T(8,128)S(1)}, u32[]{:S(2)}, u32[]{:S(2)}) collective-permute-start(f32[112,256]{1,0:T(8,128)S(1)} %get-tuple-element.186), channel_id=1, source_target_pairs={{0,4},{1,5},{2,6},{3,7},{4,0},{5,1},{6,2},{7,3},{8,12},{9,13},{10,... | collective-permute-start | bytes 344072 | tf_op jit(solution)/shard_map/ppermute | solution.py:225
  182.1 9.7 %collective-permute-start.21 = (f32[112,256]{1,0:T(8,128)S(1)}, f32[112,256]{1,0:T(8,128)S(1)}, u32[]{:S(2)}, u32[]{:S(2)}) collective-permute-start(f32[112,256]{1,0:T(8,128)S(1)} %get-tuple-element.187), channel_id=1, source_target_pairs={{0,6},{1,7},{2,4},{3,5},{4,2},{5,3},{6,0},{7,1},{8,14},{9,15},{10,... | collective-permute-start | bytes 344072 | tf_op jit(solution)/shard_map/ppermute | solution.py:225
  194.8 11.7 %collective-permute-start.24 = (f32[112,256]{1,0:T(8,128)S(1)}, f32[112,256]{1,0:T(8,128)S(1)}, u32[]{:S(2)}, u32[]{:S(2)}) collective-permute-start(f32[112,256]{1,0:T(8,128)S(1)} %shard_map.318.refs_2_.refs_0_), channel_id=1, source_target_pairs={{0,4},{1,5},{2,6},{3,7},{4,0},{5,1},{6,2},{7,3},{8,12},{9,13},{10,... | collective-permute-start | bytes 344072 | tf_op jit(solution)/shard_map/ppermute | solution.py:225
  196.3 10.1 %collective-permute-start.23 = (f32[112,256]{1,0:T(8,128)S(1)}, f32[112,256]{1,0:T(8,128)S(1)}, u32[]{:S(2)}, u32[]{:S(2)}) collective-permute-start(f32[112,256]{1,0:T(8,128)S(1)} %shard_map.318.refs_2_.refs_0_), channel_id=1, source_target_pairs={{0,2},{1,3},{2,0},{3,1},{4,6},{5,7},{6,4},{7,5},{8,10},{9,11},{10,... | collective-permute-start | bytes 344072 | tf_op jit(solution)/shard_map/ppermute | solution.py:225
  206.5 16.1 %collective-permute-start.29 = (f32[224,256]{1,0:T(8,128)S(1)}, f32[224,256]{1,0:T(8,128)S(1)}, u32[]{:S(2)}, u32[]{:S(2)}) collective-permute-start(f32[224,256]{1,0:T(8,128)S(1)} %get-tuple-element.195.refs_2_), channel_id=1, source_target_pairs={{0,8},{8,0},{16,24},{24,16},{1,9},{9,1},{17,25},{25,17},{2,10},{10... | collective-permute-start | bytes 688136 | tf_op jit(solution)/shard_map/ppermute | solution.py:225
  208.2 14.4 %collective-permute-start.28 = (f32[224,256]{1,0:T(8,128)S(1)}, f32[224,256]{1,0:T(8,128)S(1)}, u32[]{:S(2)}, u32[]{:S(2)}) collective-permute-start(f32[224,256]{1,0:T(8,128)S(1)} %get-tuple-element.190.refs_2_.refs_0_), channel_id=1, source_target_pairs={{0,16},{8,24},{16,0},{24,8},{1,17},{9,25},{17,1},{25,9},{2,18},{10... | collective-permute-start | bytes 688136 | tf_op jit(solution)/shard_map/ppermute | solution.py:225
  208.5 9.8 %collective-permute-start.22 = (f32[128,256]{1,0:T(8,128)S(1)}, f32[128,256]{1,0:T(8,128)S(1)}, u32[]{:S(2)}, u32[]{:S(2)}) collective-permute-start(f32[128,256]{1,0:T(8,128)S(1)} %get-tuple-element.189), channel_id=1, source_target_pairs={{0,16},{8,24},{16,0},{24,8},{1,17},{9,25},{17,1},{25,9},{2,18},{10... | collective-permute-start | bytes 393224 | tf_op jit(solution)/shard_map/ppermute | solution.py:225
  222.8 10.9 %collective-permute-start.33 = (f32[448,256]{1,0:T(8,128)S(1)}, f32[448,256]{1,0:T(8,128)S(1)}, u32[]{:S(2)}, u32[]{:S(2)}) collective-permute-start(f32[448,256]{1,0:T(8,128)S(1)} %get-tuple-element.197.refs_2_), channel_id=1, source_target_pairs={{0,16},{8,24},{16,0},{24,8},{1,17},{9,25},{17,1},{25,9},{2,18},{10... | collective-permute-start | bytes 1376264 | tf_op jit(solution)/shard_map/ppermute | solution.py:225
  223.1 10.6 %collective-permute-start.32 = (f32[448,256]{1,0:T(8,128)S(1)}, f32[448,256]{1,0:T(8,128)S(1)}, u32[]{:S(2)}, u32[]{:S(2)}) collective-permute-start(f32[448,256]{1,0:T(8,128)S(1)} %get-tuple-element.196.refs_2_.refs_0_), channel_id=1, source_target_pairs={{0,8},{8,0},{16,24},{24,16},{1,9},{9,1},{17,25},{25,17},{2,10},{10... | collective-permute-start | bytes 1376264 | tf_op jit(solution)/shard_map/ppermute | solution.py:225
  233.9 19.9 %collective-permute-start.37 = (f32[1792,256]{1,0:T(8,128)S(1)}, f32[1792,256]{1,0:T(8,128)S(1)}, u32[]{:S(2)}, u32[]{:S(2)}) collective-permute-start(f32[1792,256]{1,0:T(8,128)S(1)} %shard_map.327.refs_2_.refs_0_), channel_id=1, source_target_pairs={{0,1},{1,0},{2,3},{3,2},{4,5},{5,4},{6,7},{7,6},{8,9},{9,8},{10,11... | collective-permute-start | bytes 5505032 | tf_op jit(solution)/shard_map/ppermute | solution.py:225
  (55 other events, 246.5 us)

commit v3 on v2

--- a/solution.py
+++ b/solution.py
@@ -123,6 +123,25 @@
         return self.ready()[index]
 
 
+class Near:
+    def __init__(self, ref):
+        self.ref, self.shape, self.dtype = ref, ref.shape, ref.dtype
+
+    def start(self, i=None):
+        pass
+
+    ready = send = start
+
+    def finish(self):
+        pass
+
+    def __getitem__(self, index):
+        return self.ref[index]
+
+    def __setitem__(self, index, value):
+        self.ref[index] = value
+
+
 class Out:
     def __init__(self, source, target, sems, chunks):
         self.ref, self.shape, self.dtype = source, source.shape, source.dtype
@@ -156,20 +175,25 @@
         self.ref[index] = value
 
 
-def call(body, outs, ins, scratch=(), limit=60, chunks=None, out_chunks=None, after=()):
+def call(body, outs, ins, scratch=(), limit=54, chunks=None, out_chunks=None, after=(), near=(), near_outs=()):
     chunks, out_chunks = chunks or {}, out_chunks or {}
     n, m, k = len(ins), len(outs), len(after)
-    in_parts = [chunks.get(i, 1) for i in range(n)]
-    out_parts = [out_chunks.get(i, 1) for i in range(m)]
+    far = [i for i in range(n) if i not in near]
+    far_outs = [i for i in range(m) if i not in near_outs]
+    parts = [chunks.get(i, 1) for i in far] + [out_chunks.get(i, 1) for i in far_outs]
 
     def inner(*refs):
         sources, targets, local = refs[:n], refs[n + k : n + k + m], refs[n + k + m :]
-        in_sems, out_sems = local[n + m : n + m + n], local[n + m + n : n + m + n + m]
-        given = [In(sources[i], local[i], in_sems[i], in_parts[i]) for i in range(n)]
-        made = [Out(local[n + i], targets[i], out_sems[i], out_parts[i]) for i in range(m)]
+        held, sems, rest = local[: len(parts)], local[len(parts) : 2 * len(parts)], local[2 * len(parts) :]
+        given = [Near(ref) for ref in sources]
+        for at, i in enumerate(far):
+            given[i] = In(sources[i], held[at], sems[at], parts[at])
+        made = [Near(ref) for ref in targets]
+        for at, i in enumerate(far_outs, len(far)):
+            made[i] = Out(held[at], targets[i], sems[at], parts[at])
         for each in given:
             each.start()
-        body(*given, *made, *local[n + m + n + m :])
+        body(*given, *made, *rest)
         for each in given:
             each.ready()
         for each in made:
@@ -177,20 +201,24 @@
         for each in made:
             each.finish()
 
+    space = lambda count, places: [pl.BlockSpec(memory_space=pltpu.VMEM if i in places else pltpu.HBM) for i in range(count)]
     return pl.pallas_call(
         inner,
-        out_shape=[jax.ShapeDtypeStruct(shape, kind) for shape, kind in outs],
-        in_specs=[pl.BlockSpec(memory_space=pltpu.HBM)] * (n + k),
-        out_specs=[pl.BlockSpec(memory_space=pltpu.HBM)] * m,
+        out_shape=[(pltpu.VMEM if i in near_outs else pltpu.HBM)(*out) for i, out in enumerate(outs)],
+        in_specs=space(n, near) + space(k, ()),
+        out_specs=space(m, near_outs),
         scratch_shapes=[
-            *[pltpu.VMEM(a.shape, a.dtype) for a in ins],
-            *[pltpu.VMEM(shape, kind) for shape, kind in outs],
-            *[pltpu.SemaphoreType.DMA((k,)) for k in in_parts + out_parts],
+            *[pltpu.VMEM(ins[i].shape, ins[i].dtype) for i in far],
+            *[pltpu.VMEM(*outs[i]) for i in far_outs],
+            *[pltpu.SemaphoreType.DMA((k,)) for k in parts],
             *scratch,
         ],
         compiler_params=pltpu.CompilerParams(vmem_limit_bytes=limit * 2**20),
         cost_estimate=pl.CostEstimate(flops=1, bytes_accessed=1, transcendentals=0),
-    )(*ins, *after)
+    )(
+        *[pltpu.with_memory_space_constraint(a, pltpu.VMEM if i in near else pltpu.HBM) for i, a in enumerate(ins)],
+        *[pltpu.with_memory_space_constraint(a, pltpu.HBM) for a in after],
+    )
 
 
 def local_call(body, outs, ins, scratch=(), limit=16, after=()):
@@ -237,6 +265,13 @@
 
     def bits(self):
         return [Digit(self.axis, self.unit << i, 2) for i in range(self.size.bit_length() - 1)]
+
+    def trade(self, stacked):
+        count = lax.axis_size(self.axis)
+        span = self.unit * self.size
+        starts = [high + low for high in range(0, count, span) for low in range(self.unit)]
+        groups = [[start + self.unit * d for d in range(self.size)] for start in starts]
+        return lax.all_to_all(stacked, self.axis, 0, 0, axis_index_groups=groups)
 
     def scatter(self, parts, outs):
         size = outs[0].shape[0]
@@ -728,8 +763,8 @@
     pay_ref[...] = jnp.broadcast_to(tile[...][None], pay_ref.shape)
 
 
-def final_kernel(core, g7_ref, par_ref, stat_ref, dy_ref, z_ref, own_ref, th_ref, tl_ref, wh_ref, wl_ref, grad_ref,
-                 keep_ref, send_ref, out_ref, gains_ref, term):
+def final_kernel(core, g7_ref, par_ref, stat_ref, dy_ref, z_ref, own_ref, th_ref, tl_ref,
+                 keep_ref, send_ref, dzh_ref, dzl_ref, gains_ref, term):
     width = z_ref.shape[1]
     gains_ref[...] = jnp.sum(g7_ref[...], axis=0)
     cross, flat = get(gains_ref, 0, 2), get(gains_ref, 2, 2)
@@ -738,14 +773,17 @@
     normed = (z_ref[...] - mean) * inv
     scale = get(par_ref, 0, 2) * inv
     dz = scale * (dy_ref[...] - flat / count - normed * (cross / count)) * wide(own_ref[...], width)
-    parts = split(dz)
-    term[...] = product((th_ref[...], tl_ref[...]), parts, NN)
+    high, low = split(dz)
+    dzh_ref[...] = high
+    dzl_ref[...] = low
+    term[...] = product((th_ref[...], tl_ref[...]), (high, low), NN)
     core.scatter([term], [keep_ref, send_ref])
-    keep_ref.send()
-    send_ref.send()
+
+
+def images_kernel(dzh_ref, dzl_ref, wh_ref, wl_ref, grad_ref, out_ref):
     for i in range(len(grad_ref.parts)):
-        rows = slice(grad_ref.parts[i].start, grad_ref.parts[i].start + grad_ref.parts[i].size)
-        out_ref.put(i, product([part[rows] for part in parts], (wh_ref[...], wl_ref[...]), NT) + grad_ref.chunk(i))
+        left = [ref.chunk(i) for ref in (dzh_ref, dzl_ref)]
+        out_ref.put(i, product(left, (wh_ref[...], wl_ref[...]), NT) + grad_ref.chunk(i))
 
 
 def deal_kernel(plan, count, *refs):
@@ -771,6 +809,37 @@
         rows = sum(rows for _, _, rows in stretches) // digit.size
         outs += [((rows, width), f32)] * digit.size
     return local_call(functools.partial(deal_kernel, plan, len(ins)), outs, ins, after=after)
+
+
+def stack_kernel(stretches, *refs):
+    refs, out = refs[:-1], refs[-1]
+    at = 0
+    for inputs, first, rows in stretches:
+        each = rows // out.shape[0]
+        for d in range(out.shape[0]):
+            here = slice(first + d * each, first + (d + 1) * each)
+            total = refs[inputs[0]][here, :]
+            for k in inputs[1:]:
+                total = total + refs[k][here, :]
+            out[d, at : at + each, :] = total
+        at += each
+
+
+def extra_pieces(extra, stacked):
+    if extra.size == 1:
+        return [stacked]
+    total = local_call(lambda ref, out: out.__setitem__(Ellipsis, jnp.sum(ref[...], axis=0)), [(stacked.shape[1:], f32)], [stacked])[0]
+    return extra.send([total] * extra.size)
+
+
+def spread_kernel(count, *refs):
+    if count == 1:
+        total = jnp.sum(refs[0][...], axis=0)
+    else:
+        total = refs[0][...]
+        for ref in refs[1:-1]:
+            total = total + ref[...]
+    refs[-1][...] = jnp.broadcast_to(total[None], refs[-1].shape)
 
 
 def halve_kernel(blocks, whole_ref, *outs):
@@ -866,6 +935,7 @@
         [valid_rows, valid_cols, w_reduce, x],
         [tile8],
         chunks={3: 2},
+        near_outs=(3, 4, 7),
     )
     g1 = share(pay)
     above, below = halos(first, last)
@@ -882,6 +952,8 @@
         [((cells, duo), f32), ((longer, mid), f32), ((8, 128), f32), ((devices, 128), f32), pay8],
         [g1, par, z_one, ext, above, below, own, wgh, wgl],
         [tile8, pltpu.VMEM((count, tall + 2, broad, mid), f32)],
+        near=(0, 4, 5),
+        near_outs=(4,),
     )
     g2 = share(pay)
     xth, xtl = call(turned_kernel, twice(chan, cells), [x], after=[stat1])
@@ -892,6 +964,8 @@
         chunks={5: 2, 6: 2},
         out_chunks={0: 2},
         after=[xth],
+        near=(0,),
+        near_outs=(3,),
     )
     g3 = share(pay)
     slope_two, normed_two, slopes = call(
@@ -900,6 +974,7 @@
         [stat2, par, valid_rows, valid_cols, own, z_two],
         chunks={4: 2, 5: 2},
         out_chunks={0: 2, 1: 2},
+        near_outs=(2,),
     )
     mixed, z_three, weights, fc_normed, fc_pre, fc_act, fc_inv, pay = call(
         expand_kernel,
@@ -909,6 +984,8 @@
         [tile16, pltpu.VMEM((all_images, inter), f32)],
         out_chunks={1: 2},
         after=[slopes],
+        near=(0,),
+        near_outs=(7,),
     )
     g4 = share(pay)
     slopes = line.send([slopes] * line.size)
@@ -919,6 +996,8 @@
         [tile16],
         chunks={3: 4, 4: 4, 5: 4, 6: 4},
         out_chunks={0: 4, 1: 4},
+        near=(0, *range(7, 7 + line.size)),
+        near_outs=(3, 4),
     )
     g5 = share(pay)
     slopes = depth.send([slopes] * depth.size)
@@ -932,6 +1011,8 @@
         chunks={4: 2, 5: 2, 6: 2},
         out_chunks={0: 2, 1: 2},
         after=[tph],
+        near=(0, *range(14, 14 + depth.size)),
+        near_outs=(5, 6),
     )
     g6 = share(pay)
     *expand_sum, excite_term = call(
@@ -952,6 +1033,8 @@
          grad_mixed, slope_two, normed_two, wgh, wgl],
         [pltpu.VMEM((all_images, inter), f32), pltpu.VMEM((all_images, mid), f32), pltpu.VMEM((all_images, 2 * duo), f32)],
         after=[excite_term],
+        near=(0, 12, 13),
+        near_outs=(0, 1),
     )
     above, below = halos(up, down)
     group_sum = call(
@@ -960,68 +1043,88 @@
         [dzh, dzl, squeeze_term, excite_term, tph, tpl],
         [pltpu.VMEM((packed, mid), f32)],
         chunks={4: 2, 5: 2},
+        near_outs=(0, 1),
     )
     expand_sum = core.send(expand_sum)
     group_sum = core.send([group_sum[0], gate(group_sum[1], [above, below])])
-    dy_one, pay = call(
-        input_grad_kernel,
-        [((cells, mid), f32), pay8],
-        [par, stat1, dsum, z_one, own, above, below, dzh, dzl, wgh, wgl],
-        [tile8, pltpu.VMEM((count, tall, broad, mid), f32)],
-    )
     first_bit, second_bit = line.bits()
     some, more = expand_sum[0].shape[0] // 2, group_sum[0].shape[0] // 2
     both_of = lambda start, a, b: [((0, 1), start * a, a), ((2, 3), start * b, b)]
     first_half = lambda digit: (digit, both_of(0, some, more))
     second_half = lambda digit: (digit, both_of(1, some, more))
     keep_a, send_a, keep_b, send_b = deal(
-        [first_half(first_bit), second_half(second_bit)], [*expand_sum, *group_sum], after=[dy_one]
+        [first_half(first_bit), second_half(second_bit)], [*expand_sum, *group_sum]
+    )
+    come_a, come_b = first_bit.send([keep_a, send_a]), second_bit.send([keep_b, send_b])
+    dy_one, pay = call(
+        input_grad_kernel,
+        [((cells, mid), f32), pay8],
+        [par, stat1, dsum, z_one, own, above, below, dzh, dzl, wgh, wgl],
+        [tile8, pltpu.VMEM((count, tall, broad, mid), f32)],
+        after=[keep_a],
+        near=(5, 6),
+        near_outs=(1,),
     )
     g7 = share(pay)
-    come_a, come_b = first_bit.send([keep_a, send_a]), second_bit.send([keep_b, send_b])
     some, more = some // 2, more // 2
     turn = lambda k: [((k, k + 1), 0, some), ((k, k + 1), some, more)]
-    keep_a, send_a, keep_b, send_b = deal([(second_bit, turn(0)), (first_bit, turn(2))], [*come_a, *come_b])
-    *reduce_sum, grad_images, grads_one = call(
+    keep_a, send_a, keep_b, send_b = deal([(second_bit, turn(0)), (first_bit, turn(2))], [*come_a, *come_b], after=[dy_one])
+    *reduce_sum, dzh, dzl, grads_one = call(
         functools.partial(final_kernel, core),
-        [*core.outs(chan, mid), ((cells, chan), f32), ((8, 128), f32)],
-        [g7, par, stat1, dy_one, z_one, own, xth, xtl, wrh, wrl, grad_pre],
+        [*core.outs(chan, mid), *twice(cells, mid), ((8, 128), f32)],
+        [g7, par, stat1, dy_one, z_one, own, xth, xtl],
         [pltpu.VMEM((chan, mid), f32)],
-        chunks={10: 2},
-        out_chunks={2: 2},
         after=[keep_a],
+        near=(0,),
+        near_outs=(0, 1),
     )
     come_a, come_b = second_bit.send([keep_a, send_a]), first_bit.send([keep_b, send_b])
     some, more = some // 2, more // 2
-    joined = deal([(depth, turn(0) + turn(2))], [*come_a, *come_b], after=[grad_images])
-    reduce_sum[1] = gate(reduce_sum[1], [joined[1]])
-    bits = [core, *line.bits(), *depth.bits()]
-    reduce_sum = scatter_more(bits[1], bits[0].send(reduce_sum))
-    joined = finish_sum(depth.send(joined), extra, after=[reduce_sum[0]])
-    reduce_sum = scatter_more(bits[2], bits[1].send(reduce_sum), after=[joined])
-    joined = gather_more(depth, depth.send([joined] * depth.size), after=[reduce_sum[0]])
-    rows_in = joined.shape[0]
+    stretches = turn(0) + turn(2)
+    (joined,) = local_call(
+        functools.partial(stack_kernel, stretches),
+        [((depth.size, (some + more) * 2 // depth.size, mid), f32)],
+        [*come_a, *come_b],
+        after=[dzh],
+    )
+    reduce_sum[1] = gate(reduce_sum[1], [joined])
+    joined = depth.trade(joined)
+    low_bit, high_bit = depth.bits()
+    reduce_sum = scatter_more(second_bit, core.send(reduce_sum))
+    (grad_images,) = call(
+        images_kernel,
+        [((cells, chan), f32)],
+        [dzh, dzl, wrh, wrl, grad_pre],
+        chunks={0: 2, 1: 2, 4: 2},
+        out_chunks={0: 2},
+        after=[reduce_sum[0]],
+    )
+    reduce_sum = scatter_more(first_bit, second_bit.send(reduce_sum), after=[grad_images])
+    (joined,) = local_call(
+        functools.partial(spread_kernel, extra.size), [(joined.shape, f32)], extra_pieces(extra, joined), after=[reduce_sum[0]]
+    )
+    joined = depth.trade(joined)
+    reduce_sum = scatter_more(high_bit, first_bit.send(reduce_sum))
+    rows_in = joined.shape[0] * joined.shape[1]
     half_a, half_b = local_call(
-        functools.partial(halve_kernel, depth.size), [((rows_in // 2, mid), f32)] * 2, [joined]
-    )
-    for here, there in zip(bits[2:-1], bits[3:]):
-        reduce_sum = scatter_more(there, here.send(reduce_sum), after=[half_a])
+        functools.partial(halve_kernel, depth.size), [((rows_in // 2, mid), f32)] * 2, [joined.reshape(-1, mid)], after=[reduce_sum[0]]
+    )
+    reduce_sum = scatter_more(low_bit, high_bit.send(reduce_sum), after=[half_a])
     half_a, half_b = local_call(
         functools.partial(pair_kernel, [second_bit, first_bit]),
         [((rows_in, mid), f32)] * 2,
         [*second_bit.send([half_a] * 2), *first_bit.send([half_b] * 2)],
         after=[reduce_sum[0]],
     )
-    reduce_sum = finish_sum(bits[-1].send(reduce_sum), extra, after=[half_a])
-    reduce_sum = gather_more(bits[-1], bits[-1].send([reduce_sum] * 2))
+    reduce_sum = finish_sum(low_bit.send(reduce_sum), extra, after=[half_a])
+    reduce_sum = gather_more(depth, depth.send([reduce_sum] * depth.size))
     (joined,) = local_call(
         functools.partial(pair_kernel, [first_bit, second_bit]),
         [((4 * rows_in, mid), f32)],
         [*first_bit.send([half_a] * 2), *second_bit.send([half_b] * 2)],
         after=[reduce_sum],
     )
-    for here in bits[-2:0:-1]:
-        reduce_sum = gather_more(here, here.send([reduce_sum] * 2), after=[joined])
+    reduce_sum = gather_more(line, line.send([reduce_sum] * line.size), after=[joined])
     expand_map, group_map = [], []
     at = 0
     some, more = some // depth.size, more // depth.size

time: 257 us -> 238 us (0.926)
  waiting for transfers between devices: 93 us -> 71.2 us
  starting transfers between devices: 67.3 us -> 72.4 us
    ppermute x34 -> x30, waiting for transfers between devices: 70.9 us -> 36.8 us  [flip(): lax.ppermute(values, axis, [(i, i ^ bits) for i in range(lax.axis_size(ax...]
    all_to_all x0 -> x2, waiting for transfers between devices: none -> 10.8 us  [trade(): return lax.all_to_all(stacked, self.axis, 0, 0, axis_index_groups=groups)]
    all_to_all x0 -> x2, starting transfers between devices: none -> 7.08 us  [trade(): return lax.all_to_all(stacked, self.axis, 0, 0, axis_index_groups=groups)]
    unnamed x68 -> x48, local copies, waits for them, and re-layouts: 11.3 us -> 9.01 us
    ppermute x34 -> x30, starting transfers between devices: 32 us -> 30 us  [flip(): lax.ppermute(values, axis, [(i, i ^ bits) for i in range(lax.axis_size(ax...]
    pallas_call x19 -> x16, Pallas kernels: 5.16 us -> 4.91 us  [local_call(): pl.pallas_call(inner, out_shape=[jax.ShapeDtypeStruct(shape, kind) for sh...]
    pallas_call x15 -> x16, Pallas kernels: 75.3 us -> 75.1 us  [call(): pl.pallas_call(inner, out_shape=[(pltpu.VMEM if i in near_outs else pltpu...]
  transfers between devices with their start and end apart: 45 -> 43, of which waited for: 25 -> 27; matrix products, arithmetic and copies ran while one was open for 1% -> 1% of each run, Pallas kernels for 16% -> 17%
where the time goes in v3:
time: 238 us; the launch traced here: 237 us
  Pallas kernels  80 us (34%)
  starting transfers between devices  72.4 us (30%)
  waiting for transfers between devices  71.2 us (30%)
  local copies, waits for them, and re-layouts  11.3 us (5%)
    pallas_call x16, Pallas kernels, call(): pl.pallas_call(inner, out_shape=[(pltpu.VMEM if i in near_outs else pltpu...  75.1 us
    ppermute x30, waiting for transfers between devices, flip(): lax.ppermute(values, axis, [(i, i ^ bits) for i in range(lax.axis_size(ax...  36.8 us
    ppermute x30, starting transfers between devices, flip(): lax.ppermute(values, axis, [(i, i ^ bits) for i in range(lax.axis_size(ax...  30 us
    all_to_all x7, starting transfers between devices, share(): return lax.all_to_all(tile, both, 0, 0)  26.4 us
    all_to_all x7, waiting for transfers between devices, share(): return lax.all_to_all(tile, both, 0, 0)  20.5 us
    all_to_all x2, waiting for transfers between devices, trade(): return lax.all_to_all(stacked, self.axis, 0, 0, axis_index_groups=groups)  10.8 us
    unnamed x48, local copies, waits for them, and re-layouts  9.01 us
    all_to_all x2, starting transfers between devices, trade(): return lax.all_to_all(stacked, self.axis, 0, 0, axis_index_groups=groups)  7.08 us
  transfers between devices with their start and end apart: 43, of which 27 were waited for; matrix products, arithmetic and copies ran while one was open for 1% of the time, Pallas kernels for 17%

profile of v3, /device:TPU:0, one launch (start us, length us, event | category | flops | bytes accessed | tf_op | source)
XLA Modules:
  0.0 236.6 jit_solution(7109853019417882189)
XLA Ops:
  0.6 5.3 %shard_map.297 = (f32[512,256]{1,0:T(8,128)}, f32[8,6,16,128]{3,2,1,0:T(8,128)}, f32[512,128]{1,0:T(8,128)}, f32[128,256]{1,0:T(8,128)S(1)}, f32[128,256]{1,0:T(...) custom-call(s32[8,16]{1,0:T(8,128)} %refs_9_.1, s32[8,16]{1,0:T(8,128)} %refs_10_.1, ...), custom_call_target="tpu_custom_call" | custom-call | flops 1 | bytes 1 | tf_op jit(solution)/shard_map/pallas_call | solution.py:205
  6.0 7.3 %all-to-all-start = ((f32[32,8,128]{2,1,0:T(8,128)}), f32[32,8,128]{2,1,0:T(8,128)S(1)}, u32[]{:S(2)}, u32[]{:S(2)}) async-start(f32[32,8,128]{2,1,0:T(8,128)} %get-tuple-element.108), calls=%async_computation | async-start | bytes 262144 | tf_op jit(solution)/shard_map/all_to_all | solution.py:242
  13.3 3.7 %collective-permute-start = (f32[128,256]{1,0:T(8,128)S(1)}, f32[128,256]{1,0:T(8,128)S(1)}, u32[]{:S(2)}, u32[]{:S(2)}) collective-permute-start(f32[128,256]{1,0:T(8,128)S(1)} %get-tuple-element.112), channel_id=1, source_target_pairs={{0,8},{8,16},{16,24},{1,9},{9,17},{17,25},{2,10},{10,18},{18,26},{... | collective-permute-start | bytes 393224 | tf_op jit(solution)/shard_map/ppermute | solution.py:247
  18.3 3.9 %shard_map.298 = (bf16[1152,512]{1,0:T(8,128)(2,1)}, bf16[1152,512]{1,0:T(8,128)(2,1)}, bf16[256,1024]{1,0:T(8,128)(2,1)}, bf16[256,1024]{1,0:T(8,128)(2,1)}, f32[40,128]{1,0:T(8,128)}) custom-call(f32[1152,512]{1,0:T(8,128)} %bitcast.41, f32[256,1024]{1,0:T(8,128)} %refs_1_.3, f32[1,256]{1,0:T(1,128)} %bitcast.48, f32[1,256]{1,0:T(1,128)} %bitcast.49, ...), custom_call_target="tpu_custom_call" | custom-call | flops 1 | bytes 1 | tf_op jit(solution)/shard_map/pallas_call | solution.py:205
  25.2 5.9 %shard_map.299 = (f32[512,512]{1,0:T(8,128)}, f32[768,256]{1,0:T(8,128)}, f32[8,128]{1,0:T(8,128)}, f32[32,128]{1,0:T(8,128)}, f32[32,8,128]{2,1,0:T(8,128)}) custom-call(f32[32,8,128]{2,1,0:T(8,128)S(1)} %all-to-all-done.refs_0_, f32[40,128]{1,0:T(8,128)} %get-tuple-element.110.refs_1_.refs_2_.refs_3_.refs_4_.refs_0_, ...), custom_call_target="tpu_custom_call" | custom-call | flops 1 | bytes 1 | tf_op jit(solution)/shard_map/pallas_call | solution.py:205
  31.1 4.5 %all-to-all-start.1 = ((f32[32,8,128]{2,1,0:T(8,128)}), f32[32,8,128]{2,1,0:T(8,128)S(1)}, u32[]{:S(2)}, u32[]{:S(2)}) async-start(f32[32,8,128]{2,1,0:T(8,128)} %get-tuple-element.117), calls=%async_computation.1 | async-start | bytes 262144 | tf_op jit(solution)/shard_map/all_to_all | solution.py:242
  35.6 3.6 %shard_map.300 = (bf16[1024,512]{1,0:T(8,128)(2,1)}, bf16[1024,512]{1,0:T(8,128)(2,1)}) custom-call(f32[512,1024]{1,0:T(8,128)} %bitcast.39, f32[8,128]{1,0:T(8,128)} %get-tuple-element.120.refs_1_.refs_7_.refs_2_), custom_call_target="tpu_custom_call" | custom-call | flops 1 | bytes 1 | tf_op jit(solution)/shard_map/pallas_call | solution.py:205
  39.2 4.5 %all-to-all-done.1.refs_0_ = f32[32,8,128]{2,1,0:T(8,128)S(1)} async-done(((f32[32,8,128]{2,1,0:T(8,128)}), f32[32,8,128]{2,1,0:T(8,128)S(1)}, u32[]{:S(2)}, u32[]{:S(2)}) %all-to-all-start.1) | async-done | bytes 131104 | tf_op jit(solution)/shard_map/all_to_all | solution.py:242
  52.9 4.7 %all-to-all-done.2.refs_0_ = f32[32,8,128]{2,1,0:T(8,128)S(1)} async-done(((f32[32,8,128]{2,1,0:T(8,128)}), f32[32,8,128]{2,1,0:T(8,128)S(1)}, u32[]{:S(2)}, u32[]{:S(2)}) %all-to-all-start.2) | async-done | bytes 131104 | tf_op jit(solution)/shard_map/all_to_all | solution.py:242
  57.6 4.4 %shard_map.303 = (f32[512,256]{1,0:T(8,128)}, f32[512,1024]{1,0:T(8,128)}, f32[8,512]{1,0:T(8,128)}, f32[64,128]{1,0:T(8,128)}, f32[64,128]{1,0:T(8,128)}, /*ind...) custom-call(f32[32,8,128]{2,1,0:T(8,128)S(1)} %all-to-all-done.2.refs_0_, ...), custom_call_target="tpu_custom_call" | custom-call | flops 1 | bytes 1 | tf_op jit(solution)/shard_map/pallas_call | solution.py:205
  75.0 6.0 %shard_map.304 = (f32[512,1024]{1,0:T(8,128)}, f32[512,1024]{1,0:T(8,128)}, f32[16,128]{1,0:T(8,128)}, f32[8,1024]{1,0:T(8,128)S(1)}, f32[32,16,128]{2,1,0:T(8,128)}) custom-call(f32[32,16,128]{2,1,0:T(8,128)S(1)} %all-to-all-done.3.refs_0_, f32[32,128]{1,0:T(8,128)} %get-tuple-element.118.refs_1_, ...), custom_call_target="tpu_custom_call" | custom-call | flops 1 | bytes 1 | tf_op jit(solution)/shard_map/pallas_call | solution.py:205
  83.7 3.7 %collective-permute-start.7 = (f32[8,1024]{1,0:T(8,128)S(1)}, f32[8,1024]{1,0:T(8,128)S(1)}, u32[]{:S(2)}, u32[]{:S(2)}) collective-permute-start(f32[8,1024]{1,0:T(8,128)S(1)} %get-tuple-element.137.refs_14_), channel_id=1, source_target_pairs={{0,6},{1,7},{2,4},{3,5},{4,2},{5,3},{6,0},{7,1},{8,14},{9,15},{10,... | collective-permute-start | bytes 98312 | tf_op jit(solution)/shard_map/ppermute | solution.py:253
  88.1 4.0 %shard_map.305 = (bf16[2,1152,512]{2,1,0:T(8,128)(2,1)}, bf16[2,1152,512]{2,1,0:T(8,128)(2,1)}) custom-call(f32[768,256]{1,0:T(8,128)} %get-tuple-element.138.refs_0_, f32[16,128]{1,0:T(8,128)} %get-tuple-element.132.refs_1_.refs_2_), custom_call_target="tpu_custom_call" | custom-call | flops 1 | bytes 1 | tf_op jit(solution)/shard_map/pallas_call | solution.py:205
  95.9 7.2 %shard_map.306 = (bf16[512,1024]{1,0:T(8,128)(2,1)}, bf16[512,1024]{1,0:T(8,128)(2,1)}, f32[512,256]{1,0:T(8,128)}, f32[8,256]{1,0:T(8,128)}, f32[16,128]{1,0:T(...) custom-call(f32[32,16,128]{2,1,0:T(8,128)S(1)} %all-to-all-done.4.refs_0_, ...), custom_call_target="tpu_custom_call" | custom-call | flops 1 | bytes 1 | tf_op jit(solution)/shard_map/pallas_call | solution.py:205
  106.9 4.0 %shard_map.307 = (f32[512,256]{1,0:T(8,128)}, f32[512,256]{1,0:T(8,128)}, f32[128,256]{1,0:T(8,128)}) custom-call(f32[512,256]{1,0:T(8,128)} %get-tuple-element.148.refs_0_, f32[8,128]{1,0:T(8,128)} %get-tuple-element.149.refs_1_, f32[8,256]{1,0:T(8,128)} %get-tuple-element.140.refs_2_, bf16[512,1024]{1,0:T(8,128)(2,1)} %get-tuple-element.150.refs_3_, ...), custom_call_target="tpu_custom_call" | custom-call | flops 1 | bytes 1 | tf_op jit(solution)/shard_map/pallas_call | solution.py:205
  111.0 6.0 %all-to-all-done.5.refs_0_ = f32[32,16,128]{2,1,0:T(8,128)S(1)} async-done(((f32[32,16,128]{2,1,0:T(8,128)}), f32[32,16,128]{2,1,0:T(8,128)S(1)}, u32[]{:S(2)}, u32[]{:S(2)}) %all-to-all-start.5) | async-done | bytes 262176 | tf_op jit(solution)/shard_map/all_to_all | solution.py:242
  117.0 4.0 %shard_map.308 = (f32[128,256]{1,0:T(8,128)S(1)}, f32[128,256]{1,0:T(8,128)S(1)}, bf16[8,6,16,512]{3,2,1,0:T(8,128)(2,1)}, bf16[8,6,16,512]{3,2,1,0:T(8,128)(2,1...) custom-call(f32[32,16,128]{2,1,0:T(8,128)S(1)} %all-to-all-done.5.refs_0_, ...), custom_call_target="tpu_custom_call" | custom-call | flops 1 | bytes 1 | tf_op jit(solution)/shard_map/pallas_call | solution.py:205
  124.9 6.5 %shard_map.309 = (f32[1280,256]{1,0:T(8,128)S(1)}, f32[1280,256]{1,0:T(8,128)S(1)}) custom-call(bf16[8,6,16,512]{3,2,1,0:T(8,128)(2,1)} %get-tuple-element.155.refs_0_.refs_7_, bf16[8,6,16,512]{3,2,1,0:T(8,128)(2,1)} %get-tuple-element.156.refs_1_.refs_8_, f32[128,256]{1,0:T(8,128)} %get-tuple-element.159.refs_2_, ...), custom_call_target="tpu_custom_call" | custom-call | flops 1 | bytes 1 | tf_op jit(solution)/shard_map/pallas_call | solution.py:205
  141.6 6.9 %shard_map.312 = (f32[512,256]{1,0:T(8,128)}, f32[32,8,128]{2,1,0:T(8,128)}) custom-call(f32[40,128]{1,0:T(8,128)} %get-tuple-element.110.refs_1_.refs_2_.refs_3_.refs_4_.refs_0_, f32[8,128]{1,0:T(8,128)} %get-tuple-element.120.refs_1_.refs_7_.refs_2_, f32[8,256]{1,0:T(8,128)} %get-tuple-element.140.refs_2_, ...), custom_call_target="tpu_custom_call" | custom-call | flops 1 | bytes 1 | tf_op jit(solution)/shard_map/pallas_call | solution.py:205
  170.4 4.2 %shard_map.318.refs_2_ = f32[512,1024]{1,0:T(8,128)} custom-call(bf16[512,256]{1,0:T(8,128)(2,1)} %get-tuple-element.171.refs_4_.refs_0_, bf16[512,256]{1,0:T(8,128)(2,1)} %get-tuple-element.172.refs_1_, bf16[1024,256]{1,0:T(8,128)(2,1)} %get-tuple-element.173.refs_2_, bf16[1024,256]{1,0:T(8,128)(2,1)} %get-tuple-element.174.refs_3_, ...), custom_call_target="tpu_custom_call" | custom-call | flops 1 | bytes 1 | tf_op jit(solution)/shard_map/pallas_call | solution.py:205
  174.6 3.6 %collective-permute-done.18.refs_1_ = f32[256,256]{1,0:T(8,128)S(1)} collective-permute-done((f32[256,256]{1,0:T(8,128)S(1)}, f32[256,256]{1,0:T(8,128)S(1)}, u32[]{:S(2)}, u32[]{:S(2)}) %collective-permute-start.18) | collective-permute-done | bytes 262176 | tf_op jit(solution)/shard_map/ppermute | solution.py:253
  192.1 7.9 %all-to-all-done.8 = f32[4,112,256]{2,1,0:T(8,128)S(1)} async-done(((f32[4,112,256]{2,1,0:T(8,128)}), f32[4,112,256]{2,1,0:T(8,128)S(1)}, u32[]{:S(2)}, u32[]{:S(2)}) %all-to-all-start.8) | async-done | bytes 458784 | tf_op jit(solution)/shard_map/all_to_all | solution.py:274
  202.1 5.2 %collective-permute-done.20.refs_1_ = f32[64,256]{1,0:T(8,128)S(1)} collective-permute-done((f32[64,256]{1,0:T(8,128)S(1)}, f32[64,256]{1,0:T(8,128)S(1)}, u32[]{:S(2)}, u32[]{:S(2)}) %collective-permute-start.20) | collective-permute-done | bytes 65568 | tf_op jit(solution)/shard_map/ppermute | solution.py:253
  209.5 3.9 %collective-permute-done.21.refs_1_ = f32[32,256]{1,0:T(8,128)S(1)} collective-permute-done((f32[32,256]{1,0:T(8,128)S(1)}, f32[32,256]{1,0:T(8,128)S(1)}, u32[]{:S(2)}, u32[]{:S(2)}) %collective-permute-start.21) | collective-permute-done | bytes 32800 | tf_op jit(solution)/shard_map/ppermute | solution.py:253
  (150 shorter events, 114.5 us)
Async XLA Ops:
  6.0 19.2 %all-to-all-start = ((f32[32,8,128]{2,1,0:T(8,128)}), f32[32,8,128]{2,1,0:T(8,128)S(1)}, u32[]{:S(2)}, u32[]{:S(2)}) async-start(f32[32,8,128]{2,1,0:T(8,128)} %get-tuple-element.108), calls=%async_computation | async-start | bytes 262144 | tf_op jit(solution)/shard_map/all_to_all | solution.py:242
  13.3 8.9 %collective-permute-start = (f32[128,256]{1,0:T(8,128)S(1)}, f32[128,256]{1,0:T(8,128)S(1)}, u32[]{:S(2)}, u32[]{:S(2)}) collective-permute-start(f32[128,256]{1,0:T(8,128)S(1)} %get-tuple-element.112), channel_id=1, source_target_pairs={{0,8},{8,16},{16,24},{1,9},{9,17},{17,25},{2,10},{10,18},{18,26},{... | collective-permute-start | bytes 393224 | tf_op jit(solution)/shard_map/ppermute | solution.py:247
  17.0 8.2 %collective-permute-start.1 = (f32[128,256]{1,0:T(8,128)S(1)}, f32[128,256]{1,0:T(8,128)S(1)}, u32[]{:S(2)}, u32[]{:S(2)}) collective-permute-start(f32[128,256]{1,0:T(8,128)S(1)} %get-tuple-element.113), channel_id=1, source_target_pairs={{8,0},{16,8},{24,16},{9,1},{17,9},{25,17},{10,2},{18,10},{26,18},{... | collective-permute-start | bytes 393224 | tf_op jit(solution)/shard_map/ppermute | solution.py:248
  31.1 12.6 %all-to-all-start.1 = ((f32[32,8,128]{2,1,0:T(8,128)}), f32[32,8,128]{2,1,0:T(8,128)S(1)}, u32[]{:S(2)}, u32[]{:S(2)}) async-start(f32[32,8,128]{2,1,0:T(8,128)} %get-tuple-element.117), calls=%async_computation.1 | async-start | bytes 262144 | tf_op jit(solution)/shard_map/all_to_all | solution.py:242
  46.8 10.8 %all-to-all-start.2 = ((f32[32,8,128]{2,1,0:T(8,128)}), f32[32,8,128]{2,1,0:T(8,128)S(1)}, u32[]{:S(2)}, u32[]{:S(2)}) async-start(f32[32,8,128]{2,1,0:T(8,128)} %get-tuple-element.122), calls=%async_computation.2 | async-start | bytes 262144 | tf_op jit(solution)/shard_map/all_to_all | solution.py:242
  62.0 13.0 %all-to-all-start.3 = ((f32[32,16,128]{2,1,0:T(8,128)}), f32[32,16,128]{2,1,0:T(8,128)S(1)}, u32[]{:S(2)}, u32[]{:S(2)}) async-start(f32[32,16,128]{2,1,0:T(8,128)} %get-tuple-element.128), calls=%async_computation.3 | async-start | bytes 524288 | tf_op jit(solution)/shard_map/all_to_all | solution.py:242
  81.1 14.8 %all-to-all-start.4 = ((f32[32,16,128]{2,1,0:T(8,128)}), f32[32,16,128]{2,1,0:T(8,128)S(1)}, u32[]{:S(2)}, u32[]{:S(2)}) async-start(f32[32,16,128]{2,1,0:T(8,128)} %get-tuple-element.131), calls=%async_computation.4 | async-start | bytes 524288 | tf_op jit(solution)/shard_map/all_to_all | solution.py:242
  83.7 10.1 %collective-permute-start.7 = (f32[8,1024]{1,0:T(8,128)S(1)}, f32[8,1024]{1,0:T(8,128)S(1)}, u32[]{:S(2)}, u32[]{:S(2)}) collective-permute-start(f32[8,1024]{1,0:T(8,128)S(1)} %get-tuple-element.137.refs_14_), channel_id=1, source_target_pairs={{0,6},{1,7},{2,4},{3,5},{4,2},{5,3},{6,0},{7,1},{8,14},{9,15},{10,... | collective-permute-start | bytes 98312 | tf_op jit(solution)/shard_map/ppermute | solution.py:253
  87.4 8.5 %collective-permute-start.6 = (f32[8,1024]{1,0:T(8,128)S(1)}, f32[8,1024]{1,0:T(8,128)S(1)}, u32[]{:S(2)}, u32[]{:S(2)}) collective-permute-start(f32[8,1024]{1,0:T(8,128)S(1)} %get-tuple-element.137.refs_14_), channel_id=1, source_target_pairs={{0,4},{1,5},{2,6},{3,7},{4,0},{5,1},{6,2},{7,3},{8,12},{9,13},{10,... | collective-permute-start | bytes 98312 | tf_op jit(solution)/shard_map/ppermute | solution.py:253
  87.4 8.5 %collective-permute-start.5 = (f32[8,1024]{1,0:T(8,128)S(1)}, f32[8,1024]{1,0:T(8,128)S(1)}, u32[]{:S(2)}, u32[]{:S(2)}) collective-permute-start(f32[8,1024]{1,0:T(8,128)S(1)} %get-tuple-element.137.refs_14_), channel_id=1, source_target_pairs={{0,2},{1,3},{2,0},{3,1},{4,6},{5,7},{6,4},{7,5},{8,10},{9,11},{10,... | collective-permute-start | bytes 98312 | tf_op jit(solution)/shard_map/ppermute | solution.py:253
  103.1 13.9 %all-to-all-start.5 = ((f32[32,16,128]{2,1,0:T(8,128)}), f32[32,16,128]{2,1,0:T(8,128)S(1)}, u32[]{:S(2)}, u32[]{:S(2)}) async-start(f32[32,16,128]{2,1,0:T(8,128)} %get-tuple-element.141), calls=%async_computation.5 | async-start | bytes 524288 | tf_op jit(solution)/shard_map/all_to_all | solution.py:242
  121.0 11.5 %collective-permute-start.9 = (f32[128,256]{1,0:T(8,128)S(1)}, f32[128,256]{1,0:T(8,128)S(1)}, u32[]{:S(2)}, u32[]{:S(2)}) collective-permute-start(f32[128,256]{1,0:T(8,128)S(1)} %get-tuple-element.153), channel_id=1, source_target_pairs={{0,8},{8,16},{16,24},{1,9},{9,17},{17,25},{2,10},{10,18},{18,26},{... | collective-permute-start | bytes 393224 | tf_op jit(solution)/shard_map/ppermute | solution.py:247
  123.4 9.1 %collective-permute-start.10 = (f32[128,256]{1,0:T(8,128)S(1)}, f32[128,256]{1,0:T(8,128)S(1)}, u32[]{:S(2)}, u32[]{:S(2)}) collective-permute-start(f32[128,256]{1,0:T(8,128)S(1)} %get-tuple-element.154), channel_id=1, source_target_pairs={{8,0},{16,8},{24,16},{9,1},{17,9},{25,17},{10,2},{18,10},{26,18},{... | collective-permute-start | bytes 393224 | tf_op jit(solution)/shard_map/ppermute | solution.py:248
  138.0 13.6 %collective-permute-start.13 = (f32[448,256]{1,0:T(8,128)S(1)}, f32[448,256]{1,0:T(8,128)S(1)}, u32[]{:S(2)}, u32[]{:S(2)}) collective-permute-start(f32[448,256]{1,0:T(8,128)S(1)} %get-tuple-element.167), channel_id=1, source_target_pairs={{0,8},{8,0},{16,24},{24,16},{1,9},{9,1},{17,25},{25,17},{2,10},{10... | collective-permute-start | bytes 1376264 | tf_op jit(solution)/shard_map/ppermute | solution.py:253
  140.6 12.3 %collective-permute-start.14 = (f32[448,256]{1,0:T(8,128)S(1)}, f32[448,256]{1,0:T(8,128)S(1)}, u32[]{:S(2)}, u32[]{:S(2)}) collective-permute-start(f32[448,256]{1,0:T(8,128)S(1)} %get-tuple-element.169), channel_id=1, source_target_pairs={{0,16},{8,24},{16,0},{24,8},{1,17},{9,25},{17,1},{25,9},{2,18},{10... | collective-permute-start | bytes 1376264 | tf_op jit(solution)/shard_map/ppermute | solution.py:253
  148.5 11.3 %all-to-all-start.6 = ((f32[32,8,128]{2,1,0:T(8,128)}), f32[32,8,128]{2,1,0:T(8,128)S(1)}, u32[]{:S(2)}, u32[]{:S(2)}) async-start(f32[32,8,128]{2,1,0:T(8,128)} %get-tuple-element.164), calls=%async_computation.6 | async-start | bytes 262144 | tf_op jit(solution)/shard_map/all_to_all | solution.py:242
  154.7 8.2 %collective-permute-start.15 = (f32[224,256]{1,0:T(8,128)S(1)}, f32[224,256]{1,0:T(8,128)S(1)}, u32[]{:S(2)}, u32[]{:S(2)}) collective-permute-start(f32[224,256]{1,0:T(8,128)S(1)} %get-tuple-element.177), channel_id=1, source_target_pairs={{0,16},{8,24},{16,0},{24,8},{1,17},{9,25},{17,1},{25,9},{2,18},{10... | collective-permute-start | bytes 688136 | tf_op jit(solution)/shard_map/ppermute | solution.py:253
  165.4 17.4 %all-to-all-start.7 = ((f32[4,112,256]{2,1,0:T(8,128)}), f32[4,112,256]{2,1,0:T(8,128)S(1)}, u32[]{:S(2)}, u32[]{:S(2)}) async-start(f32[4,112,256]{2,1,0:T(8,128)} %copy-done.1), calls=%async_computation.7 | async-start | bytes 917504 | tf_op jit(solution)/shard_map/all_to_all | solution.py:274
  169.8 8.4 %collective-permute-start.18 = (f32[256,256]{1,0:T(8,128)S(1)}, f32[256,256]{1,0:T(8,128)S(1)}, u32[]{:S(2)}, u32[]{:S(2)}) collective-permute-start(f32[256,256]{1,0:T(8,128)S(1)} %get-tuple-element.181), channel_id=1, source_target_pairs={{0,16},{8,24},{16,0},{24,8},{1,17},{9,25},{17,1},{25,9},{2,18},{10... | collective-permute-start | bytes 786440 | tf_op jit(solution)/shard_map/ppermute | solution.py:253
  183.6 16.4 %all-to-all-start.8 = ((f32[4,112,256]{2,1,0:T(8,128)}), f32[4,112,256]{2,1,0:T(8,128)S(1)}, u32[]{:S(2)}, u32[]{:S(2)}) async-start(f32[4,112,256]{2,1,0:T(8,128)} %shard_map.321), calls=%async_computation.8 | async-start | bytes 917504 | tf_op jit(solution)/shard_map/all_to_all | solution.py:274
  207.9 12.2 %collective-permute-start.31 = (f32[448,256]{1,0:T(8,128)S(1)}, f32[448,256]{1,0:T(8,128)S(1)}, u32[]{:S(2)}, u32[]{:S(2)}) collective-permute-start(f32[448,256]{1,0:T(8,128)S(1)} %get-tuple-element.191.refs_2_), channel_id=1, source_target_pairs={{0,16},{8,24},{16,0},{24,8},{1,17},{9,25},{17,1},{25,9},{2,18},{10... | collective-permute-start | bytes 1376264 | tf_op jit(solution)/shard_map/ppermute | solution.py:253
  208.9 11.2 %collective-permute-start.30 = (f32[448,256]{1,0:T(8,128)S(1)}, f32[448,256]{1,0:T(8,128)S(1)}, u32[]{:S(2)}, u32[]{:S(2)}) collective-permute-start(f32[448,256]{1,0:T(8,128)S(1)} %get-tuple-element.190.refs_2_.refs_0_), channel_id=1, source_target_pairs={{0,8},{8,0},{16,24},{24,16},{1,9},{9,1},{17,25},{25,17},{2,10},{10... | collective-permute-start | bytes 1376264 | tf_op jit(solution)/shard_map/ppermute | solution.py:253
  220.3 14.0 %collective-permute-start.33 = (f32[1792,256]{1,0:T(8,128)S(1)}, f32[1792,256]{1,0:T(8,128)S(1)}, u32[]{:S(2)}, u32[]{:S(2)}) collective-permute-start(f32[1792,256]{1,0:T(8,128)S(1)} %shard_map.327.refs_4_.refs_0_), channel_id=1, source_target_pairs={{0,1},{1,0},{2,3},{3,2},{4,5},{5,4},{6,7},{7,6},{8,9},{9,8},{10,11... | collective-permute-start | bytes 5505032 | tf_op jit(solution)/shard_map/ppermute | solution.py:253
  223.6 7.6 %collective-permute-start.28 = (f32[128,256]{1,0:T(8,128)S(1)}, f32[128,256]{1,0:T(8,128)S(1)}, u32[]{:S(2)}, u32[]{:S(2)}) collective-permute-start(f32[128,256]{1,0:T(8,128)S(1)} %shard_map.326.refs_4_.refs_0_), channel_id=1, source_target_pairs={{0,16},{8,24},{16,0},{24,8},{1,17},{9,25},{17,1},{25,9},{2,18},{10... | collective-permute-start | bytes 393224 | tf_op jit(solution)/shard_map/ppermute | solution.py:253
  (43 other events, 201.0 us)

commit v4 on v3

--- a/solution.py
+++ b/solution.py
@@ -175,9 +175,9 @@
         self.ref[index] = value
 
 
-def call(body, outs, ins, scratch=(), limit=54, chunks=None, out_chunks=None, after=(), near=(), near_outs=()):
+def call(body, outs, ins, scratch=(), limit=54, chunks=None, out_chunks=None, after=(), beside=(), near=(), near_outs=()):
     chunks, out_chunks = chunks or {}, out_chunks or {}
-    n, m, k = len(ins), len(outs), len(after)
+    n, m, k = len(ins), len(outs), len(after) + len(beside)
     far = [i for i in range(n) if i not in near]
     far_outs = [i for i in range(m) if i not in near_outs]
     parts = [chunks.get(i, 1) for i in far] + [out_chunks.get(i, 1) for i in far_outs]
@@ -205,7 +205,7 @@
     return pl.pallas_call(
         inner,
         out_shape=[(pltpu.VMEM if i in near_outs else pltpu.HBM)(*out) for i, out in enumerate(outs)],
-        in_specs=space(n, near) + space(k, ()),
+        in_specs=space(n, near) + space(len(after), ()) + space(len(beside), range(len(beside))),
         out_specs=space(m, near_outs),
         scratch_shapes=[
             *[pltpu.VMEM(ins[i].shape, ins[i].dtype) for i in far],
@@ -218,24 +218,30 @@
     )(
         *[pltpu.with_memory_space_constraint(a, pltpu.VMEM if i in near else pltpu.HBM) for i, a in enumerate(ins)],
         *[pltpu.with_memory_space_constraint(a, pltpu.HBM) for a in after],
-    )
-
-
-def local_call(body, outs, ins, scratch=(), limit=16, after=()):
-    n, k = len(ins), len(after)
+        *[pltpu.with_memory_space_constraint(a, pltpu.VMEM) for a in beside],
+    )
+
+
+def local_call(body, outs, ins, scratch=(), limit=16, after=(), beside=()):
+    n, k = len(ins), len(after) + len(beside)
 
     def inner(*refs):
         body(*refs[:n], *refs[n + k :])
 
+    spec = lambda space, count: [pl.BlockSpec(memory_space=space)] * count
     return pl.pallas_call(
         inner,
-        out_shape=[jax.ShapeDtypeStruct(shape, kind) for shape, kind in outs],
-        in_specs=[pl.BlockSpec(memory_space=pltpu.VMEM)] * n + [pl.BlockSpec(memory_space=pl.ANY)] * k,
-        out_specs=[pl.BlockSpec(memory_space=pltpu.VMEM)] * len(outs),
+        out_shape=[pltpu.VMEM(*out) for out in outs],
+        in_specs=spec(pltpu.VMEM, n) + spec(pltpu.HBM, len(after)) + spec(pltpu.VMEM, len(beside)),
+        out_specs=spec(pltpu.VMEM, len(outs)),
         scratch_shapes=list(scratch),
         compiler_params=pltpu.CompilerParams(vmem_limit_bytes=limit * 2**20),
         cost_estimate=pl.CostEstimate(flops=1, bytes_accessed=1, transcendentals=0),
-    )(*ins, *after)
+    )(
+        *[pltpu.with_memory_space_constraint(a, pltpu.VMEM) for a in ins],
+        *[pltpu.with_memory_space_constraint(a, pltpu.HBM) for a in after],
+        *[pltpu.with_memory_space_constraint(a, pltpu.VMEM) for a in beside],
+    )
 
 
 def share(tile):
@@ -299,14 +305,15 @@
     return Digit("batch", 1, 2), Digit("rows", 1, rows), Digit("batch", 2, depth), Digit("batch", 2 * depth, batch // (2 * depth))
 
 
-def gate(value, after):
+def gate(value, beside):
     return pl.pallas_call(
         lambda *refs: None,
-        out_shape=jax.ShapeDtypeStruct(value.shape, value.dtype),
-        in_specs=[pl.BlockSpec(memory_space=pl.ANY)] * (1 + len(after)),
-        out_specs=pl.BlockSpec(memory_space=pl.ANY),
+        out_shape=pltpu.VMEM(value.shape, value.dtype),
+        in_specs=[pl.BlockSpec(memory_space=pltpu.VMEM)] * (1 + len(beside)),
+        out_specs=pl.BlockSpec(memory_space=pltpu.VMEM),
         input_output_aliases={0: 0},
-    )(value, *after)
+        cost_estimate=pl.CostEstimate(flops=1, bytes_accessed=1, transcendentals=0),
+    )(*[pltpu.with_memory_space_constraint(a, pltpu.VMEM) for a in (value, *beside)])
 
 
 def scatter_kernel(digit, count, *refs):
@@ -324,29 +331,29 @@
     digit.gather(refs[:-1], refs[-1])
 
 
-def scatter_more(digit, pieces, after=()):
+def scatter_more(digit, pieces, **order):
     rows, width = pieces[0].shape
     body = functools.partial(scatter_kernel, digit, len(pieces))
-    return local_call(body, digit.outs(rows, width), pieces, after=after)
-
-
-def add_up(pieces, after=()):
-    return local_call(sum_kernel, [(pieces[0].shape, f32)], pieces, after=after)[0]
-
-
-def finish_sum(pieces, extra, after=()):
-    total = add_up(pieces, after)
+    return local_call(body, digit.outs(rows, width), pieces, **order)
+
+
+def add_up(pieces, **order):
+    return local_call(sum_kernel, [(pieces[0].shape, f32)], pieces, **order)[0]
+
+
+def finish_sum(pieces, extra, **order):
+    total = add_up(pieces, **order)
     if extra.size > 1:
         total = add_up(extra.send([total] * extra.size))
     return total
 
 
-def gather_more(digit, pieces, after=()):
+def gather_more(digit, pieces, **order):
     rows, width = pieces[0].shape
-    return local_call(functools.partial(gather_kernel, digit), [((rows * digit.size, width), f32)], pieces, after=after)[0]
-
-
-def reduce_kernel(rows_ref, cols_ref, w_ref, x_ref, z_ref, ext_ref, own_ref, first_ref, last_ref, wrh_ref, wrl_ref, pay_ref,
+    return local_call(functools.partial(gather_kernel, digit), [((rows * digit.size, width), f32)], pieces, **order)[0]
+
+
+def reduce_kernel(rows_ref, cols_ref, w_ref, x_ref, z_ref, ext_ref, own_ref, first_ref, last_ref, pay_ref,
                   tile):
     images = rows_ref.shape[0]
     tall = x_ref.shape[0] // images // 16
@@ -363,15 +370,14 @@
     ext_ref[...] = mask
     own = mask[:, 1 : tall + 1].reshape(-1, 128)
     own_ref[...] = own
-    wrh_ref[...], wrl_ref[...] = split(w_ref[...])
-    weight = (wrh_ref[...], wrl_ref[...])
+    weight = split(w_ref[...])
     for i in range(len(x_ref.parts)):
         z_ref[x_ref.parts[i]] = product(split(x_ref.chunk(i)), weight, NN)
     z = z_ref[...]
     edges = z.reshape(images, tall, 16, -1)
     first_ref[...] = edges[:, 0].reshape(first_ref.shape)
     last_ref[...] = edges[:, tall - 1].reshape(last_ref.shape)
-    for each in (first_ref, last_ref, z_ref, ext_ref, own_ref, wrh_ref, wrl_ref):
+    for each in (first_ref, last_ref, z_ref, ext_ref, own_ref):
         each.send()
     count = column_sum(own)
     sums, squares = local_stats(z, wide(own, z.shape[1]), wide(count, z.shape[1]))
@@ -382,13 +388,13 @@
     pay_ref[...] = jnp.broadcast_to(tile[...][None], pay_ref.shape)
 
 
-def parts_kernel(wg_ref, we_ref, *refs):
-    vectors, (wgh_ref, wgl_ref, weh_ref, wel_ref, par_ref) = refs[:-5], refs[-5:]
+def parts_kernel(wg_ref, we_ref, wr_ref, *refs):
+    vectors, (wgh_ref, wgl_ref, weh_ref, wel_ref, wrh_ref, wrl_ref, par_ref) = refs[:-7], refs[-7:]
     row = 0
     for vector in vectors:
         put(par_ref, row, vector[...])
         row += vector.shape[1] // 128
-    for source, high_ref, low_ref in ((wg_ref, wgh_ref, wgl_ref), (we_ref, weh_ref, wel_ref)):
+    for source, high_ref, low_ref in ((wg_ref, wgh_ref, wgl_ref), (we_ref, weh_ref, wel_ref), (wr_ref, wrh_ref, wrl_ref)):
         for i in range(len(source.parts)):
             high, low = split(source.chunk(i))
             high_ref.put(i, high)
@@ -571,7 +577,7 @@
 
 
 def output_kernel(g4_ref, counts_ref, par_ref, own_ref, z_ref, x_ref, cot_ref, *refs):
-    slope_refs, (out_ref, grad_ref, stat_ref, slopes_ref, pay_ref, tile) = refs[:-6], refs[-6:]
+    slope_refs, (grad_ref, stat_ref, slopes_ref, pay_ref, tile) = refs[:-5], refs[-5:]
     width = z_ref.shape[1]
     groups = width // 128
     mean, inv, total = merge_stats(g4_ref[...], counts_ref[...], width)
@@ -584,7 +590,6 @@
         normed = (z_ref.chunk(i) - mean) * inv
         pre = normed * gain + shift + x_ref.chunk(i)
         sigma = jax.nn.sigmoid(pre)
-        out_ref.put(i, pre * sigma * own)
         grad = cot_ref.chunk(i) * own * (sigma * (1.0 + pre * (1.0 - sigma)))
         grad_ref.put(i, grad)
         flat = flat + column_sum(grad)
@@ -595,9 +600,20 @@
     sum_kernel(*slope_refs, slopes_ref)
 
 
+def result_kernel(stat_ref, par_ref, own_ref, z_ref, x_ref, out_ref, mark_ref):
+    width = z_ref.shape[1]
+    groups = width // 128
+    mean, inv = get(stat_ref, 0, groups), get(stat_ref, groups, groups)
+    gain, shift = get(par_ref, 18, groups), get(par_ref, 26, groups)
+    for i in range(len(z_ref.parts)):
+        pre = (z_ref.chunk(i) - mean) * inv * gain + shift + x_ref.chunk(i)
+        out_ref.put(i, pre * jax.nn.sigmoid(pre) * wide(own_ref.chunk(i), width))
+    mark_ref[...] = own_ref[:8, :]
+
+
 def mixed_kernel(digit, g5_ref, stat1_ref, stat3_ref, par_ref, own_ref, grad_ref, z_ref, wh_ref, wl_ref, a_ref, weights_ref,
                  w_ref, slope_ref, normed_ref, *refs):
-    shares, (dzh_ref, dzl_ref, gm_ref, dsum_ref, grads_ref, slopes_ref, pay_ref, tile) = refs[: digit.size], refs[digit.size :]
+    shares, (gm_ref, dsum_ref, grads_ref, slopes_ref, pay_ref, tile) = refs[: digit.size], refs[digit.size :]
     width = z_ref.shape[1]
     mid = gm_ref.shape[1]
     images = weights_ref.shape[0]
@@ -611,10 +627,7 @@
     for i in range(len(z_ref.parts)):
         normed = (z_ref.chunk(i) - mean) * inv
         dz = scale * (grad_ref.chunk(i) - flat - normed * cross) * wide(own_ref.chunk(i), width)
-        high, low = split(dz)
-        dzh_ref.put(i, high)
-        dzl_ref.put(i, low)
-        gm_ref[z_ref.parts[i]] = product((high, low), (wh_ref[...], wl_ref[...]), NT)
+        gm_ref[z_ref.parts[i]] = product(split(dz), (wh_ref[...], wl_ref[...]), NT)
     gm = gm_ref[...]
     gm_ref.send()
     a = a_ref[...]
@@ -631,12 +644,27 @@
     digit.gather(shares, slopes_ref)
 
 
-def expand_grad_kernel(core, mixed_ref, act_ref, dsum_ref, dzh_ref, dzl_ref, keep_ref, send_ref, excite_ref, term):
+def expand_grad_kernel(core, grads_ref, stat1_ref, stat3_ref, par_ref, mixed_ref, act_ref, dsum_ref, own_ref, grad_ref, z_ref,
+                       keep_ref, send_ref, excite_ref, term):
+    width = z_ref.shape[1]
+    groups = width // 128
+    count = wide(stat1_ref[4:5, :], width)
+    mean, inv = get(stat3_ref, 0, groups), get(stat3_ref, groups, groups)
+    flat = get(grads_ref, 0, groups) / count
+    cross = get(grads_ref, groups, groups) / count
+    scale = get(par_ref, 18, groups) * inv
     left = split(mixed_ref[...].T)
-    rows, width = left[0].shape[0], term.shape[1]
-    for j in range(term.shape[0] // rows):
-        cols = slice(j * width, (j + 1) * width)
-        term[j * rows : (j + 1) * rows, :] = product(left, (dzh_ref[:, cols], dzl_ref[:, cols]), NN)
+    rows, span = left[0].shape[0], term.shape[1]
+    for i, part in enumerate(z_ref.parts):
+        normed = (z_ref.chunk(i) - mean) * inv
+        dz = scale * (grad_ref.chunk(i) - flat - normed * cross) * wide(own_ref.chunk(i), width)
+        right = split(dz)
+        some = [each[:, part.start : part.start + part.size] for each in left]
+        for j in range(term.shape[0] // rows):
+            value = product(some, [each[:, j * span : (j + 1) * span] for each in right], NN)
+            if i:
+                value = value + term[j * rows : (j + 1) * rows, :]
+            term[j * rows : (j + 1) * rows, :] = value
     core.scatter([term], [keep_ref, send_ref])
     excite_ref[...] = exact(act_ref[...], dsum_ref[...], TN)
 
@@ -802,13 +830,13 @@
                 at += each
 
 
-def deal(plan, ins, after=()):
+def deal(plan, ins, **order):
     width = ins[0].shape[1]
     outs = []
     for digit, stretches in plan:
         rows = sum(rows for _, _, rows in stretches) // digit.size
         outs += [((rows, width), f32)] * digit.size
-    return local_call(functools.partial(deal_kernel, plan, len(ins)), outs, ins, after=after)
+    return local_call(functools.partial(deal_kernel, plan, len(ins)), outs, ins, **order)
 
 
 def stack_kernel(stretches, *refs):
@@ -832,22 +860,21 @@
     return extra.send([total] * extra.size)
 
 
-def spread_kernel(count, *refs):
+def stacked_kernel(count, *refs):
     if count == 1:
-        total = jnp.sum(refs[0][...], axis=0)
+        refs[-1][...] = jnp.sum(refs[0][...], axis=0)
     else:
-        total = refs[0][...]
-        for ref in refs[1:-1]:
-            total = total + ref[...]
-    refs[-1][...] = jnp.broadcast_to(total[None], refs[-1].shape)
-
-
-def halve_kernel(blocks, whole_ref, *outs):
-    each = whole_ref.shape[0] // blocks
-    half = each // 2
-    for k in range(blocks):
+        sum_kernel(*refs)
+
+
+def halves_kernel(digit, *refs):
+    pieces, outs = refs[: digit.size], refs[digit.size :]
+    half = pieces[0].shape[0] // 2
+    own = digit.own()
+    for j, piece in enumerate(pieces):
+        at = pl.ds(pl.multiple_of((own ^ j) * half, 8), half)
         for i, out in enumerate(outs):
-            out[k * half : (k + 1) * half, :] = whole_ref[k * each + i * half : k * each + (i + 1) * half, :]
+            out[at, :] = piece[i * half : (i + 1) * half, :]
 
 
 def pair_kernel(digits, *refs):
@@ -928,23 +955,23 @@
     vectors = (gain_one, shift_one, gain_two, shift_two, gain_fc, shift_fc, excite_bias, gain_three, shift_three)
     core, line, depth, extra = digits()
 
-    z_one, ext, own, first, last, wrh, wrl, pay = call(
+    z_one, ext, own, first, last, pay = call(
         reduce_kernel,
         [((cells, mid), f32), ((count, tall + 2, broad, 128), f32), ((cells, 128), f32), ((edge, mid), f32),
-         ((edge, mid), f32), *twice(chan, mid), pay8],
+         ((edge, mid), f32), pay8],
         [valid_rows, valid_cols, w_reduce, x],
         [tile8],
         chunks={3: 2},
-        near_outs=(3, 4, 7),
+        near_outs=(3, 4, 5),
     )
     g1 = share(pay)
     above, below = halos(first, last)
-    wgh, wgl, weh, wel, par = call(
+    wgh, wgl, weh, wel, wrh, wrl, par = call(
         parts_kernel,
-        [*twice(taps, duo), *twice(mid, chan), ((40, 128), f32)],
-        [flat_w, w_expand, *[v.reshape(1, -1) for v in vectors]],
-        chunks={0: 4, 1: 2},
-        out_chunks={0: 4, 1: 4, 2: 2, 3: 2},
+        [*twice(taps, duo), *twice(mid, chan), *twice(chan, mid), ((40, 128), f32)],
+        [flat_w, w_expand, w_reduce, *[v.reshape(1, -1) for v in vectors]],
+        chunks={0: 4, 1: 2, 2: 2},
+        out_chunks={0: 4, 1: 4, 2: 2, 3: 2, 4: 2, 5: 2},
         after=[z_one],
     )
     z_two, a_one, stat1, counts, pay = call(
@@ -974,7 +1001,6 @@
         [stat2, par, valid_rows, valid_cols, own, z_two],
         chunks={4: 2, 5: 2},
         out_chunks={0: 2, 1: 2},
-        near_outs=(2,),
     )
     mixed, z_three, weights, fc_normed, fc_pre, fc_act, fc_inv, pay = call(
         expand_kernel,
@@ -989,37 +1015,36 @@
     )
     g4 = share(pay)
     slopes = line.send([slopes] * line.size)
-    block_out, grad_pre, stat3, slopes, pay = call(
+    grad_pre, stat3, slopes, pay = call(
         output_kernel,
-        [((cells, chan), f32), ((cells, chan), f32), ((16, 128), f32), ((count, 2 * duo), f32), pay16],
+        [((cells, chan), f32), ((16, 128), f32), ((count, 2 * duo), f32), pay16],
         [g4, counts, par, own, z_three, x, cot, *slopes],
         [tile16],
         chunks={3: 4, 4: 4, 5: 4, 6: 4},
-        out_chunks={0: 4, 1: 4},
+        out_chunks={0: 4},
         near=(0, *range(7, 7 + line.size)),
-        near_outs=(3, 4),
+        near_outs=(2, 3),
     )
     g5 = share(pay)
     slopes = depth.send([slopes] * depth.size)
     tph, tpl = call(functools.partial(taps_kernel, count), twice(2, taps, cells), [a_one], out_chunks={0: 2, 1: 2}, after=[stat3])
-    dzh, dzl, grad_mixed, dsum, grads_three, slopes, pay = call(
+    grad_mixed, dsum, grads_three, slopes, pay = call(
         functools.partial(mixed_kernel, depth),
-        [*twice(cells, chan), ((cells, mid), f32), ((count, mid), f32),
+        [((cells, mid), f32), ((count, mid), f32),
          ((16, 128), f32), ((depth.size * count, 2 * duo), f32), pay16],
         [g5, stat1, stat3, par, own, grad_pre, z_three, weh, wel, a_two, weights, w_excite, slope_two, normed_two, *slopes],
         [tile16],
-        chunks={4: 2, 5: 2, 6: 2},
-        out_chunks={0: 2, 1: 2},
         after=[tph],
         near=(0, *range(14, 14 + depth.size)),
-        near_outs=(5, 6),
+        near_outs=(3, 4),
     )
     g6 = share(pay)
     *expand_sum, excite_term = call(
         functools.partial(expand_grad_kernel, core),
         [*core.outs(mid * chan // mid, mid), ((inter, mid), f32)],
-        [mixed, fc_act, dsum, dzh, dzl],
+        [grads_three, stat1, stat3, par, mixed, fc_act, dsum, own, grad_pre, z_three],
         [pltpu.VMEM((chan, mid), f32)],
+        chunks={7: 2, 8: 2, 9: 2},
     )
     if extra.size > 1:
         slopes = gather_more(extra, extra.send([slopes] * extra.size))
@@ -1061,7 +1086,7 @@
         [((cells, mid), f32), pay8],
         [par, stat1, dsum, z_one, own, above, below, dzh, dzl, wgh, wgl],
         [tile8, pltpu.VMEM((count, tall, broad, mid), f32)],
-        after=[keep_a],
+        beside=[keep_a],
         near=(5, 6),
         near_outs=(1,),
     )
@@ -1074,7 +1099,7 @@
         [*core.outs(chan, mid), *twice(cells, mid), ((8, 128), f32)],
         [g7, par, stat1, dy_one, z_one, own, xth, xtl],
         [pltpu.VMEM((chan, mid), f32)],
-        after=[keep_a],
+        beside=[keep_a],
         near=(0,),
         near_outs=(0, 1),
     )
@@ -1085,46 +1110,53 @@
         functools.partial(stack_kernel, stretches),
         [((depth.size, (some + more) * 2 // depth.size, mid), f32)],
         [*come_a, *come_b],
-        after=[dzh],
+        after=[grads_one],
     )
     reduce_sum[1] = gate(reduce_sum[1], [joined])
     joined = depth.trade(joined)
-    low_bit, high_bit = depth.bits()
-    reduce_sum = scatter_more(second_bit, core.send(reduce_sum))
+    reduce_sum = scatter_more(line, core.send(reduce_sum))
     (grad_images,) = call(
         images_kernel,
         [((cells, chan), f32)],
         [dzh, dzl, wrh, wrl, grad_pre],
         chunks={0: 2, 1: 2, 4: 2},
         out_chunks={0: 2},
-        after=[reduce_sum[0]],
-    )
-    reduce_sum = scatter_more(first_bit, second_bit.send(reduce_sum), after=[grad_images])
+        beside=[reduce_sum[0]],
+    )
+    reduce_sum = scatter_more(depth, line.send(reduce_sum), after=[grad_images])
     (joined,) = local_call(
-        functools.partial(spread_kernel, extra.size), [(joined.shape, f32)], extra_pieces(extra, joined), after=[reduce_sum[0]]
-    )
-    joined = depth.trade(joined)
-    reduce_sum = scatter_more(high_bit, first_bit.send(reduce_sum))
-    rows_in = joined.shape[0] * joined.shape[1]
+        functools.partial(stacked_kernel, extra.size), [(joined.shape[1:], f32)], extra_pieces(extra, joined), beside=[reduce_sum[0]]
+    )
+    rows_in = depth.size * joined.shape[0]
+    block_out, mark = call(
+        result_kernel,
+        [((cells, chan), f32), ((8, 128), f32)],
+        [stat3, par, own, z_three, x],
+        chunks={2: 4, 3: 4, 4: 4},
+        out_chunks={0: 4},
+        beside=[joined],
+    )
     half_a, half_b = local_call(
-        functools.partial(halve_kernel, depth.size), [((rows_in // 2, mid), f32)] * 2, [joined.reshape(-1, mid)], after=[reduce_sum[0]]
-    )
-    reduce_sum = scatter_more(low_bit, high_bit.send(reduce_sum), after=[half_a])
+        functools.partial(halves_kernel, depth),
+        [((rows_in // 2, mid), f32)] * 2,
+        depth.send([joined] * depth.size),
+        after=[mark],
+    )
+    reduce_sum = finish_sum(depth.send(reduce_sum), extra, beside=[half_a])
     half_a, half_b = local_call(
         functools.partial(pair_kernel, [second_bit, first_bit]),
         [((rows_in, mid), f32)] * 2,
         [*second_bit.send([half_a] * 2), *first_bit.send([half_b] * 2)],
-        after=[reduce_sum[0]],
-    )
-    reduce_sum = finish_sum(low_bit.send(reduce_sum), extra, after=[half_a])
-    reduce_sum = gather_more(depth, depth.send([reduce_sum] * depth.size))
+        beside=[reduce_sum],
+    )
+    reduce_sum = gather_more(depth, depth.send([reduce_sum] * depth.size), beside=[half_a])
     (joined,) = local_call(
         functools.partial(pair_kernel, [first_bit, second_bit]),
         [((4 * rows_in, mid), f32)],
         [*first_bit.send([half_a] * 2), *second_bit.send([half_b] * 2)],
-        after=[reduce_sum],
-    )
-    reduce_sum = gather_more(line, line.send([reduce_sum] * line.size), after=[joined])
+        beside=[reduce_sum],
+    )
+    reduce_sum = gather_more(line, line.send([reduce_sum] * line.size), beside=[joined])
     expand_map, group_map = [], []
     at = 0
     some, more = some // depth.size, more // depth.size
@@ -1137,13 +1169,16 @@
                         expand_map.append((at, block * some, some))
                         group_map.append((at + some, block * more, more))
                         at += some + more
-    grad_w_expand, grad_w_group, grad_w_excite, grad_w_squeeze = local_call(
+    grad_w_expand, grad_w_group, grad_w_excite, grad_w_squeeze = call(
         functools.partial(last_kernel, core, expand_map, group_map),
         [((mid, chan), f32), ((taps, duo), f32), ((inter, duo), f32), ((mid, inter), f32)],
         core.send([joined] * 2),
         [pltpu.VMEM((chan + packed, mid), f32)],
-    )
-    grad_w_reduce = gather_more(core, core.send([reduce_sum] * 2))
+        near=(0, 1),
+    )
+    (grad_w_reduce,) = call(
+        functools.partial(gather_kernel, core), [((chan, mid), f32)], core.send([reduce_sum] * 2), near=(0, 1)
+    )
     grads_one = grads_one.reshape(-1)
     grads_two = grads_two.reshape(-1)
     grads_three = grads_three.reshape(-1)

time: 238 us -> 229 us (0.962)
  waiting for transfers between devices: 71.2 us -> 57.9 us
  local copies, waits for them, and re-layouts: 11.3 us -> 2.3 us
  Pallas kernels: 80 us -> 86.9 us
  starting transfers between devices: 72.4 us -> 78.9 us
    ppermute x30 -> x35, starting transfers between devices: 30 us -> 40.1 us  [flip(): lax.ppermute(values, axis, [(i, i ^ bits) for i in range(lax.axis_size(ax...]
    all_to_all x2 -> x1, waiting for transfers between devices: 10.8 us -> 1.73 us  [trade(): return lax.all_to_all(stacked, self.axis, 0, 0, axis_index_groups=groups)]
    unnamed x48 -> x12, local copies, waits for them, and re-layouts: 9.01 us -> 0.03 us
    pallas_call x16 -> x19, Pallas kernels: 75.1 us -> 83.3 us  [call(): pl.pallas_call(inner, out_shape=[(pltpu.VMEM if i in near_outs else pltpu...]
    ppermute x30 -> x35, waiting for transfers between devices: 36.8 us -> 32.4 us  [flip(): lax.ppermute(values, axis, [(i, i ^ bits) for i in range(lax.axis_size(ax...]
    all_to_all x2 -> x1, starting transfers between devices: 7.08 us -> 3.73 us  [trade(): return lax.all_to_all(stacked, self.axis, 0, 0, axis_index_groups=groups)]
    pallas_call x18 -> x14, Pallas kernels: 4.91 us -> 3.53 us  [the longest x12 2.48 us: local_call(): pl.pallas_call(inner, out_shape=[pltpu.VMEM(*out) for out in outs], in_sp...]
  transfers between devices with their start and end apart: 43 -> 47, of which waited for: 27 -> 28; matrix products, arithmetic and copies ran while one was open for 1% -> 1% of each run, Pallas kernels for 17% -> 21%
where the time goes in v4:
time: 229 us; the launch traced here: 228 us
  Pallas kernels  86.9 us (38%)
  starting transfers between devices  78.9 us (34%)
  waiting for transfers between devices  57.9 us (25%)
  local copies, waits for them, and re-layouts  2.3 us (1%)
    pallas_call x19, Pallas kernels, call(): pl.pallas_call(inner, out_shape=[(pltpu.VMEM if i in near_outs else pltpu...  83.3 us
    ppermute x35, starting transfers between devices, flip(): lax.ppermute(values, axis, [(i, i ^ bits) for i in range(lax.axis_size(ax...  40.1 us
    ppermute x35, waiting for transfers between devices, flip(): lax.ppermute(values, axis, [(i, i ^ bits) for i in range(lax.axis_size(ax...  32.4 us
    all_to_all x7, starting transfers between devices, share(): return lax.all_to_all(tile, both, 0, 0)  26.2 us
    all_to_all x7, waiting for transfers between devices, share(): return lax.all_to_all(tile, both, 0, 0)  21.1 us
    ppermute x2, starting transfers between devices, halos(): above = lax.ppermute(last, 'rows', [(i, i + 1) for i in range(count - 1)])  6.09 us
  transfers between devices with their start and end apart: 47, of which 28 were waited for; matrix products, arithmetic and copies ran while one was open for 1% of the time, Pallas kernels for 21%

profile of v4, /device:TPU:0, one launch (start us, length us, event | category | flops | bytes accessed | tf_op | source)
XLA Modules:
  0.0 227.9 jit_solution(11417696018709922685)
XLA Ops:
  0.6 5.2 %shard_map.297 = (f32[512,256]{1,0:T(8,128)}, f32[8,6,16,128]{3,2,1,0:T(8,128)}, f32[512,128]{1,0:T(8,128)}, f32[128,256]{1,0:T(8,128)S(1)}, f32[128,256]{1,0:T(8,128)S(1)}, /*index=5*/f32[32,8,128]{2,1,0:T(8,128)}) custom-call(s32[8,16]{1,0:T(8,128)} %refs_9_.1, s32[8,16]{1,0:T(8,128)} %refs_10_.1, f32[1024,256]{1,0:T(8,128)} %refs_2_.5, f32[512,1024]{1,0:T(8,128)} %bitcast.35), custom_call_target="tpu_custom_call" | custom-call | flops 1 | bytes 1 | tf_op jit(solution)/shard_map/pallas_call | solution.py:205
  5.9 7.3 %all-to-all-start = ((f32[32,8,128]{2,1,0:T(8,128)}), f32[32,8,128]{2,1,0:T(8,128)S(1)}, u32[]{:S(2)}, u32[]{:S(2)}) async-start(f32[32,8,128]{2,1,0:T(8,128)} %get-tuple-element.107), calls=%async_computation | async-start | bytes 262144 | tf_op jit(solution)/shard_map/all_to_all | solution.py:248
  13.2 3.7 %collective-permute-start = (f32[128,256]{1,0:T(8,128)S(1)}, f32[128,256]{1,0:T(8,128)S(1)}, u32[]{:S(2)}, u32[]{:S(2)}) collective-permute-start(f32[128,256]{1,0:T(8,128)S(1)} %get-tuple-element.111), channel_id=1, source_target_pairs={{0,8},{8,16},{16,24},{1,9},{9,17},{17,25},{2,10},{10,18},{18,26},{... | collective-permute-start | bytes 393224 | tf_op jit(solution)/shard_map/ppermute | solution.py:253
  18.2 4.5 %shard_map.298 = (bf16[1152,512]{1,0:T(8,128)(2,1)}, bf16[1152,512]{1,0:T(8,128)(2,1)}, bf16[256,1024]{1,0:T(8,128)(2,1)}, bf16[256,1024]{1,0:T(8,128)(2,1)}, bf...) custom-call(f32[1152,512]{1,0:T(8,128)} %bitcast.40, f32[256,1024]{1,0:T(8,128)} %refs_1_.3, ...), custom_call_target="tpu_custom_call" | custom-call | flops 1 | bytes 1 | tf_op jit(solution)/shard_map/pallas_call | solution.py:205
  25.1 5.9 %shard_map.299 = (f32[512,512]{1,0:T(8,128)}, f32[768,256]{1,0:T(8,128)}, f32[8,128]{1,0:T(8,128)}, f32[32,128]{1,0:T(8,128)}, f32[32,8,128]{2,1,0:T(8,128)}) custom-call(f32[32,8,128]{2,1,0:T(8,128)S(1)} %all-to-all-done.refs_0_, f32[40,128]{1,0:T(8,128)} %get-tuple-element.109.refs_1_.refs_2_.refs_3_.refs_4_.refs_0_, ...), custom_call_target="tpu_custom_call" | custom-call | flops 1 | bytes 1 | tf_op jit(solution)/shard_map/pallas_call | solution.py:205
  31.0 4.5 %all-to-all-start.1 = ((f32[32,8,128]{2,1,0:T(8,128)}), f32[32,8,128]{2,1,0:T(8,128)S(1)}, u32[]{:S(2)}, u32[]{:S(2)}) async-start(f32[32,8,128]{2,1,0:T(8,128)} %get-tuple-element.116), calls=%async_computation.1 | async-start | bytes 262144 | tf_op jit(solution)/shard_map/all_to_all | solution.py:248
  35.5 3.5 %shard_map.300 = (bf16[1024,512]{1,0:T(8,128)(2,1)}, bf16[1024,512]{1,0:T(8,128)(2,1)}) custom-call(f32[512,1024]{1,0:T(8,128)} %bitcast.36, f32[8,128]{1,0:T(8,128)} %get-tuple-element.119.refs_1_.refs_7_.refs_2_), custom_call_target="tpu_custom_call" | custom-call | flops 1 | bytes 1 | tf_op jit(solution)/shard_map/pallas_call | solution.py:205
  39.0 4.6 %all-to-all-done.1.refs_0_ = f32[32,8,128]{2,1,0:T(8,128)S(1)} async-done(((f32[32,8,128]{2,1,0:T(8,128)}), f32[32,8,128]{2,1,0:T(8,128)S(1)}, u32[]{:S(2)}, u32[]{:S(2)}) %all-to-all-start.1) | async-done | bytes 131104 | tf_op jit(solution)/shard_map/all_to_all | solution.py:248
  52.2 5.2 %all-to-all-done.2.refs_0_ = f32[32,8,128]{2,1,0:T(8,128)S(1)} async-done(((f32[32,8,128]{2,1,0:T(8,128)}), f32[32,8,128]{2,1,0:T(8,128)S(1)}, u32[]{:S(2)}, u32[]{:S(2)}) %all-to-all-start.2) | async-done | bytes 131104 | tf_op jit(solution)/shard_map/all_to_all | solution.py:248
  57.5 4.4 %shard_map.303 = (f32[512,256]{1,0:T(8,128)}, f32[512,1024]{1,0:T(8,128)}, f32[8,512]{1,0:T(8,128)}, f32[64,128]{1,0:T(8,128)}, f32[64,128]{1,0:T(8,128)}, /*ind...) custom-call(f32[32,8,128]{2,1,0:T(8,128)S(1)} %all-to-all-done.2.refs_0_, ...), custom_call_target="tpu_custom_call" | custom-call | flops 1 | bytes 1 | tf_op jit(solution)/shard_map/pallas_call | solution.py:205
  74.9 5.8 %shard_map.304 = (f32[512,1024]{1,0:T(8,128)}, f32[16,128]{1,0:T(8,128)}, f32[8,1024]{1,0:T(8,128)S(1)}, f32[32,16,128]{2,1,0:T(8,128)}) custom-call(f32[32,16,128]{2,1,0:T(8,128)S(1)} %all-to-all-done.3.refs_0_, f32[32,128]{1,0:T(8,128)} %get-tuple-element.117.refs_1_, f32[40,128]{1,0:T(8,128)} %get-tuple-element.109.refs_1_.refs_2_.refs_3_.refs_4_.refs_0_, ...), custom_call_target="tpu_custom_call" | custom-call | flops 1 | bytes 1 | tf_op jit(solution)/shard_map/pallas_call | solution.py:205
  83.3 3.7 %collective-permute-start.7 = (f32[8,1024]{1,0:T(8,128)S(1)}, f32[8,1024]{1,0:T(8,128)S(1)}, u32[]{:S(2)}, u32[]{:S(2)}) collective-permute-start(f32[8,1024]{1,0:T(8,128)S(1)} %get-tuple-element.135.refs_14_), channel_id=1, source_target_pairs={{0,6},{1,7},{2,4},{3,5},{4,2},{5,3},{6,0},{7,1},{8,14},{9,15},{10,... | collective-permute-start | bytes 98312 | tf_op jit(solution)/shard_map/ppermute | solution.py:259
  87.8 4.0 %shard_map.305 = (bf16[2,1152,512]{2,1,0:T(8,128)(2,1)}, bf16[2,1152,512]{2,1,0:T(8,128)(2,1)}) custom-call(f32[768,256]{1,0:T(8,128)} %get-tuple-element.136.refs_0_, f32[16,128]{1,0:T(8,128)} %get-tuple-element.129.refs_1_.refs_2_.refs_0_), custom_call_target="tpu_custom_call" | custom-call | flops 1 | bytes 1 | tf_op jit(solution)/shard_map/pallas_call | solution.py:205
  95.5 7.1 %shard_map.306 = (f32[512,256]{1,0:T(8,128)}, f32[8,256]{1,0:T(8,128)}, f32[16,128]{1,0:T(8,128)}, f32[32,1024]{1,0:T(8,128)S(1)}, f32[32,16,128]{2,1,0:T(8,128)}) custom-call(f32[32,16,128]{2,1,0:T(8,128)S(1)} %all-to-all-done.4.refs_0_, f32[8,128]{1,0:T(8,128)} %get-tuple-element.119.refs_1_.refs_7_.refs_2_, ...), custom_call_target="tpu_custom_call" | custom-call | flops 1 | bytes 1 | tf_op jit(solution)/shard_map/pallas_call | solution.py:205
  102.6 3.5 %all-to-all-start.5 = ((f32[32,16,128]{2,1,0:T(8,128)}), f32[32,16,128]{2,1,0:T(8,128)S(1)}, u32[]{:S(2)}, u32[]{:S(2)}) async-start(f32[32,16,128]{2,1,0:T(8,128)} %get-tuple-element.144), calls=%async_computation.5 | async-start | bytes 524288 | tf_op jit(solution)/shard_map/all_to_all | solution.py:248
  106.5 5.2 %shard_map.307 = (f32[512,256]{1,0:T(8,128)}, f32[512,256]{1,0:T(8,128)}, f32[128,256]{1,0:T(8,128)}) custom-call(f32[16,128]{1,0:T(8,128)} %get-tuple-element.138.refs_0_, f32[8,128]{1,0:T(8,128)} %get-tuple-element.119.refs_1_.refs_7_.refs_2_, f32[16,128]{1,0:T(8,128)} %get-tuple-element.129.refs_1_.refs_2_.refs_0_, ...), custom_call_target="tpu_custom_call" | custom-call | flops 1 | bytes 1 | tf_op jit(solution)/shard_map/pallas_call | solution.py:205
  111.7 4.8 %all-to-all-done.5.refs_0_ = f32[32,16,128]{2,1,0:T(8,128)S(1)} async-done(((f32[32,16,128]{2,1,0:T(8,128)}), f32[32,16,128]{2,1,0:T(8,128)S(1)}, u32[]{:S(2)}, u32[]{:S(2)}) %all-to-all-start.5) | async-done | bytes 262176 | tf_op jit(solution)/shard_map/all_to_all | solution.py:248
  116.5 4.0 %shard_map.308 = (f32[128,256]{1,0:T(8,128)S(1)}, f32[128,256]{1,0:T(8,128)S(1)}, bf16[8,6,16,512]{3,2,1,0:T(8,128)(2,1)}, bf16[8,6,16,512]{3,2,1,0:T(8,128)(2,1...) custom-call(f32[32,16,128]{2,1,0:T(8,128)S(1)} %all-to-all-done.5.refs_0_, ...), custom_call_target="tpu_custom_call" | custom-call | flops 1 | bytes 1 | tf_op jit(solution)/shard_map/pallas_call | solution.py:205
  124.5 6.5 %shard_map.309 = (f32[1280,256]{1,0:T(8,128)S(1)}, f32[1280,256]{1,0:T(8,128)S(1)}) custom-call(bf16[8,6,16,512]{3,2,1,0:T(8,128)(2,1)} %get-tuple-element.152.refs_0_.refs_7_, bf16[8,6,16,512]{3,2,1,0:T(8,128)(2,1)} %get-tuple-element.153.refs_1_.refs_8_, f32[128,256]{1,0:T(8,128)} %get-tuple-element.154.refs_2_, ...), custom_call_target="tpu_custom_call" | custom-call | flops 1 | bytes 1 | tf_op jit(solution)/shard_map/pallas_call | solution.py:205
  139.8 6.9 %shard_map.312 = (f32[512,256]{1,0:T(8,128)}, f32[32,8,128]{2,1,0:T(8,128)}) custom-call(f32[40,128]{1,0:T(8,128)} %get-tuple-element.109.refs_1_.refs_2_.refs_3_.refs_4_.refs_0_, f32[8,128]{1,0:T(8,128)} %get-tuple-element.119.refs_1_.refs_7_.refs_2_, f32[8,256]{1,0:T(8,128)} %get-tuple-element.141.refs_6_.refs_2_, ...), custom_call_target="tpu_custom_call" | custom-call | flops 1 | bytes 1 | tf_op jit(solution)/shard_map/pallas_call | solution.py:205
  161.7 3.7 %all-to-all-start.7 = ((f32[4,112,256]{2,1,0:T(8,128)}), f32[4,112,256]{2,1,0:T(8,128)S(1)}, u32[]{:S(2)}, u32[]{:S(2)}) async-start(f32[4,112,256]{2,1,0:T(8,128)} %shard_map.315.refs_1_), calls=%async_computation.7 | async-start | bytes 917504 | tf_op jit(solution)/shard_map/all_to_all | solution.py:280
  172.2 4.2 %shard_map.318.refs_4_ = f32[512,1024]{1,0:T(8,128)} custom-call(bf16[512,256]{1,0:T(8,128)(2,1)} %get-tuple-element.178.refs_0_, bf16[512,256]{1,0:T(8,128)(2,1)} %get-tuple-element.179.refs_1_, bf16[1024,256]{1,0:T(8,128)(2,1)} %get-tuple-element.180.refs_2_, bf16[1024,256]{1,0:T(8,128)(2,1)} %get-tuple-element.181.refs_3_, ...), custom_call_target="tpu_custom_call" | custom-call | flops 1 | bytes 1 | tf_op jit(solution)/shard_map/pallas_call | solution.py:205
  183.7 3.7 %shard_map.321 = (f32[512,1024]{1,0:T(8,128)}, f32[8,128]{1,0:T(8,128)}) custom-call(f32[16,128]{1,0:T(8,128)} %get-tuple-element.129.refs_1_.refs_2_.refs_0_, f32[40,128]{1,0:T(8,128)} %get-tuple-element.109.refs_1_.refs_2_.refs_3_.refs_4_.refs_0_, f32[512,128]{1,0:T(8,128)} %get-tuple-element.113.refs_6_.refs_4_.refs_3_.refs_7_.refs_14_.refs_5_.refs_2_, ...), custom_call_target="tpu_custom_call" | custom-call | flops 1 | bytes 1 | tf_op jit(solution)/shard_map/pallas_call | solution.py:205
  197.7 3.8 %collective-permute-done.23.refs_3_ = f32[32,256]{1,0:T(8,128)S(1)} collective-permute-done((f32[32,256]{1,0:T(8,128)S(1)}, f32[32,256]{1,0:T(8,128)S(1)}, u32[]{:S(2)}, u32[]{:S(2)}) %collective-permute-start.23) | collective-permute-done | bytes 32800 | tf_op jit(solution)/shard_map/ppermute | solution.py:259
  (121 shorter events, 110.7 us)
Async XLA Ops:
  5.9 19.2 %all-to-all-start = ((f32[32,8,128]{2,1,0:T(8,128)}), f32[32,8,128]{2,1,0:T(8,128)S(1)}, u32[]{:S(2)}, u32[]{:S(2)}) async-start(f32[32,8,128]{2,1,0:T(8,128)} %get-tuple-element.107), calls=%async_computation | async-start | bytes 262144 | tf_op jit(solution)/shard_map/all_to_all | solution.py:248
  13.2 9.5 %collective-permute-start = (f32[128,256]{1,0:T(8,128)S(1)}, f32[128,256]{1,0:T(8,128)S(1)}, u32[]{:S(2)}, u32[]{:S(2)}) collective-permute-start(f32[128,256]{1,0:T(8,128)S(1)} %get-tuple-element.111), channel_id=1, source_target_pairs={{0,8},{8,16},{16,24},{1,9},{9,17},{17,25},{2,10},{10,18},{18,26},{... | collective-permute-start | bytes 393224 | tf_op jit(solution)/shard_map/ppermute | solution.py:253
  31.0 12.6 %all-to-all-start.1 = ((f32[32,8,128]{2,1,0:T(8,128)}), f32[32,8,128]{2,1,0:T(8,128)S(1)}, u32[]{:S(2)}, u32[]{:S(2)}) async-start(f32[32,8,128]{2,1,0:T(8,128)} %get-tuple-element.116), calls=%async_computation.1 | async-start | bytes 262144 | tf_op jit(solution)/shard_map/all_to_all | solution.py:248
  46.7 10.8 %all-to-all-start.2 = ((f32[32,8,128]{2,1,0:T(8,128)}), f32[32,8,128]{2,1,0:T(8,128)S(1)}, u32[]{:S(2)}, u32[]{:S(2)}) async-start(f32[32,8,128]{2,1,0:T(8,128)} %get-tuple-element.121), calls=%async_computation.2 | async-start | bytes 262144 | tf_op jit(solution)/shard_map/all_to_all | solution.py:248
  61.9 13.0 %all-to-all-start.3 = ((f32[32,16,128]{2,1,0:T(8,128)}), f32[32,16,128]{2,1,0:T(8,128)S(1)}, u32[]{:S(2)}, u32[]{:S(2)}) async-start(f32[32,16,128]{2,1,0:T(8,128)} %get-tuple-element.127), calls=%async_computation.3 | async-start | bytes 524288 | tf_op jit(solution)/shard_map/all_to_all | solution.py:248
  80.7 14.8 %all-to-all-start.4 = ((f32[32,16,128]{2,1,0:T(8,128)}), f32[32,16,128]{2,1,0:T(8,128)S(1)}, u32[]{:S(2)}, u32[]{:S(2)}) async-start(f32[32,16,128]{2,1,0:T(8,128)} %get-tuple-element.130), calls=%async_computation.4 | async-start | bytes 524288 | tf_op jit(solution)/shard_map/all_to_all | solution.py:248
  83.3 10.1 %collective-permute-start.7 = (f32[8,1024]{1,0:T(8,128)S(1)}, f32[8,1024]{1,0:T(8,128)S(1)}, u32[]{:S(2)}, u32[]{:S(2)}) collective-permute-start(f32[8,1024]{1,0:T(8,128)S(1)} %get-tuple-element.135.refs_14_), channel_id=1, source_target_pairs={{0,6},{1,7},{2,4},{3,5},{4,2},{5,3},{6,0},{7,1},{8,14},{9,15},{10,... | collective-permute-start | bytes 98312 | tf_op jit(solution)/shard_map/ppermute | solution.py:259
  87.0 8.5 %collective-permute-start.6 = (f32[8,1024]{1,0:T(8,128)S(1)}, f32[8,1024]{1,0:T(8,128)S(1)}, u32[]{:S(2)}, u32[]{:S(2)}) collective-permute-start(f32[8,1024]{1,0:T(8,128)S(1)} %get-tuple-element.135.refs_14_), channel_id=1, source_target_pairs={{0,4},{1,5},{2,6},{3,7},{4,0},{5,1},{6,2},{7,3},{8,12},{9,13},{10,... | collective-permute-start | bytes 98312 | tf_op jit(solution)/shard_map/ppermute | solution.py:259
  87.0 8.5 %collective-permute-start.5 = (f32[8,1024]{1,0:T(8,128)S(1)}, f32[8,1024]{1,0:T(8,128)S(1)}, u32[]{:S(2)}, u32[]{:S(2)}) collective-permute-start(f32[8,1024]{1,0:T(8,128)S(1)} %get-tuple-element.135.refs_14_), channel_id=1, source_target_pairs={{0,2},{1,3},{2,0},{3,1},{4,6},{5,7},{6,4},{7,5},{8,10},{9,11},{10,... | collective-permute-start | bytes 98312 | tf_op jit(solution)/shard_map/ppermute | solution.py:259
  102.6 13.9 %all-to-all-start.5 = ((f32[32,16,128]{2,1,0:T(8,128)}), f32[32,16,128]{2,1,0:T(8,128)S(1)}, u32[]{:S(2)}, u32[]{:S(2)}) async-start(f32[32,16,128]{2,1,0:T(8,128)} %get-tuple-element.144), calls=%async_computation.5 | async-start | bytes 524288 | tf_op jit(solution)/shard_map/all_to_all | solution.py:248
  120.5 10.5 %collective-permute-start.10 = (f32[128,256]{1,0:T(8,128)S(1)}, f32[128,256]{1,0:T(8,128)S(1)}, u32[]{:S(2)}, u32[]{:S(2)}) collective-permute-start(f32[128,256]{1,0:T(8,128)S(1)} %get-tuple-element.158), channel_id=1, source_target_pairs={{0,8},{8,16},{16,24},{1,9},{9,17},{17,25},{2,10},{10,18},{18,26},{... | collective-permute-start | bytes 393224 | tf_op jit(solution)/shard_map/ppermute | solution.py:253
  123.0 8.3 %collective-permute-start.11 = (f32[128,256]{1,0:T(8,128)S(1)}, f32[128,256]{1,0:T(8,128)S(1)}, u32[]{:S(2)}, u32[]{:S(2)}) collective-permute-start(f32[128,256]{1,0:T(8,128)S(1)} %get-tuple-element.159), channel_id=1, source_target_pairs={{8,0},{16,8},{24,16},{9,1},{17,9},{25,17},{10,2},{18,10},{26,18},{... | collective-permute-start | bytes 393224 | tf_op jit(solution)/shard_map/ppermute | solution.py:254
  136.4 13.5 %collective-permute-start.13 = (f32[448,256]{1,0:T(8,128)}, f32[448,256]{1,0:T(8,128)S(1)}, u32[]{:S(2)}, u32[]{:S(2)}) collective-permute-start(f32[448,256]{1,0:T(8,128)} %get-tuple-element.161), channel_id=1, source_target_pairs={{0,8},{8,0},{16,24},{24,16},{1,9},{9,1},{17,25},{25,17},{2,10},{10... | collective-permute-start | bytes 1376264 | tf_op jit(solution)/shard_map/ppermute | solution.py:259
  138.9 12.5 %collective-permute-start.14 = (f32[448,256]{1,0:T(8,128)}, f32[448,256]{1,0:T(8,128)S(1)}, u32[]{:S(2)}, u32[]{:S(2)}) collective-permute-start(f32[448,256]{1,0:T(8,128)} %get-tuple-element.163), channel_id=1, source_target_pairs={{0,16},{8,24},{16,0},{24,8},{1,17},{9,25},{17,1},{25,9},{2,18},{10... | collective-permute-start | bytes 1376264 | tf_op jit(solution)/shard_map/ppermute | solution.py:259
  146.7 11.1 %all-to-all-start.6 = ((f32[32,8,128]{2,1,0:T(8,128)}), f32[32,8,128]{2,1,0:T(8,128)S(1)}, u32[]{:S(2)}, u32[]{:S(2)}) async-start(f32[32,8,128]{2,1,0:T(8,128)} %get-tuple-element.169), calls=%async_computation.6 | async-start | bytes 262144 | tf_op jit(solution)/shard_map/all_to_all | solution.py:248
  151.5 9.4 %collective-permute-start.15 = (f32[224,256]{1,0:T(8,128)S(1)}, f32[224,256]{1,0:T(8,128)S(1)}, u32[]{:S(2)}, u32[]{:S(2)}) collective-permute-start(f32[224,256]{1,0:T(8,128)S(1)} %get-tuple-element.166), channel_id=1, source_target_pairs={{0,16},{8,24},{16,0},{24,8},{1,17},{9,25},{17,1},{25,9},{2,18},{10... | collective-permute-start | bytes 688136 | tf_op jit(solution)/shard_map/ppermute | solution.py:259
  161.7 17.5 %all-to-all-start.7 = ((f32[4,112,256]{2,1,0:T(8,128)}), f32[4,112,256]{2,1,0:T(8,128)S(1)}, u32[]{:S(2)}, u32[]{:S(2)}) async-start(f32[4,112,256]{2,1,0:T(8,128)} %shard_map.315.refs_1_), calls=%async_computation.7 | async-start | bytes 917504 | tf_op jit(solution)/shard_map/all_to_all | solution.py:280
  181.1 9.8 %collective-permute-start.25 = (f32[112,256]{1,0:T(8,128)S(1)}, f32[112,256]{1,0:T(8,128)S(1)}, u32[]{:S(2)}, u32[]{:S(2)}) collective-permute-start(f32[112,256]{1,0:T(8,128)S(1)} %shard_map.320.refs_5_.refs_0_), channel_id=1, source_target_pairs={{0,4},{1,5},{2,6},{3,7},{4,0},{5,1},{6,2},{7,3},{8,12},{9,13},{10,... | collective-permute-start | bytes 344072 | tf_op jit(solution)/shard_map/ppermute | solution.py:259
  181.1 9.8 %collective-permute-start.24 = (f32[112,256]{1,0:T(8,128)S(1)}, f32[112,256]{1,0:T(8,128)S(1)}, u32[]{:S(2)}, u32[]{:S(2)}) collective-permute-start(f32[112,256]{1,0:T(8,128)S(1)} %shard_map.320.refs_5_.refs_0_), channel_id=1, source_target_pairs={{0,2},{1,3},{2,0},{3,1},{4,6},{5,7},{6,4},{7,5},{8,10},{9,11},{10,... | collective-permute-start | bytes 344072 | tf_op jit(solution)/shard_map/ppermute | solution.py:259
  190.9 10.6 %collective-permute-start.31 = (f32[224,256]{1,0:T(8,128)S(1)}, f32[224,256]{1,0:T(8,128)S(1)}, u32[]{:S(2)}, u32[]{:S(2)}) collective-permute-start(f32[224,256]{1,0:T(8,128)S(1)} %get-tuple-element.189.refs_2_), channel_id=1, source_target_pairs={{0,8},{8,0},{16,24},{24,16},{1,9},{9,1},{17,25},{25,17},{2,10},{10... | collective-permute-start | bytes 688136 | tf_op jit(solution)/shard_map/ppermute | solution.py:259
  191.5 10.1 %collective-permute-start.30 = (f32[224,256]{1,0:T(8,128)S(1)}, f32[224,256]{1,0:T(8,128)S(1)}, u32[]{:S(2)}, u32[]{:S(2)}) collective-permute-start(f32[224,256]{1,0:T(8,128)S(1)} %get-tuple-element.188.refs_4_.refs_0_), channel_id=1, source_target_pairs={{0,16},{8,24},{16,0},{24,8},{1,17},{9,25},{17,1},{25,9},{2,18},{10... | collective-permute-start | bytes 688136 | tf_op jit(solution)/shard_map/ppermute | solution.py:259
  201.7 8.9 %collective-permute-start.36 = (f32[448,256]{1,0:T(8,128)S(1)}, f32[448,256]{1,0:T(8,128)S(1)}, u32[]{:S(2)}, u32[]{:S(2)}) collective-permute-start(f32[448,256]{1,0:T(8,128)S(1)} %get-tuple-element.191.refs_2_), channel_id=1, source_target_pairs={{0,16},{8,24},{16,0},{24,8},{1,17},{9,25},{17,1},{25,9},{2,18},{10... | collective-permute-start | bytes 1376264 | tf_op jit(solution)/shard_map/ppermute | solution.py:259
  202.4 8.9 %collective-permute-start.35 = (f32[448,256]{1,0:T(8,128)S(1)}, f32[448,256]{1,0:T(8,128)S(1)}, u32[]{:S(2)}, u32[]{:S(2)}) collective-permute-start(f32[448,256]{1,0:T(8,128)S(1)} %get-tuple-element.190.refs_4_.refs_0_), channel_id=1, source_target_pairs={{0,8},{8,0},{16,24},{24,16},{1,9},{9,1},{17,25},{25,17},{2,10},{10... | collective-permute-start | bytes 1376264 | tf_op jit(solution)/shard_map/ppermute | solution.py:259
  211.5 14.0 %collective-permute-start.38 = (f32[1792,256]{1,0:T(8,128)S(1)}, f32[1792,256]{1,0:T(8,128)S(1)}, u32[]{:S(2)}, u32[]{:S(2)}) collective-permute-start(f32[1792,256]{1,0:T(8,128)S(1)} %shard_map.326.refs_4_.refs_0_), channel_id=1, source_target_pairs={{0,1},{1,0},{2,3},{3,2},{4,5},{5,4},{6,7},{7,6},{8,9},{9,8},{10,11... | collective-permute-start | bytes 5505032 | tf_op jit(solution)/shard_map/ppermute | solution.py:259
  (29 other events, 191.5 us)

commit v5 on v4

--- a/solution.py
+++ b/solution.py
@@ -389,12 +389,17 @@
 
 
 def parts_kernel(wg_ref, we_ref, wr_ref, *refs):
-    vectors, (wgh_ref, wgl_ref, weh_ref, wel_ref, wrh_ref, wrl_ref, par_ref) = refs[:-7], refs[-7:]
+    vectors, wg_refs, (weh_ref, wel_ref, wrh_ref, wrl_ref, par_ref) = refs[:-9], refs[-9:-5], refs[-5:]
     row = 0
     for vector in vectors:
         put(par_ref, row, vector[...])
         row += vector.shape[1] // 128
-    for source, high_ref, low_ref in ((wg_ref, wgh_ref, wgl_ref), (we_ref, weh_ref, wel_ref), (wr_ref, wrh_ref, wrl_ref)):
+    half = wg_ref.shape[1] // 2
+    for i in range(len(wg_ref.parts)):
+        for j, part in enumerate(split(wg_ref.chunk(i))):
+            for g in range(2):
+                wg_refs[2 * g + j].put(i, part[:, g * half : (g + 1) * half])
+    for source, high_ref, low_ref in ((we_ref, weh_ref, wel_ref), (wr_ref, wrh_ref, wrl_ref)):
         for i in range(len(source.parts)):
             high, low = split(source.chunk(i))
             high_ref.put(i, high)
@@ -429,7 +434,7 @@
     return place[...].reshape(-1, width)
 
 
-def conv_kernel(g1_ref, par_ref, z_ref, ext_ref, above_ref, below_ref, own_ref, wh_ref, wl_ref,
+def conv_kernel(g1_ref, par_ref, z_ref, ext_ref, above_ref, below_ref, own_ref, first_high, first_low, second_high, second_low,
                 z2_ref, a_ref, stat_ref, counts_ref, pay_ref, tile, zext):
     images = zext.shape[0]
     tall = zext.shape[1] - 2
@@ -450,6 +455,8 @@
     a_ref.send()
     shifted = [split(moved(a, step)) for step in (-1, 0, 1)]
     half = z2_ref.shape[1] // 2
+    for ref in (first_high, first_low, second_high, second_low):
+        ref.ready()
     for g in range(2):
         cols = slice(g * group, (g + 1) * group)
         left = [
@@ -459,7 +466,8 @@
             for part in range(2)
         ]
         outs = slice(g * half, (g + 1) * half)
-        z2_ref[:, outs] = product(left, (wh_ref[:, outs], wl_ref[:, outs]), NN)
+        right = [ref[...] for ref in ((first_high, first_low), (second_high, second_low))[g]]
+        z2_ref[:, outs] = product(left, right, NN)
     z2_ref.send()
     z2 = z2_ref[...]
     own = own_ref[...]
@@ -613,12 +621,14 @@
 
 def mixed_kernel(digit, g5_ref, stat1_ref, stat3_ref, par_ref, own_ref, grad_ref, z_ref, wh_ref, wl_ref, a_ref, weights_ref,
                  w_ref, slope_ref, normed_ref, *refs):
-    shares, (gm_ref, dsum_ref, grads_ref, slopes_ref, pay_ref, tile) = refs[: digit.size], refs[digit.size :]
+    shares, (gm_ref, dsum_ref, grads_ref, gain_ref, shift_ref, slopes_ref, pay_ref, tile) = refs[: digit.size], refs[digit.size :]
     width = z_ref.shape[1]
     mid = gm_ref.shape[1]
     images = weights_ref.shape[0]
     groups = width // 128
     grads_ref[...] = jnp.sum(g5_ref[...], axis=0)
+    shift_ref[...] = grads_ref[:groups, :]
+    gain_ref[...] = grads_ref[groups:, :]
     count = wide(stat1_ref[4:5, :], width)
     mean, inv = get(stat3_ref, 0, groups), get(stat3_ref, groups, groups)
     flat = get(grads_ref, 0, groups) / count
@@ -669,8 +679,8 @@
     excite_ref[...] = exact(act_ref[...], dsum_ref[...], TN)
 
 
-def turned_rows(left, wh_ref, wl_ref, outs, row, taps):
-    return product(left, [ref[row * taps : (row + 1) * taps, outs] for ref in (wh_ref, wl_ref)], NT)
+def turned_rows(left, refs, row, taps):
+    return product(left, [ref[row * taps : (row + 1) * taps, :] for ref in refs], NT)
 
 
 def fold(total, group):
@@ -678,10 +688,12 @@
 
 
 def back_kernel(digit, g6_ref, pre_ref, fcn_ref, inv_ref, par_ref, wsq_ref, pooled_ref, stat1_ref, stat2_ref, rows_ref,
-                cols_ref, weights_ref, mine_ref, other_ref, own_ref, gm_ref, slope_ref, normed_ref, wh_ref, wl_ref,
-                up_ref, down_ref, dzh_ref, dzl_ref, squeeze_ref, gains_ref, fc_ref, gf, owned, slopes):
+                cols_ref, weights_ref, mine_ref, other_ref, own_ref, gm_ref, slope_ref, normed_ref, *refs):
+    w_refs, (up_ref, down_ref), dz_refs, (squeeze_ref, gain_ref, flat_ref, fc_gain_ref, fc_flat_ref, gf, owned, slopes) = (
+        refs[:4], refs[4:6], refs[6:10], refs[10:]
+    )
     images = rows_ref.shape[0]
-    tall = dzh_ref.shape[1] - 2
+    tall = dz_refs[0].shape[1] - 2
     width = normed_ref.shape[1]
     mid = width // 2
     groups = width // 128
@@ -693,8 +705,8 @@
     total = pre.shape[0]
     grad = jnp.sum(shared[:, :images].reshape(rows, total, -1), axis=0) * (sigma * (1.0 + pre * (1.0 - sigma)))
     flat, cross = column_sum(grad), column_sum(grad * fcn)
-    fc_ref[0:1, :] = cross
-    fc_ref[1:2, :] = flat
+    fc_gain_ref[...] = cross
+    fc_flat_ref[...] = flat
     gf[...] = par_ref[12:13, :] * inv_ref[...] * (grad - flat / total - fcn * cross / total)
     at = pl.multiple_of(lax.axis_index("batch") * images, images)
     mine = gf[pl.ds(at, images), :]
@@ -715,8 +727,8 @@
     gm = gm_ref[...]
     shared_part = per_image(own_spread, gm)
     mask = wide(own_ref[...], mid)
-    zero = jnp.zeros((images, 16, width), bf16)
-    for ref in (dzh_ref, dzl_ref):
+    zero = jnp.zeros((images, 16, mid), bf16)
+    for ref in dz_refs:
         ref[:, 0] = zero
         ref[:, tall + 1] = zero
     for g in range(2):
@@ -725,31 +737,28 @@
         half = groups // 2
         flat_two = get(base, g * half, half) + column_sum(spread * slopes[:, outs])
         cross_two = get(base, groups + g * half, half) + column_sum(spread * slopes[:, crosses])
-        put(gains_ref, g * half, cross_two)
-        put(gains_ref, groups + g * half, flat_two)
+        put(gain_ref, g * half, cross_two)
+        put(flat_ref, g * half, flat_two)
         scale = get(par_ref, 4 + g * half, half) * get(stat2_ref, groups + g * half, half)
         upstream = per_image(weights[:, outs], gm) * gm + shared_part
         dz = scale * (upstream * slope_ref[:, outs] - flat_two / count - normed_ref[:, outs] * (cross_two / count)) * mask
-        for ref, part in zip((dzh_ref, dzl_ref), split(dz)):
-            ref[:, 1 : tall + 1, :, outs] = part.reshape(images, tall, 16, mid)
-    dzh_ref.send()
-    dzl_ref.send()
+        for ref, part in zip(dz_refs[2 * g : 2 * g + 2], split(dz)):
+            ref[:, 1 : tall + 1] = part.reshape(images, tall, 16, mid)
+            ref.send()
     group = up_ref.shape[1] // 2
     for g in range(2):
-        outs = slice(g * mid, (g + 1) * mid)
         cols = slice(g * group, (g + 1) * group)
         for side, row, tap in ((up_ref, 1, 0), (down_ref, tall, 2)):
-            left = [ref[:, row, :, outs].reshape(-1, mid) for ref in (dzh_ref, dzl_ref)]
-            side[:, cols] = fold(turned_rows(left, wh_ref, wl_ref, outs, tap, 3 * group), group)
-
-
-def group_kernel(core, dzh_ref, dzl_ref, squeeze_ref, excite_ref, th_ref, tl_ref, keep_ref, send_ref, out_ref):
-    tall = dzh_ref.shape[1] - 2
-    mid = dzh_ref.shape[3] // 2
+            left = [ref[:, row].reshape(-1, mid) for ref in dz_refs[2 * g : 2 * g + 2]]
+            side[:, cols] = fold(turned_rows(left, w_refs[2 * g : 2 * g + 2], tap, 3 * group), group)
+
+
+def group_kernel(core, *refs):
+    dz_refs, (squeeze_ref, excite_ref, th_ref, tl_ref, keep_ref, send_ref, out_ref) = refs[:4], refs[4:]
+    tall = dz_refs[0].shape[1] - 2
     taps = th_ref.shape[1]
     for g in range(2):
-        outs = slice(g * mid, (g + 1) * mid)
-        right = [ref[:, 1 : tall + 1, :, outs].reshape(-1, mid) for ref in (dzh_ref, dzl_ref)]
+        right = [ref[:, 1 : tall + 1].reshape(-1, ref.shape[3]) for ref in dz_refs[2 * g : 2 * g + 2]]
         out_ref[g * taps : (g + 1) * taps, :] = product((th_ref.chunk(g)[0], tl_ref.chunk(g)[0]), right, NN)
     inter = excite_ref.shape[0]
     out_ref[2 * taps : 2 * taps + inter, :] = excite_ref[...]
@@ -757,50 +766,56 @@
     core.scatter([out_ref], [keep_ref, send_ref])
 
 
-def input_grad_kernel(par_ref, stat_ref, dsum_ref, z_ref, own_ref, above_ref, below_ref, dzh_ref, dzl_ref, wh_ref, wl_ref,
-                      dy_ref, pay_ref, tile, place):
-    images = dsum_ref.shape[0]
-    width = z_ref.shape[1]
-    group = width // 2
-    tall = dzh_ref.shape[1] - 2
-    half = dzh_ref.shape[3] // 2
-    grads = []
-    for g in range(2):
-        outs = slice(g * half, (g + 1) * half)
-        total = None
-        for row in range(3):
-            left = [ref[:, 2 - row : 2 - row + tall, :, outs].reshape(-1, half) for ref in (dzh_ref, dzl_ref)]
-            term = turned_rows(left, wh_ref, wl_ref, outs, row, 3 * group)
-            total = term if total is None else total + term
-        grads.append(fold(total, group))
-    place[...] = jnp.concatenate(grads, axis=1).reshape(place.shape)
-    place[:, 0] += above_ref[...].reshape(images, 16, width)
-    place[:, tall - 1] += below_ref[...].reshape(images, 16, width)
-    grad = place[...].reshape(-1, width)
-    mean, inv = get(stat_ref, 0, 2), get(stat_ref, 2, 2)
-    normed = (z_ref[...] - mean) * inv
-    y = normed * get(par_ref, 0, 2) + get(par_ref, 2, 2)
+def input_grad_kernel(g, par_ref, stat_ref, z_ref, own_ref, above_ref, below_ref, dzh_ref, dzl_ref, wh_ref, wl_ref, *refs):
+    images, tall = dzh_ref.shape[0], dzh_ref.shape[1] - 2
+    group = z_ref.shape[1] // 2
+    cols = slice(g * group, (g + 1) * group)
+    total = None
+    for row in range(3):
+        left = [ref[:, 2 - row : 2 - row + tall].reshape(-1, ref.shape[3]) for ref in (dzh_ref, dzl_ref)]
+        term = turned_rows(left, (wh_ref, wl_ref), row, 3 * group)
+        total = term if total is None else total + term
+    place = refs[-1]
+    place[...] = fold(total, group).reshape(place.shape)
+    place[:, 0] += above_ref[:, cols].reshape(images, 16, group)
+    place[:, tall - 1] += below_ref[:, cols].reshape(images, 16, group)
+    grad = place[...].reshape(-1, group)
+    mean, inv, gain, shift = [ref[row + g : row + g + 1, :] for ref, row in ((stat_ref, 0), (stat_ref, 2), (par_ref, 0), (par_ref, 2))]
+    normed = (z_ref[:, cols] - mean) * inv
+    y = normed * gain + shift
     sigma = jax.nn.sigmoid(y)
-    dy = grad * wide(own_ref[...], width) * (sigma * (1.0 + y * (1.0 - sigma)))
+    dy = grad * wide(own_ref[...], group) * (sigma * (1.0 + y * (1.0 - sigma)))
+    if g == 0:
+        dy_ref, tile = refs[:2]
+        tile[...] = jnp.zeros(tile.shape, f32)
+    else:
+        dsum_ref, before_ref, dy_ref, pay_ref, tile = refs[:5]
+        tile[...] = before_ref[...]
+        put(tile, 4, column_sum(dsum_ref[...]))
     dy_ref[...] = dy
     dy_ref.send()
-    tile[...] = jnp.zeros_like(tile)
-    put(tile, 0, column_sum(dy * normed))
-    put(tile, 2, column_sum(dy))
-    put(tile, 4, column_sum(dsum_ref[...]))
-    pay_ref[...] = jnp.broadcast_to(tile[...][None], pay_ref.shape)
-
-
-def final_kernel(core, g7_ref, par_ref, stat_ref, dy_ref, z_ref, own_ref, th_ref, tl_ref,
-                 keep_ref, send_ref, dzh_ref, dzl_ref, gains_ref, term):
+    put(tile, g, column_sum(dy * normed))
+    put(tile, 2 + g, column_sum(dy))
+    if g:
+        pay_ref[...] = jnp.broadcast_to(tile[...][None], pay_ref.shape)
+
+
+def final_kernel(core, g7_ref, par_ref, stat_ref, first_ref, second_ref, z_ref, own_ref, th_ref, tl_ref,
+                 keep_ref, send_ref, dzh_ref, dzl_ref, mark_ref, gain_ref, flat_ref, bias_ref, gains_ref, term):
     width = z_ref.shape[1]
     gains_ref[...] = jnp.sum(g7_ref[...], axis=0)
+    mark_ref[...] = gains_ref[...]
+    gain_ref[...] = gains_ref[0:2, :]
+    flat_ref[...] = gains_ref[2:4, :]
+    bias_ref[0:2, :] = gains_ref[4:6, :]
+    bias_ref[2:4, :] = -gains_ref[4:6, :]
     cross, flat = get(gains_ref, 0, 2), get(gains_ref, 2, 2)
     count = wide(stat_ref[4:5, :], width)
     mean, inv = get(stat_ref, 0, 2), get(stat_ref, 2, 2)
     normed = (z_ref[...] - mean) * inv
     scale = get(par_ref, 0, 2) * inv
-    dz = scale * (dy_ref[...] - flat / count - normed * (cross / count)) * wide(own_ref[...], width)
+    dy = jnp.concatenate([first_ref[...], second_ref[...]], axis=1)
+    dz = scale * (dy - flat / count - normed * (cross / count)) * wide(own_ref[...], width)
     high, low = split(dz)
     dzh_ref[...] = high
     dzl_ref[...] = low
@@ -966,18 +981,18 @@
     )
     g1 = share(pay)
     above, below = halos(first, last)
-    wgh, wgl, weh, wel, wrh, wrl, par = call(
+    *group_parts, weh, wel, wrh, wrl, par = call(
         parts_kernel,
-        [*twice(taps, duo), *twice(mid, chan), *twice(chan, mid), ((40, 128), f32)],
+        [*twice(taps, mid), *twice(taps, mid), *twice(mid, chan), *twice(chan, mid), ((40, 128), f32)],
         [flat_w, w_expand, w_reduce, *[v.reshape(1, -1) for v in vectors]],
         chunks={0: 4, 1: 2, 2: 2},
-        out_chunks={0: 4, 1: 4, 2: 2, 3: 2, 4: 2, 5: 2},
+        out_chunks={0: 4, 1: 4, 2: 4, 3: 4, 4: 2, 5: 2, 6: 2, 7: 2},
         after=[z_one],
     )
     z_two, a_one, stat1, counts, pay = call(
         conv_kernel,
         [((cells, duo), f32), ((longer, mid), f32), ((8, 128), f32), ((devices, 128), f32), pay8],
-        [g1, par, z_one, ext, above, below, own, wgh, wgl],
+        [g1, par, z_one, ext, above, below, own, *group_parts],
         [tile8, pltpu.VMEM((count, tall + 2, broad, mid), f32)],
         near=(0, 4, 5),
         near_outs=(4,),
@@ -1028,15 +1043,15 @@
     g5 = share(pay)
     slopes = depth.send([slopes] * depth.size)
     tph, tpl = call(functools.partial(taps_kernel, count), twice(2, taps, cells), [a_one], out_chunks={0: 2, 1: 2}, after=[stat3])
-    grad_mixed, dsum, grads_three, slopes, pay = call(
+    grad_mixed, dsum, grads_three, grad_gain_three, grad_shift_three, slopes, pay = call(
         functools.partial(mixed_kernel, depth),
         [((cells, mid), f32), ((count, mid), f32),
-         ((16, 128), f32), ((depth.size * count, 2 * duo), f32), pay16],
+         ((16, 128), f32), ((8, 128), f32), ((8, 128), f32), ((depth.size * count, 2 * duo), f32), pay16],
         [g5, stat1, stat3, par, own, grad_pre, z_three, weh, wel, a_two, weights, w_excite, slope_two, normed_two, *slopes],
         [tile16],
         after=[tph],
         near=(0, *range(14, 14 + depth.size)),
-        near_outs=(3, 4),
+        near_outs=(5, 6),
     )
     g6 = share(pay)
     *expand_sum, excite_term = call(
@@ -1050,12 +1065,12 @@
         slopes = gather_more(extra, extra.send([slopes] * extra.size))
     slopes = core.send([slopes] * 2)
     packed = 2 * taps + 2 * inter
-    up, down, dzh, dzl, squeeze_term, grads_two, grads_fc = call(
+    up, down, *dz_parts, squeeze_term, grad_gain_two, grad_shift_two, grad_gain_fc, grad_shift_fc = call(
         functools.partial(back_kernel, core),
-        [((edge, mid), f32), ((edge, mid), f32), *twice(count, tall + 2, broad, duo), ((inter, mid), f32),
-         ((8, 128), f32), ((2, inter), f32)],
+        [((edge, mid), f32), ((edge, mid), f32), *twice(count, tall + 2, broad, mid), *twice(count, tall + 2, broad, mid), ((inter, mid), f32),
+         ((duo // 128, 128), f32), ((duo // 128, 128), f32), ((1, inter), f32), ((1, inter), f32)],
         [g6, fc_pre, fc_normed, fc_inv, par, w_squeeze, pooled, stat1, stat2, valid_rows, valid_cols, weights, *slopes, own,
-         grad_mixed, slope_two, normed_two, wgh, wgl],
+         grad_mixed, slope_two, normed_two, *group_parts],
         [pltpu.VMEM((all_images, inter), f32), pltpu.VMEM((all_images, mid), f32), pltpu.VMEM((all_images, 2 * duo), f32)],
         after=[excite_term],
         near=(0, 12, 13),
@@ -1065,40 +1080,48 @@
     group_sum = call(
         functools.partial(group_kernel, core),
         core.outs(packed, mid),
-        [dzh, dzl, squeeze_term, excite_term, tph, tpl],
+        [*dz_parts, squeeze_term, excite_term, tph, tpl],
         [pltpu.VMEM((packed, mid), f32)],
-        chunks={4: 2, 5: 2},
+        chunks={6: 2, 7: 2},
         near_outs=(0, 1),
     )
     expand_sum = core.send(expand_sum)
     group_sum = core.send([group_sum[0], gate(group_sum[1], [above, below])])
+    dy_first, tile = call(
+        functools.partial(input_grad_kernel, 0),
+        [((cells, mid // 2), f32), ((8, 128), f32)],
+        [par, stat1, z_one, own, above, below, *dz_parts[:2], *group_parts[:2]],
+        [pltpu.VMEM((count, tall, broad, mid // 2), f32)],
+        near=(4, 5),
+    )
     first_bit, second_bit = line.bits()
     some, more = expand_sum[0].shape[0] // 2, group_sum[0].shape[0] // 2
     both_of = lambda start, a, b: [((0, 1), start * a, a), ((2, 3), start * b, b)]
     first_half = lambda digit: (digit, both_of(0, some, more))
     second_half = lambda digit: (digit, both_of(1, some, more))
     keep_a, send_a, keep_b, send_b = deal(
-        [first_half(first_bit), second_half(second_bit)], [*expand_sum, *group_sum]
+        [first_half(first_bit), second_half(second_bit)], [*expand_sum, *group_sum], after=[tile]
     )
     come_a, come_b = first_bit.send([keep_a, send_a]), second_bit.send([keep_b, send_b])
-    dy_one, pay = call(
-        input_grad_kernel,
-        [((cells, mid), f32), pay8],
-        [par, stat1, dsum, z_one, own, above, below, dzh, dzl, wgh, wgl],
-        [tile8, pltpu.VMEM((count, tall, broad, mid), f32)],
+    place = pltpu.VMEM((count, tall, broad, mid // 2), f32)
+    dy_second, pay = call(
+        functools.partial(input_grad_kernel, 1),
+        [((cells, mid // 2), f32), pay8],
+        [par, stat1, z_one, own, above, below, *dz_parts[2:], *group_parts[2:], dsum, tile],
+        [tile8, place],
         beside=[keep_a],
-        near=(5, 6),
+        near=(4, 5),
         near_outs=(1,),
     )
     g7 = share(pay)
     some, more = some // 2, more // 2
     turn = lambda k: [((k, k + 1), 0, some), ((k, k + 1), some, more)]
-    keep_a, send_a, keep_b, send_b = deal([(second_bit, turn(0)), (first_bit, turn(2))], [*come_a, *come_b], after=[dy_one])
-    *reduce_sum, dzh, dzl, grads_one = call(
+    keep_a, send_a, keep_b, send_b = deal([(second_bit, turn(0)), (first_bit, turn(2))], [*come_a, *come_b], after=[dy_second])
+    *reduce_sum, dzh, dzl, mark_one, grad_gain_one, grad_shift_one, grad_bias = call(
         functools.partial(final_kernel, core),
-        [*core.outs(chan, mid), *twice(cells, mid), ((8, 128), f32)],
-        [g7, par, stat1, dy_one, z_one, own, xth, xtl],
-        [pltpu.VMEM((chan, mid), f32)],
+        [*core.outs(chan, mid), *twice(cells, mid), ((8, 128), f32), *[((mid // 128, 128), f32)] * 2, ((duo // 128, 128), f32)],
+        [g7, par, stat1, dy_first, dy_second, z_one, own, xth, xtl],
+        [tile8, pltpu.VMEM((chan, mid), f32)],
         beside=[keep_a],
         near=(0,),
         near_outs=(0, 1),
@@ -1110,7 +1133,7 @@
         functools.partial(stack_kernel, stretches),
         [((depth.size, (some + more) * 2 // depth.size, mid), f32)],
         [*come_a, *come_b],
-        after=[grads_one],
+        after=[mark_one],
     )
     reduce_sum[1] = gate(reduce_sum[1], [joined])
     joined = depth.trade(joined)
@@ -1156,7 +1179,6 @@
         [*first_bit.send([half_a] * 2), *second_bit.send([half_b] * 2)],
         beside=[reduce_sum],
     )
-    reduce_sum = gather_more(line, line.send([reduce_sum] * line.size), beside=[joined])
     expand_map, group_map = [], []
     at = 0
     some, more = some // depth.size, more // depth.size
@@ -1176,30 +1198,27 @@
         [pltpu.VMEM((chan + packed, mid), f32)],
         near=(0, 1),
     )
+    reduce_sum = gather_more(line, line.send([reduce_sum] * line.size), after=[grad_w_squeeze])
     (grad_w_reduce,) = call(
         functools.partial(gather_kernel, core), [((chan, mid), f32)], core.send([reduce_sum] * 2), near=(0, 1)
     )
-    grads_one = grads_one.reshape(-1)
-    grads_two = grads_two.reshape(-1)
-    grads_three = grads_three.reshape(-1)
-    grad_bias = grads_one[duo : duo + mid]
     return (
         block_out.reshape(images.shape),
         grad_images.reshape(images.shape),
         grad_w_reduce,
-        grads_one[:mid],
-        grads_one[mid:duo],
+        grad_gain_one.reshape(-1),
+        grad_shift_one.reshape(-1),
         grad_w_group.reshape(w_group.shape),
-        grads_two[:duo],
-        grads_two[duo:],
+        grad_gain_two.reshape(-1),
+        grad_shift_two.reshape(-1),
         grad_w_squeeze,
-        grads_fc[0],
-        grads_fc[1],
+        grad_gain_fc.reshape(-1),
+        grad_shift_fc.reshape(-1),
         grad_w_excite,
-        jnp.concatenate([grad_bias, -grad_bias]),
+        grad_bias.reshape(-1),
         grad_w_expand,
-        grads_three[chan:],
-        grads_three[:chan],
+        grad_gain_three.reshape(-1),
+        grad_shift_three.reshape(-1),
     )
 
 

time: 229 us -> 225 us (0.983)
  waiting for transfers between devices: 57.9 us -> 53.7 us
    all_to_all x7, waiting for transfers between devices: 21.1 us -> 18.3 us  [share(): return lax.all_to_all(tile, both, 0, 0)]
    pallas_call x19 -> x20, Pallas kernels: 83.3 us -> 85 us  [call(): pl.pallas_call(inner, out_shape=[(pltpu.VMEM if i in near_outs else pltpu...]
  transfers between devices with their start and end apart: 47 -> 47, of which waited for: 28 -> 30; matrix products, arithmetic and copies ran while one was open for 1% -> 0% of each run, Pallas kernels for 21% -> 22%
where the time goes in v5:
time: 225 us; the launch traced here: 224 us
  Pallas kernels  88.4 us (39%)
  starting transfers between devices  79.7 us (35%)
  waiting for transfers between devices  53.7 us (24%)
    pallas_call x20, Pallas kernels, call(): pl.pallas_call(inner, out_shape=[(pltpu.VMEM if i in near_outs else pltpu...  85 us
    ppermute x35, starting transfers between devices, flip(): lax.ppermute(values, axis, [(i, i ^ bits) for i in range(lax.axis_size(ax...  40.7 us
    ppermute x35, waiting for transfers between devices, flip(): lax.ppermute(values, axis, [(i, i ^ bits) for i in range(lax.axis_size(ax...  32.4 us
    all_to_all x7, starting transfers between devices, share(): return lax.all_to_all(tile, both, 0, 0)  26.3 us
    all_to_all x7, waiting for transfers between devices, share(): return lax.all_to_all(tile, both, 0, 0)  18.3 us
    ppermute x2, starting transfers between devices, halos(): above = lax.ppermute(last, 'rows', [(i, i + 1) for i in range(count - 1)])  6.09 us
  transfers between devices with their start and end apart: 47, of which 30 were waited for; matrix products, arithmetic and copies ran while one was open for 0% of the time, Pallas kernels for 22%

profile of v5, /device:TPU:0, one launch (start us, length us, event | category | flops | bytes accessed | tf_op | source)
XLA Modules:
  0.0 223.6 jit_solution(6964943294388560400)
XLA Ops:
  0.6 5.2 %shard_map.297 = (f32[512,256]{1,0:T(8,128)}, f32[8,6,16,128]{3,2,1,0:T(8,128)}, f32[512,128]{1,0:T(8,128)}, f32[128,256]{1,0:T(8,128)S(1)}, f32[128,256]{1,0:T(8,128)S(1)}, /*index=5*/f32[32,8,128]{2,1,0:T(8,128)}) custom-call(s32[8,16]{1,0:T(8,128)} %refs_9_.1, s32[8,16]{1,0:T(8,128)} %refs_10_.1, f32[1024,256]{1,0:T(8,128)} %refs_2_.5, f32[512,1024]{1,0:T(8,128)} %bitcast.24), custom_call_target="tpu_custom_call" | custom-call | flops 1 | bytes 1 | tf_op jit(solution)/shard_map/pallas_call | solution.py:205
  5.9 7.3 %all-to-all-start = ((f32[32,8,128]{2,1,0:T(8,128)}), f32[32,8,128]{2,1,0:T(8,128)S(1)}, u32[]{:S(2)}, u32[]{:S(2)}) async-start(f32[32,8,128]{2,1,0:T(8,128)} %get-tuple-element.120), calls=%async_computation | async-start | bytes 262144 | tf_op jit(solution)/shard_map/all_to_all | solution.py:248
  13.2 3.7 %collective-permute-start = (f32[128,256]{1,0:T(8,128)S(1)}, f32[128,256]{1,0:T(8,128)S(1)}, u32[]{:S(2)}, u32[]{:S(2)}) collective-permute-start(f32[128,256]{1,0:T(8,128)S(1)} %get-tuple-element.124), channel_id=1, source_target_pairs={{0,8},{8,16},{16,24},{1,9},{9,17},{17,25},{2,10},{10,18},{18,26},{... | collective-permute-start | bytes 393224 | tf_op jit(solution)/shard_map/ppermute | solution.py:253
  18.2 4.6 %shard_map.298 = (bf16[1152,256]{1,0:T(8,128)(2,1)}, bf16[1152,256]{1,0:T(8,128)(2,1)}, bf16[1152,256]{1,0:T(8,128)(2,1)}, bf16[1152,256]{1,0:T(8,128)(2,1)}, bf...) custom-call(f32[1152,512]{1,0:T(8,128)} %bitcast.29, ...), custom_call_target="tpu_custom_call" | custom-call | flops 1 | bytes 1 | tf_op jit(solution)/shard_map/pallas_call | solution.py:205
  25.1 5.9 %shard_map.299 = (f32[512,512]{1,0:T(8,128)}, f32[768,256]{1,0:T(8,128)}, f32[8,128]{1,0:T(8,128)}, f32[32,128]{1,0:T(8,128)}, f32[32,8,128]{2,1,0:T(8,128)}) custom-call(f32[32,8,128]{2,1,0:T(8,128)S(1)} %all-to-all-done.refs_0_, f32[40,128]{1,0:T(8,128)} %get-tuple-element.122.refs_1_.refs_2_.refs_3_.refs_4_.refs_0_, ...), custom_call_target="tpu_custom_call" | custom-call | flops 1 | bytes 1 | tf_op jit(solution)/shard_map/pallas_call | solution.py:205
  31.0 4.5 %all-to-all-start.1 = ((f32[32,8,128]{2,1,0:T(8,128)}), f32[32,8,128]{2,1,0:T(8,128)S(1)}, u32[]{:S(2)}, u32[]{:S(2)}) async-start(f32[32,8,128]{2,1,0:T(8,128)} %get-tuple-element.131), calls=%async_computation.1 | async-start | bytes 262144 | tf_op jit(solution)/shard_map/all_to_all | solution.py:248
  39.0 4.6 %all-to-all-done.1.refs_0_ = f32[32,8,128]{2,1,0:T(8,128)S(1)} async-done(((f32[32,8,128]{2,1,0:T(8,128)}), f32[32,8,128]{2,1,0:T(8,128)S(1)}, u32[]{:S(2)}, u32[]{:S(2)}) %all-to-all-start.1) | async-done | bytes 131104 | tf_op jit(solution)/shard_map/all_to_all | solution.py:248
  52.3 5.3 %all-to-all-done.2.refs_0_ = f32[32,8,128]{2,1,0:T(8,128)S(1)} async-done(((f32[32,8,128]{2,1,0:T(8,128)}), f32[32,8,128]{2,1,0:T(8,128)S(1)}, u32[]{:S(2)}, u32[]{:S(2)}) %all-to-all-start.2) | async-done | bytes 131104 | tf_op jit(solution)/shard_map/all_to_all | solution.py:248
  57.5 4.5 %shard_map.303 = (f32[512,256]{1,0:T(8,128)}, f32[512,1024]{1,0:T(8,128)}, f32[8,512]{1,0:T(8,128)}, f32[64,128]{1,0:T(8,128)}, f32[64,128]{1,0:T(8,128)}, /*ind...) custom-call(f32[32,8,128]{2,1,0:T(8,128)S(1)} %all-to-all-done.2.refs_0_, ...), custom_call_target="tpu_custom_call" | custom-call | flops 1 | bytes 1 | tf_op jit(solution)/shard_map/pallas_call | solution.py:205
  75.0 5.8 %shard_map.304 = (f32[512,1024]{1,0:T(8,128)}, f32[16,128]{1,0:T(8,128)}, f32[8,1024]{1,0:T(8,128)S(1)}, f32[32,16,128]{2,1,0:T(8,128)}) custom-call(f32[32,16,128]{2,1,0:T(8,128)S(1)} %all-to-all-done.3.refs_0_, f32[32,128]{1,0:T(8,128)} %get-tuple-element.132.refs_1_, f32[40,128]{1,0:T(8,128)} %get-tuple-element.122.refs_1_.refs_2_.refs_3_.refs_4_.refs_0_, ...), custom_call_target="tpu_custom_call" | custom-call | flops 1 | bytes 1 | tf_op jit(solution)/shard_map/pallas_call | solution.py:205
  83.4 3.7 %collective-permute-start.7 = (f32[8,1024]{1,0:T(8,128)S(1)}, f32[8,1024]{1,0:T(8,128)S(1)}, u32[]{:S(2)}, u32[]{:S(2)}) collective-permute-start(f32[8,1024]{1,0:T(8,128)S(1)} %get-tuple-element.150.refs_14_), channel_id=1, source_target_pairs={{0,6},{1,7},{2,4},{3,5},{4,2},{5,3},{6,0},{7,1},{8,14},{9,15},{10,... | collective-permute-start | bytes 98312 | tf_op jit(solution)/shard_map/ppermute | solution.py:259
  87.9 4.0 %shard_map.305 = (bf16[2,1152,512]{2,1,0:T(8,128)(2,1)}, bf16[2,1152,512]{2,1,0:T(8,128)(2,1)}) custom-call(f32[768,256]{1,0:T(8,128)} %get-tuple-element.151.refs_0_, f32[16,128]{1,0:T(8,128)} %get-tuple-element.144.refs_1_.refs_2_.refs_0_), custom_call_target="tpu_custom_call" | custom-call | flops 1 | bytes 1 | tf_op jit(solution)/shard_map/pallas_call | solution.py:205
  95.6 6.7 %shard_map.306 = (f32[512,256]{1,0:T(8,128)}, f32[8,256]{1,0:T(8,128)}, f32[16,128]{1,0:T(8,128)}, f32[8,128]{1,0:T(8,128)}, f32[8,128]{1,0:T(8,128)}, /*index=5*/f32[32,1024]{1,0:T(8,128)S(1)}, f32[32,16,128]{2,1,0:T(8,128)}) custom-call(f32[32,16,128]{2,1,0:T(8,128)S(1)} %all-to-all-done.4.refs_0_, f32[8,128]{1,0:T(8,128)} %get-tuple-element.134.refs_1_.refs_7_.refs_2_, ...), custom_call_target="tpu_custom_call" | custom-call | flops 1 | bytes 1 | tf_op jit(solution)/shard_map/pallas_call | solution.py:205
  106.1 5.2 %shard_map.307 = (f32[512,256]{1,0:T(8,128)}, f32[512,256]{1,0:T(8,128)}, f32[128,256]{1,0:T(8,128)}) custom-call(f32[16,128]{1,0:T(8,128)} %get-tuple-element.153.refs_0_, f32[8,128]{1,0:T(8,128)} %get-tuple-element.134.refs_1_.refs_7_.refs_2_, f32[16,128]{1,0:T(8,128)} %get-tuple-element.144.refs_1_.refs_2_.refs_0_, ...), custom_call_target="tpu_custom_call" | custom-call | flops 1 | bytes 1 | tf_op jit(solution)/shard_map/pallas_call | solution.py:205
  111.4 4.8 %all-to-all-done.5.refs_0_ = f32[32,16,128]{2,1,0:T(8,128)S(1)} async-done(((f32[32,16,128]{2,1,0:T(8,128)}), f32[32,16,128]{2,1,0:T(8,128)S(1)}, u32[]{:S(2)}, u32[]{:S(2)}) %all-to-all-start.5) | async-done | bytes 262176 | tf_op jit(solution)/shard_map/all_to_all | solution.py:248
  116.2 4.1 %shard_map.308 = (f32[128,256]{1,0:T(8,128)S(1)}, f32[128,256]{1,0:T(8,128)S(1)}, bf16[8,6,16,256]{3,2,1,0:T(8,128)(2,1)}, bf16[8,6,16,256]{3,2,1,0:T(8,128)(2,1...) custom-call(f32[32,16,128]{2,1,0:T(8,128)S(1)} %all-to-all-done.5.re, ...), custom_call_target="tpu_custom_call" | custom-call | flops 1 | bytes 1 | tf_op jit(solution)/shard_map/pallas_call | solution.py:205
  124.2 6.3 %shard_map.309 = (f32[1280,256]{1,0:T(8,128)S(1)}, f32[1280,256]{1,0:T(8,128)S(1)}) custom-call(bf16[8,6,16,256]{3,2,1,0:T(8,128)(2,1)} %get-tuple-element.167.refs_0_.refs_6_, bf16[8,6,16,256]{3,2,1,0:T(8,128)(2,1)} %get-tuple-element.168.refs_1_.refs_7_, bf16[8,6,16,256]{3,2,1,0:T(8,128)(2,1)} %get-tuple-element.169.refs_2_.refs_6_, ...), custom_call_target="tpu_custom_call" | custom-call | flops 1 | bytes 1 | tf_op jit(solution)/shard_map/pallas_call | solution.py:205
  132.0 4.1 %shard_map.311 = (f32[512,128]{1,0:T(8,128)}, f32[8,128]{1,0:T(8,128)}) custom-call(f32[40,128]{1,0:T(8,128)} %get-tuple-element.122.refs_1_.refs_2_.refs_3_.refs_4_.refs_0_, f32[8,128]{1,0:T(8,128)} %get-tuple-element.134.refs_1_.refs_7_.refs_2_, f32[512,256]{1,0:T(8,128)} %get-tuple-element.121.refs_12_.refs_2_.refs_5_, ...), custom_call_target="tpu_custom_call" | custom-call | flops 1 | bytes 1 | tf_op jit(solution)/shard_map/pallas_call | solution.py:205
  140.4 4.8 %shard_map.313 = (f32[512,128]{1,0:T(8,128)}, f32[32,8,128]{2,1,0:T(8,128)}) custom-call(f32[40,128]{1,0:T(8,128)} %get-tuple-element.122.refs_1_.refs_2_.refs_3_.refs_4_.refs_0_, f32[8,128]{1,0:T(8,128)} %get-tuple-element.134.refs_1_.refs_7_.refs_2_, f32[512,256]{1,0:T(8,128)} %get-tuple-element.121.refs_12_.refs_2_.refs_5_, ...), custom_call_target="tpu_custom_call" | custom-call | flops 1 | bytes 1 | tf_op jit(solution)/shard_map/pallas_call | solution.py:205
  161.3 3.7 %all-to-all-start.7 = ((f32[4,112,256]{2,1,0:T(8,128)}), f32[4,112,256]{2,1,0:T(8,128)S(1)}, u32[]{:S(2)}, u32[]{:S(2)}) async-start(f32[4,112,256]{2,1,0:T(8,128)} %shard_map.316.refs_1_), calls=%async_computation.7 | async-start | bytes 917504 | tf_op jit(solution)/shard_map/all_to_all | solution.py:280
  171.6 4.2 %shard_map.319.refs_4_ = f32[512,1024]{1,0:T(8,128)} custom-call(bf16[512,256]{1,0:T(8,128)(2,1)} %get-tuple-element.197.refs_0_, bf16[512,256]{1,0:T(8,128)(2,1)} %get-tuple-element.198.refs_1_, bf16[1024,256]{1,0:T(8,128)(2,1)} %get-tuple-element.199.refs_2_, bf16[1024,256]{1,0:T(8,128)(2,1)} %get-tuple-element.200.refs_3_, ...), custom_call_target="tpu_custom_call" | custom-call | flops 1 | bytes 1 | tf_op jit(solution)/shard_map/pallas_call | solution.py:205
  182.3 3.7 %shard_map.322 = (f32[512,1024]{1,0:T(8,128)}, f32[8,128]{1,0:T(8,128)}) custom-call(f32[16,128]{1,0:T(8,128)} %get-tuple-element.144.refs_1_.refs_2_.refs_0_, f32[40,128]{1,0:T(8,128)} %get-tuple-element.122.refs_1_.refs_2_.refs_3_.refs_4_.refs_0_, f32[512,128]{1,0:T(8,128)} %get-tuple-element.126.refs_6_.refs_4_.refs_3_.refs_7_.refs_14_.refs_2_, ...), custom_call_target="tpu_custom_call" | custom-call | flops 1 | bytes 1 | tf_op jit(solution)/shard_map/pallas_call | solution.py:205
  186.0 4.0 %collective-permute-done.25.refs_2_ = f32[112,256]{1,0:T(8,128)S(1)} collective-permute-done((f32[112,256]{1,0:T(8,128)S(1)}, f32[112,256]{1,0:T(8,128)S(1)}, u32[]{:S(2)}, u32[]{:S(2)}) %collective-permute-start.25) | collective-permute-done | bytes 114720 | tf_op jit(solution)/shard_map/ppermute | solution.py:259
  197.5 3.6 %collective-permute-done.23.refs_3_ = f32[32,256]{1,0:T(8,128)S(1)} collective-permute-done((f32[32,256]{1,0:T(8,128)S(1)}, f32[32,256]{1,0:T(8,128)S(1)}, u32[]{:S(2)}, u32[]{:S(2)}) %collective-permute-start.23) | collective-permute-done | bytes 32800 | tf_op jit(solution)/shard_map/ppermute | solution.py:259
  (110 shorter events, 108.1 us)
Async XLA Ops:
  5.9 19.2 %all-to-all-start = ((f32[32,8,128]{2,1,0:T(8,128)}), f32[32,8,128]{2,1,0:T(8,128)S(1)}, u32[]{:S(2)}, u32[]{:S(2)}) async-start(f32[32,8,128]{2,1,0:T(8,128)} %get-tuple-element.120), calls=%async_computation | async-start | bytes 262144 | tf_op jit(solution)/shard_map/all_to_all | solution.py:248
  13.2 9.6 %collective-permute-start = (f32[128,256]{1,0:T(8,128)S(1)}, f32[128,256]{1,0:T(8,128)S(1)}, u32[]{:S(2)}, u32[]{:S(2)}) collective-permute-start(f32[128,256]{1,0:T(8,128)S(1)} %get-tuple-element.124), channel_id=1, source_target_pairs={{0,8},{8,16},{16,24},{1,9},{9,17},{17,25},{2,10},{10,18},{18,26},{... | collective-permute-start | bytes 393224 | tf_op jit(solution)/shard_map/ppermute | solution.py:253
  16.9 8.2 %collective-permute-start.1 = (f32[128,256]{1,0:T(8,128)S(1)}, f32[128,256]{1,0:T(8,128)S(1)}, u32[]{:S(2)}, u32[]{:S(2)}) collective-permute-start(f32[128,256]{1,0:T(8,128)S(1)} %get-tuple-element.125), channel_id=1, source_target_pairs={{8,0},{16,8},{24,16},{9,1},{17,9},{25,17},{10,2},{18,10},{26,18},{... | collective-permute-start | bytes 393224 | tf_op jit(solution)/shard_map/ppermute | solution.py:254
  31.0 12.6 %all-to-all-start.1 = ((f32[32,8,128]{2,1,0:T(8,128)}), f32[32,8,128]{2,1,0:T(8,128)S(1)}, u32[]{:S(2)}, u32[]{:S(2)}) async-start(f32[32,8,128]{2,1,0:T(8,128)} %get-tuple-element.131), calls=%async_computation.1 | async-start | bytes 262144 | tf_op jit(solution)/shard_map/all_to_all | solution.py:248
  46.8 10.8 %all-to-all-start.2 = ((f32[32,8,128]{2,1,0:T(8,128)}), f32[32,8,128]{2,1,0:T(8,128)S(1)}, u32[]{:S(2)}, u32[]{:S(2)}) async-start(f32[32,8,128]{2,1,0:T(8,128)} %get-tuple-element.136), calls=%async_computation.2 | async-start | bytes 262144 | tf_op jit(solution)/shard_map/all_to_all | solution.py:248
  62.0 13.0 %all-to-all-start.3 = ((f32[32,16,128]{2,1,0:T(8,128)}), f32[32,16,128]{2,1,0:T(8,128)S(1)}, u32[]{:S(2)}, u32[]{:S(2)}) async-start(f32[32,16,128]{2,1,0:T(8,128)} %get-tuple-element.142), calls=%async_computation.3 | async-start | bytes 524288 | tf_op jit(solution)/shard_map/all_to_all | solution.py:248
  80.8 14.8 %all-to-all-start.4 = ((f32[32,16,128]{2,1,0:T(8,128)}), f32[32,16,128]{2,1,0:T(8,128)S(1)}, u32[]{:S(2)}, u32[]{:S(2)}) async-start(f32[32,16,128]{2,1,0:T(8,128)} %get-tuple-element.145), calls=%async_computation.4 | async-start | bytes 524288 | tf_op jit(solution)/shard_map/all_to_all | solution.py:248
  83.4 10.1 %collective-permute-start.7 = (f32[8,1024]{1,0:T(8,128)S(1)}, f32[8,1024]{1,0:T(8,128)S(1)}, u32[]{:S(2)}, u32[]{:S(2)}) collective-permute-start(f32[8,1024]{1,0:T(8,128)S(1)} %get-tuple-element.150.refs_14_), channel_id=1, source_target_pairs={{0,6},{1,7},{2,4},{3,5},{4,2},{5,3},{6,0},{7,1},{8,14},{9,15},{10,... | collective-permute-start | bytes 98312 | tf_op jit(solution)/shard_map/ppermute | solution.py:259
  87.1 8.5 %collective-permute-start.6 = (f32[8,1024]{1,0:T(8,128)S(1)}, f32[8,1024]{1,0:T(8,128)S(1)}, u32[]{:S(2)}, u32[]{:S(2)}) collective-permute-start(f32[8,1024]{1,0:T(8,128)S(1)} %get-tuple-element.150.refs_14_), channel_id=1, source_target_pairs={{0,4},{1,5},{2,6},{3,7},{4,0},{5,1},{6,2},{7,3},{8,12},{9,13},{10,... | collective-permute-start | bytes 98312 | tf_op jit(solution)/shard_map/ppermute | solution.py:259
  87.1 8.5 %collective-permute-start.5 = (f32[8,1024]{1,0:T(8,128)S(1)}, f32[8,1024]{1,0:T(8,128)S(1)}, u32[]{:S(2)}, u32[]{:S(2)}) collective-permute-start(f32[8,1024]{1,0:T(8,128)S(1)} %get-tuple-element.150.refs_14_), channel_id=1, source_target_pairs={{0,2},{1,3},{2,0},{3,1},{4,6},{5,7},{6,4},{7,5},{8,10},{9,11},{10,... | collective-permute-start | bytes 98312 | tf_op jit(solution)/shard_map/ppermute | solution.py:259
  102.3 13.9 %all-to-all-start.5 = ((f32[32,16,128]{2,1,0:T(8,128)}), f32[32,16,128]{2,1,0:T(8,128)S(1)}, u32[]{:S(2)}, u32[]{:S(2)}) async-start(f32[32,16,128]{2,1,0:T(8,128)} %get-tuple-element.159), calls=%async_computation.5 | async-start | bytes 524288 | tf_op jit(solution)/shard_map/all_to_all | solution.py:248
  120.3 10.3 %collective-permute-start.10 = (f32[128,256]{1,0:T(8,128)S(1)}, f32[128,256]{1,0:T(8,128)S(1)}, u32[]{:S(2)}, u32[]{:S(2)}) collective-permute-start(f32[128,256]{1,0:T(8,128)S(1)} %get-tuple-element.175), channel_id=1, source_target_pairs={{0,8},{8,16},{16,24},{1,9},{9,17},{17,25},{2,10},{10,18},{18,26},{... | collective-permute-start | bytes 393224 | tf_op jit(solution)/shard_map/ppermute | solution.py:253
  122.7 8.3 %collective-permute-start.11 = (f32[128,256]{1,0:T(8,128)S(1)}, f32[128,256]{1,0:T(8,128)S(1)}, u32[]{:S(2)}, u32[]{:S(2)}) collective-permute-start(f32[128,256]{1,0:T(8,128)S(1)} %get-tuple-element.176), channel_id=1, source_target_pairs={{8,0},{16,8},{24,16},{9,1},{17,9},{25,17},{10,2},{18,10},{26,18},{... | collective-permute-start | bytes 393224 | tf_op jit(solution)/shard_map/ppermute | solution.py:254
  137.1 13.6 %collective-permute-start.13 = (f32[448,256]{1,0:T(8,128)}, f32[448,256]{1,0:T(8,128)S(1)}, u32[]{:S(2)}, u32[]{:S(2)}) collective-permute-start(f32[448,256]{1,0:T(8,128)} %get-tuple-element.179), channel_id=1, source_target_pairs={{0,8},{8,0},{16,24},{24,16},{1,9},{9,1},{17,25},{25,17},{2,10},{10... | collective-permute-start | bytes 1376264 | tf_op jit(solution)/shard_map/ppermute | solution.py:259
  139.5 12.6 %collective-permute-start.14 = (f32[448,256]{1,0:T(8,128)S(1)}, f32[448,256]{1,0:T(8,128)S(1)}, u32[]{:S(2)}, u32[]{:S(2)}) collective-permute-start(f32[448,256]{1,0:T(8,128)S(1)} %get-tuple-element.181), channel_id=1, source_target_pairs={{0,16},{8,24},{16,0},{24,8},{1,17},{9,25},{17,1},{25,9},{2,18},{10... | collective-permute-start | bytes 1376264 | tf_op jit(solution)/shard_map/ppermute | solution.py:259
  145.2 11.2 %all-to-all-start.6 = ((f32[32,8,128]{2,1,0:T(8,128)}), f32[32,8,128]{2,1,0:T(8,128)S(1)}, u32[]{:S(2)}, u32[]{:S(2)}) async-start(f32[32,8,128]{2,1,0:T(8,128)} %get-tuple-element.187), calls=%async_computation.6 | async-start | bytes 262144 | tf_op jit(solution)/shard_map/all_to_all | solution.py:248
  161.3 16.6 %all-to-all-start.7 = ((f32[4,112,256]{2,1,0:T(8,128)}), f32[4,112,256]{2,1,0:T(8,128)S(1)}, u32[]{:S(2)}, u32[]{:S(2)}) async-start(f32[4,112,256]{2,1,0:T(8,128)} %shard_map.316.refs_1_), calls=%async_computation.7 | async-start | bytes 917504 | tf_op jit(solution)/shard_map/all_to_all | solution.py:280
  177.9 8.1 %collective-permute-start.26 = (f32[112,256]{1,0:T(8,128)S(1)}, f32[112,256]{1,0:T(8,128)S(1)}, u32[]{:S(2)}, u32[]{:S(2)}) collective-permute-start(f32[112,256]{1,0:T(8,128)S(1)} %shard_map.321.refs_5_.refs_0_), channel_id=1, source_target_pairs={{0,6},{1,7},{2,4},{3,5},{4,2},{5,3},{6,0},{7,1},{8,14},{9,15},{10,... | collective-permute-start | bytes 344072 | tf_op jit(solution)/shard_map/ppermute | solution.py:259
  181.3 8.7 %collective-permute-start.25 = (f32[112,256]{1,0:T(8,128)S(1)}, f32[112,256]{1,0:T(8,128)S(1)}, u32[]{:S(2)}, u32[]{:S(2)}) collective-permute-start(f32[112,256]{1,0:T(8,128)S(1)} %shard_map.321.refs_5_.refs_0_), channel_id=1, source_target_pairs={{0,4},{1,5},{2,6},{3,7},{4,0},{5,1},{6,2},{7,3},{8,12},{9,13},{10,... | collective-permute-start | bytes 344072 | tf_op jit(solution)/shard_map/ppermute | solution.py:259
  181.3 8.7 %collective-permute-start.24 = (f32[112,256]{1,0:T(8,128)S(1)}, f32[112,256]{1,0:T(8,128)S(1)}, u32[]{:S(2)}, u32[]{:S(2)}) collective-permute-start(f32[112,256]{1,0:T(8,128)S(1)} %shard_map.321.refs_5_.refs_0_), channel_id=1, source_target_pairs={{0,2},{1,3},{2,0},{3,1},{4,6},{5,7},{6,4},{7,5},{8,10},{9,11},{10,... | collective-permute-start | bytes 344072 | tf_op jit(solution)/shard_map/ppermute | solution.py:259
  190.1 11.1 %collective-permute-start.31 = (f32[224,256]{1,0:T(8,128)S(1)}, f32[224,256]{1,0:T(8,128)S(1)}, u32[]{:S(2)}, u32[]{:S(2)}) collective-permute-start(f32[224,256]{1,0:T(8,128)S(1)} %get-tuple-element.208.refs_2_), channel_id=1, source_target_pairs={{0,8},{8,0},{16,24},{24,16},{1,9},{9,1},{17,25},{25,17},{2,10},{10... | collective-permute-start | bytes 688136 | tf_op jit(solution)/shard_map/ppermute | solution.py:259
  190.9 10.3 %collective-permute-start.30 = (f32[224,256]{1,0:T(8,128)S(1)}, f32[224,256]{1,0:T(8,128)S(1)}, u32[]{:S(2)}, u32[]{:S(2)}) collective-permute-start(f32[224,256]{1,0:T(8,128)S(1)} %get-tuple-element.207.refs_4_.refs_0_), channel_id=1, source_target_pairs={{0,16},{8,24},{16,0},{24,8},{1,17},{9,25},{17,1},{25,9},{2,18},{10... | collective-permute-start | bytes 688136 | tf_op jit(solution)/shard_map/ppermute | solution.py:259
  201.3 8.6 %collective-permute-start.36 = (f32[448,256]{1,0:T(8,128)S(1)}, f32[448,256]{1,0:T(8,128)S(1)}, u32[]{:S(2)}, u32[]{:S(2)}) collective-permute-start(f32[448,256]{1,0:T(8,128)S(1)} %get-tuple-element.210.refs_2_), channel_id=1, source_target_pairs={{0,16},{8,24},{16,0},{24,8},{1,17},{9,25},{17,1},{25,9},{2,18},{10... | collective-permute-start | bytes 1376264 | tf_op jit(solution)/shard_map/ppermute | solution.py:259
  201.8 8.5 %collective-permute-start.35 = (f32[448,256]{1,0:T(8,128)S(1)}, f32[448,256]{1,0:T(8,128)S(1)}, u32[]{:S(2)}, u32[]{:S(2)}) collective-permute-start(f32[448,256]{1,0:T(8,128)S(1)} %get-tuple-element.209.refs_4_.refs_0_), channel_id=1, source_target_pairs={{0,8},{8,0},{16,24},{24,16},{1,9},{9,1},{17,25},{25,17},{2,10},{10... | collective-permute-start | bytes 1376264 | tf_op jit(solution)/shard_map/ppermute | solution.py:259
  (26 other events, 146.4 us)

commit v6 on v5

--- a/solution.py
+++ b/solution.py
@@ -755,6 +755,8 @@
 
 def group_kernel(core, *refs):
     dz_refs, (squeeze_ref, excite_ref, th_ref, tl_ref, keep_ref, send_ref, out_ref) = refs[:4], refs[4:]
+    for ref in (*dz_refs, squeeze_ref, excite_ref, th_ref, tl_ref):
+        ref.ready()
     tall = dz_refs[0].shape[1] - 2
     taps = th_ref.shape[1]
     for g in range(2):
@@ -976,7 +978,6 @@
          ((edge, mid), f32), pay8],
         [valid_rows, valid_cols, w_reduce, x],
         [tile8],
-        chunks={3: 2},
         near_outs=(3, 4, 5),
     )
     g1 = share(pay)
@@ -1135,7 +1136,6 @@
         [*come_a, *come_b],
         after=[mark_one],
     )
-    reduce_sum[1] = gate(reduce_sum[1], [joined])
     joined = depth.trade(joined)
     reduce_sum = scatter_more(line, core.send(reduce_sum))
     (grad_images,) = call(

time: 225 us -> 222 us (0.987)
  Pallas kernels: 88.4 us -> 85.6 us
  transfers between devices with their start and end apart: 47 -> 47, of which waited for: 30 -> 29; matrix products, arithmetic and copies ran while one was open for 0% -> 0% of each run, Pallas kernels for 22% -> 22%
where the time goes in v6:
time: 222 us; the launch traced here: 221 us
  Pallas kernels  85.6 us (39%)
  starting transfers between devices  78.7 us (35%)
  waiting for transfers between devices  55.8 us (25%)
    pallas_call x20, Pallas kernels, call(): pl.pallas_call(inner, out_shape=[(pltpu.VMEM if i in near_outs else pltpu...  83.3 us
    ppermute x35, starting transfers between devices, flip(): lax.ppermute(values, axis, [(i, i ^ bits) for i in range(lax.axis_size(ax...  40.1 us
    ppermute x35, waiting for transfers between devices, flip(): lax.ppermute(values, axis, [(i, i ^ bits) for i in range(lax.axis_size(ax...  32.3 us
    all_to_all x7, starting transfers between devices, share(): return lax.all_to_all(tile, both, 0, 0)  26.2 us
    all_to_all x7, waiting for transfers between devices, share(): return lax.all_to_all(tile, both, 0, 0)  18.3 us
    ppermute x2, starting transfers between devices, halos(): above = lax.ppermute(last, 'rows', [(i, i + 1) for i in range(count - 1)])  6.09 us
  transfers between devices with their start and end apart: 47, of which 29 were waited for; matrix products, arithmetic and copies ran while one was open for 0% of the time, Pallas kernels for 22%

profile of v6, /device:TPU:0, one launch (start us, length us, event | category | flops | bytes accessed | tf_op | source)
XLA Modules:
  0.0 221.5 jit_solution(5234789486632377844)
XLA Ops:
  0.6 4.5 %shard_map.297 = (f32[512,256]{1,0:T(8,128)}, f32[8,6,16,128]{3,2,1,0:T(8,128)}, f32[512,128]{1,0:T(8,128)}, f32[128,256]{1,0:T(8,128)S(1)}, f32[128,256]{1,0:T(8,128)S(1)}, /*index=5*/f32[32,8,128]{2,1,0:T(8,128)}) custom-call(s32[8,16]{1,0:T(8,128)} %refs_9_.1, s32[8,16]{1,0:T(8,128)} %refs_10_.1, f32[1024,256]{1,0:T(8,128)} %refs_2_.5, f32[512,1024]{1,0:T(8,128)} %bitcast.24), custom_call_target="tpu_custom_call" | custom-call | flops 1 | bytes 1 | tf_op jit(solution)/shard_map/pallas_call | solution.py:205
  5.1 7.3 %all-to-all-start = ((f32[32,8,128]{2,1,0:T(8,128)}), f32[32,8,128]{2,1,0:T(8,128)S(1)}, u32[]{:S(2)}, u32[]{:S(2)}) async-start(f32[32,8,128]{2,1,0:T(8,128)} %get-tuple-element.120), calls=%async_computation | async-start | bytes 262144 | tf_op jit(solution)/shard_map/all_to_all | solution.py:248
  12.4 3.7 %collective-permute-start = (f32[128,256]{1,0:T(8,128)S(1)}, f32[128,256]{1,0:T(8,128)S(1)}, u32[]{:S(2)}, u32[]{:S(2)}) collective-permute-start(f32[128,256]{1,0:T(8,128)S(1)} %get-tuple-element.124), channel_id=1, source_target_pairs={{0,8},{8,16},{16,24},{1,9},{9,17},{17,25},{2,10},{10,18},{18,26},{... | collective-permute-start | bytes 393224 | tf_op jit(solution)/shard_map/ppermute | solution.py:253
  17.4 4.6 %shard_map.298 = (bf16[1152,256]{1,0:T(8,128)(2,1)}, bf16[1152,256]{1,0:T(8,128)(2,1)}, bf16[1152,256]{1,0:T(8,128)(2,1)}, bf16[1152,256]{1,0:T(8,128)(2,1)}, bf...) custom-call(f32[1152,512]{1,0:T(8,128)} %bitcast.29, ...), custom_call_target="tpu_custom_call" | custom-call | flops 1 | bytes 1 | tf_op jit(solution)/shard_map/pallas_call | solution.py:205
  24.3 5.9 %shard_map.299 = (f32[512,512]{1,0:T(8,128)}, f32[768,256]{1,0:T(8,128)}, f32[8,128]{1,0:T(8,128)}, f32[32,128]{1,0:T(8,128)}, f32[32,8,128]{2,1,0:T(8,128)}) custom-call(f32[32,8,128]{2,1,0:T(8,128)S(1)} %all-to-all-done.refs_0_, f32[40,128]{1,0:T(8,128)} %get-tuple-element.122.refs_1_.refs_2_.refs_3_.refs_4_.refs_0_, ...), custom_call_target="tpu_custom_call" | custom-call | flops 1 | bytes 1 | tf_op jit(solution)/shard_map/pallas_call | solution.py:205
  30.2 4.5 %all-to-all-start.1 = ((f32[32,8,128]{2,1,0:T(8,128)}), f32[32,8,128]{2,1,0:T(8,128)S(1)}, u32[]{:S(2)}, u32[]{:S(2)}) async-start(f32[32,8,128]{2,1,0:T(8,128)} %get-tuple-element.131), calls=%async_computation.1 | async-start | bytes 262144 | tf_op jit(solution)/shard_map/all_to_all | solution.py:248
  34.7 3.5 %shard_map.300 = (bf16[1024,512]{1,0:T(8,128)(2,1)}, bf16[1024,512]{1,0:T(8,128)(2,1)}) custom-call(f32[512,1024]{1,0:T(8,128)} %bitcast.25, f32[8,128]{1,0:T(8,128)} %get-tuple-element.134.refs_1_.refs_7_.refs_2_), custom_call_target="tpu_custom_call" | custom-call | flops 1 | bytes 1 | tf_op jit(solution)/shard_map/pallas_call | solution.py:205
  38.2 4.6 %all-to-all-done.1.refs_0_ = f32[32,8,128]{2,1,0:T(8,128)S(1)} async-done(((f32[32,8,128]{2,1,0:T(8,128)}), f32[32,8,128]{2,1,0:T(8,128)S(1)}, u32[]{:S(2)}, u32[]{:S(2)}) %all-to-all-start.1) | async-done | bytes 131104 | tf_op jit(solution)/shard_map/all_to_all | solution.py:248
  51.5 5.3 %all-to-all-done.2.refs_0_ = f32[32,8,128]{2,1,0:T(8,128)S(1)} async-done(((f32[32,8,128]{2,1,0:T(8,128)}), f32[32,8,128]{2,1,0:T(8,128)S(1)}, u32[]{:S(2)}, u32[]{:S(2)}) %all-to-all-start.2) | async-done | bytes 131104 | tf_op jit(solution)/shard_map/all_to_all | solution.py:248
  56.8 4.5 %shard_map.303 = (f32[512,256]{1,0:T(8,128)}, f32[512,1024]{1,0:T(8,128)}, f32[8,512]{1,0:T(8,128)}, f32[64,128]{1,0:T(8,128)}, f32[64,128]{1,0:T(8,128)}, /*ind...) custom-call(f32[32,8,128]{2,1,0:T(8,128)S(1)} %all-to-all-done.2.refs_0_, ...), custom_call_target="tpu_custom_call" | custom-call | flops 1 | bytes 1 | tf_op jit(solution)/shard_map/pallas_call | solution.py:205
  74.2 5.8 %shard_map.304 = (f32[512,1024]{1,0:T(8,128)}, f32[16,128]{1,0:T(8,128)}, f32[8,1024]{1,0:T(8,128)S(1)}, f32[32,16,128]{2,1,0:T(8,128)}) custom-call(f32[32,16,128]{2,1,0:T(8,128)S(1)} %all-to-all-done.3.refs_0_, f32[32,128]{1,0:T(8,128)} %get-tuple-element.132.refs_1_, f32[40,128]{1,0:T(8,128)} %get-tuple-element.122.refs_1_.refs_2_.refs_3_.refs_4_.refs_0_, ...), custom_call_target="tpu_custom_call" | custom-call | flops 1 | bytes 1 | tf_op jit(solution)/shard_map/pallas_call | solution.py:205
  82.6 3.7 %collective-permute-start.7 = (f32[8,1024]{1,0:T(8,128)S(1)}, f32[8,1024]{1,0:T(8,128)S(1)}, u32[]{:S(2)}, u32[]{:S(2)}) collective-permute-start(f32[8,1024]{1,0:T(8,128)S(1)} %get-tuple-element.150.refs_14_), channel_id=1, source_target_pairs={{0,6},{1,7},{2,4},{3,5},{4,2},{5,3},{6,0},{7,1},{8,14},{9,15},{10,... | collective-permute-start | bytes 98312 | tf_op jit(solution)/shard_map/ppermute | solution.py:259
  87.1 4.0 %shard_map.305 = (bf16[2,1152,512]{2,1,0:T(8,128)(2,1)}, bf16[2,1152,512]{2,1,0:T(8,128)(2,1)}) custom-call(f32[768,256]{1,0:T(8,128)} %get-tuple-element.151.refs_0_, f32[16,128]{1,0:T(8,128)} %get-tuple-element.144.refs_1_.refs_2_.refs_0_), custom_call_target="tpu_custom_call" | custom-call | flops 1 | bytes 1 | tf_op jit(solution)/shard_map/pallas_call | solution.py:205
  94.8 6.7 %shard_map.306 = (f32[512,256]{1,0:T(8,128)}, f32[8,256]{1,0:T(8,128)}, f32[16,128]{1,0:T(8,128)}, f32[8,128]{1,0:T(8,128)}, f32[8,128]{1,0:T(8,128)}, /*index=5*/f32[32,1024]{1,0:T(8,128)S(1)}, f32[32,16,128]{2,1,0:T(8,128)}) custom-call(f32[32,16,128]{2,1,0:T(8,128)S(1)} %all-to-all-done.4.refs_0_, f32[8,128]{1,0:T(8,128)} %get-tuple-element.134.refs_1_.refs_7_.refs_2_, ...), custom_call_target="tpu_custom_call" | custom-call | flops 1 | bytes 1 | tf_op jit(solution)/shard_map/pallas_call | solution.py:205
  101.5 3.6 %all-to-all-start.5 = ((f32[32,16,128]{2,1,0:T(8,128)}), f32[32,16,128]{2,1,0:T(8,128)S(1)}, u32[]{:S(2)}, u32[]{:S(2)}) async-start(f32[32,16,128]{2,1,0:T(8,128)} %get-tuple-element.159), calls=%async_computation.5 | async-start | bytes 524288 | tf_op jit(solution)/shard_map/all_to_all | solution.py:248
  105.4 5.2 %shard_map.307 = (f32[512,256]{1,0:T(8,128)}, f32[512,256]{1,0:T(8,128)}, f32[128,256]{1,0:T(8,128)}) custom-call(f32[16,128]{1,0:T(8,128)} %get-tuple-element.153.refs_0_, f32[8,128]{1,0:T(8,128)} %get-tuple-element.134.refs_1_.refs_7_.refs_2_, f32[16,128]{1,0:T(8,128)} %get-tuple-element.144.refs_1_.refs_2_.refs_0_, ...), custom_call_target="tpu_custom_call" | custom-call | flops 1 | bytes 1 | tf_op jit(solution)/shard_map/pallas_call | solution.py:205
  110.7 4.8 %all-to-all-done.5.refs_0_ = f32[32,16,128]{2,1,0:T(8,128)S(1)} async-done(((f32[32,16,128]{2,1,0:T(8,128)}), f32[32,16,128]{2,1,0:T(8,128)S(1)}, u32[]{:S(2)}, u32[]{:S(2)}) %all-to-all-start.5) | async-done | bytes 262176 | tf_op jit(solution)/shard_map/all_to_all | solution.py:248
  115.5 4.1 %shard_map.308 = (f32[128,256]{1,0:T(8,128)S(1)}, f32[128,256]{1,0:T(8,128)S(1)}, bf16[8,6,16,256]{3,2,1,0:T(8,128)(2,1)}, bf16[8,6,16,256]{3,2,1,0:T(8,128)(2,1...) custom-call(f32[32,16,128]{2,1,0:T(8,128)S(1)} %all-to-all-done.5.re, ...), custom_call_target="tpu_custom_call" | custom-call | flops 1 | bytes 1 | tf_op jit(solution)/shard_map/pallas_call | solution.py:205
  123.5 5.3 %shard_map.309 = (f32[1280,256]{1,0:T(8,128)S(1)}, f32[1280,256]{1,0:T(8,128)S(1)}) custom-call(bf16[8,6,16,256]{3,2,1,0:T(8,128)(2,1)} %get-tuple-element.167.refs_0_.refs_6_, bf16[8,6,16,256]{3,2,1,0:T(8,128)(2,1)} %get-tuple-element.168.refs_1_.refs_7_, bf16[8,6,16,256]{3,2,1,0:T(8,128)(2,1)} %get-tuple-element.169.refs_2_.refs_6_, ...), custom_call_target="tpu_custom_call" | custom-call | flops 1 | bytes 1 | tf_op jit(solution)/shard_map/pallas_call | solution.py:205
  130.8 4.1 %shard_map.311 = (f32[512,128]{1,0:T(8,128)}, f32[8,128]{1,0:T(8,128)}) custom-call(f32[40,128]{1,0:T(8,128)} %get-tuple-element.122.refs_1_.refs_2_.refs_3_.refs_4_.refs_0_, f32[8,128]{1,0:T(8,128)} %get-tuple-element.134.refs_1_.refs_7_.refs_2_, f32[512,256]{1,0:T(8,128)} %get-tuple-element.121.refs_12_.refs_2_.refs_5_, ...), custom_call_target="tpu_custom_call" | custom-call | flops 1 | bytes 1 | tf_op jit(solution)/shard_map/pallas_call | solution.py:205
  138.8 4.8 %shard_map.313 = (f32[512,128]{1,0:T(8,128)}, f32[32,8,128]{2,1,0:T(8,128)}) custom-call(f32[40,128]{1,0:T(8,128)} %get-tuple-element.122.refs_1_.refs_2_.refs_3_.refs_4_.refs_0_, f32[8,128]{1,0:T(8,128)} %get-tuple-element.134.refs_1_.refs_7_.refs_2_, f32[512,256]{1,0:T(8,128)} %get-tuple-element.121.refs_12_.refs_2_.refs_5_, ...), custom_call_target="tpu_custom_call" | custom-call | flops 1 | bytes 1 | tf_op jit(solution)/shard_map/pallas_call | solution.py:205
  168.6 4.2 %shard_map.318.refs_4_ = f32[512,1024]{1,0:T(8,128)} custom-call(bf16[512,256]{1,0:T(8,128)(2,1)} %get-tuple-element.197.refs_0_, bf16[512,256]{1,0:T(8,128)(2,1)} %get-tuple-element.198.refs_1_, bf16[1024,256]{1,0:T(8,128)(2,1)} %get-tuple-element.199.refs_2_, bf16[1024,256]{1,0:T(8,128)(2,1)} %get-tuple-element.200.refs_3_, ...), custom_call_target="tpu_custom_call" | custom-call | flops 1 | bytes 1 | tf_op jit(solution)/shard_map/pallas_call | solution.py:205
  180.6 3.7 %shard_map.321 = (f32[512,1024]{1,0:T(8,128)}, f32[8,128]{1,0:T(8,128)}) custom-call(f32[16,128]{1,0:T(8,128)} %get-tuple-element.144.refs_1_.refs_2_.refs_0_, f32[40,128]{1,0:T(8,128)} %get-tuple-element.122.refs_1_.refs_2_.refs_3_.refs_4_.refs_0_, f32[512,128]{1,0:T(8,128)} %get-tuple-element.126.refs_6_.refs_4_.refs_3_.refs_7_.refs_14_.refs_2_, ...), custom_call_target="tpu_custom_call" | custom-call | flops 1 | bytes 1 | tf_op jit(solution)/shard_map/pallas_call | solution.py:205
  184.3 4.0 %collective-permute-done.25.refs_2_ = f32[112,256]{1,0:T(8,128)S(1)} collective-permute-done((f32[112,256]{1,0:T(8,128)S(1)}, f32[112,256]{1,0:T(8,128)S(1)}, u32[]{:S(2)}, u32[]{:S(2)}) %collective-permute-start.25) | collective-permute-done | bytes 114720 | tf_op jit(solution)/shard_map/ppermute | solution.py:259
  (109 shorter events, 108.0 us)
Async XLA Ops:
  5.1 19.2 %all-to-all-start = ((f32[32,8,128]{2,1,0:T(8,128)}), f32[32,8,128]{2,1,0:T(8,128)S(1)}, u32[]{:S(2)}, u32[]{:S(2)}) async-start(f32[32,8,128]{2,1,0:T(8,128)} %get-tuple-element.120), calls=%async_computation | async-start | bytes 262144 | tf_op jit(solution)/shard_map/all_to_all | solution.py:248
  12.4 9.6 %collective-permute-start = (f32[128,256]{1,0:T(8,128)S(1)}, f32[128,256]{1,0:T(8,128)S(1)}, u32[]{:S(2)}, u32[]{:S(2)}) collective-permute-start(f32[128,256]{1,0:T(8,128)S(1)} %get-tuple-element.124), channel_id=1, source_target_pairs={{0,8},{8,16},{16,24},{1,9},{9,17},{17,25},{2,10},{10,18},{18,26},{... | collective-permute-start | bytes 393224 | tf_op jit(solution)/shard_map/ppermute | solution.py:253
  16.1 8.2 %collective-permute-start.1 = (f32[128,256]{1,0:T(8,128)S(1)}, f32[128,256]{1,0:T(8,128)S(1)}, u32[]{:S(2)}, u32[]{:S(2)}) collective-permute-start(f32[128,256]{1,0:T(8,128)S(1)} %get-tuple-element.125), channel_id=1, source_target_pairs={{8,0},{16,8},{24,16},{9,1},{17,9},{25,17},{10,2},{18,10},{26,18},{... | collective-permute-start | bytes 393224 | tf_op jit(solution)/shard_map/ppermute | solution.py:254
  30.2 12.6 %all-to-all-start.1 = ((f32[32,8,128]{2,1,0:T(8,128)}), f32[32,8,128]{2,1,0:T(8,128)S(1)}, u32[]{:S(2)}, u32[]{:S(2)}) async-start(f32[32,8,128]{2,1,0:T(8,128)} %get-tuple-element.131), calls=%async_computation.1 | async-start | bytes 262144 | tf_op jit(solution)/shard_map/all_to_all | solution.py:248
  46.0 10.8 %all-to-all-start.2 = ((f32[32,8,128]{2,1,0:T(8,128)}), f32[32,8,128]{2,1,0:T(8,128)S(1)}, u32[]{:S(2)}, u32[]{:S(2)}) async-start(f32[32,8,128]{2,1,0:T(8,128)} %get-tuple-element.136), calls=%async_computation.2 | async-start | bytes 262144 | tf_op jit(solution)/shard_map/all_to_all | solution.py:248
  61.2 13.0 %all-to-all-start.3 = ((f32[32,16,128]{2,1,0:T(8,128)}), f32[32,16,128]{2,1,0:T(8,128)S(1)}, u32[]{:S(2)}, u32[]{:S(2)}) async-start(f32[32,16,128]{2,1,0:T(8,128)} %get-tuple-element.142), calls=%async_computation.3 | async-start | bytes 524288 | tf_op jit(solution)/shard_map/all_to_all | solution.py:248
  80.0 14.8 %all-to-all-start.4 = ((f32[32,16,128]{2,1,0:T(8,128)}), f32[32,16,128]{2,1,0:T(8,128)S(1)}, u32[]{:S(2)}, u32[]{:S(2)}) async-start(f32[32,16,128]{2,1,0:T(8,128)} %get-tuple-element.145), calls=%async_computation.4 | async-start | bytes 524288 | tf_op jit(solution)/shard_map/all_to_all | solution.py:248
  82.6 10.1 %collective-permute-start.7 = (f32[8,1024]{1,0:T(8,128)S(1)}, f32[8,1024]{1,0:T(8,128)S(1)}, u32[]{:S(2)}, u32[]{:S(2)}) collective-permute-start(f32[8,1024]{1,0:T(8,128)S(1)} %get-tuple-element.150.refs_14_), channel_id=1, source_target_pairs={{0,6},{1,7},{2,4},{3,5},{4,2},{5,3},{6,0},{7,1},{8,14},{9,15},{10,... | collective-permute-start | bytes 98312 | tf_op jit(solution)/shard_map/ppermute | solution.py:259
  86.3 8.5 %collective-permute-start.6 = (f32[8,1024]{1,0:T(8,128)S(1)}, f32[8,1024]{1,0:T(8,128)S(1)}, u32[]{:S(2)}, u32[]{:S(2)}) collective-permute-start(f32[8,1024]{1,0:T(8,128)S(1)} %get-tuple-element.150.refs_14_), channel_id=1, source_target_pairs={{0,4},{1,5},{2,6},{3,7},{4,0},{5,1},{6,2},{7,3},{8,12},{9,13},{10,... | collective-permute-start | bytes 98312 | tf_op jit(solution)/shard_map/ppermute | solution.py:259
  86.3 8.5 %collective-permute-start.5 = (f32[8,1024]{1,0:T(8,128)S(1)}, f32[8,1024]{1,0:T(8,128)S(1)}, u32[]{:S(2)}, u32[]{:S(2)}) collective-permute-start(f32[8,1024]{1,0:T(8,128)S(1)} %get-tuple-element.150.refs_14_), channel_id=1, source_target_pairs={{0,2},{1,3},{2,0},{3,1},{4,6},{5,7},{6,4},{7,5},{8,10},{9,11},{10,... | collective-permute-start | bytes 98312 | tf_op jit(solution)/shard_map/ppermute | solution.py:259
  101.5 13.9 %all-to-all-start.5 = ((f32[32,16,128]{2,1,0:T(8,128)}), f32[32,16,128]{2,1,0:T(8,128)S(1)}, u32[]{:S(2)}, u32[]{:S(2)}) async-start(f32[32,16,128]{2,1,0:T(8,128)} %get-tuple-element.159), calls=%async_computation.5 | async-start | bytes 524288 | tf_op jit(solution)/shard_map/all_to_all | solution.py:248
  119.5 9.3 %collective-permute-start.10 = (f32[128,256]{1,0:T(8,128)S(1)}, f32[128,256]{1,0:T(8,128)S(1)}, u32[]{:S(2)}, u32[]{:S(2)}) collective-permute-start(f32[128,256]{1,0:T(8,128)S(1)} %get-tuple-element.175), channel_id=1, source_target_pairs={{0,8},{8,16},{16,24},{1,9},{9,17},{17,25},{2,10},{10,18},{18,26},{... | collective-permute-start | bytes 393224 | tf_op jit(solution)/shard_map/ppermute | solution.py:253
  122.0 8.3 %collective-permute-start.11 = (f32[128,256]{1,0:T(8,128)S(1)}, f32[128,256]{1,0:T(8,128)S(1)}, u32[]{:S(2)}, u32[]{:S(2)}) collective-permute-start(f32[128,256]{1,0:T(8,128)S(1)} %get-tuple-element.176), channel_id=1, source_target_pairs={{8,0},{16,8},{24,16},{9,1},{17,9},{25,17},{10,2},{18,10},{26,18},{... | collective-permute-start | bytes 393224 | tf_op jit(solution)/shard_map/ppermute | solution.py:254
  135.9 13.1 %collective-permute-start.13 = (f32[448,256]{1,0:T(8,128)}, f32[448,256]{1,0:T(8,128)S(1)}, u32[]{:S(2)}, u32[]{:S(2)}) collective-permute-start(f32[448,256]{1,0:T(8,128)} %get-tuple-element.179), channel_id=1, source_target_pairs={{0,8},{8,0},{16,24},{24,16},{1,9},{9,1},{17,25},{25,17},{2,10},{10... | collective-permute-start | bytes 1376264 | tf_op jit(solution)/shard_map/ppermute | solution.py:259
  137.9 12.5 %collective-permute-start.14 = (f32[448,256]{1,0:T(8,128)S(1)}, f32[448,256]{1,0:T(8,128)S(1)}, u32[]{:S(2)}, u32[]{:S(2)}) collective-permute-start(f32[448,256]{1,0:T(8,128)S(1)} %get-tuple-element.181), channel_id=1, source_target_pairs={{0,16},{8,24},{16,0},{24,8},{1,17},{9,25},{17,1},{25,9},{2,18},{10... | collective-permute-start | bytes 1376264 | tf_op jit(solution)/shard_map/ppermute | solution.py:259
  143.6 11.1 %all-to-all-start.6 = ((f32[32,8,128]{2,1,0:T(8,128)}), f32[32,8,128]{2,1,0:T(8,128)S(1)}, u32[]{:S(2)}, u32[]{:S(2)}) async-start(f32[32,8,128]{2,1,0:T(8,128)} %get-tuple-element.187), calls=%async_computation.6 | async-start | bytes 262144 | tf_op jit(solution)/shard_map/all_to_all | solution.py:248
  159.5 16.6 %all-to-all-start.7 = ((f32[4,112,256]{2,1,0:T(8,128)}), f32[4,112,256]{2,1,0:T(8,128)S(1)}, u32[]{:S(2)}, u32[]{:S(2)}) async-start(f32[4,112,256]{2,1,0:T(8,128)} %shard_map.316), calls=%async_computation.7 | async-start | bytes 917504 | tf_op jit(solution)/shard_map/all_to_all | solution.py:280
  176.2 8.1 %collective-permute-start.26 = (f32[112,256]{1,0:T(8,128)S(1)}, f32[112,256]{1,0:T(8,128)S(1)}, u32[]{:S(2)}, u32[]{:S(2)}) collective-permute-start(f32[112,256]{1,0:T(8,128)S(1)} %shard_map.320.refs_5_.refs_0_), channel_id=1, source_target_pairs={{0,6},{1,7},{2,4},{3,5},{4,2},{5,3},{6,0},{7,1},{8,14},{9,15},{10,... | collective-permute-start | bytes 344072 | tf_op jit(solution)/shard_map/ppermute | solution.py:259
  178.5 9.8 %collective-permute-start.25 = (f32[112,256]{1,0:T(8,128)S(1)}, f32[112,256]{1,0:T(8,128)S(1)}, u32[]{:S(2)}, u32[]{:S(2)}) collective-permute-start(f32[112,256]{1,0:T(8,128)S(1)} %shard_map.320.refs_5_.refs_0_), channel_id=1, source_target_pairs={{0,4},{1,5},{2,6},{3,7},{4,0},{5,1},{6,2},{7,3},{8,12},{9,13},{10,... | collective-permute-start | bytes 344072 | tf_op jit(solution)/shard_map/ppermute | solution.py:259
  178.5 9.8 %collective-permute-start.24 = (f32[112,256]{1,0:T(8,128)S(1)}, f32[112,256]{1,0:T(8,128)S(1)}, u32[]{:S(2)}, u32[]{:S(2)}) collective-permute-start(f32[112,256]{1,0:T(8,128)S(1)} %shard_map.320.refs_5_.refs_0_), channel_id=1, source_target_pairs={{0,2},{1,3},{2,0},{3,1},{4,6},{5,7},{6,4},{7,5},{8,10},{9,11},{10,... | collective-permute-start | bytes 344072 | tf_op jit(solution)/shard_map/ppermute | solution.py:259
  188.4 10.1 %collective-permute-start.31 = (f32[224,256]{1,0:T(8,128)S(1)}, f32[224,256]{1,0:T(8,128)S(1)}, u32[]{:S(2)}, u32[]{:S(2)}) collective-permute-start(f32[224,256]{1,0:T(8,128)S(1)} %get-tuple-element.208.refs_2_), channel_id=1, source_target_pairs={{0,8},{8,0},{16,24},{24,16},{1,9},{9,1},{17,25},{25,17},{2,10},{10... | collective-permute-start | bytes 688136 | tf_op jit(solution)/shard_map/ppermute | solution.py:259
  188.4 10.0 %collective-permute-start.30 = (f32[224,256]{1,0:T(8,128)S(1)}, f32[224,256]{1,0:T(8,128)S(1)}, u32[]{:S(2)}, u32[]{:S(2)}) collective-permute-start(f32[224,256]{1,0:T(8,128)S(1)} %get-tuple-element.207.refs_4_.refs_0_), channel_id=1, source_target_pairs={{0,16},{8,24},{16,0},{24,8},{1,17},{9,25},{17,1},{25,9},{2,18},{10... | collective-permute-start | bytes 688136 | tf_op jit(solution)/shard_map/ppermute | solution.py:259
  198.5 9.4 %collective-permute-start.36 = (f32[448,256]{1,0:T(8,128)S(1)}, f32[448,256]{1,0:T(8,128)S(1)}, u32[]{:S(2)}, u32[]{:S(2)}) collective-permute-start(f32[448,256]{1,0:T(8,128)S(1)} %get-tuple-element.210.refs_2_), channel_id=1, source_target_pairs={{0,16},{8,24},{16,0},{24,8},{1,17},{9,25},{17,1},{25,9},{2,18},{10... | collective-permute-start | bytes 1376264 | tf_op jit(solution)/shard_map/ppermute | solution.py:259
  199.3 9.0 %collective-permute-start.35 = (f32[448,256]{1,0:T(8,128)S(1)}, f32[448,256]{1,0:T(8,128)S(1)}, u32[]{:S(2)}, u32[]{:S(2)}) collective-permute-start(f32[448,256]{1,0:T(8,128)S(1)} %get-tuple-element.209.refs_4_.refs_0_), channel_id=1, source_target_pairs={{0,8},{8,0},{16,24},{24,16},{1,9},{9,1},{17,25},{25,17},{2,10},{10... | collective-permute-start | bytes 1376264 | tf_op jit(solution)/shard_map/ppermute | solution.py:259
  (26 other events, 145.2 us)

commit v7 on v6

--- a/solution.py
+++ b/solution.py
@@ -1036,8 +1036,8 @@
         [((cells, chan), f32), ((16, 128), f32), ((count, 2 * duo), f32), pay16],
         [g4, counts, par, own, z_three, x, cot, *slopes],
         [tile16],
-        chunks={3: 4, 4: 4, 5: 4, 6: 4},
-        out_chunks={0: 4},
+        chunks={3: 2, 4: 2, 5: 2, 6: 2},
+        out_chunks={0: 2},
         near=(0, *range(7, 7 + line.size)),
         near_outs=(2, 3),
     )

time: 222 us -> 222 us (level)
  no operation moved by 1% of the time
where the time goes in v7:
time: 222 us; the launch traced here: 221 us
  Pallas kernels  85.3 us (38%)
  starting transfers between devices  78.7 us (35%)
  waiting for transfers between devices  55.8 us (25%)
    pallas_call x20, Pallas kernels, call(): pl.pallas_call(inner, out_shape=[(pltpu.VMEM if i in near_outs else pltpu...  83 us
    ppermute x35, starting transfers between devices, flip(): lax.ppermute(values, axis, [(i, i ^ bits) for i in range(lax.axis_size(ax...  40.1 us
    ppermute x35, waiting for transfers between devices, flip(): lax.ppermute(values, axis, [(i, i ^ bits) for i in range(lax.axis_size(ax...  32.3 us
    all_to_all x7, starting transfers between devices, share(): return lax.all_to_all(tile, both, 0, 0)  26.2 us
    all_to_all x7, waiting for transfers between devices, share(): return lax.all_to_all(tile, both, 0, 0)  18.3 us
    ppermute x2, starting transfers between devices, halos(): above = lax.ppermute(last, 'rows', [(i, i + 1) for i in range(count - 1)])  6.09 us
  transfers between devices with their start and end apart: 47, of which 29 were waited for; matrix products, arithmetic and copies ran while one was open for 0% of the time, Pallas kernels for 22%

profile of v7, /device:TPU:0, one launch (start us, length us, event | category | flops | bytes accessed | tf_op | source)
XLA Modules:
  0.0 221.1 jit_solution(8944304290179792530)
XLA Ops:
  0.6 4.5 %shard_map.297 = (f32[512,256]{1,0:T(8,128)}, f32[8,6,16,128]{3,2,1,0:T(8,128)}, f32[512,128]{1,0:T(8,128)}, f32[128,256]{1,0:T(8,128)S(1)}, f32[128,256]{1,0:T(8,128)S(1)}, /*index=5*/f32[32,8,128]{2,1,0:T(8,128)}) custom-call(s32[8,16]{1,0:T(8,128)} %refs_9_.1, s32[8,16]{1,0:T(8,128)} %refs_10_.1, f32[1024,256]{1,0:T(8,128)} %refs_2_.5, f32[512,1024]{1,0:T(8,128)} %bitcast.24), custom_call_target="tpu_custom_call" | custom-call | flops 1 | bytes 1 | tf_op jit(solution)/shard_map/pallas_call | solution.py:205
  5.1 7.3 %all-to-all-start = ((f32[32,8,128]{2,1,0:T(8,128)}), f32[32,8,128]{2,1,0:T(8,128)S(1)}, u32[]{:S(2)}, u32[]{:S(2)}) async-start(f32[32,8,128]{2,1,0:T(8,128)} %get-tuple-element.120), calls=%async_computation | async-start | bytes 262144 | tf_op jit(solution)/shard_map/all_to_all | solution.py:248
  12.4 3.7 %collective-permute-start = (f32[128,256]{1,0:T(8,128)S(1)}, f32[128,256]{1,0:T(8,128)S(1)}, u32[]{:S(2)}, u32[]{:S(2)}) collective-permute-start(f32[128,256]{1,0:T(8,128)S(1)} %get-tuple-element.124), channel_id=1, source_target_pairs={{0,8},{8,16},{16,24},{1,9},{9,17},{17,25},{2,10},{10,18},{18,26},{... | collective-permute-start | bytes 393224 | tf_op jit(solution)/shard_map/ppermute | solution.py:253
  17.4 4.6 %shard_map.298 = (bf16[1152,256]{1,0:T(8,128)(2,1)}, bf16[1152,256]{1,0:T(8,128)(2,1)}, bf16[1152,256]{1,0:T(8,128)(2,1)}, bf16[1152,256]{1,0:T(8,128)(2,1)}, bf...) custom-call(f32[1152,512]{1,0:T(8,128)} %bitcast.29, ...), custom_call_target="tpu_custom_call" | custom-call | flops 1 | bytes 1 | tf_op jit(solution)/shard_map/pallas_call | solution.py:205
  24.3 5.9 %shard_map.299 = (f32[512,512]{1,0:T(8,128)}, f32[768,256]{1,0:T(8,128)}, f32[8,128]{1,0:T(8,128)}, f32[32,128]{1,0:T(8,128)}, f32[32,8,128]{2,1,0:T(8,128)}) custom-call(f32[32,8,128]{2,1,0:T(8,128)S(1)} %all-to-all-done.refs_0_, f32[40,128]{1,0:T(8,128)} %get-tuple-element.122.refs_1_.refs_2_.refs_3_.refs_4_.refs_0_, ...), custom_call_target="tpu_custom_call" | custom-call | flops 1 | bytes 1 | tf_op jit(solution)/shard_map/pallas_call | solution.py:205
  30.2 4.5 %all-to-all-start.1 = ((f32[32,8,128]{2,1,0:T(8,128)}), f32[32,8,128]{2,1,0:T(8,128)S(1)}, u32[]{:S(2)}, u32[]{:S(2)}) async-start(f32[32,8,128]{2,1,0:T(8,128)} %get-tuple-element.131), calls=%async_computation.1 | async-start | bytes 262144 | tf_op jit(solution)/shard_map/all_to_all | solution.py:248
  34.7 3.5 %shard_map.300 = (bf16[1024,512]{1,0:T(8,128)(2,1)}, bf16[1024,512]{1,0:T(8,128)(2,1)}) custom-call(f32[512,1024]{1,0:T(8,128)} %bitcast.25, f32[8,128]{1,0:T(8,128)} %get-tuple-element.134.refs_1_.refs_7_.refs_2_), custom_call_target="tpu_custom_call" | custom-call | flops 1 | bytes 1 | tf_op jit(solution)/shard_map/pallas_call | solution.py:205
  38.2 4.6 %all-to-all-done.1.refs_0_ = f32[32,8,128]{2,1,0:T(8,128)S(1)} async-done(((f32[32,8,128]{2,1,0:T(8,128)}), f32[32,8,128]{2,1,0:T(8,128)S(1)}, u32[]{:S(2)}, u32[]{:S(2)}) %all-to-all-start.1) | async-done | bytes 131104 | tf_op jit(solution)/shard_map/all_to_all | solution.py:248
  51.5 5.3 %all-to-all-done.2.refs_0_ = f32[32,8,128]{2,1,0:T(8,128)S(1)} async-done(((f32[32,8,128]{2,1,0:T(8,128)}), f32[32,8,128]{2,1,0:T(8,128)S(1)}, u32[]{:S(2)}, u32[]{:S(2)}) %all-to-all-start.2) | async-done | bytes 131104 | tf_op jit(solution)/shard_map/all_to_all | solution.py:248
  56.8 4.5 %shard_map.303 = (f32[512,256]{1,0:T(8,128)}, f32[512,1024]{1,0:T(8,128)}, f32[8,512]{1,0:T(8,128)}, f32[64,128]{1,0:T(8,128)}, f32[64,128]{1,0:T(8,128)}, /*ind...) custom-call(f32[32,8,128]{2,1,0:T(8,128)S(1)} %all-to-all-done.2.refs_0_, ...), custom_call_target="tpu_custom_call" | custom-call | flops 1 | bytes 1 | tf_op jit(solution)/shard_map/pallas_call | solution.py:205
  74.2 5.5 %shard_map.304 = (f32[512,1024]{1,0:T(8,128)}, f32[16,128]{1,0:T(8,128)}, f32[8,1024]{1,0:T(8,128)S(1)}, f32[32,16,128]{2,1,0:T(8,128)}) custom-call(f32[32,16,128]{2,1,0:T(8,128)S(1)} %all-to-all-done.3.refs_0_, f32[32,128]{1,0:T(8,128)} %get-tuple-element.132.refs_1_, f32[40,128]{1,0:T(8,128)} %get-tuple-element.122.refs_1_.refs_2_.refs_3_.refs_4_.refs_0_, ...), custom_call_target="tpu_custom_call" | custom-call | flops 1 | bytes 1 | tf_op jit(solution)/shard_map/pallas_call | solution.py:205
  82.3 3.7 %collective-permute-start.7 = (f32[8,1024]{1,0:T(8,128)S(1)}, f32[8,1024]{1,0:T(8,128)S(1)}, u32[]{:S(2)}, u32[]{:S(2)}) collective-permute-start(f32[8,1024]{1,0:T(8,128)S(1)} %get-tuple-element.150.refs_14_), channel_id=1, source_target_pairs={{0,6},{1,7},{2,4},{3,5},{4,2},{5,3},{6,0},{7,1},{8,14},{9,15},{10,... | collective-permute-start | bytes 98312 | tf_op jit(solution)/shard_map/ppermute | solution.py:259
  86.8 4.0 %shard_map.305 = (bf16[2,1152,512]{2,1,0:T(8,128)(2,1)}, bf16[2,1152,512]{2,1,0:T(8,128)(2,1)}) custom-call(f32[768,256]{1,0:T(8,128)} %get-tuple-element.151.refs_0_, f32[16,128]{1,0:T(8,128)} %get-tuple-element.144.refs_1_.refs_2_.refs_0_), custom_call_target="tpu_custom_call" | custom-call | flops 1 | bytes 1 | tf_op jit(solution)/shard_map/pallas_call | solution.py:205
  94.5 6.7 %shard_map.306 = (f32[512,256]{1,0:T(8,128)}, f32[8,256]{1,0:T(8,128)}, f32[16,128]{1,0:T(8,128)}, f32[8,128]{1,0:T(8,128)}, f32[8,128]{1,0:T(8,128)}, /*index=5*/f32[32,1024]{1,0:T(8,128)S(1)}, f32[32,16,128]{2,1,0:T(8,128)}) custom-call(f32[32,16,128]{2,1,0:T(8,128)S(1)} %all-to-all-done.4.refs_0_, f32[8,128]{1,0:T(8,128)} %get-tuple-element.134.refs_1_.refs_7_.refs_2_, ...), custom_call_target="tpu_custom_call" | custom-call | flops 1 | bytes 1 | tf_op jit(solution)/shard_map/pallas_call | solution.py:205
  101.2 3.6 %all-to-all-start.5 = ((f32[32,16,128]{2,1,0:T(8,128)}), f32[32,16,128]{2,1,0:T(8,128)S(1)}, u32[]{:S(2)}, u32[]{:S(2)}) async-start(f32[32,16,128]{2,1,0:T(8,128)} %get-tuple-element.159), calls=%async_computation.5 | async-start | bytes 524288 | tf_op jit(solution)/shard_map/all_to_all | solution.py:248
  105.1 5.2 %shard_map.307 = (f32[512,256]{1,0:T(8,128)}, f32[512,256]{1,0:T(8,128)}, f32[128,256]{1,0:T(8,128)}) custom-call(f32[16,128]{1,0:T(8,128)} %get-tuple-element.153.refs_0_, f32[8,128]{1,0:T(8,128)} %get-tuple-element.134.refs_1_.refs_7_.refs_2_, f32[16,128]{1,0:T(8,128)} %get-tuple-element.144.refs_1_.refs_2_.refs_0_, ...), custom_call_target="tpu_custom_call" | custom-call | flops 1 | bytes 1 | tf_op jit(solution)/shard_map/pallas_call | solution.py:205
  110.3 4.8 %all-to-all-done.5.refs_0_ = f32[32,16,128]{2,1,0:T(8,128)S(1)} async-done(((f32[32,16,128]{2,1,0:T(8,128)}), f32[32,16,128]{2,1,0:T(8,128)S(1)}, u32[]{:S(2)}, u32[]{:S(2)}) %all-to-all-start.5) | async-done | bytes 262176 | tf_op jit(solution)/shard_map/all_to_all | solution.py:248
  115.1 4.1 %shard_map.308 = (f32[128,256]{1,0:T(8,128)S(1)}, f32[128,256]{1,0:T(8,128)S(1)}, bf16[8,6,16,256]{3,2,1,0:T(8,128)(2,1)}, bf16[8,6,16,256]{3,2,1,0:T(8,128)(2,1...) custom-call(f32[32,16,128]{2,1,0:T(8,128)S(1)} %all-to-all-done.5.re, ...), custom_call_target="tpu_custom_call" | custom-call | flops 1 | bytes 1 | tf_op jit(solution)/shard_map/pallas_call | solution.py:205
  123.2 5.3 %shard_map.309 = (f32[1280,256]{1,0:T(8,128)S(1)}, f32[1280,256]{1,0:T(8,128)S(1)}) custom-call(bf16[8,6,16,256]{3,2,1,0:T(8,128)(2,1)} %get-tuple-element.167.refs_0_.refs_6_, bf16[8,6,16,256]{3,2,1,0:T(8,128)(2,1)} %get-tuple-element.168.refs_1_.refs_7_, bf16[8,6,16,256]{3,2,1,0:T(8,128)(2,1)} %get-tuple-element.169.refs_2_.refs_6_, ...), custom_call_target="tpu_custom_call" | custom-call | flops 1 | bytes 1 | tf_op jit(solution)/shard_map/pallas_call | solution.py:205
  130.5 4.1 %shard_map.311 = (f32[512,128]{1,0:T(8,128)}, f32[8,128]{1,0:T(8,128)}) custom-call(f32[40,128]{1,0:T(8,128)} %get-tuple-element.122.refs_1_.refs_2_.refs_3_.refs_4_.refs_0_, f32[8,128]{1,0:T(8,128)} %get-tuple-element.134.refs_1_.refs_7_.refs_2_, f32[512,256]{1,0:T(8,128)} %get-tuple-element.121.refs_12_.refs_2_.refs_5_, ...), custom_call_target="tpu_custom_call" | custom-call | flops 1 | bytes 1 | tf_op jit(solution)/shard_map/pallas_call | solution.py:205
  138.5 4.8 %shard_map.313 = (f32[512,128]{1,0:T(8,128)}, f32[32,8,128]{2,1,0:T(8,128)}) custom-call(f32[40,128]{1,0:T(8,128)} %get-tuple-element.122.refs_1_.refs_2_.refs_3_.refs_4_.refs_0_, f32[8,128]{1,0:T(8,128)} %get-tuple-element.134.refs_1_.refs_7_.refs_2_, f32[512,256]{1,0:T(8,128)} %get-tuple-element.121.refs_12_.refs_2_.refs_5_, ...), custom_call_target="tpu_custom_call" | custom-call | flops 1 | bytes 1 | tf_op jit(solution)/shard_map/pallas_call | solution.py:205
  168.2 4.2 %shard_map.318.refs_4_ = f32[512,1024]{1,0:T(8,128)} custom-call(bf16[512,256]{1,0:T(8,128)(2,1)} %get-tuple-element.197.refs_0_, bf16[512,256]{1,0:T(8,128)(2,1)} %get-tuple-element.198.refs_1_, bf16[1024,256]{1,0:T(8,128)(2,1)} %get-tuple-element.199.refs_2_, bf16[1024,256]{1,0:T(8,128)(2,1)} %get-tuple-element.200.refs_3_, ...), custom_call_target="tpu_custom_call" | custom-call | flops 1 | bytes 1 | tf_op jit(solution)/shard_map/pallas_call | solution.py:205
  180.3 3.7 %shard_map.321 = (f32[512,1024]{1,0:T(8,128)}, f32[8,128]{1,0:T(8,128)}) custom-call(f32[16,128]{1,0:T(8,128)} %get-tuple-element.144.refs_1_.refs_2_.refs_0_, f32[40,128]{1,0:T(8,128)} %get-tuple-element.122.refs_1_.refs_2_.refs_3_.refs_4_.refs_0_, f32[512,128]{1,0:T(8,128)} %get-tuple-element.126.refs_6_.refs_4_.refs_3_.refs_7_.refs_14_.refs_2_, ...), custom_call_target="tpu_custom_call" | custom-call | flops 1 | bytes 1 | tf_op jit(solution)/shard_map/pallas_call | solution.py:205
  184.0 4.0 %collective-permute-done.25.refs_2_ = f32[112,256]{1,0:T(8,128)S(1)} collective-permute-done((f32[112,256]{1,0:T(8,128)S(1)}, f32[112,256]{1,0:T(8,128)S(1)}, u32[]{:S(2)}, u32[]{:S(2)}) %collective-permute-start.25) | collective-permute-done | bytes 114720 | tf_op jit(solution)/shard_map/ppermute | solution.py:259
  (109 shorter events, 108.0 us)
Async XLA Ops:
  5.1 19.2 %all-to-all-start = ((f32[32,8,128]{2,1,0:T(8,128)}), f32[32,8,128]{2,1,0:T(8,128)S(1)}, u32[]{:S(2)}, u32[]{:S(2)}) async-start(f32[32,8,128]{2,1,0:T(8,128)} %get-tuple-element.120), calls=%async_computation | async-start | bytes 262144 | tf_op jit(solution)/shard_map/all_to_all | solution.py:248
  12.4 9.6 %collective-permute-start = (f32[128,256]{1,0:T(8,128)S(1)}, f32[128,256]{1,0:T(8,128)S(1)}, u32[]{:S(2)}, u32[]{:S(2)}) collective-permute-start(f32[128,256]{1,0:T(8,128)S(1)} %get-tuple-element.124), channel_id=1, source_target_pairs={{0,8},{8,16},{16,24},{1,9},{9,17},{17,25},{2,10},{10,18},{18,26},{... | collective-permute-start | bytes 393224 | tf_op jit(solution)/shard_map/ppermute | solution.py:253
  16.1 8.2 %collective-permute-start.1 = (f32[128,256]{1,0:T(8,128)S(1)}, f32[128,256]{1,0:T(8,128)S(1)}, u32[]{:S(2)}, u32[]{:S(2)}) collective-permute-start(f32[128,256]{1,0:T(8,128)S(1)} %get-tuple-element.125), channel_id=1, source_target_pairs={{8,0},{16,8},{24,16},{9,1},{17,9},{25,17},{10,2},{18,10},{26,18},{... | collective-permute-start | bytes 393224 | tf_op jit(solution)/shard_map/ppermute | solution.py:254
  30.2 12.6 %all-to-all-start.1 = ((f32[32,8,128]{2,1,0:T(8,128)}), f32[32,8,128]{2,1,0:T(8,128)S(1)}, u32[]{:S(2)}, u32[]{:S(2)}) async-start(f32[32,8,128]{2,1,0:T(8,128)} %get-tuple-element.131), calls=%async_computation.1 | async-start | bytes 262144 | tf_op jit(solution)/shard_map/all_to_all | solution.py:248
  46.0 10.8 %all-to-all-start.2 = ((f32[32,8,128]{2,1,0:T(8,128)}), f32[32,8,128]{2,1,0:T(8,128)S(1)}, u32[]{:S(2)}, u32[]{:S(2)}) async-start(f32[32,8,128]{2,1,0:T(8,128)} %get-tuple-element.136), calls=%async_computation.2 | async-start | bytes 262144 | tf_op jit(solution)/shard_map/all_to_all | solution.py:248
  61.2 13.0 %all-to-all-start.3 = ((f32[32,16,128]{2,1,0:T(8,128)}), f32[32,16,128]{2,1,0:T(8,128)S(1)}, u32[]{:S(2)}, u32[]{:S(2)}) async-start(f32[32,16,128]{2,1,0:T(8,128)} %get-tuple-element.142), calls=%async_computation.3 | async-start | bytes 524288 | tf_op jit(solution)/shard_map/all_to_all | solution.py:248
  79.7 14.8 %all-to-all-start.4 = ((f32[32,16,128]{2,1,0:T(8,128)}), f32[32,16,128]{2,1,0:T(8,128)S(1)}, u32[]{:S(2)}, u32[]{:S(2)}) async-start(f32[32,16,128]{2,1,0:T(8,128)} %get-tuple-element.145), calls=%async_computation.4 | async-start | bytes 524288 | tf_op jit(solution)/shard_map/all_to_all | solution.py:248
  82.3 10.1 %collective-permute-start.7 = (f32[8,1024]{1,0:T(8,128)S(1)}, f32[8,1024]{1,0:T(8,128)S(1)}, u32[]{:S(2)}, u32[]{:S(2)}) collective-permute-start(f32[8,1024]{1,0:T(8,128)S(1)} %get-tuple-element.150.refs_14_), channel_id=1, source_target_pairs={{0,6},{1,7},{2,4},{3,5},{4,2},{5,3},{6,0},{7,1},{8,14},{9,15},{10,... | collective-permute-start | bytes 98312 | tf_op jit(solution)/shard_map/ppermute | solution.py:259
  86.0 8.5 %collective-permute-start.6 = (f32[8,1024]{1,0:T(8,128)S(1)}, f32[8,1024]{1,0:T(8,128)S(1)}, u32[]{:S(2)}, u32[]{:S(2)}) collective-permute-start(f32[8,1024]{1,0:T(8,128)S(1)} %get-tuple-element.150.refs_14_), channel_id=1, source_target_pairs={{0,4},{1,5},{2,6},{3,7},{4,0},{5,1},{6,2},{7,3},{8,12},{9,13},{10,... | collective-permute-start | bytes 98312 | tf_op jit(solution)/shard_map/ppermute | solution.py:259
  86.0 8.5 %collective-permute-start.5 = (f32[8,1024]{1,0:T(8,128)S(1)}, f32[8,1024]{1,0:T(8,128)S(1)}, u32[]{:S(2)}, u32[]{:S(2)}) collective-permute-start(f32[8,1024]{1,0:T(8,128)S(1)} %get-tuple-element.150.refs_14_), channel_id=1, source_target_pairs={{0,2},{1,3},{2,0},{3,1},{4,6},{5,7},{6,4},{7,5},{8,10},{9,11},{10,... | collective-permute-start | bytes 98312 | tf_op jit(solution)/shard_map/ppermute | solution.py:259
  101.2 13.9 %all-to-all-start.5 = ((f32[32,16,128]{2,1,0:T(8,128)}), f32[32,16,128]{2,1,0:T(8,128)S(1)}, u32[]{:S(2)}, u32[]{:S(2)}) async-start(f32[32,16,128]{2,1,0:T(8,128)} %get-tuple-element.159), calls=%async_computation.5 | async-start | bytes 524288 | tf_op jit(solution)/shard_map/all_to_all | solution.py:248
  119.2 9.3 %collective-permute-start.10 = (f32[128,256]{1,0:T(8,128)S(1)}, f32[128,256]{1,0:T(8,128)S(1)}, u32[]{:S(2)}, u32[]{:S(2)}) collective-permute-start(f32[128,256]{1,0:T(8,128)S(1)} %get-tuple-element.175), channel_id=1, source_target_pairs={{0,8},{8,16},{16,24},{1,9},{9,17},{17,25},{2,10},{10,18},{18,26},{... | collective-permute-start | bytes 393224 | tf_op jit(solution)/shard_map/ppermute | solution.py:253
  121.6 8.3 %collective-permute-start.11 = (f32[128,256]{1,0:T(8,128)S(1)}, f32[128,256]{1,0:T(8,128)S(1)}, u32[]{:S(2)}, u32[]{:S(2)}) collective-permute-start(f32[128,256]{1,0:T(8,128)S(1)} %get-tuple-element.176), channel_id=1, source_target_pairs={{8,0},{16,8},{24,16},{9,1},{17,9},{25,17},{10,2},{18,10},{26,18},{... | collective-permute-start | bytes 393224 | tf_op jit(solution)/shard_map/ppermute | solution.py:254
  135.6 13.1 %collective-permute-start.13 = (f32[448,256]{1,0:T(8,128)}, f32[448,256]{1,0:T(8,128)S(1)}, u32[]{:S(2)}, u32[]{:S(2)}) collective-permute-start(f32[448,256]{1,0:T(8,128)} %get-tuple-element.179), channel_id=1, source_target_pairs={{0,8},{8,0},{16,24},{24,16},{1,9},{9,1},{17,25},{25,17},{2,10},{10... | collective-permute-start | bytes 1376264 | tf_op jit(solution)/shard_map/ppermute | solution.py:259
  137.5 12.5 %collective-permute-start.14 = (f32[448,256]{1,0:T(8,128)S(1)}, f32[448,256]{1,0:T(8,128)S(1)}, u32[]{:S(2)}, u32[]{:S(2)}) collective-permute-start(f32[448,256]{1,0:T(8,128)S(1)} %get-tuple-element.181), channel_id=1, source_target_pairs={{0,16},{8,24},{16,0},{24,8},{1,17},{9,25},{17,1},{25,9},{2,18},{10... | collective-permute-start | bytes 1376264 | tf_op jit(solution)/shard_map/ppermute | solution.py:259
  143.3 11.1 %all-to-all-start.6 = ((f32[32,8,128]{2,1,0:T(8,128)}), f32[32,8,128]{2,1,0:T(8,128)S(1)}, u32[]{:S(2)}, u32[]{:S(2)}) async-start(f32[32,8,128]{2,1,0:T(8,128)} %get-tuple-element.187), calls=%async_computation.6 | async-start | bytes 262144 | tf_op jit(solution)/shard_map/all_to_all | solution.py:248
  159.2 16.6 %all-to-all-start.7 = ((f32[4,112,256]{2,1,0:T(8,128)}), f32[4,112,256]{2,1,0:T(8,128)S(1)}, u32[]{:S(2)}, u32[]{:S(2)}) async-start(f32[4,112,256]{2,1,0:T(8,128)} %shard_map.316), calls=%async_computation.7 | async-start | bytes 917504 | tf_op jit(solution)/shard_map/all_to_all | solution.py:280
  175.8 8.1 %collective-permute-start.26 = (f32[112,256]{1,0:T(8,128)S(1)}, f32[112,256]{1,0:T(8,128)S(1)}, u32[]{:S(2)}, u32[]{:S(2)}) collective-permute-start(f32[112,256]{1,0:T(8,128)S(1)} %shard_map.320.refs_5_.refs_0_), channel_id=1, source_target_pairs={{0,6},{1,7},{2,4},{3,5},{4,2},{5,3},{6,0},{7,1},{8,14},{9,15},{10,... | collective-permute-start | bytes 344072 | tf_op jit(solution)/shard_map/ppermute | solution.py:259
  178.2 9.8 %collective-permute-start.25 = (f32[112,256]{1,0:T(8,128)S(1)}, f32[112,256]{1,0:T(8,128)S(1)}, u32[]{:S(2)}, u32[]{:S(2)}) collective-permute-start(f32[112,256]{1,0:T(8,128)S(1)} %shard_map.320.refs_5_.refs_0_), channel_id=1, source_target_pairs={{0,4},{1,5},{2,6},{3,7},{4,0},{5,1},{6,2},{7,3},{8,12},{9,13},{10,... | collective-permute-start | bytes 344072 | tf_op jit(solution)/shard_map/ppermute | solution.py:259
  178.2 9.8 %collective-permute-start.24 = (f32[112,256]{1,0:T(8,128)S(1)}, f32[112,256]{1,0:T(8,128)S(1)}, u32[]{:S(2)}, u32[]{:S(2)}) collective-permute-start(f32[112,256]{1,0:T(8,128)S(1)} %shard_map.320.refs_5_.refs_0_), channel_id=1, source_target_pairs={{0,2},{1,3},{2,0},{3,1},{4,6},{5,7},{6,4},{7,5},{8,10},{9,11},{10,... | collective-permute-start | bytes 344072 | tf_op jit(solution)/shard_map/ppermute | solution.py:259
  188.0 10.1 %collective-permute-start.31 = (f32[224,256]{1,0:T(8,128)S(1)}, f32[224,256]{1,0:T(8,128)S(1)}, u32[]{:S(2)}, u32[]{:S(2)}) collective-permute-start(f32[224,256]{1,0:T(8,128)S(1)} %get-tuple-element.208.refs_2_), channel_id=1, source_target_pairs={{0,8},{8,0},{16,24},{24,16},{1,9},{9,1},{17,25},{25,17},{2,10},{10... | collective-permute-start | bytes 688136 | tf_op jit(solution)/shard_map/ppermute | solution.py:259
  188.1 10.0 %collective-permute-start.30 = (f32[224,256]{1,0:T(8,128)S(1)}, f32[224,256]{1,0:T(8,128)S(1)}, u32[]{:S(2)}, u32[]{:S(2)}) collective-permute-start(f32[224,256]{1,0:T(8,128)S(1)} %get-tuple-element.207.refs_4_.refs_0_), channel_id=1, source_target_pairs={{0,16},{8,24},{16,0},{24,8},{1,17},{9,25},{17,1},{25,9},{2,18},{10... | collective-permute-start | bytes 688136 | tf_op jit(solution)/shard_map/ppermute | solution.py:259
  198.2 9.4 %collective-permute-start.36 = (f32[448,256]{1,0:T(8,128)S(1)}, f32[448,256]{1,0:T(8,128)S(1)}, u32[]{:S(2)}, u32[]{:S(2)}) collective-permute-start(f32[448,256]{1,0:T(8,128)S(1)} %get-tuple-element.210.refs_2_), channel_id=1, source_target_pairs={{0,16},{8,24},{16,0},{24,8},{1,17},{9,25},{17,1},{25,9},{2,18},{10... | collective-permute-start | bytes 1376264 | tf_op jit(solution)/shard_map/ppermute | solution.py:259
  199.0 9.0 %collective-permute-start.35 = (f32[448,256]{1,0:T(8,128)S(1)}, f32[448,256]{1,0:T(8,128)S(1)}, u32[]{:S(2)}, u32[]{:S(2)}) collective-permute-start(f32[448,256]{1,0:T(8,128)S(1)} %get-tuple-element.209.refs_4_.refs_0_), channel_id=1, source_target_pairs={{0,8},{8,0},{16,24},{24,16},{1,9},{9,1},{17,25},{25,17},{2,10},{10... | collective-permute-start | bytes 1376264 | tf_op jit(solution)/shard_map/ppermute | solution.py:259
  (26 other events, 145.2 us)

commit v8 on v7

--- a/solution.py
+++ b/solution.py
@@ -521,10 +521,10 @@
     normed = (values - mean) * inv
     y = normed * gain + shift
     sigma = jax.nn.sigmoid(y)
-    return sigma * (1.0 + y * (1.0 - sigma)), normed
-
-
-def slope_kernel(stat_ref, par_ref, rows_ref, cols_ref, own_ref, z_ref, slope_ref, normed_ref, sums_ref):
+    return sigma * (1.0 + y * (1.0 - sigma)), normed, y * sigma
+
+
+def slope_kernel(stat_ref, par_ref, rows_ref, cols_ref, own_ref, z_ref, slope_ref, normed_ref, lead_ref, sums_ref):
     images = rows_ref.shape[0]
     width = z_ref.shape[1]
     mean, inv = get(stat_ref, 0, 4), get(stat_ref, 4, 4)
@@ -532,8 +532,10 @@
     pieces = len(z_ref.parts)
     sums, cross = [], []
     for i in range(pieces):
-        slope, normed = slope_of(z_ref.chunk(i), mean, inv, gain, shift)
-        slope = slope * wide(own_ref.chunk(i), width)
+        slope, normed, a = slope_of(z_ref.chunk(i), mean, inv, gain, shift)
+        mask = wide(own_ref.chunk(i), width)
+        slope, a = slope * mask, a * mask
+        lead_ref.put(i, a[:, : width // 2] - a[:, width // 2 :])
         normed_ref.put(i, normed)
         slope_ref.put(i, slope)
         sums.append(image_sum(slope, images // pieces))
@@ -640,9 +642,8 @@
         gm_ref[z_ref.parts[i]] = product(split(dz), (wh_ref[...], wl_ref[...]), NT)
     gm = gm_ref[...]
     gm_ref.send()
-    a = a_ref[...]
     weights = weights_ref[...]
-    gate = image_sum(gm * (a[:, :mid] - a[:, mid:]), images)
+    gate = image_sum(gm * a_ref[...], images)
     dsum = weights[:, :mid] * weights[:, mid:] * gate
     dsum_ref[...] = dsum
     tile[...] = jnp.zeros_like(tile)
@@ -1011,12 +1012,12 @@
         near_outs=(3,),
     )
     g3 = share(pay)
-    slope_two, normed_two, slopes = call(
+    slope_two, normed_two, lead_two, slopes = call(
         slope_kernel,
-        [((cells, duo), f32), ((cells, duo), f32), ((count, 2 * duo), f32)],
+        [((cells, duo), f32), ((cells, duo), f32), ((cells, mid), f32), ((count, 2 * duo), f32)],
         [stat2, par, valid_rows, valid_cols, own, z_two],
         chunks={4: 2, 5: 2},
-        out_chunks={0: 2, 1: 2},
+        out_chunks={0: 2, 1: 2, 2: 2},
     )
     mixed, z_three, weights, fc_normed, fc_pre, fc_act, fc_inv, pay = call(
         expand_kernel,
@@ -1048,7 +1049,7 @@
         functools.partial(mixed_kernel, depth),
         [((cells, mid), f32), ((count, mid), f32),
          ((16, 128), f32), ((8, 128), f32), ((8, 128), f32), ((depth.size * count, 2 * duo), f32), pay16],
-        [g5, stat1, stat3, par, own, grad_pre, z_three, weh, wel, a_two, weights, w_excite, slope_two, normed_two, *slopes],
+        [g5, stat1, stat3, par, own, grad_pre, z_three, weh, wel, lead_two, weights, w_excite, slope_two, normed_two, *slopes],
         [tile16],
         after=[tph],
         near=(0, *range(14, 14 + depth.size)),

time: 222 us -> 222 us (level)
  no operation moved by 1% of the time
where the time goes in v8:
time: 222 us; the launch traced here: 221 us
  Pallas kernels  85.4 us (38%)
  starting transfers between devices  78.7 us (35%)
  waiting for transfers between devices  55.6 us (25%)
    pallas_call x20, Pallas kernels, call(): pl.pallas_call(inner, out_shape=[(pltpu.VMEM if i in near_outs else pltpu...  83 us
    ppermute x35, starting transfers between devices, flip(): lax.ppermute(values, axis, [(i, i ^ bits) for i in range(lax.axis_size(ax...  40.1 us
    ppermute x35, waiting for transfers between devices, flip(): lax.ppermute(values, axis, [(i, i ^ bits) for i in range(lax.axis_size(ax...  32.3 us
    all_to_all x7, starting transfers between devices, share(): return lax.all_to_all(tile, both, 0, 0)  26.2 us
    all_to_all x7, waiting for transfers between devices, share(): return lax.all_to_all(tile, both, 0, 0)  18.1 us
    ppermute x2, starting transfers between devices, halos(): above = lax.ppermute(last, 'rows', [(i, i + 1) for i in range(count - 1)])  6.09 us
  transfers between devices with their start and end apart: 47, of which 29 were waited for; matrix products, arithmetic and copies ran while one was open for 0% of the time, Pallas kernels for 22%

profile of v8, /device:TPU:0, one launch (start us, length us, event | category | flops | bytes accessed | tf_op | source)
XLA Modules:
  0.0 221.0 jit_solution(9315632018107576710)
XLA Ops:
  0.6 4.5 %shard_map.297 = (f32[512,256]{1,0:T(8,128)}, f32[8,6,16,128]{3,2,1,0:T(8,128)}, f32[512,128]{1,0:T(8,128)}, f32[128,256]{1,0:T(8,128)S(1)}, f32[128,256]{1,0:T(8,128)S(1)}, /*index=5*/f32[32,8,128]{2,1,0:T(8,128)}) custom-call(s32[8,16]{1,0:T(8,128)} %refs_9_.1, s32[8,16]{1,0:T(8,128)} %refs_10_.1, f32[1024,256]{1,0:T(8,128)} %refs_2_.5, f32[512,1024]{1,0:T(8,128)} %bitcast.24), custom_call_target="tpu_custom_call" | custom-call | flops 1 | bytes 1 | tf_op jit(solution)/shard_map/pallas_call | solution.py:205
  5.1 7.3 %all-to-all-start = ((f32[32,8,128]{2,1,0:T(8,128)}), f32[32,8,128]{2,1,0:T(8,128)S(1)}, u32[]{:S(2)}, u32[]{:S(2)}) async-start(f32[32,8,128]{2,1,0:T(8,128)} %get-tuple-element.121), calls=%async_computation | async-start | bytes 262144 | tf_op jit(solution)/shard_map/all_to_all | solution.py:248
  12.4 3.7 %collective-permute-start = (f32[128,256]{1,0:T(8,128)S(1)}, f32[128,256]{1,0:T(8,128)S(1)}, u32[]{:S(2)}, u32[]{:S(2)}) collective-permute-start(f32[128,256]{1,0:T(8,128)S(1)} %get-tuple-element.125), channel_id=1, source_target_pairs={{0,8},{8,16},{16,24},{1,9},{9,17},{17,25},{2,10},{10,18},{18,26},{... | collective-permute-start | bytes 393224 | tf_op jit(solution)/shard_map/ppermute | solution.py:253
  17.4 4.5 %shard_map.298 = (bf16[1152,256]{1,0:T(8,128)(2,1)}, bf16[1152,256]{1,0:T(8,128)(2,1)}, bf16[1152,256]{1,0:T(8,128)(2,1)}, bf16[1152,256]{1,0:T(8,128)(2,1)}, bf...) custom-call(f32[1152,512]{1,0:T(8,128)} %bitcast.29, ...), custom_call_target="tpu_custom_call" | custom-call | flops 1 | bytes 1 | tf_op jit(solution)/shard_map/pallas_call | solution.py:205
  24.3 5.9 %shard_map.299 = (f32[512,512]{1,0:T(8,128)}, f32[768,256]{1,0:T(8,128)}, f32[8,128]{1,0:T(8,128)}, f32[32,128]{1,0:T(8,128)}, f32[32,8,128]{2,1,0:T(8,128)}) custom-call(f32[32,8,128]{2,1,0:T(8,128)S(1)} %all-to-all-done.refs_0_, f32[40,128]{1,0:T(8,128)} %get-tuple-element.123.refs_1_.refs_2_.refs_3_.refs_4_.refs_0_, ...), custom_call_target="tpu_custom_call" | custom-call | flops 1 | bytes 1 | tf_op jit(solution)/shard_map/pallas_call | solution.py:205
  30.2 4.5 %all-to-all-start.1 = ((f32[32,8,128]{2,1,0:T(8,128)}), f32[32,8,128]{2,1,0:T(8,128)S(1)}, u32[]{:S(2)}, u32[]{:S(2)}) async-start(f32[32,8,128]{2,1,0:T(8,128)} %get-tuple-element.132), calls=%async_computation.1 | async-start | bytes 262144 | tf_op jit(solution)/shard_map/all_to_all | solution.py:248
  34.7 3.5 %shard_map.300 = (bf16[1024,512]{1,0:T(8,128)(2,1)}, bf16[1024,512]{1,0:T(8,128)(2,1)}) custom-call(f32[512,1024]{1,0:T(8,128)} %bitcast.25, f32[8,128]{1,0:T(8,128)} %get-tuple-element.135.refs_1_.refs_7_.refs_2_), custom_call_target="tpu_custom_call" | custom-call | flops 1 | bytes 1 | tf_op jit(solution)/shard_map/pallas_call | solution.py:205
  38.3 4.6 %all-to-all-done.1.refs_0_ = f32[32,8,128]{2,1,0:T(8,128)S(1)} async-done(((f32[32,8,128]{2,1,0:T(8,128)}), f32[32,8,128]{2,1,0:T(8,128)S(1)}, u32[]{:S(2)}, u32[]{:S(2)}) %all-to-all-start.1) | async-done | bytes 131104 | tf_op jit(solution)/shard_map/all_to_all | solution.py:248
  51.7 5.0 %all-to-all-done.2.refs_0_ = f32[32,8,128]{2,1,0:T(8,128)S(1)} async-done(((f32[32,8,128]{2,1,0:T(8,128)}), f32[32,8,128]{2,1,0:T(8,128)S(1)}, u32[]{:S(2)}, u32[]{:S(2)}) %all-to-all-start.2) | async-done | bytes 131104 | tf_op jit(solution)/shard_map/all_to_all | solution.py:248
  56.7 4.4 %shard_map.303 = (f32[512,256]{1,0:T(8,128)}, f32[512,1024]{1,0:T(8,128)}, f32[8,512]{1,0:T(8,128)}, f32[64,128]{1,0:T(8,128)}, f32[64,128]{1,0:T(8,128)}, /*ind...) custom-call(f32[32,8,128]{2,1,0:T(8,128)S(1)} %all-to-all-done.2.refs_0_, ...), custom_call_target="tpu_custom_call" | custom-call | flops 1 | bytes 1 | tf_op jit(solution)/shard_map/pallas_call | solution.py:205
  74.2 5.4 %shard_map.304 = (f32[512,1024]{1,0:T(8,128)}, f32[16,128]{1,0:T(8,128)}, f32[8,1024]{1,0:T(8,128)S(1)}, f32[32,16,128]{2,1,0:T(8,128)}) custom-call(f32[32,16,128]{2,1,0:T(8,128)S(1)} %all-to-all-done.3.refs_0_, f32[32,128]{1,0:T(8,128)} %get-tuple-element.133.refs_1_, f32[40,128]{1,0:T(8,128)} %get-tuple-element.123.refs_1_.refs_2_.refs_3_.refs_4_.refs_0_, ...), custom_call_target="tpu_custom_call" | custom-call | flops 1 | bytes 1 | tf_op jit(solution)/shard_map/pallas_call | solution.py:205
  82.2 3.7 %collective-permute-start.7 = (f32[8,1024]{1,0:T(8,128)S(1)}, f32[8,1024]{1,0:T(8,128)S(1)}, u32[]{:S(2)}, u32[]{:S(2)}) collective-permute-start(f32[8,1024]{1,0:T(8,128)S(1)} %get-tuple-element.152.refs_14_), channel_id=1, source_target_pairs={{0,6},{1,7},{2,4},{3,5},{4,2},{5,3},{6,0},{7,1},{8,14},{9,15},{10,... | collective-permute-start | bytes 98312 | tf_op jit(solution)/shard_map/ppermute | solution.py:259
  86.7 4.1 %shard_map.305 = (bf16[2,1152,512]{2,1,0:T(8,128)(2,1)}, bf16[2,1152,512]{2,1,0:T(8,128)(2,1)}) custom-call(f32[768,256]{1,0:T(8,128)} %get-tuple-element.153.refs_0_, f32[16,128]{1,0:T(8,128)} %get-tuple-element.145.refs_1_.refs_2_.refs_0_), custom_call_target="tpu_custom_call" | custom-call | flops 1 | bytes 1 | tf_op jit(solution)/shard_map/pallas_call | solution.py:205
  94.4 6.6 %shard_map.306 = (f32[512,256]{1,0:T(8,128)}, f32[8,256]{1,0:T(8,128)}, f32[16,128]{1,0:T(8,128)}, f32[8,128]{1,0:T(8,128)}, f32[8,128]{1,0:T(8,128)}, /*index=5*/f32[32,1024]{1,0:T(8,128)S(1)}, f32[32,16,128]{2,1,0:T(8,128)}) custom-call(f32[32,16,128]{2,1,0:T(8,128)S(1)} %all-to-all-done.4.refs_0_, f32[8,128]{1,0:T(8,128)} %get-tuple-element.135.refs_1_.refs_7_.refs_2_, ...), custom_call_target="tpu_custom_call" | custom-call | flops 1 | bytes 1 | tf_op jit(solution)/shard_map/pallas_call | solution.py:205
  101.0 3.5 %all-to-all-start.5 = ((f32[32,16,128]{2,1,0:T(8,128)}), f32[32,16,128]{2,1,0:T(8,128)S(1)}, u32[]{:S(2)}, u32[]{:S(2)}) async-start(f32[32,16,128]{2,1,0:T(8,128)} %get-tuple-element.161), calls=%async_computation.5 | async-start | bytes 524288 | tf_op jit(solution)/shard_map/all_to_all | solution.py:248
  104.9 5.2 %shard_map.307 = (f32[512,256]{1,0:T(8,128)}, f32[512,256]{1,0:T(8,128)}, f32[128,256]{1,0:T(8,128)}) custom-call(f32[16,128]{1,0:T(8,128)} %get-tuple-element.155.refs_0_, f32[8,128]{1,0:T(8,128)} %get-tuple-element.135.refs_1_.refs_7_.refs_2_, f32[16,128]{1,0:T(8,128)} %get-tuple-element.145.refs_1_.refs_2_.refs_0_, ...), custom_call_target="tpu_custom_call" | custom-call | flops 1 | bytes 1 | tf_op jit(solution)/shard_map/pallas_call | solution.py:205
  110.1 4.8 %all-to-all-done.5.refs_0_ = f32[32,16,128]{2,1,0:T(8,128)S(1)} async-done(((f32[32,16,128]{2,1,0:T(8,128)}), f32[32,16,128]{2,1,0:T(8,128)S(1)}, u32[]{:S(2)}, u32[]{:S(2)}) %all-to-all-start.5) | async-done | bytes 262176 | tf_op jit(solution)/shard_map/all_to_all | solution.py:248
  114.9 4.1 %shard_map.308 = (f32[128,256]{1,0:T(8,128)S(1)}, f32[128,256]{1,0:T(8,128)S(1)}, bf16[8,6,16,256]{3,2,1,0:T(8,128)(2,1)}, bf16[8,6,16,256]{3,2,1,0:T(8,128)(2,1...) custom-call(f32[32,16,128]{2,1,0:T(8,128)S(1)} %all-to-all-done.5.re, ...), custom_call_target="tpu_custom_call" | custom-call | flops 1 | bytes 1 | tf_op jit(solution)/shard_map/pallas_call | solution.py:205
  123.0 5.4 %shard_map.309 = (f32[1280,256]{1,0:T(8,128)S(1)}, f32[1280,256]{1,0:T(8,128)S(1)}) custom-call(bf16[8,6,16,256]{3,2,1,0:T(8,128)(2,1)} %get-tuple-element.169.refs_0_.refs_6_, bf16[8,6,16,256]{3,2,1,0:T(8,128)(2,1)} %get-tuple-element.170.refs_1_.refs_7_, bf16[8,6,16,256]{3,2,1,0:T(8,128)(2,1)} %get-tuple-element.171.refs_2_.refs_6_, ...), custom_call_target="tpu_custom_call" | custom-call | flops 1 | bytes 1 | tf_op jit(solution)/shard_map/pallas_call | solution.py:205
  130.3 4.1 %shard_map.311 = (f32[512,128]{1,0:T(8,128)}, f32[8,128]{1,0:T(8,128)}) custom-call(f32[40,128]{1,0:T(8,128)} %get-tuple-element.123.refs_1_.refs_2_.refs_3_.refs_4_.refs_0_, f32[8,128]{1,0:T(8,128)} %get-tuple-element.135.refs_1_.refs_7_.refs_2_, f32[512,256]{1,0:T(8,128)} %get-tuple-element.122.refs_12_.refs_2_.refs_5_, ...), custom_call_target="tpu_custom_call" | custom-call | flops 1 | bytes 1 | tf_op jit(solution)/shard_map/pallas_call | solution.py:205
  138.3 4.8 %shard_map.313 = (f32[512,128]{1,0:T(8,128)}, f32[32,8,128]{2,1,0:T(8,128)}) custom-call(f32[40,128]{1,0:T(8,128)} %get-tuple-element.123.refs_1_.refs_2_.refs_3_.refs_4_.refs_0_, f32[8,128]{1,0:T(8,128)} %get-tuple-element.135.refs_1_.refs_7_.refs_2_, f32[512,256]{1,0:T(8,128)} %get-tuple-element.122.refs_12_.refs_2_.refs_5_, ...), custom_call_target="tpu_custom_call" | custom-call | flops 1 | bytes 1 | tf_op jit(solution)/shard_map/pallas_call | solution.py:205
  168.1 4.2 %shard_map.318.refs_4_ = f32[512,1024]{1,0:T(8,128)} custom-call(bf16[512,256]{1,0:T(8,128)(2,1)} %get-tuple-element.199.refs_0_, bf16[512,256]{1,0:T(8,128)(2,1)} %get-tuple-element.200.refs_1_, bf16[1024,256]{1,0:T(8,128)(2,1)} %get-tuple-element.201.refs_2_, bf16[1024,256]{1,0:T(8,128)(2,1)} %get-tuple-element.202.refs_3_, ...), custom_call_target="tpu_custom_call" | custom-call | flops 1 | bytes 1 | tf_op jit(solution)/shard_map/pallas_call | solution.py:205
  180.2 3.7 %shard_map.321 = (f32[512,1024]{1,0:T(8,128)}, f32[8,128]{1,0:T(8,128)}) custom-call(f32[16,128]{1,0:T(8,128)} %get-tuple-element.145.refs_1_.refs_2_.refs_0_, f32[40,128]{1,0:T(8,128)} %get-tuple-element.123.refs_1_.refs_2_.refs_3_.refs_4_.refs_0_, f32[512,128]{1,0:T(8,128)} %get-tuple-element.127.refs_6_.refs_4_.refs_3_.refs_7_.refs_14_.refs_2_, ...), custom_call_target="tpu_custom_call" | custom-call | flops 1 | bytes 1 | tf_op jit(solution)/shard_map/pallas_call | solution.py:205
  183.8 4.0 %collective-permute-done.25.refs_2_ = f32[112,256]{1,0:T(8,128)S(1)} collective-permute-done((f32[112,256]{1,0:T(8,128)S(1)}, f32[112,256]{1,0:T(8,128)S(1)}, u32[]{:S(2)}, u32[]{:S(2)}) %collective-permute-start.25) | collective-permute-done | bytes 114720 | tf_op jit(solution)/shard_map/ppermute | solution.py:259
  (109 shorter events, 108.1 us)
Async XLA Ops:
  5.1 19.2 %all-to-all-start = ((f32[32,8,128]{2,1,0:T(8,128)}), f32[32,8,128]{2,1,0:T(8,128)S(1)}, u32[]{:S(2)}, u32[]{:S(2)}) async-start(f32[32,8,128]{2,1,0:T(8,128)} %get-tuple-element.121), calls=%async_computation | async-start | bytes 262144 | tf_op jit(solution)/shard_map/all_to_all | solution.py:248
  12.4 9.5 %collective-permute-start = (f32[128,256]{1,0:T(8,128)S(1)}, f32[128,256]{1,0:T(8,128)S(1)}, u32[]{:S(2)}, u32[]{:S(2)}) collective-permute-start(f32[128,256]{1,0:T(8,128)S(1)} %get-tuple-element.125), channel_id=1, source_target_pairs={{0,8},{8,16},{16,24},{1,9},{9,17},{17,25},{2,10},{10,18},{18,26},{... | collective-permute-start | bytes 393224 | tf_op jit(solution)/shard_map/ppermute | solution.py:253
  16.1 8.2 %collective-permute-start.1 = (f32[128,256]{1,0:T(8,128)S(1)}, f32[128,256]{1,0:T(8,128)S(1)}, u32[]{:S(2)}, u32[]{:S(2)}) collective-permute-start(f32[128,256]{1,0:T(8,128)S(1)} %get-tuple-element.126), channel_id=1, source_target_pairs={{8,0},{16,8},{24,16},{9,1},{17,9},{25,17},{10,2},{18,10},{26,18},{... | collective-permute-start | bytes 393224 | tf_op jit(solution)/shard_map/ppermute | solution.py:254
  30.2 12.6 %all-to-all-start.1 = ((f32[32,8,128]{2,1,0:T(8,128)}), f32[32,8,128]{2,1,0:T(8,128)S(1)}, u32[]{:S(2)}, u32[]{:S(2)}) async-start(f32[32,8,128]{2,1,0:T(8,128)} %get-tuple-element.132), calls=%async_computation.1 | async-start | bytes 262144 | tf_op jit(solution)/shard_map/all_to_all | solution.py:248
  46.0 10.8 %all-to-all-start.2 = ((f32[32,8,128]{2,1,0:T(8,128)}), f32[32,8,128]{2,1,0:T(8,128)S(1)}, u32[]{:S(2)}, u32[]{:S(2)}) async-start(f32[32,8,128]{2,1,0:T(8,128)} %get-tuple-element.137), calls=%async_computation.2 | async-start | bytes 262144 | tf_op jit(solution)/shard_map/all_to_all | solution.py:248
  61.2 13.0 %all-to-all-start.3 = ((f32[32,16,128]{2,1,0:T(8,128)}), f32[32,16,128]{2,1,0:T(8,128)S(1)}, u32[]{:S(2)}, u32[]{:S(2)}) async-start(f32[32,16,128]{2,1,0:T(8,128)} %get-tuple-element.143), calls=%async_computation.3 | async-start | bytes 524288 | tf_op jit(solution)/shard_map/all_to_all | solution.py:248
  79.6 14.8 %all-to-all-start.4 = ((f32[32,16,128]{2,1,0:T(8,128)}), f32[32,16,128]{2,1,0:T(8,128)S(1)}, u32[]{:S(2)}, u32[]{:S(2)}) async-start(f32[32,16,128]{2,1,0:T(8,128)} %get-tuple-element.146), calls=%async_computation.4 | async-start | bytes 524288 | tf_op jit(solution)/shard_map/all_to_all | solution.py:248
  82.2 10.1 %collective-permute-start.7 = (f32[8,1024]{1,0:T(8,128)S(1)}, f32[8,1024]{1,0:T(8,128)S(1)}, u32[]{:S(2)}, u32[]{:S(2)}) collective-permute-start(f32[8,1024]{1,0:T(8,128)S(1)} %get-tuple-element.152.refs_14_), channel_id=1, source_target_pairs={{0,6},{1,7},{2,4},{3,5},{4,2},{5,3},{6,0},{7,1},{8,14},{9,15},{10,... | collective-permute-start | bytes 98312 | tf_op jit(solution)/shard_map/ppermute | solution.py:259
  85.9 8.5 %collective-permute-start.6 = (f32[8,1024]{1,0:T(8,128)S(1)}, f32[8,1024]{1,0:T(8,128)S(1)}, u32[]{:S(2)}, u32[]{:S(2)}) collective-permute-start(f32[8,1024]{1,0:T(8,128)S(1)} %get-tuple-element.152.refs_14_), channel_id=1, source_target_pairs={{0,4},{1,5},{2,6},{3,7},{4,0},{5,1},{6,2},{7,3},{8,12},{9,13},{10,... | collective-permute-start | bytes 98312 | tf_op jit(solution)/shard_map/ppermute | solution.py:259
  85.9 8.5 %collective-permute-start.5 = (f32[8,1024]{1,0:T(8,128)S(1)}, f32[8,1024]{1,0:T(8,128)S(1)}, u32[]{:S(2)}, u32[]{:S(2)}) collective-permute-start(f32[8,1024]{1,0:T(8,128)S(1)} %get-tuple-element.152.refs_14_), channel_id=1, source_target_pairs={{0,2},{1,3},{2,0},{3,1},{4,6},{5,7},{6,4},{7,5},{8,10},{9,11},{10,... | collective-permute-start | bytes 98312 | tf_op jit(solution)/shard_map/ppermute | solution.py:259
  101.0 13.9 %all-to-all-start.5 = ((f32[32,16,128]{2,1,0:T(8,128)}), f32[32,16,128]{2,1,0:T(8,128)S(1)}, u32[]{:S(2)}, u32[]{:S(2)}) async-start(f32[32,16,128]{2,1,0:T(8,128)} %get-tuple-element.161), calls=%async_computation.5 | async-start | bytes 524288 | tf_op jit(solution)/shard_map/all_to_all | solution.py:248
  119.0 9.3 %collective-permute-start.10 = (f32[128,256]{1,0:T(8,128)S(1)}, f32[128,256]{1,0:T(8,128)S(1)}, u32[]{:S(2)}, u32[]{:S(2)}) collective-permute-start(f32[128,256]{1,0:T(8,128)S(1)} %get-tuple-element.177), channel_id=1, source_target_pairs={{0,8},{8,16},{16,24},{1,9},{9,17},{17,25},{2,10},{10,18},{18,26},{... | collective-permute-start | bytes 393224 | tf_op jit(solution)/shard_map/ppermute | solution.py:253
  121.5 8.3 %collective-permute-start.11 = (f32[128,256]{1,0:T(8,128)S(1)}, f32[128,256]{1,0:T(8,128)S(1)}, u32[]{:S(2)}, u32[]{:S(2)}) collective-permute-start(f32[128,256]{1,0:T(8,128)S(1)} %get-tuple-element.178), channel_id=1, source_target_pairs={{8,0},{16,8},{24,16},{9,1},{17,9},{25,17},{10,2},{18,10},{26,18},{... | collective-permute-start | bytes 393224 | tf_op jit(solution)/shard_map/ppermute | solution.py:254
  135.4 13.2 %collective-permute-start.13 = (f32[448,256]{1,0:T(8,128)}, f32[448,256]{1,0:T(8,128)S(1)}, u32[]{:S(2)}, u32[]{:S(2)}) collective-permute-start(f32[448,256]{1,0:T(8,128)} %get-tuple-element.181), channel_id=1, source_target_pairs={{0,8},{8,0},{16,24},{24,16},{1,9},{9,1},{17,25},{25,17},{2,10},{10... | collective-permute-start | bytes 1376264 | tf_op jit(solution)/shard_map/ppermute | solution.py:259
  137.4 12.5 %collective-permute-start.14 = (f32[448,256]{1,0:T(8,128)S(1)}, f32[448,256]{1,0:T(8,128)S(1)}, u32[]{:S(2)}, u32[]{:S(2)}) collective-permute-start(f32[448,256]{1,0:T(8,128)S(1)} %get-tuple-element.183), channel_id=1, source_target_pairs={{0,16},{8,24},{16,0},{24,8},{1,17},{9,25},{17,1},{25,9},{2,18},{10... | collective-permute-start | bytes 1376264 | tf_op jit(solution)/shard_map/ppermute | solution.py:259
  143.1 11.1 %all-to-all-start.6 = ((f32[32,8,128]{2,1,0:T(8,128)}), f32[32,8,128]{2,1,0:T(8,128)S(1)}, u32[]{:S(2)}, u32[]{:S(2)}) async-start(f32[32,8,128]{2,1,0:T(8,128)} %get-tuple-element.189), calls=%async_computation.6 | async-start | bytes 262144 | tf_op jit(solution)/shard_map/all_to_all | solution.py:248
  159.0 16.6 %all-to-all-start.7 = ((f32[4,112,256]{2,1,0:T(8,128)}), f32[4,112,256]{2,1,0:T(8,128)S(1)}, u32[]{:S(2)}, u32[]{:S(2)}) async-start(f32[4,112,256]{2,1,0:T(8,128)} %shard_map.316), calls=%async_computation.7 | async-start | bytes 917504 | tf_op jit(solution)/shard_map/all_to_all | solution.py:280
  175.7 8.1 %collective-permute-start.26 = (f32[112,256]{1,0:T(8,128)S(1)}, f32[112,256]{1,0:T(8,128)S(1)}, u32[]{:S(2)}, u32[]{:S(2)}) collective-permute-start(f32[112,256]{1,0:T(8,128)S(1)} %shard_map.320.refs_5_.refs_0_), channel_id=1, source_target_pairs={{0,6},{1,7},{2,4},{3,5},{4,2},{5,3},{6,0},{7,1},{8,14},{9,15},{10,... | collective-permute-start | bytes 344072 | tf_op jit(solution)/shard_map/ppermute | solution.py:259
  178.1 9.8 %collective-permute-start.25 = (f32[112,256]{1,0:T(8,128)S(1)}, f32[112,256]{1,0:T(8,128)S(1)}, u32[]{:S(2)}, u32[]{:S(2)}) collective-permute-start(f32[112,256]{1,0:T(8,128)S(1)} %shard_map.320.refs_5_.refs_0_), channel_id=1, source_target_pairs={{0,4},{1,5},{2,6},{3,7},{4,0},{5,1},{6,2},{7,3},{8,12},{9,13},{10,... | collective-permute-start | bytes 344072 | tf_op jit(solution)/shard_map/ppermute | solution.py:259
  178.1 9.8 %collective-permute-start.24 = (f32[112,256]{1,0:T(8,128)S(1)}, f32[112,256]{1,0:T(8,128)S(1)}, u32[]{:S(2)}, u32[]{:S(2)}) collective-permute-start(f32[112,256]{1,0:T(8,128)S(1)} %shard_map.320.refs_5_.refs_0_), channel_id=1, source_target_pairs={{0,2},{1,3},{2,0},{3,1},{4,6},{5,7},{6,4},{7,5},{8,10},{9,11},{10,... | collective-permute-start | bytes 344072 | tf_op jit(solution)/shard_map/ppermute | solution.py:259
  187.9 10.1 %collective-permute-start.31 = (f32[224,256]{1,0:T(8,128)S(1)}, f32[224,256]{1,0:T(8,128)S(1)}, u32[]{:S(2)}, u32[]{:S(2)}) collective-permute-start(f32[224,256]{1,0:T(8,128)S(1)} %get-tuple-element.210.refs_2_), channel_id=1, source_target_pairs={{0,8},{8,0},{16,24},{24,16},{1,9},{9,1},{17,25},{25,17},{2,10},{10... | collective-permute-start | bytes 688136 | tf_op jit(solution)/shard_map/ppermute | solution.py:259
  188.0 10.0 %collective-permute-start.30 = (f32[224,256]{1,0:T(8,128)S(1)}, f32[224,256]{1,0:T(8,128)S(1)}, u32[]{:S(2)}, u32[]{:S(2)}) collective-permute-start(f32[224,256]{1,0:T(8,128)S(1)} %get-tuple-element.209.refs_4_.refs_0_), channel_id=1, source_target_pairs={{0,16},{8,24},{16,0},{24,8},{1,17},{9,25},{17,1},{25,9},{2,18},{10... | collective-permute-start | bytes 688136 | tf_op jit(solution)/shard_map/ppermute | solution.py:259
  198.1 9.4 %collective-permute-start.36 = (f32[448,256]{1,0:T(8,128)S(1)}, f32[448,256]{1,0:T(8,128)S(1)}, u32[]{:S(2)}, u32[]{:S(2)}) collective-permute-start(f32[448,256]{1,0:T(8,128)S(1)} %get-tuple-element.212.refs_2_), channel_id=1, source_target_pairs={{0,16},{8,24},{16,0},{24,8},{1,17},{9,25},{17,1},{25,9},{2,18},{10... | collective-permute-start | bytes 1376264 | tf_op jit(solution)/shard_map/ppermute | solution.py:259
  198.9 9.0 %collective-permute-start.35 = (f32[448,256]{1,0:T(8,128)S(1)}, f32[448,256]{1,0:T(8,128)S(1)}, u32[]{:S(2)}, u32[]{:S(2)}) collective-permute-start(f32[448,256]{1,0:T(8,128)S(1)} %get-tuple-element.211.refs_4_.refs_0_), channel_id=1, source_target_pairs={{0,8},{8,0},{16,24},{24,16},{1,9},{9,1},{17,25},{25,17},{2,10},{10... | collective-permute-start | bytes 1376264 | tf_op jit(solution)/shard_map/ppermute | solution.py:259
  (26 other events, 144.9 us)
